TPU v7x, 32 devices: a whole 2x2x4 slice. The times are simulated.
32 devices in a mesh: dp: 16 (over z, y, x), mp: 2 (over core).
Axes of the slice: x: 2, y: 2, z: 4, core: 2. Of those that a mesh axis runs over, the one named last changes fastest.
Arguments:
- inputs: bfloat16 [4, 2048, 2048], P(None, 'dp'), may hold values from -6 to 6
- doc_spans: int32 [4, 2], replicated, may hold values from 32 to 2016, as said below
- doc_lengths: int32 [4, 2], replicated, may hold values from 1 to 2016, as said below
- state_in: float32 [4, 2, 2560], P(None, None, 'mp'), may hold values from -6 to 6
- conv_in: bfloat16 [4, 2, 3, 2560], P(None, None, None, 'mp'), may hold values from -6 to 6
- norm_gains: bfloat16 [2, 2048], P(None, 'dp'), may hold values from 0.5 to 1.5
- w_x: bfloat16 [2048, 2560], P('dp', 'mp'), may hold values from -0.125 to 0.125
- w_g: bfloat16 [2048, 2560], P('dp', 'mp'), may hold values from -0.125 to 0.125
- rec_params: bfloat16 [2, 1280, 8], P('mp', 'dp')
- gate_weights: bfloat16 [2, 1280, 320], P('mp', 'dp'), may hold values from -0.5 to 0.5
- w_o: bfloat16 [2560, 2048], P('mp', 'dp'), may hold values from -0.125 to 0.125
- w_gate: bfloat16 [2048, 6144], P('dp', 'mp'), may hold values from -0.125 to 0.125
- w_up: bfloat16 [2048, 6144], P('dp', 'mp'), may hold values from -0.125 to 0.125
- w_down: bfloat16 [6144, 2048], P('mp', 'dp'), may hold values from -0.078125 to 0.078125
- cotangent: bfloat16 [4, 2048, 2048], P(None, 'dp'), may hold values from -6 to 6
Outputs:
- output: bfloat16 [4, 2048, 2048], P(None, 'dp')
- input_grad: bfloat16 [4, 2048, 2048], P(None, 'dp')
- final_state: float32 [4, 2, 2, 1280], P(None, None, 'mp', 'dp')
- final_conv: bfloat16 [4, 2, 3, 2, 1280], P(None, None, None, 'mp', 'dp')
- grad_gains: float32 [2, 2048], P(None, 'dp')
- grad_w_x: float32 [2048, 2560], P('dp', 'mp')
- grad_w_g: float32 [2048, 2560], P('dp', 'mp')
- grad_rec_params: float32 [2, 1280, 8], P('mp', 'dp')
- grad_gate_weights: float32 [2, 1280, 320], P('mp', 'dp')
- grad_w_o: float32 [2560, 2048], P('mp', 'dp')
- grad_w_gate: float32 [2048, 6144], P('dp', 'mp')
- grad_w_up: float32 [2048, 6144], P('dp', 'mp')
- grad_w_down: float32 [6144, 2048], P('mp', 'dp')
Inputs may be any that keep to these rules, and one draw needn't show every extreme that they name: Each stream is cut into two documents: the first takes doc_spans[s, 0] positions from the start, the second the remaining doc_spans[s, 1]; the two sum to 2048. Document d of stream s has doc_lengths[s, d] real tokens at the start of its positions, then padding; doc_lengths[s, d] <= doc_spans[s, d].
All inputs are finite; a program needn't handle non-finite values.
Results may differ from a plain program's by a relative error of at most 0.013.
Values may be sent and summed in bfloat16 or wider, within the bound.
A program may use at most 320 MiB of HBM per device.

v0:
```python
from functools import partial

import jax
import jax.numpy as jnp
from jax import lax
from jax.sharding import PartitionSpec as P

HEAD_DIM = 160


EPSILON = 1e-06


def shifted(block, axis, distance):
    devices = range(lax.axis_size(axis))
    route = [(i - distance, i) for i in devices if i - distance in devices]
    return lax.ppermute(block, axis, route)


def prefix(value, axis, join, neutral, backward):
    count, mine = (lax.axis_size(axis), lax.axis_index(axis))
    pieces = jax.tree.map(lambda part: lax.all_gather(part, axis), value)
    if backward:
        pieces = jax.tree.map(lambda part: part[::-1], pieces)
        mine = count - 1 - mine
    subtotal = jax.tree.map(
        lambda part, zero: jnp.full_like(part, 0) + jnp.asarray(zero, part.dtype), value, neutral
    )

    def turn(position, subtotal):
        longer = join(subtotal, jax.tree.map(lambda part: part[position], pieces))
        return jax.tree.map(lambda new, old: jnp.where(position < mine, new, old), longer, subtotal)

    return lax.fori_loop(0, count - 1, turn, subtotal)


def in_blocks(array, dim, size):
    before, after = (array.shape[:dim], array.shape[dim + 1 :])
    return jnp.moveaxis(array.reshape(*before, size, -1, *after), dim, 0)


def sent_and_summed(array, axis, dim):
    size = lax.axis_size(axis)
    tiles = lax.all_to_all(in_blocks(array, dim, size), axis, 0, 0, tiled=True)
    return jnp.sum(tiles.astype(jnp.float32), axis=0)


def in_one_piece(arrays, axis, dim, along):
    widths = [a.shape[along] for a in arrays]
    both = jnp.concatenate(arrays, axis=along)
    whole = sent_and_summed(both, axis, dim)
    return tuple(jnp.split(whole, [sum(widths[:k]) for k in range(1, len(widths))], axis=along))


def rms_norm(values, norm_gain):
    factor = lax.rsqrt(jnp.mean(values * values, axis=-1, keepdims=True) + EPSILON)
    return values * factor * norm_gain


def gate_math(pre_rate, pre_entry, lam_param, conv_value):
    rate_gate = jax.nn.sigmoid(pre_rate)
    entry_gate = jax.nn.sigmoid(pre_entry)
    log_decay = -8.0 * rate_gate * jax.nn.softplus(lam_param)
    retain = jnp.exp(log_decay)
    factor = jnp.sqrt(-jnp.expm1(2.0 * log_decay))
    return (retain, factor * entry_gate * conv_value)


def mix_gelu(gate_value, up_value):
    return jax.nn.gelu(gate_value) * up_value


def chain(earlier, latter):
    return (earlier[0] * latter[0], latter[0] * earlier[1] + latter[1])


def convolve(extended, conv_taps, conv_bias, fill_values, insides):
    n_rows = extended.shape[1] - 3
    result = conv_bias + conv_taps[:, 0] * extended[:, 3:]
    for offset in (1, 2, 3):
        window = extended[:, 3 - offset : 3 - offset + n_rows]
        result = result + conv_taps[:, offset] * jnp.where(
            insides[offset - 1], window, fill_values[offset - 1]
        )
    return result


def reduce_second(g_gain_two, g_wo, g_gate, g_up, g_down):
    return (
        lax.psum_scatter(g_gain_two[None], "dp", scatter_dimension=1, tiled=True),
        lax.psum_scatter(g_wo, "dp", scatter_dimension=1, tiled=True),
        lax.psum_scatter(g_gate, "dp", scatter_dimension=0, tiled=True),
        lax.psum_scatter(g_up, "dp", scatter_dimension=0, tiled=True),
        lax.psum_scatter(g_down, "dp", scatter_dimension=1, tiled=True),
    )


def shards(
    inputs,
    doc_spans,
    doc_lengths,
    state_in,
    conv_in,
    norm_gains,
    w_x,
    w_g,
    rec_params,
    gate_weights,
    w_o,
    w_gate,
    w_up,
    w_down,
    cotangent,
):
    n_streams, n_rows, model_width = inputs.shape
    tokens = n_streams * n_rows
    gathered = (
        lax.all_gather(norm_gains, "dp", axis=1, tiled=True),
        lax.all_gather(w_x, "dp", axis=0, tiled=True),
        lax.all_gather(w_g, "dp", axis=0, tiled=True),
        lax.all_gather(rec_params, "dp", axis=1, tiled=True),
        lax.all_gather(gate_weights, "dp", axis=1, tiled=True),
        lax.all_gather(w_o, "dp", axis=1, tiled=True),
        lax.all_gather(w_gate, "dp", axis=0, tiled=True),
        lax.all_gather(w_up, "dp", axis=0, tiled=True),
        lax.all_gather(w_down, "dp", axis=1, tiled=True),
    )
    gains_all = gathered[0].astype(jnp.float32)
    wx_all = gathered[1]
    wg_all = gathered[2]
    params_all = gathered[3][0].astype(jnp.float32)
    rec_width = wx_all.shape[1]
    heads_here = rec_width // HEAD_DIM
    gates_all = gathered[4][0].reshape(heads_here, HEAD_DIM, 2 * HEAD_DIM)
    wo_all = gathered[5]
    wgate_all = gathered[6]
    wup_all = gathered[7]
    wdown_all = gathered[8]
    dp_index = lax.axis_index("dp")
    position = dp_index * n_rows + jnp.arange(n_rows, dtype=jnp.int32)
    second_start = doc_spans[:, 0:1]
    doc_id = (position[None, :] >= second_start).astype(jnp.int32)
    doc_start = doc_id * second_start
    doc_stop = doc_start + jnp.where(doc_id == 1, doc_lengths[:, 1:2], doc_lengths[:, 0:1])
    live_rows = (position[None, :] < doc_stop).astype(jnp.float32).reshape(tokens, 1)
    flat_in = inputs.reshape(tokens, model_width).astype(jnp.float32)
    normed_one, norm_one_back = jax.vjp(rms_norm, flat_in, gains_all[0])
    normed_low = normed_one.astype(jnp.bfloat16)
    conv_source = jnp.dot(normed_low, wx_all, preferred_element_type=jnp.float32).astype(
        jnp.bfloat16
    )
    branch_pre = jnp.dot(normed_low, wg_all, preferred_element_type=jnp.float32)
    branch, branch_back = jax.vjp(jax.nn.gelu, branch_pre)
    source_rows = conv_source.reshape(n_streams, n_rows, rec_width)
    rim_rows = shifted(source_rows[:, n_rows - 3 :], "dp", 1)
    extended = jnp.concatenate([rim_rows, source_rows], axis=1).astype(jnp.float32)
    slot_range = jnp.arange(3, dtype=jnp.int32)
    doc_range = jnp.arange(2, dtype=jnp.int32)
    fill_values = []
    insides = []
    for offset in (1, 2, 3):
        earlier_pos = position[None, :] - offset
        insides.append((earlier_pos >= doc_start)[..., None])
        slot_pick = (doc_id[..., None, None] == doc_range[:, None]) & (
            (3 + earlier_pos - doc_start)[..., None, None] == slot_range
        )
        fill_values.append(
            jnp.einsum(
                "btds,bdsc->btc",
                slot_pick.astype(jnp.bfloat16),
                conv_in,
                preferred_element_type=jnp.float32,
            )
        )
    conv_value, conv_back = jax.vjp(
        partial(convolve, fill_values=fill_values, insides=insides),
        extended,
        params_all[:, 0:4],
        params_all[:, 4],
    )
    conv_flat = conv_value.reshape(tokens, rec_width)
    conv_low = conv_flat.astype(jnp.bfloat16).reshape(tokens, heads_here, HEAD_DIM)
    gate_mixed = jnp.einsum("nhk,hko->nho", conv_low, gates_all, preferred_element_type=jnp.float32)
    pre_rate = gate_mixed[..., :HEAD_DIM].reshape(tokens, rec_width) + params_all[:, 5]
    pre_entry = gate_mixed[..., HEAD_DIM:].reshape(tokens, rec_width) + params_all[:, 6]
    (retain, drive_term), gate_back = jax.vjp(
        gate_math, pre_rate, pre_entry, params_all[:, 7], conv_flat
    )
    reset_rows = (position[None, :] == doc_start)[..., None]
    carried = jnp.where((doc_id == 1)[..., None], state_in[:, None, 1], state_in[:, None, 0])
    retain_rows = retain.reshape(n_streams, n_rows, rec_width)
    retain_eff = jnp.where(reset_rows, 0.0, retain_rows)
    drive_eff = drive_term.reshape(n_streams, n_rows, rec_width) + jnp.where(
        reset_rows, retain_rows * carried, 0.0
    )
    local_keep, local_state = lax.associative_scan(chain, (retain_eff, drive_eff), axis=1)
    last_keep = local_keep[:, -1]
    last_state = local_state[:, -1]
    state_before = prefix(
        (last_keep, last_state),
        "dp",
        chain,
        (jnp.ones_like(last_keep), jnp.zeros_like(last_state)),
        False,
    )[1]
    states = local_state + local_keep * state_before[:, None]
    starts_doc = jnp.concatenate([jnp.zeros_like(doc_spans[:, :1]), doc_spans[:, :1]], axis=1)
    stops_doc = starts_doc + doc_lengths
    is_last = position[None, :, None] == (stops_doc - 1)[:, None, :]
    final_part = jnp.sum(jnp.where(is_last[..., None], states[:, :, None, :], 0.0), axis=1)
    tail_pos = stops_doc[..., None] - 3 + slot_range
    from_rows = (position[None, :, None, None] == tail_pos[:, None]) & (
        tail_pos >= starts_doc[..., None]
    )[:, None]
    conv_part = jnp.einsum(
        "btdj,btc->bdjc",
        from_rows.astype(jnp.bfloat16),
        source_rows,
        preferred_element_type=jnp.float32,
    )
    from_state = (
        (tail_pos < starts_doc[..., None])[..., None]
        & ((doc_lengths[..., None] + slot_range)[..., None] == slot_range)
        & (dp_index == 0)
    )
    conv_part = conv_part + jnp.einsum(
        "bdjs,bdsc->bdjc",
        from_state.astype(jnp.bfloat16),
        conv_in,
        preferred_element_type=jnp.float32,
    )
    final_state, final_conv = (
        lax.psum_scatter(final_part, "dp", scatter_dimension=2, tiled=True),
        lax.psum_scatter(conv_part, "dp", scatter_dimension=3, tiled=True),
    )
    states_flat = states.reshape(tokens, rec_width)
    mixed_rows = (states_flat * branch).astype(jnp.bfloat16)
    rec_part = jnp.dot(mixed_rows, wo_all, preferred_element_type=jnp.float32)
    rec_total = lax.psum(rec_part, "mp")
    hidden_one = flat_in + live_rows * rec_total
    normed_two, norm_two_back = jax.vjp(rms_norm, hidden_one, gains_all[1])
    second_low = normed_two.astype(jnp.bfloat16)
    gate_value = jnp.dot(second_low, wgate_all, preferred_element_type=jnp.float32)
    up_value = jnp.dot(second_low, wup_all, preferred_element_type=jnp.float32)
    activated, mix_back = jax.vjp(mix_gelu, gate_value, up_value)
    act_low = activated.astype(jnp.bfloat16)
    down_part = jnp.dot(act_low, wdown_all, preferred_element_type=jnp.float32)
    mlp_total = lax.psum(down_part.astype(jnp.bfloat16), "mp").astype(jnp.float32)
    out_flat = (hidden_one + live_rows * mlp_total).astype(jnp.bfloat16)
    d_out = cotangent.reshape(tokens, model_width).astype(jnp.float32)
    d_down = (d_out * live_rows).astype(jnp.bfloat16)
    d_act = jnp.dot(d_down, wdown_all.T, preferred_element_type=jnp.float32)
    g_down = jnp.dot(act_low.T, d_down, preferred_element_type=jnp.float32)
    d_gate_f, d_up_f = mix_back(d_act)
    d_gate = d_gate_f.astype(jnp.bfloat16)
    d_up = d_up_f.astype(jnp.bfloat16)
    g_gate = jnp.dot(second_low.T, d_gate, preferred_element_type=jnp.float32)
    g_up = jnp.dot(second_low.T, d_up, preferred_element_type=jnp.float32)
    second_part = jnp.dot(d_gate, wgate_all.T, preferred_element_type=jnp.float32) + jnp.dot(
        d_up, wup_all.T, preferred_element_type=jnp.float32
    )
    second_total = lax.psum(second_part, "mp")
    d_hidden_norm, g_gain_two = norm_two_back(second_total)
    d_hidden = d_out + d_hidden_norm
    d_rec = (d_hidden * live_rows).astype(jnp.bfloat16)
    g_wo = jnp.dot(mixed_rows.T, d_rec, preferred_element_type=jnp.float32)
    d_mixed = jnp.dot(d_rec, wo_all.T, preferred_element_type=jnp.float32)
    grad_state = (d_mixed * branch).reshape(n_streams, n_rows, rec_width)
    d_branch_f = d_mixed * states_flat
    branch_low = branch_back(d_branch_f)[0].astype(jnp.bfloat16)
    next_keep = jnp.concatenate([retain_eff[:, 1:], jnp.ones_like(retain_eff[:, :1])], axis=1)
    flip_keep, flip_sum = lax.associative_scan(
        chain, (next_keep[:, ::-1], grad_state[:, ::-1]), axis=1
    )
    later_keep = flip_keep[:, ::-1]
    later_sum = flip_sum[:, ::-1]
    send_keep = retain_eff[:, 0] * later_keep[:, 0]
    send_sum = retain_eff[:, 0] * later_sum[:, 0]
    carried_grad = prefix(
        (send_keep, send_sum),
        "dp",
        chain,
        (jnp.ones_like(send_keep), jnp.zeros_like(send_sum)),
        True,
    )[1]
    adjoint = later_sum + later_keep * carried_grad[:, None]
    state_prev = jnp.concatenate([state_before[:, None], states[:, :-1]], axis=1)
    state_prev = jnp.where(reset_rows, carried, state_prev)
    d_retain = (adjoint * state_prev).reshape(tokens, rec_width)
    d_rate, d_entry, g_lam, d_conv_direct = gate_back(
        (d_retain, adjoint.reshape(tokens, rec_width))
    )
    rate_low = d_rate.astype(jnp.bfloat16)
    entry_low = d_entry.astype(jnp.bfloat16)
    grad_gates = jnp.concatenate(
        [
            rate_low.reshape(tokens, heads_here, HEAD_DIM),
            entry_low.reshape(tokens, heads_here, HEAD_DIM),
        ],
        axis=2,
    )
    g_gates = jnp.einsum(
        "nhk,nho->hko", conv_low, grad_gates, preferred_element_type=jnp.float32
    ).reshape(rec_width, 2 * HEAD_DIM)
    d_conv_gates = jnp.einsum(
        "nho,hko->nhk", grad_gates, gates_all, preferred_element_type=jnp.float32
    ).reshape(tokens, rec_width)
    d_conv = (d_conv_direct + d_conv_gates).reshape(n_streams, n_rows, rec_width)
    d_extended, g_taps, g_conv_bias = conv_back(d_conv)
    rim_grad = shifted(d_extended[:, :3].astype(jnp.bfloat16), "dp", -1).astype(jnp.float32)
    d_source = jnp.concatenate([d_extended[:, 3:n_rows], d_extended[:, n_rows:] + rim_grad], axis=1)
    source_low = d_source.reshape(tokens, rec_width).astype(jnp.bfloat16)
    g_wx = jnp.dot(normed_low.T, source_low, preferred_element_type=jnp.float32)
    g_wg = jnp.dot(normed_low.T, branch_low, preferred_element_type=jnp.float32)
    first_part = jnp.dot(source_low, wx_all.T, preferred_element_type=jnp.float32) + jnp.dot(
        branch_low, wg_all.T, preferred_element_type=jnp.float32
    )
    first_total = lax.psum(first_part.astype(jnp.bfloat16), "mp").astype(jnp.float32)
    d_input_norm, g_gain_one = norm_one_back(first_total)
    input_grad = (
        (d_hidden + d_input_norm).astype(jnp.bfloat16).reshape(n_streams, n_rows, model_width)
    )
    g_params = jnp.concatenate(
        [
            g_taps,
            g_conv_bias[:, None],
            jnp.sum(rate_low.astype(jnp.float32), axis=0)[:, None],
            jnp.sum(entry_low.astype(jnp.float32), axis=0)[:, None],
            g_lam[:, None],
        ],
        axis=1,
    )
    second_summed = reduce_second(g_gain_two, g_wo, g_gate, g_up, g_down)
    first_summed = (
        sent_and_summed(g_gain_one[None].astype(jnp.bfloat16), "dp", 1),
        *in_one_piece((g_wx.astype(jnp.bfloat16), g_wg.astype(jnp.bfloat16)), "dp", 0, 1),
        *in_one_piece(
            (g_params[None].astype(jnp.bfloat16), g_gates[None].astype(jnp.bfloat16)), "dp", 1, 2
        ),
    )
    grad_gains = jnp.concatenate([first_summed[0], second_summed[0]], axis=0)
    output = out_flat.reshape(n_streams, n_rows, model_width)
    state_block = final_state[:, :, None, :]
    conv_block = final_conv.astype(jnp.bfloat16)[:, :, :, None, :]
    return (
        output,
        input_grad,
        state_block,
        conv_block,
        grad_gains,
        first_summed[1],
        first_summed[2],
        first_summed[3],
        first_summed[4],
        second_summed[1],
        second_summed[2],
        second_summed[3],
        second_summed[4],
    )


def solution(mesh):
    placed = (
        P(None, "dp", None),
        P(),
        P(),
        P(None, None, "mp"),
        P(None, None, None, "mp"),
        P(None, "dp"),
        P("dp", "mp"),
        P("dp", "mp"),
        P("mp", "dp", None),
        P("mp", "dp", None),
        P("mp", "dp"),
        P("dp", "mp"),
        P("dp", "mp"),
        P("mp", "dp"),
        P(None, "dp", None),
    )
    return jax.shard_map(
        shards,
        mesh=mesh,
        in_specs=placed,
        out_specs=(
            P(None, "dp", None),
            P(None, "dp", None),
            P(None, None, "mp", "dp"),
            P(None, None, None, "mp", "dp"),
            P(None, "dp"),
            P("dp", "mp"),
            P("dp", "mp"),
            P("mp", "dp", None),
            P("mp", "dp", None),
            P("mp", "dp"),
            P("dp", "mp"),
            P("dp", "mp"),
            P("mp", "dp"),
        ),
        check_vma=False,
    )
```

profile of v0, /device:TPU:0, one launch (start us, length us, event | category | flops | bytes accessed | tf_op | source)
XLA Modules:
  0.0 3322.7 jit_solution(8028112711792788509)
XLA Ops:
  11.0 42.4 %all_gather.42 = bf16[2,2048]{1,0:T(2,128)(2,1)S(1)} all-gather(bf16[2,128]{1,0:T(2,128)(2,1)} %param.24), channel_id=1, replica_groups=mesh['dp'=16,'mp'=2] {'dp'}, dimensions={1}, use_global_device_ids=true | all-gather | bytes 8704 | tf_op jit(solution)/shard_map/all_gather | solution.py:118
  55.7 42.7 %all_gather.41 = bf16[1,1280,8]{2,0,1:T(2,128)(2,1)S(1)} all-gather(bf16[1,80,8]{2,0,1:T(2,128)(2,1)S(1)} %copy.131), channel_id=1, replica_groups=mesh['dp'=16,'mp'=2] {'dp'}, dimensions={1}, use_global_device_ids=true | all-gather | bytes 21760 | tf_op jit(solution)/shard_map/all_gather | solution.py:121
  99.6 47.6 %all_gather.44 = bf16[1,1280,320]{2,1,0:T(8,128)(2,1)S(1)} all-gather(bf16[1,80,320]{2,1,0:T(8,128)(2,1)S(1)} %copy-done.96), channel_id=1, replica_groups=mesh['dp'=16,'mp'=2] {'dp'}, dimensions={1}, use_global_device_ids=true | all-gather | bytes 870400 | tf_op jit(solution)/shard_map/all_gather | solution.py:122
  151.8 6.0 convolution_convert_fusion.2
  199.8 7.1 fusion.22
  207.0 7.5 slice.546
  214.5 7.5 slice.547
  222.0 7.5 slice.545
  229.5 7.5 slice.549
  314.3 7.7 slice.544
  322.0 7.6 slice.593
  399.6 41.8 %all-gather.1 = f32[64,1,1280]{2,1,0:T(1,128)} all-gather(f32[4,1,1280]{2,1,0:T(1,128)S(1)} %slice_add_fusion.3), channel_id=3, replica_groups=mesh['dp'=16,'mp'=2] {'dp'}, dimensions={0}, use_global_device_ids=true | all-gather | bytes 348160 | tf_op jit(solution)/shard_map/all_gather | solution.py:22
  458.7 37.3 %all-gather = f32[64,1,1280]{2,1,0:T(1,128)S(1)} all-gather(f32[4,1,1280]{2,1,0:T(1,128)S(1)} %slice_add_fusion.4), channel_id=2, replica_groups=mesh['dp'=16,'mp'=2] {'dp'}, dimensions={0}, use_global_device_ids=true | all-gather | bytes 348160 | tf_op jit(solution)/shard_map/all_gather | solution.py:22
  496.9 11.6 while.28
  508.5 6.2 multiply_add_fusion.3
  514.7 8.6 fusion.37
  523.3 7.4 fusion.119
  532.8 24.2 all-reduce.72.cloned.1.call-done
  565.2 148.0 %all-gather.17.cloned.1.call-done = bf16[2048,3072]{1,0:T(8,128)(2,1)} async-done(((bf16[128,3072]{1,0:T(8,128)(2,1)}), bf16[2048,3072]{1,0:T(8,128)(2,1)}) %all-gather.17.cloned.1.call-update) | async-done | bytes 12582928 | tf_op jit(solution)/shard_map/all_gather | solution.py:124
  713.2 11.5 fusion.120
  724.7 141.8 %all-gather.19.cloned.1.call-done = bf16[2048,3072]{1,0:T(8,128)(2,1)} async-done(((bf16[128,3072]{1,0:T(8,128)(2,1)}), bf16[2048,3072]{1,0:T(8,128)(2,1)}) %all-gather.19.cloned.1.call-update) | async-done | bytes 12582928 | tf_op jit(solution)/shard_map/all_gather | solution.py:125
  866.5 11.6 fusion.121
  878.1 185.7 %all-gather.21.cloned.1.call-done = bf16[3072,2048]{1,0:T(8,128)(2,1)} async-done(((bf16[3072,128]{1,0:T(8,128)(2,1)}), bf16[3072,2048]{1,0:T(8,128)(2,1)}) %all-gather.21.cloned.1.call-update) | async-done | bytes 12582928 | tf_op jit(solution)/shard_map/all_gather | solution.py:126
  1063.7 19.5 multiply_convert_fusion
  1083.2 12.1 fusion.122
  1095.4 11.7 convolution_add_fusion
  1111.2 8.1 slice.614
  1119.3 7.6 slice.621
  1126.9 7.6 slice.612
  1135.2 6.4 slice.615
  1141.6 6.4 slice.622
  1148.0 6.4 slice.613
  1164.1 6.3 fusion.30
  1170.4 7.5 slice.616
  1177.9 7.5 slice.618
  1185.4 6.4 slice.617
  1191.8 6.4 slice.619
  1275.2 7.5 slice.666
  1365.5 6.5 slice.667
  1398.6 39.9 %all-gather.2 = f32[64,1,1280]{2,1,0:T(1,128)S(1)} all-gather(f32[4,1,1280]{2,1,0:T(1,128)S(1)} %get-tuple-element.370), channel_id=4, replica_groups=mesh['dp'=16,'mp'=2] {'dp'}, dimensions={0}, use_global_device_ids=true | all-gather | bytes 348160 | tf_op jit(solution)/shard_map/all_gather | solution.py:22
  1440.2 37.3 %all-gather.3 = f32[64,1,1280]{2,1,0:T(1,128)S(1)} all-gather(f32[4,1,1280]{2,1,0:T(1,128)S(1)} %get-tuple-element.369), channel_id=5, replica_groups=mesh['dp'=16,'mp'=2] {'dp'}, dimensions={0}, use_global_device_ids=true | all-gather | bytes 348160 | tf_op jit(solution)/shard_map/all_gather | solution.py:22
  1478.4 11.6 while.29
  1490.0 13.0 rev.15
  1503.0 20.9 rev.14
  1524.1 9.1 fusion.46
  1547.0 5.9 fusion.102
  1568.4 8.9 multiply_reduce_fusion.7
  1582.3 9.6 convolution_convert_fusion.1
  1612.1 8.7 reshape.1106
  1622.3 8.3 fusion.100
  1632.2 13.8 fusion.124
  1646.1 14.0 fusion.125
  1661.6 13.9 fusion.126
  1693.1 7.3 convolution_convert_fusion
  1709.5 7.0 all-to-all-start
  1716.5 11.7 copy_bitcast_fusion
  1728.2 7.2 all-to-all-start.1
  1737.1 58.8 %reduce-scatter.24.cloned.1.call-done = f32[80,24]{1,0:T(8,128)} async-done(((f32[1280,24]{1,0:T(8,128)}), f32[80,24]{1,0:T(8,128)}) %reduce-scatter.24.cloned.1.call-update) | async-done | bytes 7696
  1797.6 186.2 %reduce-scatter.26.cloned.1.call-done = f32[128,1]{1,0:T(8,128)} async-done(((f32[2048,1]{1,0:T(8,128)}), f32[128,1]{1,0:T(8,128)}) %reduce-scatter.26.cloned.1.call-update) | async-done | bytes 528
  1994.7 6.1 convert_reduce_fusion
  2003.0 207.2 %reduce-scatter.14.cloned.1.call-done = f32[1280,128]{1,0:T(8,128)} async-done(((f32[1280,2048]{1,0:T(8,128)}), f32[1280,128]{1,0:T(8,128)}) %reduce-scatter.14.cloned.1.call-update) | async-done | bytes 655376 | tf_op jit(solution)/shard_map/reduce_scatter | solution.py:91
  2210.2 371.5 %reduce-scatter.16.cloned.1.call-done = f32[128,3072]{1,0:T(8,128)} async-done(((f32[2048,3072]{1,0:T(8,128)}), f32[128,3072]{1,0:T(8,128)}) %reduce-scatter.16.cloned.1.call-update) | async-done | bytes 1572880 | tf_op jit(solution)/shard_map/reduce_scatter | solution.py:92
  2581.7 367.0 %reduce-scatter.18.cloned.1.call-done = f32[128,3072]{1,0:T(8,128)} async-done(((f32[2048,3072]{1,0:T(8,128)}), f32[128,3072]{1,0:T(8,128)}) %reduce-scatter.18.cloned.1.call-update) | async-done | bytes 1572880 | tf_op jit(solution)/shard_map/reduce_scatter | solution.py:93
  2948.7 367.2 %reduce-scatter.20.cloned.1.call-done = f32[3072,128]{1,0:T(8,128)} async-done(((f32[3072,2048]{1,0:T(8,128)}), f32[3072,128]{1,0:T(8,128)}) %reduce-scatter.20.cloned.1.call-update) | async-done | bytes 1572880 | tf_op jit(solution)/shard_map/reduce_scatter | solution.py:94
  (711 shorter events, 555.9 us)
Async XLA Ops:
  7.2 142.6 %copy-start = (bf16[4,2,3,1280]{3,1,2,0:T(2,128)(2,1)S(1)}, bf16[4,2,3,1280]{3,1,2,0:T(2,128)(2,1)}, u32[]{:S(2)}) copy-start(bf16[4,2,3,1280]{3,1,2,0:T(2,128)(2,1)} %param.23) | copy-start | bytes 184324
  7.2 48.3 %copy-start.133 = (bf16[1,80,8]{1,2,0:T(8,128)(2,1)S(1)}, bf16[1,80,8]{1,2,0:T(8,128)(2,1)}, u32[]{:S(2)}) copy-start(bf16[1,80,8]{1,2,0:T(8,128)(2,1)} %param.27) | copy-start | bytes 3844
  7.2 92.3 %copy-start.96 = (bf16[1,80,320]{2,1,0:T(8,128)(2,1)S(1)}, bf16[1,80,320]{2,1,0:T(8,128)(2,1)}, u32[]{:S(2)}) copy-start(bf16[1,80,320]{2,1,0:T(8,128)(2,1)} %param.28) | copy-start | bytes 153604
  7.2 144.6 %all-gather.11.cloned.1.call-start = ((), (), s32[]{:S(2)}) async-start(), calls=%async_computation.10 | async-start | bytes 5570560 | tf_op jit(solution)/shard_map/all_gather | solution.py:119
  7.9 506.8 %all-gather.13.cloned.1.call-start = ((), (), s32[]{:S(2)}) async-start(), calls=%async_computation.11 | async-start | bytes 5570560 | tf_op jit(solution)/shard_map/all_gather | solution.py:120
  8.7 139.1 %copy-start.97 = (f32[4,2,1280]{2,1,0:T(2,128)S(1)}, f32[4,2,1280]{2,1,0:T(2,128)}, u32[]{:S(2)}) copy-start(f32[4,2,1280]{2,1,0:T(2,128)} %param.22) | copy-start | bytes 122884
  8.7 139.2 %copy-start.6 = (bf16[4,128,2048]{2,1,0:T(8,128)(2,1)S(1)}, bf16[4,128,2048]{2,1,0:T(8,128)(2,1)}, u32[]{:S(2)}) copy-start(bf16[4,128,2048]{2,1,0:T(8,128)(2,1)} %param.19) | copy-start | bytes 6291460
  8.7 514.6 %all-gather.15.cloned.1.call-start = ((), (), s32[]{:S(2)}) async-start(), calls=%async_computation.12 | async-start | bytes 5570560 | tf_op jit(solution)/shard_map/all_gather | solution.py:123
  9.5 547.5 %all-reduce.72.cloned.1.call-start = ((), (), s32[]{:S(2)}) async-start(), calls=%async_computation.13 | async-start | bytes 8388608 | tf_op jit(solution)/shard_map/psum | solution.py:239
  9.5 137.6 %copy-start.117 = (s32[128]{0:T(128)}, s32[128]{0:T(128)S(1)}, u32[]{:S(2)}) copy-start(s32[128]{0:T(128)S(1)} %iota_add_fusion.2) | copy-start | bytes 1540
  10.8 88.0 %copy-start.126 = (s32[4]{0:T(128)}, s32[4]{0:T(128)S(1)}, u32[]{:S(2)}) copy-start(s32[4]{0:T(128)S(1)} %get-tuple-element.447) | copy-start | bytes 52
  10.8 153.3 %copy-start.120 = (pred[4,128]{1,0:T(4,128)(4,1)}, pred[4,128]{1,0:T(4,128)(4,1)S(1)}, u32[]{:S(2)}) copy-start(pred[4,128]{1,0:T(4,128)(4,1)S(1)} %get-tuple-element.452) | copy-start | bytes 1540
  10.8 153.3 %copy-start.122 = (pred[4,128]{1,0:T(4,128)(4,1)}, pred[4,128]{1,0:T(4,128)(4,1)S(1)}, u32[]{:S(2)}) copy-start(pred[4,128]{1,0:T(4,128)(4,1)S(1)} %get-tuple-element.454) | copy-start | bytes 1540
  10.8 153.3 %copy-start.124 = (pred[4,128]{1,0:T(4,128)(4,1)}, pred[4,128]{1,0:T(4,128)(4,1)S(1)}, u32[]{:S(2)}) copy-start(pred[4,128]{1,0:T(4,128)(4,1)S(1)} %get-tuple-element.455) | copy-start | bytes 1540
  10.9 188.9 %copy-start.128 = (pred[4,128]{1,0:T(4,128)(4,1)}, pred[4,128]{1,0:T(4,128)(4,1)S(1)}, u32[]{:S(2)}) copy-start(pred[4,128]{1,0:T(4,128)(4,1)S(1)} %get-tuple-element.450) | copy-start | bytes 1540
  10.9 188.9 %copy-start.130 = (pred[4,128]{1,0:T(4,128)(4,1)}, pred[4,128]{1,0:T(4,128)(4,1)S(1)}, u32[]{:S(2)}) copy-start(pred[4,128]{1,0:T(4,128)(4,1)S(1)} %get-tuple-element.453) | copy-start | bytes 1540
  53.4 96.3 %copy-start.67 = (f32[1,2048]{1,0:T(1,128)}, f32[1,2048]{1,0:T(1,128)S(1)}, u32[]{:S(2)}) copy-start(f32[1,2048]{1,0:T(1,128)S(1)} %get-tuple-element.440) | copy-start | bytes 24580
  55.5 43.2 %copy-start.102 = (f32[4,128]{1,0:T(4,128)}, f32[4,128]{1,0:T(4,128)S(1)}, u32[]{:S(2)}) copy-start(f32[4,128]{1,0:T(4,128)S(1)} %fusion.18) | copy-start | bytes 6148
  55.6 94.2 %copy-start.113 = (f32[512]{0:T(512)}, f32[512]{0:T(512)S(1)}, u32[]{:S(2)}) copy-start(f32[512]{0:T(512)S(1)} %bitcast_rsqrt_fusion) | copy-start | bytes 6148
  99.5 50.2 %copy-start.94 = (f32[1280]{0:T(1024)}, f32[1280]{0:T(1024)S(1)}, u32[]{:S(2)}) copy-start(f32[1280]{0:T(1024)S(1)} %get-tuple-element.314) | copy-start | bytes 15364
  99.5 64.6 %copy-start.105 = (f32[1280]{0:T(1024)}, f32[1280]{0:T(1024)S(1)}, u32[]{:S(2)}) copy-start(f32[1280]{0:T(1024)S(1)} %get-tuple-element.316) | copy-start | bytes 15364
  99.5 64.6 %copy-start.107 = (f32[1280]{0:T(1024)}, f32[1280]{0:T(1024)S(1)}, u32[]{:S(2)}) copy-start(f32[1280]{0:T(1024)S(1)} %get-tuple-element.317) | copy-start | bytes 15364
  99.5 64.6 %copy-start.109 = (f32[1280]{0:T(1024)}, f32[1280]{0:T(1024)S(1)}, u32[]{:S(2)}) copy-start(f32[1280]{0:T(1024)S(1)} %get-tuple-element.318) | copy-start | bytes 15364
  99.5 64.6 %copy-start.111 = (f32[1280]{0:T(1024)}, f32[1280]{0:T(1024)S(1)}, u32[]{:S(2)}) copy-start(f32[1280]{0:T(1024)S(1)} %get-tuple-element.319) | copy-start | bytes 15364
  99.6 100.2 %copy-start.53 = (f32[1280]{0:T(1024)}, f32[1280]{0:T(1024)S(1)}, u32[]{:S(2)}) copy-start(f32[1280]{0:T(1024)S(1)} %get-tuple-element.313) | copy-start | bytes 15364
  99.6 100.2 %copy-start.55 = (f32[1280]{0:T(1024)}, f32[1280]{0:T(1024)S(1)}, u32[]{:S(2)}) copy-start(f32[1280]{0:T(1024)S(1)} %get-tuple-element.315) | copy-start | bytes 15364
  147.1 30.1 copy-start.21
  147.8 52.0 %copy-start.65 = (f32[1280]{0:T(1024)}, f32[1280]{0:T(1024)S(1)}, u32[]{:S(2)}) copy-start(f32[1280]{0:T(1024)S(1)} %get-tuple-element.438) | copy-start | bytes 15364
  149.8 50.1 %copy-start.58 = (f32[4,1280]{1,0:T(4,128)}, f32[4,1280]{1,0:T(4,128)S(1)}, u32[]{:S(2)}) copy-start(f32[4,1280]{1,0:T(4,128)S(1)} %get-tuple-element.466) | copy-start | bytes 61444
  149.8 50.1 %copy-start.60 = (f32[4,1280]{1,0:T(4,128)}, f32[4,1280]{1,0:T(4,128)S(1)}, u32[]{:S(2)}) copy-start(f32[4,1280]{1,0:T(4,128)S(1)} %get-tuple-element.467) | copy-start | bytes 61444
  159.0 3.4 collective-permute-start
  314.2 17.5 copy-start.49
  530.8 182.5 %all-gather.17.cloned.1.call-start = ((), (), s32[]{:S(2)}) async-start(), calls=%async_computation.14 | async-start | bytes 13369344 | tf_op jit(solution)/shard_map/all_gather | solution.py:124
  531.4 335.1 %all-gather.19.cloned.1.call-start = ((), (), s32[]{:S(2)}) async-start(), calls=%async_computation.15 | async-start | bytes 13369344 | tf_op jit(solution)/shard_map/all_gather | solution.py:125
  531.9 531.8 %all-gather.21.cloned.1.call-start = ((), (), s32[]{:S(2)}) async-start(), calls=%async_computation.16 | async-start | bytes 13369344 | tf_op jit(solution)/shard_map/all_gather | solution.py:126
  532.7 621.7 %all-reduce.74.cloned.1.call-start = ((), (), s32[]{:S(2)}) async-start(), calls=%async_computation.17 | async-start | bytes 8388608 | tf_op jit(solution)/shard_map/psum | solution.py:262
  532.8 630.4 %copy-start.98 = (f32[512]{0:T(512)}, f32[512]{0:T(512)S(1)}, u32[]{:S(2)}) copy-start(f32[512]{0:T(512)S(1)} %fusion.95) | copy-start | bytes 6148
  565.2 301.3 %copy-start.39 = (bf16[512,2048]{1,0:T(8,128)(2,1)}, bf16[512,2048]{1,0:T(8,128)(2,1)S(1)}, u32[]{:S(2)}) copy-start(bf16[512,2048]{1,0:T(8,128)(2,1)S(1)} %multiply_convert_fusion.3) | copy-start | bytes 6291460
  1107.1 598.4 %all-reduce.76.cloned.1.call-start = ((), (), s32[]{:S(2)}) async-start(), calls=%async_computation.25 | async-start | bytes 8388608 | tf_op jit(solution)/shard_map/psum | solution.py:248
  1265.1 19.1 copy-start.78
  1265.1 19.1 copy-start.79
  1265.1 19.2 copy-start.62
  1265.1 19.3 copy-start.74
  1265.1 19.3 copy-start.75
  1398.6 91.4 %copy-start.20 = (f32[4,128,1280]{2,1,0:T(8,128)S(1)}, f32[4,128,1280]{2,1,0:T(8,128)}, u32[]{:S(2)}) copy-start(f32[4,128,1280]{2,1,0:T(8,128)} %add.788) | copy-start | bytes 7864324
  1503.0 21.0 copy-start.8
  1503.0 21.0 copy-start.59
  1503.0 21.0 copy-start.61
  1503.0 21.0 copy-start.66
  1503.0 21.0 copy-start.69
  1503.0 21.0 copy-start.100
  1503.0 21.0 copy-start.129
  1503.0 21.0 copy-start.131
  1579.4 12.7 collective-permute-start.1
  1599.6 135.9 %reduce-scatter.22.cloned.1.call-start = ((), (), s32[]{:S(2)}) async-start(), calls=%async_computation.22 | async-start | bytes 696320
  1606.8 189.1 %reduce-scatter.24.cloned.1.call-start = ((), (), s32[]{:S(2)}) async-start(), calls=%async_computation.23 | async-start | bytes 696320
  1620.8 363.0 %reduce-scatter.26.cloned.1.call-start = ((), (), s32[]{:S(2)}) async-start(), calls=%async_computation.24 | async-start | bytes 1114112
  1622.3 588.0 %reduce-scatter.14.cloned.1.call-start = ((), (), s32[]{:S(2)}) async-start(), calls=%async_computation.18 | async-start | bytes 11141120 | tf_op jit(solution)/shard_map/reduce_scatter | solution.py:91
  1630.6 951.1 %reduce-scatter.16.cloned.1.call-start = ((), (), s32[]{:S(2)}) async-start(), calls=%async_computation.19 | async-start | bytes 26738688 | tf_op jit(solution)/shard_map/reduce_scatter | solution.py:92
  1646.0 1302.7 %reduce-scatter.18.cloned.1.call-start = ((), (), s32[]{:S(2)}) async-start(), calls=%async_computation.20 | async-start | bytes 26738688 | tf_op jit(solution)/shard_map/reduce_scatter | solution.py:93
  1660.1 1655.8 %reduce-scatter.20.cloned.1.call-start = ((), (), s32[]{:S(2)}) async-start(), calls=%async_computation.21 | async-start | bytes 26738688 | tf_op jit(solution)/shard_map/reduce_scatter | solution.py:94
  1688.8 20.7 all-to-all-start.2
  1709.5 18.7 all-to-all-start
  1728.2 266.4 %all-to-all-start.1 = ((bf16[16,128,2560]{1,2,0:T(8,128)(2,1)}), bf16[16,128,2560]{1,2,0:T(8,128)(2,1)}, u32[]{:S(2)}, u32[]{:S(2)}) async-start(bf16[16,128,2560]{1,2,0:T(8,128)(2,1)} %copy_bitcast_fusion), calls=%async_computation.1 | async-start | bytes 20971520 | tf_op jit(solution)/shard_map/all_to_all | solution.py:44
  (105 other events, 616.7 us)
Sparse Core Ops, SparseCore 0:
  10.8 101.3 all-gather.10
  115.0 86.5 all-gather.12
  204.2 100.6 all-gather.14
  530.9 26.0 all-reduce.71
  560.0 153.1 all-gather.16
  716.2 150.1 all-gather.18
  869.5 194.1 all-gather.20
  1107.3 26.5 all-reduce.73
  1599.7 27.0 all-reduce.75
  1629.6 79.6 reduce-scatter.21
  1712.1 83.7 reduce-scatter.23
  1798.1 185.6 reduce-scatter.25
  1986.7 223.4 reduce-scatter.13
  2216.4 365.2 reduce-scatter.15
  2587.9 360.7 reduce-scatter.17
  2954.9 360.9 reduce-scatter.19
where the time goes:
time: 3340 us; the launch traced here: 3320 us
  waiting for transfers between devices  2060 us (62%)
  local copies, waits for them, and re-layouts  512 us (15%)
  blocking collectives  289 us (9%)
  other arithmetic  229 us (7%)
  matrix products  192 us (6%)
    reduce_scatter x1, waiting for transfers between devices, reduce_second(): lax.psum_scatter(g_gate, 'dp', scatter_dimension=0, tiled=True)  371 us
    reduce_scatter x1, waiting for transfers between devices, reduce_second(): lax.psum_scatter(g_down, 'dp', scatter_dimension=1, tiled=True)  367 us
    reduce_scatter x1, waiting for transfers between devices, reduce_second(): lax.psum_scatter(g_up, 'dp', scatter_dimension=0, tiled=True)  367 us
    unnamed x19, waiting for transfers between devices  249 us
    reduce_scatter x1, waiting for transfers between devices, reduce_second(): lax.psum_scatter(g_wo, 'dp', scatter_dimension=1, tiled=True)  207 us
    all_gather x1, waiting for transfers between devices, shards(): lax.all_gather(w_down, 'dp', axis=1, tiled=True)  186 us
    all_gather x4, blocking collectives, prefix(): pieces = jax.tree.map(lambda part: lax.all_gather(part, axis), value)  156 us
    all_gather x1, waiting for transfers between devices, shards(): lax.all_gather(w_gate, 'dp', axis=0, tiled=True)  148 us
  transfers between devices with their start and end apart: 21, of which 10 were waited for; matrix products, arithmetic and copies ran while one was open for 16% of the time, Pallas kernels for 0%

commit v1 on v0

v1 whole, which is shorter than its diff:
```python
from functools import partial

import jax
import jax.numpy as jnp
from jax import lax
from jax.experimental import pallas as pl
from jax.experimental.pallas import tpu as pltpu
from jax.sharding import Mesh
from jax.sharding import PartitionSpec as P

HEAD_DIM = 160
PLANE = 4
SEGMENTS = 8
EPSILON = 1e-06
BF16 = jnp.bfloat16
F32 = jnp.float32


def dot(left, right, left_dim, right_dim):
    return lax.dot_general(
        left, right, (((left_dim,), (right_dim,)), ((), ())), preferred_element_type=F32
    )


def to_partner(block, bit):
    return lax.ppermute(block, "j", [(i, i ^ bit) for i in range(PLANE)])


def at(block, index, axis):
    return lax.dynamic_index_in_dim(block, index, axis, keepdims=False)


def put(whole, block, index, axis):
    return lax.dynamic_update_index_in_dim(whole, block, index, axis)


def plane_gather(own):
    mine = lax.axis_index("j")
    streams, rows, width = own.shape
    half = streams // 2
    from_x = to_partner(own, 1)
    from_y = to_partner(own, 2)
    first = to_partner(from_x[:half], 2)
    second = to_partner(from_y[half:], 1)
    whole = jnp.zeros((streams, PLANE, rows, width), own.dtype)
    whole = put(whole, own, mine, 1)
    whole = put(whole, from_x, mine ^ 1, 1)
    whole = put(whole, from_y, mine ^ 2, 1)
    whole = put(whole, jnp.concatenate([first, second], axis=0), mine ^ 3, 1)
    return whole.reshape(streams, PLANE * rows, width)


def plane_sum(part, streams):
    mine = lax.axis_index("j")
    width = part.shape[-1]
    part = part.astype(BF16).reshape(streams, PLANE, -1, width)
    half = streams // 2
    far = at(part, mine ^ 3, 1)
    via_x = to_partner(far[:half], 1).astype(F32)
    via_y = to_partner(far[half:], 2).astype(F32)
    for_x = at(part, mine ^ 1, 1)
    for_y = at(part, mine ^ 2, 1)
    for_x = jnp.concatenate([for_x[:half], (for_x[half:] + via_y).astype(BF16)], axis=0)
    for_y = jnp.concatenate([(for_y[:half] + via_x).astype(BF16), for_y[half:]], axis=0)
    from_x = to_partner(for_x, 1)
    from_y = to_partner(for_y, 2)
    own = at(part, mine, 1)
    return own.astype(F32) + from_x.astype(F32) + from_y.astype(F32)


def plane_swap(blocks):
    mine = lax.axis_index("j")
    swapped = blocks
    for bit in (1, 2, 3):
        swapped = put(swapped, to_partner(at(blocks, mine ^ bit, 0), bit), mine ^ bit, 0)
    return swapped


def spread(weight):
    rows, four, columns = weight.shape
    blocks = plane_swap(jnp.moveaxis(weight, 1, 0)).reshape(four * rows, columns)
    return lax.all_gather(blocks, ("c", "z"), axis=0, tiled=False).reshape(
        lax.axis_size("c"), -1, columns
    )


def collect(grads, rows):
    halves, all_rows, columns = grads.shape
    summed = lax.psum_scatter(
        grads.reshape(halves * all_rows, columns), ("c", "z"), scatter_dimension=0, tiled=True
    )
    return jnp.moveaxis(plane_swap(summed.reshape(PLANE, rows, columns)), 0, 1).astype(F32)


def with_other_core(array, dim):
    core = lax.axis_index("c")
    count = array.shape[0] // 2
    mine = lax.dynamic_slice_in_dim(array, core * count, count, 0)
    other = lax.dynamic_slice_in_dim(array, (1 - core) * count, count, 0)
    other = lax.ppermute(other, "c", [(0, 1), (1, 0)])
    return jnp.where(
        core == 0,
        jnp.concatenate([mine, other], axis=dim),
        jnp.concatenate([other, mine], axis=dim),
    )


def all_streams(own):
    core = lax.axis_index("c")
    other = lax.ppermute(own, "c", [(0, 1), (1, 0)])
    count = own.shape[0]
    whole = jnp.zeros((2 * count, *own.shape[1:]), own.dtype)
    whole = lax.dynamic_update_slice_in_dim(whole, own, core * count, 0)
    return lax.dynamic_update_slice_in_dim(whole, other, (1 - core) * count, 0)


def shifted(block, distance):
    size = lax.axis_size("z")
    return lax.ppermute(
        block, "z", [(i - distance, i) for i in range(size) if 0 <= i - distance < size]
    )


def entering(keep, state, backward):
    size, mine = lax.axis_size("z"), lax.axis_index("z")
    pair = jnp.stack([keep, state])
    result = jnp.zeros_like(state)
    for distance in range(size - 1, 0, -1):
        got = shifted(pair, -distance if backward else distance)
        there = mine + distance < size if backward else mine >= distance
        result = jnp.where(there, got[0] * result + got[1], result)
    return result


def scan_kernel(backward, keep_ref, add_ref, product_ref, state_ref):
    streams, rows, width = keep_ref.shape
    steps = rows // SEGMENTS
    for s in range(streams):

        def step(number, carry):
            product, state = carry
            place = steps - 1 - number if backward else number
            at_once = pl.ds(place, SEGMENTS, stride=steps)
            keep = keep_ref[s, at_once, :]
            state = keep * state + add_ref[s, at_once, :]
            product = keep * product
            product_ref[s, at_once, :] = product
            state_ref[s, at_once, :] = state
            return product, state

        product, state = lax.fori_loop(
            0,
            steps,
            step,
            (jnp.ones((SEGMENTS, width), F32), jnp.zeros((SEGMENTS, width), F32)),
            unroll=8,
        )
        product_in = jnp.ones((1, width), F32)
        state_in = jnp.zeros((1, width), F32)
        order = range(SEGMENTS - 1, -1, -1) if backward else range(SEGMENTS)
        for k in order:
            here = pl.ds(k * steps, steps)
            local = product_ref[s, here, :]
            state_ref[s, here, :] = state_ref[s, here, :] + local * state_in
            product_ref[s, here, :] = local * product_in
            state_in = product[k : k + 1] * state_in + state[k : k + 1]
            product_in = product[k : k + 1] * product_in


def local_scan(keep, add, backward):
    streams, rows, width = keep.shape
    block = pl.BlockSpec((streams, rows, 128), lambda i: (0, 0, i))
    return pl.pallas_call(
        partial(scan_kernel, backward),
        grid=(width // 128,),
        in_specs=[block, block],
        out_specs=[block, block],
        out_shape=[jax.ShapeDtypeStruct(keep.shape, F32)] * 2,
        compiler_params=pltpu.CompilerParams(vmem_limit_bytes=32 * 1024 * 1024),
        cost_estimate=pl.CostEstimate(
            flops=8 * streams * rows * width,
            bytes_accessed=16 * streams * rows * width,
            transcendentals=0,
        ),
    )(keep, add)


def rms_norm(values, norm_gain):
    factor = lax.rsqrt(jnp.mean(values * values, axis=-1, keepdims=True) + EPSILON)
    return values * factor * norm_gain


def gate_math(pre_rate, pre_entry, lam_param, conv_value):
    rate_gate = jax.nn.sigmoid(pre_rate)
    entry_gate = jax.nn.sigmoid(pre_entry)
    log_decay = -8.0 * rate_gate * jax.nn.softplus(lam_param)
    retain = jnp.exp(log_decay)
    factor = jnp.sqrt(-jnp.expm1(2.0 * log_decay))
    return (retain, factor * entry_gate * conv_value)


def mix_gelu(gate_value, up_value):
    return jax.nn.gelu(gate_value) * up_value


def convolve(extended, conv_taps, conv_bias, fill_values, insides):
    n_rows = extended.shape[1] - 3
    result = conv_bias + conv_taps[:, 0] * extended[:, 3:]
    for offset in (1, 2, 3):
        window = extended[:, 3 - offset : 3 - offset + n_rows]
        result = result + conv_taps[:, offset] * jnp.where(
            insides[offset - 1], window, fill_values[offset - 1]
        )
    return result


def halves_together(weight, parts):
    halves, rows, columns = weight.shape
    each = columns // parts
    return jnp.concatenate(
        [weight[h, :, p * each : (p + 1) * each] for p in range(parts) for h in range(halves)],
        axis=1,
    )


def halves_apart(grads, halves):
    each = grads[0].shape[1] // halves
    return jnp.stack(
        [
            jnp.concatenate([g[:, h * each : (h + 1) * each] for g in grads], axis=1)
            for h in range(halves)
        ]
    )


def shards(
    inputs,
    doc_spans,
    doc_lengths,
    state_in,
    conv_in,
    norm_gains,
    w_x,
    w_g,
    rec_params,
    gate_weights,
    w_o,
    w_gate,
    w_up,
    w_down,
    cotangent,
):
    all_streams_count, own_rows, model_width = inputs.shape
    halves = lax.axis_size("c")
    z_size = lax.axis_size("z")
    z_index, j_index, core = lax.axis_index("z"), lax.axis_index("j"), lax.axis_index("c")
    n_streams = all_streams_count // halves
    n_rows = own_rows * PLANE
    tokens = n_streams * n_rows
    own_tokens = n_streams * own_rows
    weight_rows = w_x.shape[0]
    half_width = w_x.shape[1]
    part_width = half_width // PLANE
    rec_width = part_width * halves
    heads_here = rec_width // HEAD_DIM
    ff_part = w_gate.shape[1] // PLANE

    first_stream = core * n_streams

    def own_streams(array):
        return lax.dynamic_slice_in_dim(array, first_stream, n_streams, 0)

    spans = own_streams(doc_spans)
    lengths = own_streams(doc_lengths)
    own_in = own_streams(inputs)
    own_cot = own_streams(cotangent)
    whole_in = plane_gather(own_in)
    gains_all = lax.all_gather(norm_gains, ("z", "j"), axis=1, tiled=True).astype(F32)
    small = lax.all_gather(
        jnp.concatenate([rec_params[0], gate_weights[0]], axis=1), ("c", "z", "j"), axis=0
    ).reshape(halves, half_width, -1)
    small = lax.dynamic_slice_in_dim(small, j_index * part_width, part_width, 1)
    small = small.reshape(rec_width, -1)
    params_all = small[:, :8].astype(F32)
    gates_all = small[:, 8:].reshape(heads_here, HEAD_DIM, 2 * HEAD_DIM)

    def by_chip(weight):
        return weight.reshape(weight_rows, PLANE, -1)

    w_rec = halves_together(spread(jnp.concatenate([by_chip(w_x), by_chip(w_g)], axis=2)), 2)
    w_back = halves_together(spread(by_chip(w_o.T)), 1)
    w_wide = spread(jnp.concatenate([by_chip(w_gate), by_chip(w_up)], axis=2))
    w_narrow = spread(by_chip(w_down.T))

    def live_at(position):
        second_start = spans[:, 0:1]
        doc_id = (position[None, :] >= second_start).astype(jnp.int32)
        doc_start = doc_id * second_start
        doc_stop = doc_start + jnp.where(doc_id == 1, lengths[:, 1:2], lengths[:, 0:1])
        live = (position[None, :] < doc_stop).astype(F32)
        return doc_id, doc_start, live

    own_first = (z_index * PLANE + j_index) * own_rows
    own_live = live_at(own_first + jnp.arange(own_rows, dtype=jnp.int32))[2]
    own_live = own_live.reshape(own_tokens, 1)
    position = z_index * n_rows + jnp.arange(n_rows, dtype=jnp.int32)
    doc_id, doc_start, _ = live_at(position)

    d_out = own_cot.reshape(own_tokens, model_width).astype(F32)
    own_down = (d_out * own_live).astype(BF16).reshape(n_streams, own_rows, model_width)
    d_down = plane_gather(own_down).reshape(tokens, model_width)

    flat_in = own_in.reshape(own_tokens, model_width).astype(F32)
    _, norm_one_back = jax.vjp(rms_norm, flat_in, gains_all[0])
    normed_low = rms_norm(
        whole_in.reshape(tokens, model_width).astype(F32), gains_all[0]
    ).astype(BF16)
    projected = dot(normed_low, w_rec, 1, 0)
    source_rows = projected[:, :rec_width].astype(BF16).reshape(n_streams, n_rows, rec_width)
    branch, branch_back = jax.vjp(jax.nn.gelu, projected[:, rec_width:])
    rim_rows = shifted(source_rows[:, n_rows - 3 :], 1)
    extended = jnp.concatenate([rim_rows, source_rows], axis=1).astype(F32)

    conv_here = with_other_core(
        lax.dynamic_slice_in_dim(conv_in, j_index * part_width, part_width, 3), 3
    )
    state_here = with_other_core(
        lax.dynamic_slice_in_dim(state_in, j_index * part_width, part_width, 2), 2
    )
    slot_range = jnp.arange(3, dtype=jnp.int32)
    doc_range = jnp.arange(2, dtype=jnp.int32)
    fill_values = []
    insides = []
    for offset in (1, 2, 3):
        earlier_pos = position[None, :] - offset
        insides.append((earlier_pos >= doc_start)[..., None])
        slot_pick = (doc_id[..., None, None] == doc_range[:, None]) & (
            (3 + earlier_pos - doc_start)[..., None, None] == slot_range
        )
        fill_values.append(
            jnp.einsum(
                "btds,bdsc->btc",
                slot_pick.astype(BF16),
                conv_here,
                preferred_element_type=F32,
            )
        )
    conv_value, conv_back = jax.vjp(
        partial(convolve, fill_values=fill_values, insides=insides),
        extended,
        params_all[:, 0:4],
        params_all[:, 4],
    )
    conv_flat = conv_value.reshape(tokens, rec_width)
    conv_low = conv_flat.astype(BF16).reshape(tokens, heads_here, HEAD_DIM)
    gate_mixed = jnp.einsum("nhk,hko->nho", conv_low, gates_all, preferred_element_type=F32)
    pre_rate = gate_mixed[..., :HEAD_DIM].reshape(tokens, rec_width) + params_all[:, 5]
    pre_entry = gate_mixed[..., HEAD_DIM:].reshape(tokens, rec_width) + params_all[:, 6]
    (retain, drive_term), gate_back = jax.vjp(
        gate_math, pre_rate, pre_entry, params_all[:, 7], conv_flat
    )
    reset_rows = (position[None, :] == doc_start)[..., None]
    carried = jnp.where((doc_id == 1)[..., None], state_here[:, None, 1], state_here[:, None, 0])
    retain_rows = retain.reshape(n_streams, n_rows, rec_width)
    retain_eff = jnp.where(reset_rows, 0.0, retain_rows)
    drive_eff = drive_term.reshape(n_streams, n_rows, rec_width) + jnp.where(
        reset_rows, retain_rows * carried, 0.0
    )
    local_keep, local_state = local_scan(retain_eff, drive_eff, False)
    state_before = entering(local_keep[:, -1], local_state[:, -1], False)
    states = local_state + local_keep * state_before[:, None]

    starts_doc = jnp.concatenate([jnp.zeros_like(spans[:, :1]), spans[:, :1]], axis=1)
    stops_doc = starts_doc + lengths
    is_last = position[None, :, None] == (stops_doc - 1)[:, None, :]
    final_part = jnp.sum(jnp.where(is_last[..., None], states[:, :, None, :], 0.0), axis=1)
    tail_pos = stops_doc[..., None] - 3 + slot_range
    from_rows = (position[None, :, None, None] == tail_pos[:, None]) & (
        tail_pos >= starts_doc[..., None]
    )[:, None]
    conv_part = jnp.einsum(
        "btdj,btc->bdjc", from_rows.astype(BF16), source_rows, preferred_element_type=F32
    )
    from_state = (
        (tail_pos < starts_doc[..., None])[..., None]
        & ((lengths[..., None] + slot_range)[..., None] == slot_range)
        & (z_index == 0)
    )
    conv_part = conv_part + jnp.einsum(
        "bdjs,bdsc->bdjc", from_state.astype(BF16), conv_here, preferred_element_type=F32
    )
    finals = jnp.concatenate([final_part[:, :, None], conv_part], axis=2)
    finals = lax.all_gather(finals, ("z", "j", "c"), axis=0)
    finals = finals.reshape(z_size, PLANE, halves * n_streams, 2, 4, halves, part_width)
    finals = jnp.sum(finals, axis=0)
    finals = at(finals, core, 4)
    finals = jnp.moveaxis(finals, 0, 3).reshape(all_streams_count, 2, 4, half_width)
    dp_index = z_index * PLANE + j_index
    out_width = half_width // (z_size * PLANE)
    finals = lax.dynamic_slice_in_dim(finals, dp_index * out_width, out_width, 3)
    state_block = finals[:, :, 0][:, :, None]
    conv_block = finals[:, :, 1:].astype(BF16)[:, :, :, None]

    states_flat = states.reshape(tokens, rec_width)
    mixed_rows = (states_flat * branch).astype(BF16)
    rec_part = dot(mixed_rows, w_back, 1, 1)
    rec_total = plane_sum(rec_part, n_streams).reshape(own_tokens, model_width)
    hidden_one = flat_in + own_live * rec_total
    normed_two, norm_two_back = jax.vjp(rms_norm, hidden_one, gains_all[1])
    own_second = normed_two.astype(BF16).reshape(n_streams, own_rows, model_width)
    second_low = plane_gather(own_second).reshape(tokens, model_width)

    down_part = second_part = 0.0
    g_narrow, g_wide = [], []
    for h in range(halves):
        both = dot(second_low, w_wide[h], 1, 0)
        activated, mix_back = jax.vjp(mix_gelu, both[:, :ff_part], both[:, ff_part:])
        act_low = activated.astype(BF16)
        down_part = down_part + dot(act_low, w_narrow[h], 1, 1)
        d_act = dot(d_down, w_narrow[h], 1, 0)
        d_both = jnp.concatenate([d.astype(BF16) for d in mix_back(d_act)], axis=1)
        second_part = second_part + dot(d_both, w_wide[h], 1, 1)
        g_narrow.append(dot(d_down, act_low, 0, 0).astype(BF16))
        g_wide.append(dot(second_low, d_both, 0, 0).astype(BF16))
    out_narrow = collect(jnp.stack(g_narrow), weight_rows)
    out_wide = collect(jnp.stack(g_wide), weight_rows)

    mlp_total = plane_sum(down_part, n_streams).reshape(own_tokens, model_width)
    out_flat = (hidden_one + own_live * mlp_total).astype(BF16)
    output = all_streams(out_flat.reshape(n_streams, own_rows, model_width))

    second_total = plane_sum(second_part, n_streams).reshape(own_tokens, model_width)
    d_hidden_norm, g_gain_two = norm_two_back(second_total)
    d_hidden = d_out + d_hidden_norm
    own_rec = (d_hidden * own_live).astype(BF16).reshape(n_streams, own_rows, model_width)
    d_rec = plane_gather(own_rec).reshape(tokens, model_width)
    d_mixed = dot(d_rec, w_back, 1, 0)
    g_back = dot(d_rec, mixed_rows, 0, 0).astype(BF16)
    out_back = collect(halves_apart([g_back], halves), weight_rows)

    grad_state = (d_mixed * branch).reshape(n_streams, n_rows, rec_width)
    branch_low = branch_back(d_mixed * states_flat)[0].astype(BF16)
    next_keep = jnp.concatenate([retain_eff[:, 1:], jnp.ones_like(retain_eff[:, :1])], axis=1)
    later_keep, later_sum = local_scan(next_keep, grad_state, True)
    carried_grad = entering(
        retain_eff[:, 0] * later_keep[:, 0], retain_eff[:, 0] * later_sum[:, 0], True
    )
    adjoint = later_sum + later_keep * carried_grad[:, None]
    state_prev = jnp.concatenate([state_before[:, None], states[:, :-1]], axis=1)
    state_prev = jnp.where(reset_rows, carried, state_prev)
    d_retain = (adjoint * state_prev).reshape(tokens, rec_width)
    d_rate, d_entry, g_lam, d_conv_direct = gate_back(
        (d_retain, adjoint.reshape(tokens, rec_width))
    )
    rate_low = d_rate.astype(BF16)
    entry_low = d_entry.astype(BF16)
    grad_gates = jnp.concatenate(
        [
            rate_low.reshape(tokens, heads_here, HEAD_DIM),
            entry_low.reshape(tokens, heads_here, HEAD_DIM),
        ],
        axis=2,
    )
    g_gates = jnp.einsum(
        "nhk,nho->hko", conv_low, grad_gates, preferred_element_type=F32
    ).reshape(rec_width, 2 * HEAD_DIM)
    d_conv_gates = jnp.einsum(
        "nho,hko->nhk", grad_gates, gates_all, preferred_element_type=F32
    ).reshape(tokens, rec_width)
    d_conv = (d_conv_direct + d_conv_gates).reshape(n_streams, n_rows, rec_width)
    d_extended, g_taps, g_conv_bias = conv_back(d_conv)
    rim_grad = shifted(d_extended[:, :3].astype(BF16), -1).astype(F32)
    d_source = jnp.concatenate([d_extended[:, 3:n_rows], d_extended[:, n_rows:] + rim_grad], axis=1)
    d_projected = jnp.concatenate(
        [d_source.reshape(tokens, rec_width).astype(BF16), branch_low], axis=1
    )
    first_part = dot(d_projected, w_rec, 1, 1)
    g_rec = dot(normed_low, d_projected, 0, 0).astype(BF16)
    out_rec = collect(
        halves_apart([g_rec[:, :rec_width], g_rec[:, rec_width:]], halves), weight_rows
    )
    g_small = jnp.concatenate(
        [
            g_taps,
            g_conv_bias[:, None],
            jnp.sum(rate_low.astype(F32), axis=0)[:, None],
            jnp.sum(entry_low.astype(F32), axis=0)[:, None],
            g_lam[:, None],
            g_gates,
        ],
        axis=1,
    ).astype(BF16)
    g_small = lax.psum_scatter(g_small, ("c", "z"), scatter_dimension=0, tiled=True)
    route = [(z * PLANE + j, j * z_size + z) for z in range(z_size) for j in range(PLANE)]
    g_small = lax.ppermute(g_small, ("z", "j"), route).astype(F32)[None]

    first_total = plane_sum(first_part, n_streams).reshape(own_tokens, model_width)
    d_input_norm, g_gain_one = norm_one_back(first_total)
    input_grad = all_streams(
        (d_hidden + d_input_norm).astype(BF16).reshape(n_streams, own_rows, model_width)
    )
    g_gains = lax.psum(jnp.stack([g_gain_one, g_gain_two]), ("z", "j", "c"))
    gain_width = norm_gains.shape[1]
    g_gains = lax.dynamic_slice_in_dim(g_gains, dp_index * gain_width, gain_width, 1)

    def flat(blocks):
        return blocks.reshape(weight_rows, -1)

    return (
        output,
        input_grad,
        state_block,
        conv_block,
        g_gains,
        flat(out_rec[..., :part_width]),
        flat(out_rec[..., part_width:]),
        g_small[..., :8],
        g_small[..., 8:],
        flat(out_back).T,
        flat(out_wide[..., :ff_part]),
        flat(out_wide[..., ff_part:]),
        flat(out_narrow).T,
    )


def solution(mesh):
    devices = mesh.devices.reshape(-1, PLANE, mesh.shape["mp"])
    planes = Mesh(devices, ("z", "j", "c"))
    dp, mp = ("z", "j"), "c"
    return jax.shard_map(
        shards,
        mesh=planes,
        in_specs=(
            P(None, dp, None),
            P(),
            P(),
            P(None, None, mp),
            P(None, None, None, mp),
            P(None, dp),
            P(dp, mp),
            P(dp, mp),
            P(mp, dp, None),
            P(mp, dp, None),
            P(mp, dp),
            P(dp, mp),
            P(dp, mp),
            P(mp, dp),
            P(None, dp, None),
        ),
        out_specs=(
            P(None, dp, None),
            P(None, dp, None),
            P(None, None, mp, dp),
            P(None, None, None, mp, dp),
            P(None, dp),
            P(dp, mp),
            P(dp, mp),
            P(mp, dp, None),
            P(mp, dp, None),
            P(mp, dp),
            P(dp, mp),
            P(dp, mp),
            P(mp, dp),
        ),
        check_vma=False,
    )
```

time: 3340 us -> 1290 us (0.39)
  waiting for transfers between devices: 2060 us -> 531 us
  local copies, waits for them, and re-layouts: 512 us -> 277 us
  blocking collectives: 289 us -> 94.6 us
  other arithmetic: 229 us -> 107 us
  starting transfers between devices: 22 us -> 79 us
  matrix products: 192 us -> 155 us
    reduce_scatter x4 -> x5, waiting for transfers between devices: 1310 us -> 322 us  [the longest x4 322 us: collect(): lax.psum_scatter(grads.reshape(halves * all_rows, columns), ('c', 'z'), s...]
    all_gather x6, waiting for transfers between devices: 475 us -> 0.02 us  [the longest x1 0.01 us: shards(): finals = lax.all_gather(finals, ('z', 'j', 'c'), axis=0)]
    unnamed x19 -> x11, waiting for transfers between devices: 249 us -> 0.18 us
    all_gather x7 -> x1, blocking collectives: 289 us -> 41.2 us  [shards(): lax.all_gather(norm_gains, ('z', 'j'), axis=1, tiled=True).astype(F32)]
    slice x97 -> x31, local copies, waits for them, and re-layouts: 256 us -> 26.4 us  [the longest x1 5.86 us: shards(): down_part = down_part + dot(act_low, w_narrow[h], 1, 1)]
    ppermute x2 -> x69, waiting for transfers between devices: 0.01 us -> 209 us  [the longest x56 198 us: to_partner(): return lax.ppermute(block, 'j', [(i, i ^ bit) for i in range(PLANE)])]
    pad x48 -> x0, local copies, waits for them, and re-layouts: 115 us -> none  [the longest x24 63.9 us: shards(): lax.associative_scan(chain, (next_keep[:, ::-1], grad_state[:, ::-1]), ax...]
    dynamic_update_slice x0 -> x37, local copies, waits for them, and re-layouts: none -> 84.2 us  [the longest x35 81.8 us: put(): return lax.dynamic_update_index_in_dim(whole, block, index, axis)]
  transfers between devices with their start and end apart: 21 -> 80, of which waited for: 10 -> 50; matrix products, arithmetic and copies ran while one was open for 16% -> 31% of each run, Pallas kernels for 0% -> 1%
where the time goes in v1:
time: 1290 us; the launch traced here: 1280 us
  waiting for transfers between devices  531 us (41%)
  local copies, waits for them, and re-layouts  277 us (21%)
  matrix products  155 us (12%)
  other arithmetic  107 us (8%)
  blocking collectives  94.6 us (7%)
  starting transfers between devices  79 us (6%)
  Pallas kernels  17.1 us (1%)
  between operations  16.6 us (1%)
    reduce_scatter x4, waiting for transfers between devices, collect(): lax.psum_scatter(grads.reshape(halves * all_rows, columns), ('c', 'z'), s...  322 us
    ppermute x56, waiting for transfers between devices, to_partner(): return lax.ppermute(block, 'j', [(i, i ^ bit) for i in range(PLANE)])  198 us
    dot_general x18, matrix products, dot(): lax.dot_general(left, right, (((left_dim,), (right_dim,)), ((), ())), pre...  143 us
    dynamic_update_slice x35, local copies, waits for them, and re-layouts, put(): return lax.dynamic_update_index_in_dim(whole, block, index, axis)  81.8 us
    ppermute x56, starting transfers between devices, to_partner(): return lax.ppermute(block, 'j', [(i, i ^ bit) for i in range(PLANE)])  61.3 us
    psum x1, blocking collectives, shards(): g_gains = lax.psum(jnp.stack([g_gain_one, g_gain_two]), ('z', 'j', 'c'))  53.4 us
    all_gather x1, blocking collectives, shards(): lax.all_gather(norm_gains, ('z', 'j'), axis=1, tiled=True).astype(F32)  41.2 us
    unnamed x254, local copies, waits for them, and re-layouts  35.4 us
  transfers between devices with their start and end apart: 80, of which 50 were waited for; matrix products, arithmetic and copies ran while one was open for 31% of the time, Pallas kernels for 1%

profile of v1, /device:TPU:0, one launch (start us, length us, event | category | flops | bytes accessed | tf_op | source)
XLA Modules:
  0.0 1277.9 jit_solution(6133681904131155679)
XLA Ops:
  72.7 21.2 %collective-permute-done.24 = bf16[128,1536]{1,0:T(8,128)(2,1)} collective-permute-done((bf16[128,1536]{1,0:T(8,128)(2,1)}, bf16[128,1536]{1,0:T(8,128)(2,1)}, u32[]{:S(2)}, u32[]{:S(2)}) %collective-permute-start.24) | collective-permute-done | bytes 393248 | tf_op jit(solution)/shard_map/ppermute | solution.py:26
  105.7 41.2 %all_gather.29 = bf16[2,2048]{1,0:T(2,128)(2,1)S(1)} all-gather(bf16[2,128]{1,0:T(2,128)(2,1)S(1)} %copy-done.99), channel_id=1, replica_groups=mesh['z'=4,'j'=4,'c'=2] {'z','j'}, dimensions={1}, use_global_device_ids=true | all-gather | bytes 8704 | tf_op jit(solution)/shard_map/all_gather | solution.py:278
  166.8 5.2 fusion.1
  180.3 6.5 slice_bitcast_fusion
  186.8 9.4 concatenate.107
  196.1 8.9 fusion.159
  223.4 4.8 reshape.1582
  228.2 5.2 copy.662
  236.7 5.4 copy.661
  242.1 5.4 fusion.21
  247.5 8.0 shard_map.246
  259.7 4.2 collective-permute-start.12
  272.5 3.9 convolution_convert_fusion.4
  284.5 7.0 collective-permute-done.16
  294.4 19.6 %collective-permute-done.36 = bf16[2,128,2048]{2,1,0:T(8,128)(2,1)S(1)} collective-permute-done((bf16[2,128,2048]{2,1,0:T(8,128)(2,1)S(1)}, bf16[2,128,2048]{2,1,0:T(8,128)(2,1)S(1)}, u32[]{:S(2)}, u32[]{:S(2)}) %collective-permute-start.36) | collective-permute-done | bytes 1048608 | tf_op jit(solution)/shard_map/ppermute | solution.py:26
  317.2 19.3 %collective-permute-done.19 = bf16[2,128,2048]{2,1,0:T(8,128)(2,1)S(1)} collective-permute-done((bf16[2,128,2048]{2,1,0:T(8,128)(2,1)S(1)}, bf16[2,128,2048]{2,1,0:T(8,128)(2,1)S(1)}, u32[]{:S(2)}, u32[]{:S(2)}) %collective-permute-start.19) | collective-permute-done | bytes 1048608 | tf_op jit(solution)/shard_map/ppermute | solution.py:26
  344.7 4.6 collective-permute-done.38
  350.4 5.9 fusion.151
  356.3 8.9 collective-permute-done.21
  377.7 5.6 fusion.150
  383.3 10.2 fusion.160
  393.4 8.6 fusion.162
  402.1 11.5 fusion.10
  413.6 10.3 fusion.17
  423.9 9.0 fusion.53
  432.9 9.3 add_convert_fusion
  449.2 11.2 collective-permute-done.39
  472.8 6.4 collective-permute-done.42
  479.2 5.3 collective-permute-done.40
  489.2 4.3 bitcast_dynamic-update-slice_fusion.2
  498.8 15.8 %collective-permute-done.44 = bf16[2,128,2048]{2,1,0:T(8,128)(2,1)} collective-permute-done((bf16[2,128,2048]{2,1,0:T(8,128)(2,1)}, bf16[2,128,2048]{2,1,0:T(8,128)(2,1)}, u32[]{:S(2)}, u32[]{:S(2)}) %collective-permute-start.44) | collective-permute-done | bytes 1048608 | tf_op jit(solution)/shard_map/ppermute | solution.py:26
  529.0 9.2 fusion.70
  538.2 9.1 shard_map.247
  557.0 6.0 fusion.56
  569.8 5.1 copy.710
  574.9 4.8 reshape.1592
  579.7 5.8 fusion.142
  585.6 6.4 multiply_reduce_fusion.1
  598.3 5.3 copy.711
  603.6 9.6 fusion.141
  620.0 5.2 convolution_convert_fusion.7
  628.8 5.9 fusion.19
  634.7 5.7 fusion.18
  649.5 3.8 collective-permute-done.50
  654.5 6.3 convolution_convert_fusion.2
  664.8 7.9 copy.719
  672.8 9.7 fusion.3
  682.5 9.6 fusion.2
  692.1 5.5 pad_maximum_fusion
  699.5 7.3 fusion.161
  706.8 6.0 add_convert_fusion.1
  716.1 6.3 convolution_convert_fusion.3
  733.5 5.8 collective-permute-done.51
  755.7 3.8 constant_dynamic-update-slice_fusion.3
  760.8 4.3 collective-permute-done.54
  780.9 53.4 %psum.7 = f32[2,2048]{1,0:T(2,128)S(1)} all-reduce(f32[2,2048]{1,0:T(2,128)S(1)} %pad_maximum_fusion.30), channel_id=1, replica_groups=mesh['z'=4,'j'=4,'c'=2] {'z','j','c'}, use_global_device_ids=true, to_apply=%region_9.10 | all-reduce | flops 4096 | bytes 32768 | tf_op jit(solution)/shard_map/psum | solution.py:502
  863.7 92.4 %reduce-scatter.6.cloned.1.call-done = bf16[512,640]{1,0:T(8,128)(2,1)} async-done(((bf16[4096,640]{1,0:T(8,128)(2,1)}), bf16[512,640]{1,0:T(8,128)(2,1)}) %reduce-scatter.6.cloned.1.call-update) | async-done | bytes 655376 | tf_op jit(solution)/shard_map/reduce_scatter | solution.py:89
  958.6 4.9 collective-permute-done.56
  969.3 4.9 collective-permute-done.57
  974.3 229.9 %reduce-scatter.12.cloned.1.call-done = bf16[512,1536]{1,0:T(8,128)(2,1)} async-done(((bf16[4096,1536]{1,0:T(8,128)(2,1)}), bf16[512,1536]{1,0:T(8,128)(2,1)}) %reduce-scatter.12.cloned.1.call-update) | async-done | bytes 1572880 | tf_op jit(solution)/shard_map/reduce_scatter | solution.py:89
  1220.3 7.0 collective-permute-done.64
  1231.3 11.0 dynamic_update_slice.175
  1242.3 11.1 dynamic_update_slice.176
  1253.4 13.9 %dynamic_update_slice.177 = bf16[4,128,1536]{2,0,1:T(4,128)(2,1)S(1)} dynamic-update-slice(bf16[4,128,1536]{2,0,1:T(4,128)(2,1)S(1)} %dynamic_update_slice.176, bf16[1,128,1536]{2,0,1:T(2,128)(2,1)} %copy.735, s32[]{:T(128)S(6)} %select_n.321, s32[]{:T(128)} %constant.331.clone.1, s32[]{:T(128)} %constant.331.clone.1) | dynamic-update-slice | bytes 786436 | tf_op jit(solution)/shard_map/jit(dynamic_update_index_in_dim)/dynamic_update_slice | solution.py:34
  (669 shorter events, 376.4 us)
Async XLA Ops:
  7.2 164.7 %all-gather.17.cloned.1.call-start = ((), (), s32[]{:S(2)}) async-start(), calls=%async_computation.14 | async-start | bytes 2027520 | tf_op jit(solution)/shard_map/all_gather | solution.py:279
  10.8 165.3 %all-gather.11.cloned.1.call-start = ((), (), s32[]{:S(2)}) async-start(), calls=%async_computation.6 | async-start | bytes 2949120 | tf_op jit(solution)/shard_map/all_gather | solution.py:82
  33.3 147.0 %all-gather.9.cloned.1.call-start = ((), (), s32[]{:S(2)}) async-start(), calls=%async_computation.5 | async-start | bytes 5898240 | tf_op jit(solution)/shard_map/all_gather | solution.py:82
  34.0 6.8 collective-permute-start.4
  34.8 8.7 collective-permute-start.5
  35.8 8.6 collective-permute-start.6
  45.7 304.7 %all-gather.15.cloned.1.call-start = ((), (), s32[]{:S(2)}) async-start(), calls=%async_computation.8 | async-start | bytes 7077888 | tf_op jit(solution)/shard_map/all_gather | solution.py:82
  46.8 6.7 collective-permute-start.28
  48.2 6.6 collective-permute-start.29
  56.0 321.6 %all-gather.13.cloned.1.call-start = ((), (), s32[]{:S(2)}) async-start(), calls=%async_computation.7 | async-start | bytes 14155776 | tf_op jit(solution)/shard_map/all_gather | solution.py:82
  58.2 94.1 %collective-permute-start = (bf16[2,128,2048]{2,1,0:T(8,128)(2,1)S(1)}, bf16[2,128,2048]{2,1,0:T(8,128)(2,1)}, u32[]{:S(2)}, u32[]{:S(2)}) collective-permute-start(bf16[2,128,2048]{2,1,0:T(8,128)(2,1)S(1)} %get-tuple-element.161), channel_id=1, source_target_pairs={{0,2},{2,0},{4,6},{6,4},{1,3},{3,1},{5,7},{7,5},{8,10},{10,8},{12,... | collective-permute-start | bytes 3145736 | tf_op jit(solution)/shard_map/ppermute | solution.py:26
  59.6 91.5 %collective-permute-start.1 = (bf16[2,128,2048]{2,1,0:T(8,128)(2,1)S(1)}, bf16[2,128,2048]{2,1,0:T(8,128)(2,1)}, u32[]{:S(2)}, u32[]{:S(2)}) collective-permute-start(bf16[2,128,2048]{2,1,0:T(8,128)(2,1)S(1)} %get-tuple-element.161), channel_id=1, source_target_pairs={{0,4},{2,6},{4,0},{6,2},{1,5},{3,7},{5,1},{7,3},{8,12},{10,14},{12... | collective-permute-start | bytes 3145736 | tf_op jit(solution)/shard_map/ppermute | solution.py:26
  64.3 29.6 %collective-permute-start.24 = (bf16[128,1536]{1,0:T(8,128)(2,1)}, bf16[128,1536]{1,0:T(8,128)(2,1)}, u32[]{:S(2)}, u32[]{:S(2)}) collective-permute-start(bf16[128,1536]{1,0:T(8,128)(2,1)} %bitcast.626), channel_id=1, source_target_pairs={{0,2},{2,0},{4,6},{6,4},{1,3},{3,1},{5,7},{7,5},{8,10},{10,8},{12,... | collective-permute-start | bytes 1179656 | tf_op jit(solution)/shard_map/ppermute | solution.py:26
  66.2 32.2 %collective-permute-start.25 = (bf16[128,1536]{1,0:T(8,128)(2,1)}, bf16[128,1536]{1,0:T(8,128)(2,1)S(1)}, u32[]{:S(2)}, u32[]{:S(2)}) collective-permute-start(bf16[128,1536]{1,0:T(8,128)(2,1)} %bitcast.625), channel_id=1, source_target_pairs={{0,4},{2,6},{4,0},{6,2},{1,5},{3,7},{5,1},{7,3},{8,12},{10,14},{12... | collective-permute-start | bytes 1179656 | tf_op jit(solution)/shard_map/ppermute | solution.py:26
  67.7 32.2 %collective-permute-start.26 = (bf16[128,1536]{1,0:T(8,128)(2,1)}, bf16[128,1536]{1,0:T(8,128)(2,1)S(1)}, u32[]{:S(2)}, u32[]{:S(2)}) collective-permute-start(bf16[128,1536]{1,0:T(8,128)(2,1)} %bitcast.623), channel_id=1, source_target_pairs={{0,6},{2,4},{4,2},{6,0},{1,7},{3,5},{5,3},{7,1},{8,14},{10,12},{12... | collective-permute-start | bytes 1179656 | tf_op jit(solution)/shard_map/ppermute | solution.py:26
  94.0 57.1 %collective-permute-start.8 = (bf16[2,2,3,320]{3,1,2,0:T(2,128)(2,1)S(1)}, bf16[2,2,3,320]{3,1,2,0:T(2,128)(2,1)S(1)}, u32[]{:S(2)}, u32[]{:S(2)}) collective-permute-start(bf16[2,2,3,320]{3,1,2,0:T(2,128)(2,1)S(1)} %get-tuple-element.259), channel_id=1, source_target_pairs={{0,1},{1,0},{2,3},{3,2},{4,5},{5,4},{6,7},{7,6},{8,9},{9,8},{10,11... | collective-permute-start | bytes 23048 | tf_op jit(solution)/shard_map/ppermute | solution.py:100
  98.4 52.5 %collective-permute-start.9 = (f32[2,2,320]{2,1,0:T(2,128)S(1)}, f32[2,2,320]{2,1,0:T(2,128)S(1)}, u32[]{:S(2)}, u32[]{:S(2)}) collective-permute-start(f32[2,2,320]{2,1,0:T(2,128)S(1)} %get-tuple-element.261), channel_id=1, source_target_pairs={{0,1},{1,0},{2,3},{3,2},{4,5},{5,4},{6,7},{7,6},{8,9},{9,8},{10,11... | collective-permute-start | bytes 15368 | tf_op jit(solution)/shard_map/ppermute | solution.py:100
  105.1 639.7 %all-gather.19.cloned.1.call-start = ((), (), s32[]{:S(2)}) async-start(), calls=%async_computation.15 | async-start | bytes 1351680 | tf_op jit(solution)/shard_map/all_gather | solution.py:393
  152.2 9.2 collective-permute-start.3
  153.4 9.2 collective-permute-start.2
  259.7 8.5 collective-permute-start.12
  276.6 14.9 %collective-permute-start.16 = (bf16[1,128,2048]{2,1,0:T(8,128)(2,1)S(1)}, bf16[1,128,2048]{2,1,0:T(8,128)(2,1)S(1)}, u32[]{:S(2)}, u32[]{:S(2)}) collective-permute-start(bf16[1,128,2048]{2,1,0:T(8,128)(2,1)S(1)} %get-tuple-element.213), channel_id=1, source_target_pairs={{0,4},{2,6},{4,0},{6,2},{1,5},{3,7},{5,1},{7,3},{8,12},{10,14},{12... | collective-permute-start | bytes 1572872 | tf_op jit(solution)/shard_map/ppermute | solution.py:26
  278.3 14.9 %collective-permute-start.18 = (bf16[1,128,2048]{2,1,0:T(8,128)(2,1)S(1)}, bf16[1,128,2048]{2,1,0:T(8,128)(2,1)S(1)}, u32[]{:S(2)}, u32[]{:S(2)}) collective-permute-start(bf16[1,128,2048]{2,1,0:T(8,128)(2,1)S(1)} %get-tuple-element.215), channel_id=1, source_target_pairs={{0,2},{2,0},{4,6},{6,4},{1,3},{3,1},{5,7},{7,5},{8,10},{10,8},{12,... | collective-permute-start | bytes 1572872 | tf_op jit(solution)/shard_map/ppermute | solution.py:26
  282.1 33.6 %collective-permute-start.35 = (bf16[2,128,2048]{2,1,0:T(8,128)(2,1)S(1)}, bf16[2,128,2048]{2,1,0:T(8,128)(2,1)S(1)}, u32[]{:S(2)}, u32[]{:S(2)}) collective-permute-start(bf16[2,128,2048]{2,1,0:T(8,128)(2,1)S(1)} %get-tuple-element.163), channel_id=1, source_target_pairs={{0,2},{2,0},{4,6},{6,4},{1,3},{3,1},{5,7},{7,5},{8,10},{10,8},{12,... | collective-permute-start | bytes 3145736 | tf_op jit(solution)/shard_map/ppermute | solution.py:26
  284.1 29.9 %collective-permute-start.36 = (bf16[2,128,2048]{2,1,0:T(8,128)(2,1)S(1)}, bf16[2,128,2048]{2,1,0:T(8,128)(2,1)S(1)}, u32[]{:S(2)}, u32[]{:S(2)}) collective-permute-start(bf16[2,128,2048]{2,1,0:T(8,128)(2,1)S(1)} %get-tuple-element.163), channel_id=1, source_target_pairs={{0,4},{2,6},{4,0},{6,2},{1,5},{3,7},{5,1},{7,3},{8,12},{10,14},{12... | collective-permute-start | bytes 3145736 | tf_op jit(solution)/shard_map/ppermute | solution.py:26
  293.8 42.7 %collective-permute-start.19 = (bf16[2,128,2048]{2,1,0:T(8,128)(2,1)S(1)}, bf16[2,128,2048]{2,1,0:T(8,128)(2,1)S(1)}, u32[]{:S(2)}, u32[]{:S(2)}) collective-permute-start(bf16[2,128,2048]{2,1,0:T(8,128)(2,1)S(1)} %pad_maximum_fusion.20), channel_id=1, source_target_pairs={{0,4},{2,6},{4,0},{6,2},{1,5},{3,7},{5,1},{7,3},{8,12},{10,14},{12... | collective-permute-start | bytes 3145736 | tf_op jit(solution)/shard_map/ppermute | solution.py:26
  294.3 43.8 %collective-permute-start.17 = (bf16[2,128,2048]{2,1,0:T(8,128)(2,1)S(1)}, bf16[2,128,2048]{2,1,0:T(8,128)(2,1)S(1)}, u32[]{:S(2)}, u32[]{:S(2)}) collective-permute-start(bf16[2,128,2048]{2,1,0:T(8,128)(2,1)S(1)} %pad_maximum_fusion.19), channel_id=1, source_target_pairs={{0,2},{2,0},{4,6},{6,4},{1,3},{3,1},{5,7},{7,5},{8,10},{10,8},{12,... | collective-permute-start | bytes 3145736 | tf_op jit(solution)/shard_map/ppermute | solution.py:26
  314.1 35.2 %collective-permute-start.38 = (bf16[1,128,2048]{2,1,0:T(8,128)(2,1)S(1)}, bf16[1,128,2048]{2,1,0:T(8,128)(2,1)S(1)}, u32[]{:S(2)}, u32[]{:S(2)}) collective-permute-start(bf16[1,128,2048]{2,1,0:T(8,128)(2,1)S(1)} %slice.583), channel_id=1, source_target_pairs={{0,2},{2,0},{4,6},{6,4},{1,3},{3,1},{5,7},{7,5},{8,10},{10,8},{12,... | collective-permute-start | bytes 1572872 | tf_op jit(solution)/shard_map/ppermute | solution.py:26
  315.7 33.6 %collective-permute-start.37 = (bf16[1,128,2048]{2,1,0:T(8,128)(2,1)S(1)}, bf16[1,128,2048]{2,1,0:T(8,128)(2,1)S(1)}, u32[]{:S(2)}, u32[]{:S(2)}) collective-permute-start(bf16[1,128,2048]{2,1,0:T(8,128)(2,1)S(1)} %slice.582), channel_id=1, source_target_pairs={{0,4},{2,6},{4,0},{6,2},{1,5},{3,7},{5,1},{7,3},{8,12},{10,14},{12... | collective-permute-start | bytes 1572872 | tf_op jit(solution)/shard_map/ppermute | solution.py:26
  343.2 23.0 %collective-permute-start.20 = (bf16[2,128,2048]{2,1,0:T(8,128)(2,1)}, bf16[2,128,2048]{2,1,0:T(8,128)(2,1)}, u32[]{:S(2)}, u32[]{:S(2)}) collective-permute-start(bf16[2,128,2048]{2,1,0:T(8,128)(2,1)} %get-tuple-element.167), channel_id=1, source_target_pairs={{0,2},{2,0},{4,6},{6,4},{1,3},{3,1},{5,7},{7,5},{8,10},{10,8},{12,... | collective-permute-start | bytes 3145736 | tf_op jit(solution)/shard_map/ppermute | solution.py:26
  343.2 21.9 %collective-permute-start.21 = (bf16[2,128,2048]{2,1,0:T(8,128)(2,1)}, bf16[2,128,2048]{2,1,0:T(8,128)(2,1)}, u32[]{:S(2)}, u32[]{:S(2)}) collective-permute-start(bf16[2,128,2048]{2,1,0:T(8,128)(2,1)} %get-tuple-element.167), channel_id=1, source_target_pairs={{0,4},{2,6},{4,0},{6,2},{1,5},{3,7},{5,1},{7,3},{8,12},{10,14},{12... | collective-permute-start | bytes 3145736 | tf_op jit(solution)/shard_map/ppermute | solution.py:26
  366.2 9.2 collective-permute-start.23
  367.4 9.2 collective-permute-start.22
  445.4 14.9 %collective-permute-start.39 = (bf16[1,128,2048]{2,1,0:T(8,128)(2,1)}, bf16[1,128,2048]{2,1,0:T(8,128)(2,1)}, u32[]{:S(2)}, u32[]{:S(2)}) collective-permute-start(bf16[1,128,2048]{2,1,0:T(8,128)(2,1)} %get-tuple-element.201), channel_id=1, source_target_pairs={{0,4},{2,6},{4,0},{6,2},{1,5},{3,7},{5,1},{7,3},{8,12},{10,14},{12... | collective-permute-start | bytes 1572872 | tf_op jit(solution)/shard_map/ppermute | solution.py:26
  446.5 14.6 %collective-permute-start.41 = (bf16[1,128,2048]{2,1,0:T(8,128)(2,1)}, bf16[1,128,2048]{2,1,0:T(8,128)(2,1)}, u32[]{:S(2)}, u32[]{:S(2)}) collective-permute-start(bf16[1,128,2048]{2,1,0:T(8,128)(2,1)} %get-tuple-element.203), channel_id=1, source_target_pairs={{0,2},{2,0},{4,6},{6,4},{1,3},{3,1},{5,7},{7,5},{8,10},{10,8},{12,... | collective-permute-start | bytes 1572872 | tf_op jit(solution)/shard_map/ppermute | solution.py:26
  464.1 15.1 %collective-permute-start.42 = (bf16[2,128,2048]{2,1,0:T(8,128)(2,1)}, bf16[2,128,2048]{2,1,0:T(8,128)(2,1)}, u32[]{:S(2)}, u32[]{:S(2)}) collective-permute-start(bf16[2,128,2048]{2,1,0:T(8,128)(2,1)} %pad_maximum_fusion.24), channel_id=1, source_target_pairs={{0,4},{2,6},{4,0},{6,2},{1,5},{3,7},{5,1},{7,3},{8,12},{10,14},{12... | collective-permute-start | bytes 3145736 | tf_op jit(solution)/shard_map/ppermute | solution.py:26
  466.1 18.4 %collective-permute-start.40 = (bf16[2,128,2048]{2,1,0:T(8,128)(2,1)}, bf16[2,128,2048]{2,1,0:T(8,128)(2,1)}, u32[]{:S(2)}, u32[]{:S(2)}) collective-permute-start(bf16[2,128,2048]{2,1,0:T(8,128)(2,1)} %pad_maximum_fusion.23), channel_id=1, source_target_pairs={{0,2},{2,0},{4,6},{6,4},{1,3},{3,1},{5,7},{7,5},{8,10},{10,8},{12,... | collective-permute-start | bytes 3145736 | tf_op jit(solution)/shard_map/ppermute | solution.py:26
  493.5 23.5 %collective-permute-start.43 = (bf16[2,128,2048]{2,1,0:T(8,128)(2,1)}, bf16[2,128,2048]{2,1,0:T(8,128)(2,1)}, u32[]{:S(2)}, u32[]{:S(2)}) collective-permute-start(bf16[2,128,2048]{2,1,0:T(8,128)(2,1)} %get-tuple-element.158), channel_id=1, source_target_pairs={{0,2},{2,0},{4,6},{6,4},{1,3},{3,1},{5,7},{7,5},{8,10},{10,8},{12,... | collective-permute-start | bytes 3145736 | tf_op jit(solution)/shard_map/ppermute | solution.py:26
  495.9 18.7 %collective-permute-start.44 = (bf16[2,128,2048]{2,1,0:T(8,128)(2,1)}, bf16[2,128,2048]{2,1,0:T(8,128)(2,1)}, u32[]{:S(2)}, u32[]{:S(2)}) collective-permute-start(bf16[2,128,2048]{2,1,0:T(8,128)(2,1)} %get-tuple-element.158), channel_id=1, source_target_pairs={{0,4},{2,6},{4,0},{6,2},{1,5},{3,7},{5,1},{7,3},{8,12},{10,14},{12... | collective-permute-start | bytes 3145736 | tf_op jit(solution)/shard_map/ppermute | solution.py:26
  498.7 277.0 %reduce-scatter.8.cloned.1.call-start = ((), (), s32[]{:S(2)}) async-start(), calls=%async_computation.10 | async-start | bytes 552960 | tf_op jit(solution)/shard_map/reduce_scatter | solution.py:493
  515.7 9.2 collective-permute-start.46
  518.0 9.9 collective-permute-start.45
  547.3 7.4 collective-permute-start.49
  549.9 7.0 collective-permute-start.48
  619.9 215.0 %reduce-scatter.10.cloned.1.call-start = ((), (), s32[]{:S(2)}) async-start(), calls=%async_computation.11 | async-start | bytes 2949120 | tf_op jit(solution)/shard_map/reduce_scatter | solution.py:89
  627.5 228.3 %reduce-scatter.14.cloned.1.call-start = ((), (), s32[]{:S(2)}) async-start(), calls=%async_computation.13 | async-start | bytes 7077888 | tf_op jit(solution)/shard_map/reduce_scatter | solution.py:89
  643.8 312.2 %reduce-scatter.6.cloned.1.call-start = ((), (), s32[]{:S(2)}) async-start(), calls=%async_computation.9 | async-start | bytes 5898240 | tf_op jit(solution)/shard_map/reduce_scatter | solution.py:89
  672.7 531.5 %reduce-scatter.12.cloned.1.call-start = ((), (), s32[]{:S(2)}) async-start(), calls=%async_computation.12 | async-start | bytes 14155776 | tf_op jit(solution)/shard_map/reduce_scatter | solution.py:89
  713.1 14.9 %collective-permute-start.30 = (bf16[1,128,2048]{2,1,0:T(8,128)(2,1)S(1)}, bf16[1,128,2048]{2,1,0:T(8,128)(2,1)S(1)}, u32[]{:S(2)}, u32[]{:S(2)}) collective-permute-start(bf16[1,128,2048]{2,1,0:T(8,128)(2,1)S(1)} %get-tuple-element.207), channel_id=1, source_target_pairs={{0,4},{2,6},{4,0},{6,2},{1,5},{3,7},{5,1},{7,3},{8,12},{10,14},{12... | collective-permute-start | bytes 1572872 | tf_op jit(solution)/shard_map/ppermute | solution.py:26
  714.2 14.9 %collective-permute-start.32 = (bf16[1,128,2048]{2,1,0:T(8,128)(2,1)S(1)}, bf16[1,128,2048]{2,1,0:T(8,128)(2,1)S(1)}, u32[]{:S(2)}, u32[]{:S(2)}) collective-permute-start(bf16[1,128,2048]{2,1,0:T(8,128)(2,1)S(1)} %get-tuple-element.209), channel_id=1, source_target_pairs={{0,2},{2,0},{4,6},{6,4},{1,3},{3,1},{5,7},{7,5},{8,10},{10,8},{12,... | collective-permute-start | bytes 1572872 | tf_op jit(solution)/shard_map/ppermute | solution.py:26
  722.7 16.6 %collective-permute-start.51 = (bf16[1,128,2048]{2,1,0:T(8,128)(2,1)S(1)}, bf16[1,128,2048]{2,1,0:T(8,128)(2,1)S(1)}, u32[]{:S(2)}, u32[]{:S(2)}) collective-permute-start(bf16[1,128,2048]{2,1,0:T(8,128)(2,1)S(1)} %get-tuple-element.195), channel_id=1, source_target_pairs={{0,4},{2,6},{4,0},{6,2},{1,5},{3,7},{5,1},{7,3},{8,12},{10,14},{12... | collective-permute-start | bytes 1572872 | tf_op jit(solution)/shard_map/ppermute | solution.py:26
  723.8 16.6 %collective-permute-start.53 = (bf16[1,128,2048]{2,1,0:T(8,128)(2,1)S(1)}, bf16[1,128,2048]{2,1,0:T(8,128)(2,1)S(1)}, u32[]{:S(2)}, u32[]{:S(2)}) collective-permute-start(bf16[1,128,2048]{2,1,0:T(8,128)(2,1)S(1)} %get-tuple-element.197), channel_id=1, source_target_pairs={{0,2},{2,0},{4,6},{6,4},{1,3},{3,1},{5,7},{7,5},{8,10},{10,8},{12,... | collective-permute-start | bytes 1572872 | tf_op jit(solution)/shard_map/ppermute | solution.py:26
  730.6 23.4 %collective-permute-start.33 = (bf16[2,128,2048]{2,1,0:T(8,128)(2,1)}, bf16[2,128,2048]{2,1,0:T(8,128)(2,1)}, u32[]{:S(2)}, u32[]{:S(2)}) collective-permute-start(bf16[2,128,2048]{2,1,0:T(8,128)(2,1)} %pad_maximum_fusion.22), channel_id=1, source_target_pairs={{0,4},{2,6},{4,0},{6,2},{1,5},{3,7},{5,1},{7,3},{8,12},{10,14},{12... | collective-permute-start | bytes 3145736 | tf_op jit(solution)/shard_map/ppermute | solution.py:26
  732.6 22.8 %collective-permute-start.31 = (bf16[2,128,2048]{2,1,0:T(8,128)(2,1)}, bf16[2,128,2048]{2,1,0:T(8,128)(2,1)}, u32[]{:S(2)}, u32[]{:S(2)}) collective-permute-start(bf16[2,128,2048]{2,1,0:T(8,128)(2,1)} %pad_maximum_fusion.21), channel_id=1, source_target_pairs={{0,2},{2,0},{4,6},{6,4},{1,3},{3,1},{5,7},{7,5},{8,10},{10,8},{12,... | collective-permute-start | bytes 3145736 | tf_op jit(solution)/shard_map/ppermute | solution.py:26
  741.8 23.3 %collective-permute-start.54 = (bf16[2,128,2048]{2,1,0:T(8,128)(2,1)}, bf16[2,128,2048]{2,1,0:T(8,128)(2,1)S(1)}, u32[]{:S(2)}, u32[]{:S(2)}) collective-permute-start(bf16[2,128,2048]{2,1,0:T(8,128)(2,1)} %pad_maximum_fusion.26), channel_id=1, source_target_pairs={{0,4},{2,6},{4,0},{6,2},{1,5},{3,7},{5,1},{7,3},{8,12},{10,14},{12... | collective-permute-start | bytes 3145736 | tf_op jit(solution)/shard_map/ppermute | solution.py:26
  743.9 22.7 %collective-permute-start.52 = (bf16[2,128,2048]{2,1,0:T(8,128)(2,1)}, bf16[2,128,2048]{2,1,0:T(8,128)(2,1)}, u32[]{:S(2)}, u32[]{:S(2)}) collective-permute-start(bf16[2,128,2048]{2,1,0:T(8,128)(2,1)} %pad_maximum_fusion.25), channel_id=1, source_target_pairs={{0,2},{2,0},{4,6},{6,4},{1,3},{3,1},{5,7},{7,5},{8,10},{10,8},{12,... | collective-permute-start | bytes 3145736 | tf_op jit(solution)/shard_map/ppermute | solution.py:26
  760.8 16.3 %collective-permute-start.34 = (bf16[2,128,2048]{2,1,0:T(8,128)(2,1)}, bf16[2,128,2048]{2,1,0:T(8,128)(2,1)}, u32[]{:S(2)}, u32[]{:S(2)}) collective-permute-start(bf16[2,128,2048]{2,1,0:T(8,128)(2,1)} %get-tuple-element.165), channel_id=1, source_target_pairs={{0,1},{1,0},{2,3},{3,2},{4,5},{5,4},{6,7},{7,6},{8,9},{9,8},{10,11... | collective-permute-start | bytes 3145736 | tf_op jit(solution)/shard_map/ppermute | solution.py:110
  774.1 67.9 %collective-permute-start.55 = (bf16[2,128,2048]{2,1,0:T(8,128)(2,1)}, bf16[2,128,2048]{2,1,0:T(8,128)(2,1)S(1)}, u32[]{:S(2)}, u32[]{:S(2)}) collective-permute-start(bf16[2,128,2048]{2,1,0:T(8,128)(2,1)} %get-tuple-element.154), channel_id=1, source_target_pairs={{0,1},{1,0},{2,3},{3,2},{4,5},{5,4},{6,7},{7,6},{8,9},{9,8},{10,11... | collective-permute-start | bytes 3145736 | tf_op jit(solution)/shard_map/ppermute | solution.py:110
  859.5 99.0 %collective-permute-start.67 = (bf16[128,768]{0,1:T(8,128)(2,1)S(1)}, bf16[128,768]{0,1:T(8,128)(2,1)S(1)}, u32[]{:S(2)}, u32[]{:S(2)}) collective-permute-start(bf16[128,768]{0,1:T(8,128)(2,1)S(1)} %bitcast.628), channel_id=1, source_target_pairs={{0,4},{2,6},{4,0},{6,2},{1,5},{3,7},{5,1},{7,3},{8,12},{10,14},{12... | collective-permute-start | bytes 589832 | tf_op jit(solution)/shard_map/ppermute | solution.py:26
  861.6 105.0 %collective-permute-start.68 = (bf16[128,768]{0,1:T(8,128)(2,1)S(1)}, bf16[128,768]{0,1:T(8,128)(2,1)S(1)}, u32[]{:S(2)}, u32[]{:S(2)}) collective-permute-start(bf16[128,768]{0,1:T(8,128)(2,1)S(1)} %bitcast.627), channel_id=1, source_target_pairs={{0,6},{2,4},{4,2},{6,0},{1,7},{3,5},{5,3},{7,1},{8,14},{10,12},{12... | collective-permute-start | bytes 589832 | tf_op jit(solution)/shard_map/ppermute | solution.py:26
  965.2 9.0 collective-permute-start.57
  1206.4 12.3 collective-permute-start.63
  1207.9 19.4 %collective-permute-start.64 = (bf16[128,1536]{1,0:T(8,128)(2,1)}, bf16[128,1536]{1,0:T(8,128)(2,1)}, u32[]{:S(2)}, u32[]{:S(2)}) collective-permute-start(bf16[128,1536]{1,0:T(8,128)(2,1)} %get-tuple-element.233), channel_id=1, source_target_pairs={{0,4},{2,6},{4,0},{6,2},{1,5},{3,7},{5,1},{7,3},{8,12},{10,14},{12... | collective-permute-start | bytes 1179656 | tf_op jit(solution)/shard_map/ppermute | solution.py:26
  1209.3 19.5 %collective-permute-start.65 = (bf16[128,1536]{1,0:T(8,128)(2,1)S(1)}, bf16[128,1536]{1,0:T(8,128)(2,1)}, u32[]{:S(2)}, u32[]{:S(2)}) collective-permute-start(bf16[128,1536]{1,0:T(8,128)(2,1)S(1)} %get-tuple-element.232), channel_id=1, source_target_pairs={{0,6},{2,4},{4,2},{6,0},{1,7},{3,5},{5,3},{7,1},{8,14},{10,12},{12... | collective-permute-start | bytes 1179656 | tf_op jit(solution)/shard_map/ppermute | solution.py:26
  (134 other events, 2020.9 us)
Sparse Core Ops, SparseCore 0:
  11.5 60.5 all-gather.16
  74.3 32.8 all-gather.10
  109.4 55.0 all-gather.8
  165.9 63.4 all-gather.14
  231.4 115.4 all-gather.12
  498.8 54.5 all-gather.18
  620.0 31.0 reduce-scatter.7
  653.6 57.7 reduce-scatter.9
  713.8 131.4 reduce-scatter.13
  847.5 108.5 reduce-scatter.5
  958.5 245.6 reduce-scatter.11

commit v2 on v1

--- a/solution.py
+++ b/solution.py
@@ -32,6 +32,12 @@
 
 def put(whole, block, index, axis):
     return lax.dynamic_update_index_in_dim(whole, block, index, axis)
+
+
+def in_order(found, index):
+    low, high = index % 2 == 1, index // 2 == 1
+    found = [jnp.where(low, found[k ^ 1], found[k]) for k in range(PLANE)]
+    return [jnp.where(high, found[k ^ 2], found[k]) for k in range(PLANE)]
 
 
 def plane_gather(own):
@@ -70,26 +76,50 @@
 
 def plane_swap(blocks):
     mine = lax.axis_index("j")
-    swapped = blocks
-    for bit in (1, 2, 3):
-        swapped = put(swapped, to_partner(at(blocks, mine ^ bit, 0), bit), mine ^ bit, 0)
-    return swapped
-
-
-def spread(weight):
-    rows, four, columns = weight.shape
-    blocks = plane_swap(jnp.moveaxis(weight, 1, 0)).reshape(four * rows, columns)
-    return lax.all_gather(blocks, ("c", "z"), axis=0, tiled=False).reshape(
-        lax.axis_size("c"), -1, columns
-    )
-
-
-def collect(grads, rows):
-    halves, all_rows, columns = grads.shape
-    summed = lax.psum_scatter(
-        grads.reshape(halves * all_rows, columns), ("c", "z"), scatter_dimension=0, tiled=True
-    )
-    return jnp.moveaxis(plane_swap(summed.reshape(PLANE, rows, columns)), 0, 1).astype(F32)
+    found = [at(blocks, mine, 0)]
+    found += [to_partner(at(blocks, mine ^ bit, 0), bit) for bit in (1, 2, 3)]
+    return in_order(found, mine)
+
+
+def to_chips(weight):
+    rows, columns = weight.shape
+    blocks = weight.reshape(rows, PLANE, columns // PLANE)
+    return jnp.moveaxis(blocks, 1, 0)
+
+
+def to_core(block):
+    return lax.ppermute(block, "c", [(0, 1), (1, 0)])
+
+
+def along_z(block):
+    own = lax.all_gather(block, "z", axis=0, tiled=True)
+    return own, to_core(own)
+
+
+def collect(own, other):
+    total = (own.astype(F32) + to_core(other).astype(F32)).astype(BF16)
+    summed = lax.psum_scatter(total, "z", scatter_dimension=0, tiled=True)
+    return plane_swap(summed.reshape(PLANE, -1, summed.shape[1]))
+
+
+def z_gather(block):
+    size, mine = lax.axis_size("z"), lax.axis_index("z")
+    whole = jnp.zeros((size, *block.shape), block.dtype)
+    whole = put(whole, block, mine, 0)
+    for step in range(1, size):
+        got = lax.ppermute(block, "z", [(i, (i + step) % size) for i in range(size)])
+        whole = put(whole, got, (mine - step) % size, 0)
+    return whole
+
+
+def sum_of_all(array):
+    for axis, pairs in (
+        ("c", [(0, 1), (1, 0)]),
+        ("j", [(i, i ^ 1) for i in range(PLANE)]),
+        ("j", [(i, i ^ 2) for i in range(PLANE)]),
+    ):
+        array = array + lax.ppermute(array, axis, pairs)
+    return jnp.sum(z_gather(array), axis=0)
 
 
 def with_other_core(array, dim):
@@ -97,17 +127,12 @@
     count = array.shape[0] // 2
     mine = lax.dynamic_slice_in_dim(array, core * count, count, 0)
     other = lax.dynamic_slice_in_dim(array, (1 - core) * count, count, 0)
-    other = lax.ppermute(other, "c", [(0, 1), (1, 0)])
-    return jnp.where(
-        core == 0,
-        jnp.concatenate([mine, other], axis=dim),
-        jnp.concatenate([other, mine], axis=dim),
-    )
+    return jnp.concatenate([mine, to_core(other)], axis=dim)
 
 
 def all_streams(own):
     core = lax.axis_index("c")
-    other = lax.ppermute(own, "c", [(0, 1), (1, 0)])
+    other = to_core(own)
     count = own.shape[0]
     whole = jnp.zeros((2 * count, *own.shape[1:]), own.dtype)
     whole = lax.dynamic_update_slice_in_dim(whole, own, core * count, 0)
@@ -212,25 +237,6 @@
             insides[offset - 1], window, fill_values[offset - 1]
         )
     return result
-
-
-def halves_together(weight, parts):
-    halves, rows, columns = weight.shape
-    each = columns // parts
-    return jnp.concatenate(
-        [weight[h, :, p * each : (p + 1) * each] for p in range(parts) for h in range(halves)],
-        axis=1,
-    )
-
-
-def halves_apart(grads, halves):
-    each = grads[0].shape[1] // halves
-    return jnp.stack(
-        [
-            jnp.concatenate([g[:, h * each : (h + 1) * each] for g in grads], axis=1)
-            for h in range(halves)
-        ]
-    )
 
 
 def shards(
@@ -274,23 +280,40 @@
     lengths = own_streams(doc_lengths)
     own_in = own_streams(inputs)
     own_cot = own_streams(cotangent)
+    small_rows = rec_params.shape[1]
+    small = jnp.concatenate([rec_params[0], gate_weights[0]], axis=1)
+    small_width = small.shape[1]
+    gain_width = norm_gains.shape[1]
+    tails = jnp.pad(norm_gains, ((0, 0), (0, small_width - gain_width)))
+    small = jnp.concatenate([small, tails], axis=0)
+
+    first_blocks = jnp.concatenate([to_chips(w_x), to_chips(w_g), to_chips(w_o.T)], axis=2)
+    first_rows = jnp.concatenate(plane_swap(first_blocks), axis=0)
     whole_in = plane_gather(own_in)
-    gains_all = lax.all_gather(norm_gains, ("z", "j"), axis=1, tiled=True).astype(F32)
-    small = lax.all_gather(
-        jnp.concatenate([rec_params[0], gate_weights[0]], axis=1), ("c", "z", "j"), axis=0
-    ).reshape(halves, half_width, -1)
-    small = lax.dynamic_slice_in_dim(small, j_index * part_width, part_width, 1)
-    small = small.reshape(rec_width, -1)
+    found = [small] + [to_partner(small, bit) for bit in (1, 2, 3)]
+    small = z_gather(jnp.stack(in_order(found, j_index)))
+    gains_all = jnp.moveaxis(small[:, :, small_rows:, :gain_width], 2, 0)
+    gains_all = gains_all.reshape(2, model_width).astype(F32)
+    small = small[:, :, :small_rows].reshape(half_width, small_width)
+    small = lax.dynamic_slice_in_dim(small, j_index * part_width, part_width, 0)
+    small = jnp.concatenate([small, to_core(small)], axis=0)
     params_all = small[:, :8].astype(F32)
     gates_all = small[:, 8:].reshape(heads_here, HEAD_DIM, 2 * HEAD_DIM)
 
-    def by_chip(weight):
-        return weight.reshape(weight_rows, PLANE, -1)
-
-    w_rec = halves_together(spread(jnp.concatenate([by_chip(w_x), by_chip(w_g)], axis=2)), 2)
-    w_back = halves_together(spread(by_chip(w_o.T)), 1)
-    w_wide = spread(jnp.concatenate([by_chip(w_gate), by_chip(w_up)], axis=2))
-    w_narrow = spread(by_chip(w_down.T))
+    w_first = along_z(first_rows)
+    w_rec = jnp.concatenate(
+        [w[:, p * part_width : (p + 1) * part_width] for p in (0, 1) for w in w_first], axis=1
+    )
+    w_back = jnp.concatenate([w[:, 2 * part_width :] for w in w_first], axis=1)
+    later = (w_gate, w_up, w_down)
+    later, whole_in = lax.optimization_barrier((later, whole_in))
+    wide_blocks = jnp.concatenate([to_chips(later[0]), to_chips(later[1])], axis=2)
+    wide_rows = jnp.concatenate(plane_swap(wide_blocks), axis=0)
+    narrow_rows = jnp.concatenate(plane_swap(to_chips(later[2].T)), axis=0)
+    own_cot, narrow_rows = lax.optimization_barrier((own_cot, narrow_rows))
+    w_wide = along_z(wide_rows)
+    narrow_rows, w_wide = lax.optimization_barrier((narrow_rows, w_wide))
+    w_narrow = along_z(narrow_rows)
 
     def live_at(position):
         second_start = spans[:, 0:1]
@@ -390,11 +413,14 @@
         "bdjs,bdsc->bdjc", from_state.astype(BF16), conv_here, preferred_element_type=F32
     )
     finals = jnp.concatenate([final_part[:, :, None], conv_part], axis=2)
-    finals = lax.all_gather(finals, ("z", "j", "c"), axis=0)
-    finals = finals.reshape(z_size, PLANE, halves * n_streams, 2, 4, halves, part_width)
-    finals = jnp.sum(finals, axis=0)
-    finals = at(finals, core, 4)
-    finals = jnp.moveaxis(finals, 0, 3).reshape(all_streams_count, 2, 4, half_width)
+    finals = jnp.concatenate(
+        [finals[..., :part_width], to_core(finals[..., part_width:])], axis=0
+    )
+    finals = jnp.where(core == 0, finals, jnp.roll(finals, n_streams, 0))
+    finals = lax.all_gather(finals, ("z", "j"), axis=0)
+    finals = finals.reshape(z_size, PLANE, all_streams_count, 2, 4, part_width)
+    finals = jnp.moveaxis(jnp.sum(finals, axis=0), 0, 3)
+    finals = finals.reshape(all_streams_count, 2, 4, half_width)
     dp_index = z_index * PLANE + j_index
     out_width = half_width // (z_size * PLANE)
     finals = lax.dynamic_slice_in_dim(finals, dp_index * out_width, out_width, 3)
@@ -422,8 +448,6 @@
         second_part = second_part + dot(d_both, w_wide[h], 1, 1)
         g_narrow.append(dot(d_down, act_low, 0, 0).astype(BF16))
         g_wide.append(dot(second_low, d_both, 0, 0).astype(BF16))
-    out_narrow = collect(jnp.stack(g_narrow), weight_rows)
-    out_wide = collect(jnp.stack(g_wide), weight_rows)
 
     mlp_total = plane_sum(down_part, n_streams).reshape(own_tokens, model_width)
     out_flat = (hidden_one + own_live * mlp_total).astype(BF16)
@@ -434,9 +458,11 @@
     d_hidden = d_out + d_hidden_norm
     own_rec = (d_hidden * own_live).astype(BF16).reshape(n_streams, own_rows, model_width)
     d_rec = plane_gather(own_rec).reshape(tokens, model_width)
+    d_rec, g_narrow, g_wide = lax.optimization_barrier((d_rec, g_narrow, g_wide))
+    out_wide = collect(*g_wide)
+    out_narrow = collect(*g_narrow)
     d_mixed = dot(d_rec, w_back, 1, 0)
     g_back = dot(d_rec, mixed_rows, 0, 0).astype(BF16)
-    out_back = collect(halves_apart([g_back], halves), weight_rows)
 
     grad_state = (d_mixed * branch).reshape(n_streams, n_rows, rec_width)
     branch_low = branch_back(d_mixed * states_flat)[0].astype(BF16)
@@ -476,8 +502,17 @@
     )
     first_part = dot(d_projected, w_rec, 1, 1)
     g_rec = dot(normed_low, d_projected, 0, 0).astype(BF16)
-    out_rec = collect(
-        halves_apart([g_rec[:, :rec_width], g_rec[:, rec_width:]], halves), weight_rows
+    out_first = collect(
+        *(
+            jnp.concatenate(
+                [
+                    g[:, start + h * part_width : start + (h + 1) * part_width]
+                    for g, start in ((g_rec, 0), (g_rec, rec_width), (g_back, 0))
+                ],
+                axis=1,
+            )
+            for h in range(halves)
+        )
     )
     g_small = jnp.concatenate(
         [
@@ -490,7 +525,8 @@
         ],
         axis=1,
     ).astype(BF16)
-    g_small = lax.psum_scatter(g_small, ("c", "z"), scatter_dimension=0, tiled=True)
+    g_small = g_small[:part_width].astype(F32) + to_core(g_small[part_width:]).astype(F32)
+    g_small = lax.psum_scatter(g_small.astype(BF16), "z", scatter_dimension=0, tiled=True)
     route = [(z * PLANE + j, j * z_size + z) for z in range(z_size) for j in range(PLANE)]
     g_small = lax.ppermute(g_small, ("z", "j"), route).astype(F32)[None]
 
@@ -499,12 +535,11 @@
     input_grad = all_streams(
         (d_hidden + d_input_norm).astype(BF16).reshape(n_streams, own_rows, model_width)
     )
-    g_gains = lax.psum(jnp.stack([g_gain_one, g_gain_two]), ("z", "j", "c"))
-    gain_width = norm_gains.shape[1]
+    g_gains = sum_of_all(jnp.stack([g_gain_one, g_gain_two]))
     g_gains = lax.dynamic_slice_in_dim(g_gains, dp_index * gain_width, gain_width, 1)
 
-    def flat(blocks):
-        return blocks.reshape(weight_rows, -1)
+    def flat(blocks, start, stop):
+        return jnp.concatenate([b[:, start:stop] for b in blocks], axis=1).astype(F32)
 
     return (
         output,
@@ -512,14 +547,14 @@
         state_block,
         conv_block,
         g_gains,
-        flat(out_rec[..., :part_width]),
-        flat(out_rec[..., part_width:]),
+        flat(out_first, 0, part_width),
+        flat(out_first, part_width, 2 * part_width),
         g_small[..., :8],
         g_small[..., 8:],
-        flat(out_back).T,
-        flat(out_wide[..., :ff_part]),
-        flat(out_wide[..., ff_part:]),
-        flat(out_narrow).T,
+        flat(out_first, 2 * part_width, 3 * part_width).T,
+        flat(out_wide, 0, ff_part),
+        flat(out_wide, ff_part, 2 * ff_part),
+        flat(out_narrow, 0, ff_part).T,
     )
 
 

time: 1290 us -> 975 us (0.76)
  waiting for transfers between devices: 531 us -> 298 us
  local copies, waits for them, and re-layouts: 277 us -> 155 us
  starting transfers between devices: 79 us -> 115 us
  other arithmetic: 107 us -> 126 us
    reduce_scatter x5 -> x4, waiting for transfers between devices: 322 us -> 34.2 us  [the longest x3 34.2 us: collect(): summed = lax.psum_scatter(total, 'z', scatter_dimension=0, tiled=True)]
    dynamic_update_slice x35 -> x17, local copies, waits for them, and re-layouts: 81.8 us -> 9.41 us  [put(): return lax.dynamic_update_index_in_dim(whole, block, index, axis)]
    psum x1 -> x0, blocking collectives: 53.4 us -> none  [shards(): g_gains = lax.psum(jnp.stack([g_gain_one, g_gain_two]), ('z', 'j', 'c'))]
    ppermute x4 -> x22, waiting for transfers between devices: 0.01 us -> 48 us  [the longest x6 33.6 us: z_gather(): lax.ppermute(block, 'z', [(i, (i + step) % size) for i in range(size)])]
    all_gather x1, blocking collectives: 41.2 us -> 85.6 us  [shards(): finals = lax.all_gather(finals, ('z', 'j'), axis=0)]
    all_gather x6 -> x3, waiting for transfers between devices: 0.02 us -> 36.6 us  [along_z(): own = lax.all_gather(block, 'z', axis=0, tiled=True)]
    ppermute x56 -> x53, waiting for transfers between devices: 198 us -> 175 us  [to_partner(): return lax.ppermute(block, 'j', [(i, i ^ bit) for i in range(PLANE)])]
    convert_element_type x2 -> x9, other arithmetic: 0.53 us -> 22 us  [the longest x3 17.7 us: collect(): total = (own.astype(F32) + to_core(other).astype(F32)).astype(BF16)]
  transfers between devices with their start and end apart: 80 -> 91, of which waited for: 50 -> 45; matrix products, arithmetic and copies ran while one was open for 31% -> 37% of each run, Pallas kernels for 1% -> 1%
where the time goes in v2:
time: 975 us; the launch traced here: 968 us
  waiting for transfers between devices  298 us (31%)
  local copies, waits for them, and re-layouts  155 us (16%)
  matrix products  154 us (16%)
  other arithmetic  126 us (13%)
  starting transfers between devices  115 us (12%)
  blocking collectives  85.6 us (9%)
  between operations  17.3 us (2%)
  Pallas kernels  17 us (2%)
    ppermute x53, waiting for transfers between devices, to_partner(): return lax.ppermute(block, 'j', [(i, i ^ bit) for i in range(PLANE)])  175 us
    dot_general x18, matrix products, dot(): lax.dot_general(left, right, (((left_dim,), (right_dim,)), ((), ())), pre...  142 us
    all_gather x1, blocking collectives, shards(): finals = lax.all_gather(finals, ('z', 'j'), axis=0)  85.6 us
    ppermute x53, starting transfers between devices, to_partner(): return lax.ppermute(block, 'j', [(i, i ^ bit) for i in range(PLANE)])  66.8 us
    all_gather x3, waiting for transfers between devices, along_z(): own = lax.all_gather(block, 'z', axis=0, tiled=True)  36.6 us
    unnamed x342, local copies, waits for them, and re-layouts  34.7 us
    reduce_scatter x3, waiting for transfers between devices, collect(): summed = lax.psum_scatter(total, 'z', scatter_dimension=0, tiled=True)  34.2 us
    ppermute x6, waiting for transfers between devices, z_gather(): lax.ppermute(block, 'z', [(i, (i + step) % size) for i in range(size)])  33.6 us
  transfers between devices with their start and end apart: 91, of which 45 were waited for; matrix products, arithmetic and copies ran while one was open for 37% of the time, Pallas kernels for 1%

profile of v2, /device:TPU:0, one launch (start us, length us, event | category | flops | bytes accessed | tf_op | source)
XLA Modules:
  0.0 968.0 jit_solution(3424097348118226093)
XLA Ops:
  26.6 16.8 %collective-permute-done.11 = bf16[128,960]{0,1:T(8,128)(2,1)} collective-permute-done((bf16[128,960]{0,1:T(8,128)(2,1)}, bf16[128,960]{0,1:T(8,128)(2,1)}, u32[]{:S(2)}, u32[]{:S(2)}) %collective-permute-start.11) | collective-permute-done | bytes 245792 | tf_op jit(solution)/shard_map/ppermute | solution.py:26
  44.9 4.3 collective-permute-done.12
  64.0 8.1 collective-permute-done.10
  85.1 10.7 %collective-permute-done.33 = bf16[128,1536]{1,0:T(8,128)(2,1)S(1)} collective-permute-done((bf16[128,1536]{1,0:T(8,128)(2,1)}, bf16[128,1536]{1,0:T(8,128)(2,1)S(1)}, u32[]{:S(2)}, u32[]{:S(2)}) %collective-permute-start.33) | collective-permute-done | bytes 393248 | tf_op jit(solution)/shard_map/ppermute | solution.py:26
  101.5 27.2 %all-gather.4.cloned.1.call-done = bf16[2048,960]{0,1:T(8,128)(2,1)} async-done(((bf16[512,960]{0,1:T(8,128)(2,1)}), bf16[2048,960]{0,1:T(8,128)(2,1)}) %all-gather.4.cloned.1.call-update) | async-done | bytes 3932176 | tf_op jit(solution)/shard_map/all_gather | solution.py:95
  133.5 6.6 collective-permute-done.3
  140.2 24.2 %collective-permute-done.4 = bf16[4,82,328]{2,1,0:T(8,128)(2,1)S(1)} collective-permute-done((bf16[4,82,328]{2,1,0:T(8,128)(2,1)S(1)}, bf16[4,82,328]{2,1,0:T(8,128)(2,1)S(1)}, u32[]{:S(2)}, u32[]{:S(2)}) %collective-permute-start.4) | collective-permute-done | bytes 215200 | tf_op jit(solution)/shard_map/ppermute | solution.py:110
  176.1 4.4 fusion.160
  180.6 5.6 fusion.67
  186.4 22.6 %collective-permute-start.15 = (bf16[2,3,640]{2,1,0:T(4,128)(2,1)S(1)}, bf16[2,3,640]{2,1,0:T(4,128)(2,1)S(1)}, u32[]{:S(2)}, u32[]{:S(2)}) collective-permute-start(bf16[2,3,640]{2,1,0:T(4,128)(2,1)S(1)} %slice.609), channel_id=1, source_target_pairs={{0,8},{8,16},{16,24},{1,9},{9,17},{17,25},{2,10},{10,18},{18,26},{... | collective-permute-start | bytes 23048 | tf_op jit(solution)/shard_map/ppermute | solution.py:144
  228.1 4.8 reshape.1575
  232.8 5.2 copy.534
  241.3 5.2 copy.533
  246.6 5.4 fusion.17
  252.0 8.0 shard_map.246
  267.4 3.9 copy.535
  299.5 6.0 collective-permute-done.21
  315.1 12.9 %collective-permute-done.43 = bf16[2,128,2048]{2,1,0:T(8,128)(2,1)} collective-permute-done((bf16[2,128,2048]{2,1,0:T(8,128)(2,1)}, bf16[2,128,2048]{2,1,0:T(8,128)(2,1)}, u32[]{:S(2)}, u32[]{:S(2)}) %collective-permute-start.43) | collective-permute-done | bytes 1048608 | tf_op jit(solution)/shard_map/ppermute | solution.py:26
  337.0 13.4 %collective-permute-done.24 = bf16[2,128,2048]{2,1,0:T(8,128)(2,1)} collective-permute-done((bf16[2,128,2048]{2,1,0:T(8,128)(2,1)}, bf16[2,128,2048]{2,1,0:T(8,128)(2,1)}, u32[]{:S(2)}, u32[]{:S(2)}) %collective-permute-start.24) | collective-permute-done | bytes 1048608 | tf_op jit(solution)/shard_map/ppermute | solution.py:26
  351.9 3.9 multiply_reduce_fusion.8
  367.2 15.4 %collective-permute-done.26 = bf16[2,128,2048]{2,1,0:T(8,128)(2,1)S(1)} collective-permute-done((bf16[2,128,2048]{2,1,0:T(8,128)(2,1)S(1)}, bf16[2,128,2048]{2,1,0:T(8,128)(2,1)S(1)}, u32[]{:S(2)}, u32[]{:S(2)}) %collective-permute-start.26) | collective-permute-done | bytes 1048608 | tf_op jit(solution)/shard_map/ppermute | solution.py:26
  386.0 9.0 collective-permute-done.28
  398.4 10.8 %fusion.173 = f32[1024,1536]{1,0:T(8,128)} fusion(bf16[1024,2048]{1,0:T(8,128)(2,1)S(1)} %bitcast.536, bf16[2048,1536]{1,0:T(8,128)(2,1)} %collective-permute-done.35), kind=kOutput, calls=%fused_computation.522 | convolution fusion | flops 6442450944 | bytes 16777216 | tf_op jit(solution)/shard_map/dot_general | solution.py:20
  409.2 9.3 all-gather.8.cloned.1.call-done
  418.5 12.0 %fusion.172 = f32[1024,1536]{1,0:T(8,128)} fusion(bf16[1024,2048]{1,0:T(8,128)(2,1)} %bitcast.537, bf16[2048,1536]{1,0:T(8,128)(2,1)} %all-gather.6.cloned.1.call-done), kind=kOutput, calls=%fused_computation.521 | convolution fusion | flops 6442450944 | bytes 16777216 | tf_op jit(solution)/shard_map/dot_general | solution.py:20
  430.5 11.2 %fusion.8 = (bf16[1024,768]{1,0:T(8,128)(2,1)S(1)}, bf16[1024,768]{1,0:T(8,128)(2,1)}, bf16[1024,768]{1,0:T(8,128)(2,1)}) fusion(f32[1024,1536]{1,0:T(8,128)} %fusion.172, bf16[1024,2048]{1,0:T(8,128)(2,1)} %bitcast.97, bf16[2048,768]{0,1:T(8,128)(2,1)S(1)} %copy-done.136), kind=kOutput, calls=%fused_computation.42 | convolution fusion | flops 3241672704 | bytes 18350080 | tf_op jit(solution)/shard_map/dot_general | solution.py:20
  441.7 10.7 %fusion.15 = (bf16[1024,768]{1,0:T(8,128)(2,1)S(1)}, bf16[1024,768]{1,0:T(8,128)(2,1)S(1)}, bf16[1024,768]{1,0:T(8,128)(2,1)}) fusion(f32[1024,1536]{1,0:T(8,128)S(1)} %bitcast.599, bf16[1024,2048]{1,0:T(8,128)(2,1)} %bitcast.97, bf16[2048,768]{0,1:T(8,128)(2,1)S(1)} %collective-permute-done.36), kind=kOutput, calls=%fused_computation.49 | convolution fusion | flops 3241672704 | bytes 18350080 | tf_op jit(solution)/shard_map/dot_general | solution.py:20
  452.4 12.0 %fusion.49 = f32[1024,2048]{1,0:T(8,128)} fusion(bf16[2048,1536]{1,0:T(8,128)(2,1)} %collective-permute-done.35, bf16[1024,768]{1,0:T(8,128)(2,1)S(1)} %get-tuple-element.209, bf16[1024,768]{1,0:T(8,128)(2,1)S(1)} %get-tuple-element.208), kind=kOutput, calls=%fused_computation.145 | convolution fusion | flops 6448742400 | bytes 17825792 | tf_op jit(solution)/shard_map/dot_general | solution.py:20
  464.5 9.4 add_convert_fusion.1
  477.1 11.4 %collective-permute-done.46 = bf16[1,128,2048]{2,1,0:T(8,128)(2,1)S(1)} collective-permute-done((bf16[1,128,2048]{2,1,0:T(8,128)(2,1)S(1)}, bf16[1,128,2048]{2,1,0:T(8,128)(2,1)S(1)}, u32[]{:S(2)}, u32[]{:S(2)}) %collective-permute-start.46) | collective-permute-done | bytes 524320 | tf_op jit(solution)/shard_map/ppermute | solution.py:26
  493.0 9.3 convolution_convert_fusion.2
  502.4 7.6 convolution_convert_fusion.6
  509.9 5.0 collective-permute-done.49
  523.6 9.2 convolution_convert_fusion.1
  532.8 7.4 convolution_convert_fusion.5
  540.2 5.0 collective-permute-done.51
  547.7 8.7 collective-permute-done.53
  557.0 5.9 fusion.66
  563.0 9.1 shard_map.247
  583.4 6.5 fusion.52
  589.9 3.9 copy.563
  597.1 5.2 copy.568
  602.3 5.0 reshape.1584
  607.3 6.2 fusion.148
  613.5 6.1 multiply_reduce_fusion.1
  626.0 5.4 copy.569
  631.4 8.2 fusion.147
  653.0 5.3 add_convert_fusion.4
  660.0 8.3 convolution_convert_fusion
  670.6 6.4 collective-permute-done.70
  685.5 5.6 collective-permute-done.76
  691.0 9.1 add_convert_fusion
  701.5 5.5 fusion.174
  714.4 5.8 convolution_convert_fusion.3
  732.0 5.2 collective-permute-done.58
  743.2 85.6 %all_gather.16 = f32[16,4,2,4,320]{4,3,2,1,0:T(4,128)S(1)} all-gather(f32[1,4,2,4,320]{4,3,2,1,0:T(4,128)S(1)} %maximum_select_fusion), channel_id=1, replica_groups=mesh['z'=4,'j'=4,'c'=2] {'z','j'}, dimensions={0}, use_global_device_ids=true | all-gather | bytes 696320 | tf_op jit(solution)/shard_map/all_gather | solution.py:420
  832.3 4.1 constant_dynamic-update-slice_fusion.3
  843.1 4.0 constant_dynamic-update-slice_fusion.1
  854.7 3.7 collective-permute-start.69
  890.4 4.8 collective-permute-done.71
  895.2 4.2 collective-permute-done.72
  902.1 34.2 %reduce-scatter.9.cloned.1.call-done = bf16[512,1536]{1,0:T(8,128)(2,1)} async-done(((bf16[2048,1536]{1,0:T(8,128)(2,1)}), bf16[512,1536]{1,0:T(8,128)(2,1)}) %reduce-scatter.9.cloned.1.call-update) | async-done | bytes 1572880 | tf_op jit(solution)/shard_map/reduce_scatter | solution.py:101
  944.1 6.5 collective-permute-done.77
  950.6 6.5 collective-permute-done.78
  (752 shorter events, 321.8 us)
Async XLA Ops:
  7.2 121.6 %all-gather.4.cloned.1.call-start = ((), (), s32[]{:S(2)}) async-start(), calls=%async_computation.4 | async-start | bytes 4915200 | tf_op jit(solution)/shard_map/all_gather | solution.py:95
  9.5 48.3 %collective-permute-start.7 = (bf16[2,128,2048]{2,1,0:T(8,128)(2,1)S(1)}, bf16[2,128,2048]{2,1,0:T(8,128)(2,1)}, u32[]{:S(2)}, u32[]{:S(2)}) collective-permute-start(bf16[2,128,2048]{2,1,0:T(8,128)(2,1)S(1)} %get-tuple-element.193), channel_id=1, source_target_pairs={{0,2},{2,0},{4,6},{6,4},{1,3},{3,1},{5,7},{7,5},{8,10},{10,8},{12,... | collective-permute-start | bytes 3145736 | tf_op jit(solution)/shard_map/ppermute | solution.py:26
  12.5 44.1 %collective-permute-start.8 = (bf16[2,128,2048]{2,1,0:T(8,128)(2,1)S(1)}, bf16[2,128,2048]{2,1,0:T(8,128)(2,1)}, u32[]{:S(2)}, u32[]{:S(2)}) collective-permute-start(bf16[2,128,2048]{2,1,0:T(8,128)(2,1)S(1)} %get-tuple-element.193), channel_id=1, source_target_pairs={{0,4},{2,6},{4,0},{6,2},{1,5},{3,7},{5,1},{7,3},{8,12},{10,14},{12... | collective-permute-start | bytes 3145736 | tf_op jit(solution)/shard_map/ppermute | solution.py:26
  20.0 23.4 %collective-permute-start.11 = (bf16[128,960]{0,1:T(8,128)(2,1)}, bf16[128,960]{0,1:T(8,128)(2,1)}, u32[]{:S(2)}, u32[]{:S(2)}) collective-permute-start(bf16[128,960]{0,1:T(8,128)(2,1)} %get-tuple-element.289), channel_id=1, source_target_pairs={{0,6},{2,4},{4,2},{6,0},{1,7},{3,5},{5,3},{7,1},{8,14},{10,12},{12... | collective-permute-start | bytes 737288 | tf_op jit(solution)/shard_map/ppermute | solution.py:26
  20.0 29.2 %collective-permute-start.12 = (bf16[128,960]{0,1:T(8,128)(2,1)}, bf16[128,960]{0,1:T(8,128)(2,1)}, u32[]{:S(2)}, u32[]{:S(2)}) collective-permute-start(bf16[128,960]{0,1:T(8,128)(2,1)} %get-tuple-element.288), channel_id=1, source_target_pairs={{0,4},{2,6},{4,0},{6,2},{1,5},{3,7},{5,1},{7,3},{8,12},{10,14},{12... | collective-permute-start | bytes 737288 | tf_op jit(solution)/shard_map/ppermute | solution.py:26
  22.0 27.2 %collective-permute-start.13 = (bf16[128,960]{0,1:T(8,128)(2,1)S(1)}, bf16[128,960]{0,1:T(8,128)(2,1)}, u32[]{:S(2)}, u32[]{:S(2)}) collective-permute-start(bf16[128,960]{0,1:T(8,128)(2,1)S(1)} %get-tuple-element.287), channel_id=1, source_target_pairs={{0,2},{2,0},{4,6},{6,4},{1,3},{3,1},{5,7},{7,5},{8,10},{10,8},{12,... | collective-permute-start | bytes 737288 | tf_op jit(solution)/shard_map/ppermute | solution.py:26
  43.4 55.5 %collective-permute-start = (bf16[82,328]{1,0:T(8,128)(2,1)}, bf16[82,328]{1,0:T(8,128)(2,1)}, u32[]{:S(2)}, u32[]{:S(2)}) collective-permute-start(bf16[82,328]{1,0:T(8,128)(2,1)} %fusion.78), channel_id=1, source_target_pairs={{0,6},{2,4},{4,2},{6,0},{1,7},{3,5},{5,3},{7,1},{8,14},{10,12},{12... | collective-permute-start | bytes 161384 | tf_op jit(solution)/shard_map/ppermute | solution.py:26
  49.2 32.6 %collective-permute-start.17 = (f32[2,2,320]{2,1,0:T(2,128)}, f32[2,2,320]{2,1,0:T(2,128)}, u32[]{:S(2)}, u32[]{:S(2)}) collective-permute-start(f32[2,2,320]{2,1,0:T(2,128)} %get-tuple-element.334), channel_id=1, source_target_pairs={{0,1},{1,0},{2,3},{3,2},{4,5},{5,4},{6,7},{7,6},{8,9},{9,8},{10,11... | collective-permute-start | bytes 15368 | tf_op jit(solution)/shard_map/ppermute | solution.py:91
  51.7 215.0 %all-gather.6.cloned.1.call-start = ((), (), s32[]{:S(2)}) async-start(), calls=%async_computation.5 | async-start | bytes 7864320 | tf_op jit(solution)/shard_map/all_gather | solution.py:95
  57.7 14.4 %collective-permute-start.10 = (bf16[1,128,2048]{2,1,0:T(8,128)(2,1)S(1)}, bf16[1,128,2048]{2,1,0:T(8,128)(2,1)S(1)}, u32[]{:S(2)}, u32[]{:S(2)}) collective-permute-start(bf16[1,128,2048]{2,1,0:T(8,128)(2,1)S(1)} %slice.601), channel_id=1, source_target_pairs={{0,2},{2,0},{4,6},{6,4},{1,3},{3,1},{5,7},{7,5},{8,10},{10,8},{12,... | collective-permute-start | bytes 1572872 | tf_op jit(solution)/shard_map/ppermute | solution.py:26
  58.9 14.4 %collective-permute-start.9 = (bf16[1,128,2048]{2,1,0:T(8,128)(2,1)S(1)}, bf16[1,128,2048]{2,1,0:T(8,128)(2,1)S(1)}, u32[]{:S(2)}, u32[]{:S(2)}) collective-permute-start(bf16[1,128,2048]{2,1,0:T(8,128)(2,1)S(1)} %slice.600), channel_id=1, source_target_pairs={{0,4},{2,6},{4,0},{6,2},{1,5},{3,7},{5,1},{7,3},{8,12},{10,14},{12... | collective-permute-start | bytes 1572872 | tf_op jit(solution)/shard_map/ppermute | solution.py:26
  75.6 20.2 %collective-permute-start.33 = (bf16[128,1536]{1,0:T(8,128)(2,1)}, bf16[128,1536]{1,0:T(8,128)(2,1)S(1)}, u32[]{:S(2)}, u32[]{:S(2)}) collective-permute-start(bf16[128,1536]{1,0:T(8,128)(2,1)} %get-tuple-element.276), channel_id=1, source_target_pairs={{0,4},{2,6},{4,0},{6,2},{1,5},{3,7},{5,1},{7,3},{8,12},{10,14},{12... | collective-permute-start | bytes 1179656 | tf_op jit(solution)/shard_map/ppermute | solution.py:26
  77.3 19.9 %collective-permute-start.32 = (bf16[128,1536]{1,0:T(8,128)(2,1)S(1)}, bf16[128,1536]{1,0:T(8,128)(2,1)S(1)}, u32[]{:S(2)}, u32[]{:S(2)}) collective-permute-start(bf16[128,1536]{1,0:T(8,128)(2,1)S(1)} %get-tuple-element.275), channel_id=1, source_target_pairs={{0,6},{2,4},{4,2},{6,0},{1,7},{3,5},{5,3},{7,1},{8,14},{10,12},{12... | collective-permute-start | bytes 1179656 | tf_op jit(solution)/shard_map/ppermute | solution.py:26
  78.8 18.4 %collective-permute-start.34 = (bf16[128,1536]{1,0:T(8,128)(2,1)S(1)}, bf16[128,1536]{1,0:T(8,128)(2,1)S(1)}, u32[]{:S(2)}, u32[]{:S(2)}) collective-permute-start(bf16[128,1536]{1,0:T(8,128)(2,1)S(1)} %get-tuple-element.274), channel_id=1, source_target_pairs={{0,2},{2,0},{4,6},{6,4},{1,3},{3,1},{5,7},{7,5},{8,10},{10,8},{12,... | collective-permute-start | bytes 1179656 | tf_op jit(solution)/shard_map/ppermute | solution.py:26
  81.8 17.1 %collective-permute-start.1 = (bf16[82,328]{1,0:T(8,128)(2,1)}, bf16[82,328]{1,0:T(8,128)(2,1)}, u32[]{:S(2)}, u32[]{:S(2)}) collective-permute-start(bf16[82,328]{1,0:T(8,128)(2,1)} %fusion.78), channel_id=1, source_target_pairs={{0,4},{2,6},{4,0},{6,2},{1,5},{3,7},{5,1},{7,3},{8,12},{10,14},{12... | collective-permute-start | bytes 161384 | tf_op jit(solution)/shard_map/ppermute | solution.py:26
  97.2 116.5 %collective-permute-start.16 = (bf16[2,2,3,320]{3,2,1,0:T(4,128)(2,1)}, bf16[2,2,3,320]{3,2,1,0:T(4,128)(2,1)S(1)}, u32[]{:S(2)}, u32[]{:S(2)}) collective-permute-start(bf16[2,2,3,320]{3,2,1,0:T(4,128)(2,1)} %copy.609), channel_id=1, source_target_pairs={{0,1},{1,0},{2,3},{3,2},{4,5},{5,4},{6,7},{7,6},{8,9},{9,8},{10,11... | collective-permute-start | bytes 23048 | tf_op jit(solution)/shard_map/ppermute | solution.py:91
  98.9 319.6 %all-gather.8.cloned.1.call-start = ((), (), s32[]{:S(2)}) async-start(), calls=%async_computation.6 | async-start | bytes 3932160 | tf_op jit(solution)/shard_map/all_gather | solution.py:95
  128.8 47.4 %collective-permute-start.14 = (bf16[2048,960]{0,1:T(8,128)(2,1)}, bf16[2048,960]{0,1:T(8,128)(2,1)}, u32[]{:S(2)}, u32[]{:S(2)}) collective-permute-start(bf16[2048,960]{0,1:T(8,128)(2,1)} %all-gather.4.cloned.1.call-done), channel_id=1, source_target_pairs={{0,1},{1,0},{2,3},{3,2},{4,5},{5,4},{6,7},{7,6},{8,9},{9,8},{10,11... | collective-permute-start | bytes 11796488 | tf_op jit(solution)/shard_map/ppermute | solution.py:91
  128.9 35.6 %collective-permute-start.4 = (bf16[4,82,328]{2,1,0:T(8,128)(2,1)S(1)}, bf16[4,82,328]{2,1,0:T(8,128)(2,1)S(1)}, u32[]{:S(2)}, u32[]{:S(2)}) collective-permute-start(bf16[4,82,328]{2,1,0:T(8,128)(2,1)S(1)} %get-tuple-element.311), channel_id=1, source_target_pairs={{0,16},{8,24},{16,0},{24,8},{1,17},{9,25},{17,1},{25,9},{2,18},{10... | collective-permute-start | bytes 645512 | tf_op jit(solution)/shard_map/ppermute | solution.py:110
  130.1 34.4 %collective-permute-start.5 = (bf16[4,82,328]{2,1,0:T(8,128)(2,1)S(1)}, bf16[4,82,328]{2,1,0:T(8,128)(2,1)S(1)}, u32[]{:S(2)}, u32[]{:S(2)}) collective-permute-start(bf16[4,82,328]{2,1,0:T(8,128)(2,1)S(1)} %get-tuple-element.311), channel_id=1, source_target_pairs={{0,24},{8,0},{16,8},{24,16},{1,25},{9,1},{17,9},{25,17},{2,26},{10... | collective-permute-start | bytes 645512 | tf_op jit(solution)/shard_map/ppermute | solution.py:110
  186.4 27.0 %collective-permute-start.15 = (bf16[2,3,640]{2,1,0:T(4,128)(2,1)S(1)}, bf16[2,3,640]{2,1,0:T(4,128)(2,1)S(1)}, u32[]{:S(2)}, u32[]{:S(2)}) collective-permute-start(bf16[2,3,640]{2,1,0:T(4,128)(2,1)S(1)} %slice.609), channel_id=1, source_target_pairs={{0,8},{8,16},{16,24},{1,9},{9,17},{17,25},{2,10},{10,18},{18,26},{... | collective-permute-start | bytes 23048 | tf_op jit(solution)/shard_map/ppermute | solution.py:144
  209.9 62.7 %collective-permute-start.29 = (bf16[128,768]{0,1:T(8,128)(2,1)}, bf16[128,768]{0,1:T(8,128)(2,1)S(1)}, u32[]{:S(2)}, u32[]{:S(2)}) collective-permute-start(bf16[128,768]{0,1:T(8,128)(2,1)} %get-tuple-element.300), channel_id=1, source_target_pairs={{0,6},{2,4},{4,2},{6,0},{1,7},{3,5},{5,3},{7,1},{8,14},{10,12},{12... | collective-permute-start | bytes 589832 | tf_op jit(solution)/shard_map/ppermute | solution.py:26
  212.3 60.3 %collective-permute-start.30 = (bf16[128,768]{0,1:T(8,128)(2,1)}, bf16[128,768]{0,1:T(8,128)(2,1)S(1)}, u32[]{:S(2)}, u32[]{:S(2)}) collective-permute-start(bf16[128,768]{0,1:T(8,128)(2,1)} %get-tuple-element.299), channel_id=1, source_target_pairs={{0,4},{2,6},{4,0},{6,2},{1,5},{3,7},{5,1},{7,3},{8,12},{10,14},{12... | collective-permute-start | bytes 589832 | tf_op jit(solution)/shard_map/ppermute | solution.py:26
  212.8 59.8 %collective-permute-start.31 = (bf16[128,768]{0,1:T(8,128)(2,1)}, bf16[128,768]{0,1:T(8,128)(2,1)}, u32[]{:S(2)}, u32[]{:S(2)}) collective-permute-start(bf16[128,768]{0,1:T(8,128)(2,1)} %get-tuple-element.298), channel_id=1, source_target_pairs={{0,2},{2,0},{4,6},{6,4},{1,3},{3,1},{5,7},{7,5},{8,10},{10,8},{12,... | collective-permute-start | bytes 589832 | tf_op jit(solution)/shard_map/ppermute | solution.py:26
  266.7 89.2 %collective-permute-start.35 = (bf16[2048,1536]{1,0:T(8,128)(2,1)}, bf16[2048,1536]{1,0:T(8,128)(2,1)}, u32[]{:S(2)}, u32[]{:S(2)}) collective-permute-start(bf16[2048,1536]{1,0:T(8,128)(2,1)} %all-gather.6.cloned.1.call-done), channel_id=1, source_target_pairs={{0,1},{1,0},{2,3},{3,2},{4,5},{5,4},{6,7},{7,6},{8,9},{9,8},{10,11... | collective-permute-start | bytes 18874376 | tf_op jit(solution)/shard_map/ppermute | solution.py:91
  290.4 15.2 %collective-permute-start.21 = (bf16[1,128,2048]{2,1,0:T(8,128)(2,1)}, bf16[1,128,2048]{2,1,0:T(8,128)(2,1)}, u32[]{:S(2)}, u32[]{:S(2)}) collective-permute-start(bf16[1,128,2048]{2,1,0:T(8,128)(2,1)} %get-tuple-element.239), channel_id=1, source_target_pairs={{0,4},{2,6},{4,0},{6,2},{1,5},{3,7},{5,1},{7,3},{8,12},{10,14},{12... | collective-permute-start | bytes 1572872 | tf_op jit(solution)/shard_map/ppermute | solution.py:26
  291.8 15.2 %collective-permute-start.23 = (bf16[1,128,2048]{2,1,0:T(8,128)(2,1)}, bf16[1,128,2048]{2,1,0:T(8,128)(2,1)}, u32[]{:S(2)}, u32[]{:S(2)}) collective-permute-start(bf16[1,128,2048]{2,1,0:T(8,128)(2,1)} %get-tuple-element.241), channel_id=1, source_target_pairs={{0,2},{2,0},{4,6},{6,4},{1,3},{3,1},{5,7},{7,5},{8,10},{10,8},{12,... | collective-permute-start | bytes 1572872 | tf_op jit(solution)/shard_map/ppermute | solution.py:26
  298.5 32.9 %collective-permute-start.42 = (bf16[2,128,2048]{2,1,0:T(8,128)(2,1)}, bf16[2,128,2048]{2,1,0:T(8,128)(2,1)}, u32[]{:S(2)}, u32[]{:S(2)}) collective-permute-start(bf16[2,128,2048]{2,1,0:T(8,128)(2,1)} %get-tuple-element.195), channel_id=1, source_target_pairs={{0,2},{2,0},{4,6},{6,4},{1,3},{3,1},{5,7},{7,5},{8,10},{10,8},{12,... | collective-permute-start | bytes 3145736 | tf_op jit(solution)/shard_map/ppermute | solution.py:26
  299.0 29.0 %collective-permute-start.43 = (bf16[2,128,2048]{2,1,0:T(8,128)(2,1)}, bf16[2,128,2048]{2,1,0:T(8,128)(2,1)}, u32[]{:S(2)}, u32[]{:S(2)}) collective-permute-start(bf16[2,128,2048]{2,1,0:T(8,128)(2,1)} %get-tuple-element.195), channel_id=1, source_target_pairs={{0,4},{2,6},{4,0},{6,2},{1,5},{3,7},{5,1},{7,3},{8,12},{10,14},{12... | collective-permute-start | bytes 3145736 | tf_op jit(solution)/shard_map/ppermute | solution.py:26
  310.0 40.5 %collective-permute-start.24 = (bf16[2,128,2048]{2,1,0:T(8,128)(2,1)}, bf16[2,128,2048]{2,1,0:T(8,128)(2,1)}, u32[]{:S(2)}, u32[]{:S(2)}) collective-permute-start(bf16[2,128,2048]{2,1,0:T(8,128)(2,1)} %pad_maximum_fusion.22), channel_id=1, source_target_pairs={{0,4},{2,6},{4,0},{6,2},{1,5},{3,7},{5,1},{7,3},{8,12},{10,14},{12... | collective-permute-start | bytes 3145736 | tf_op jit(solution)/shard_map/ppermute | solution.py:26
  311.6 40.3 %collective-permute-start.22 = (bf16[2,128,2048]{2,1,0:T(8,128)(2,1)}, bf16[2,128,2048]{2,1,0:T(8,128)(2,1)}, u32[]{:S(2)}, u32[]{:S(2)}) collective-permute-start(bf16[2,128,2048]{2,1,0:T(8,128)(2,1)} %pad_maximum_fusion.21), channel_id=1, source_target_pairs={{0,2},{2,0},{4,6},{6,4},{1,3},{3,1},{5,7},{7,5},{8,10},{10,8},{12,... | collective-permute-start | bytes 3145736 | tf_op jit(solution)/shard_map/ppermute | solution.py:26
  329.9 33.2 %collective-permute-start.45 = (bf16[1,128,2048]{2,1,0:T(8,128)(2,1)}, bf16[1,128,2048]{2,1,0:T(8,128)(2,1)S(1)}, u32[]{:S(2)}, u32[]{:S(2)}) collective-permute-start(bf16[1,128,2048]{2,1,0:T(8,128)(2,1)} %slice.643), channel_id=1, source_target_pairs={{0,2},{2,0},{4,6},{6,4},{1,3},{3,1},{5,7},{7,5},{8,10},{10,8},{12,... | collective-permute-start | bytes 1572872 | tf_op jit(solution)/shard_map/ppermute | solution.py:26
  333.2 29.9 %collective-permute-start.44 = (bf16[1,128,2048]{2,1,0:T(8,128)(2,1)}, bf16[1,128,2048]{2,1,0:T(8,128)(2,1)}, u32[]{:S(2)}, u32[]{:S(2)}) collective-permute-start(bf16[1,128,2048]{2,1,0:T(8,128)(2,1)} %slice.642), channel_id=1, source_target_pairs={{0,4},{2,6},{4,0},{6,2},{1,5},{3,7},{5,1},{7,3},{8,12},{10,14},{12... | collective-permute-start | bytes 1572872 | tf_op jit(solution)/shard_map/ppermute | solution.py:26
  355.9 480.5 %reduce-scatter.7.cloned.1.call-start = ((), (), s32[]{:S(2)}) async-start(), calls=%async_computation.8 | async-start | bytes 307200 | tf_op jit(solution)/shard_map/reduce_scatter | solution.py:529
  357.8 26.4 %collective-permute-start.25 = (bf16[2,128,2048]{2,1,0:T(8,128)(2,1)S(1)}, bf16[2,128,2048]{2,1,0:T(8,128)(2,1)S(1)}, u32[]{:S(2)}, u32[]{:S(2)}) collective-permute-start(bf16[2,128,2048]{2,1,0:T(8,128)(2,1)S(1)} %get-tuple-element.201), channel_id=1, source_target_pairs={{0,2},{2,0},{4,6},{6,4},{1,3},{3,1},{5,7},{7,5},{8,10},{10,8},{12,... | collective-permute-start | bytes 3145736 | tf_op jit(solution)/shard_map/ppermute | solution.py:26
  359.4 23.2 %collective-permute-start.26 = (bf16[2,128,2048]{2,1,0:T(8,128)(2,1)S(1)}, bf16[2,128,2048]{2,1,0:T(8,128)(2,1)S(1)}, u32[]{:S(2)}, u32[]{:S(2)}) collective-permute-start(bf16[2,128,2048]{2,1,0:T(8,128)(2,1)S(1)} %get-tuple-element.201), channel_id=1, source_target_pairs={{0,4},{2,6},{4,0},{6,2},{1,5},{3,7},{5,1},{7,3},{8,12},{10,14},{12... | collective-permute-start | bytes 3145736 | tf_op jit(solution)/shard_map/ppermute | solution.py:26
  382.7 12.4 %collective-permute-start.28 = (bf16[1,128,2048]{2,1,0:T(8,128)(2,1)S(1)}, bf16[1,128,2048]{2,1,0:T(8,128)(2,1)S(1)}, u32[]{:S(2)}, u32[]{:S(2)}) collective-permute-start(bf16[1,128,2048]{2,1,0:T(8,128)(2,1)S(1)} %slice.637), channel_id=1, source_target_pairs={{0,2},{2,0},{4,6},{6,4},{1,3},{3,1},{5,7},{7,5},{8,10},{10,8},{12,... | collective-permute-start | bytes 1572872 | tf_op jit(solution)/shard_map/ppermute | solution.py:26
  418.5 23.2 %collective-permute-start.36 = (bf16[2048,768]{0,1:T(8,128)(2,1)}, bf16[2048,768]{0,1:T(8,128)(2,1)S(1)}, u32[]{:S(2)}, u32[]{:S(2)}) collective-permute-start(bf16[2048,768]{0,1:T(8,128)(2,1)} %all-gather.8.cloned.1.call-done), channel_id=1, source_target_pairs={{0,1},{1,0},{2,3},{3,2},{4,5},{5,4},{6,7},{7,6},{8,9},{9,8},{10,11... | collective-permute-start | bytes 9437192 | tf_op jit(solution)/shard_map/ppermute | solution.py:91
  474.1 14.5 %collective-permute-start.46 = (bf16[1,128,2048]{2,1,0:T(8,128)(2,1)S(1)}, bf16[1,128,2048]{2,1,0:T(8,128)(2,1)S(1)}, u32[]{:S(2)}, u32[]{:S(2)}) collective-permute-start(bf16[1,128,2048]{2,1,0:T(8,128)(2,1)S(1)} %get-tuple-element.227), channel_id=1, source_target_pairs={{0,4},{2,6},{4,0},{6,2},{1,5},{3,7},{5,1},{7,3},{8,12},{10,14},{12... | collective-permute-start | bytes 1572872 | tf_op jit(solution)/shard_map/ppermute | solution.py:26
  475.6 14.2 %collective-permute-start.48 = (bf16[1,128,2048]{2,1,0:T(8,128)(2,1)S(1)}, bf16[1,128,2048]{2,1,0:T(8,128)(2,1)S(1)}, u32[]{:S(2)}, u32[]{:S(2)}) collective-permute-start(bf16[1,128,2048]{2,1,0:T(8,128)(2,1)S(1)} %get-tuple-element.229), channel_id=1, source_target_pairs={{0,2},{2,0},{4,6},{6,4},{1,3},{3,1},{5,7},{7,5},{8,10},{10,8},{12,... | collective-permute-start | bytes 1572872 | tf_op jit(solution)/shard_map/ppermute | solution.py:26
  490.3 24.7 %collective-permute-start.49 = (bf16[2,128,2048]{2,1,0:T(8,128)(2,1)S(1)}, bf16[2,128,2048]{2,1,0:T(8,128)(2,1)S(1)}, u32[]{:S(2)}, u32[]{:S(2)}) collective-permute-start(bf16[2,128,2048]{2,1,0:T(8,128)(2,1)S(1)} %pad_maximum_fusion.26), channel_id=1, source_target_pairs={{0,4},{2,6},{4,0},{6,2},{1,5},{3,7},{5,1},{7,3},{8,12},{10,14},{12... | collective-permute-start | bytes 3145736 | tf_op jit(solution)/shard_map/ppermute | solution.py:26
  491.0 24.4 %collective-permute-start.47 = (bf16[2,128,2048]{2,1,0:T(8,128)(2,1)S(1)}, bf16[2,128,2048]{2,1,0:T(8,128)(2,1)S(1)}, u32[]{:S(2)}, u32[]{:S(2)}) collective-permute-start(bf16[2,128,2048]{2,1,0:T(8,128)(2,1)S(1)} %pad_maximum_fusion.25), channel_id=1, source_target_pairs={{0,2},{2,0},{4,6},{6,4},{1,3},{3,1},{5,7},{7,5},{8,10},{10,8},{12,... | collective-permute-start | bytes 3145736 | tf_op jit(solution)/shard_map/ppermute | solution.py:26
  520.6 25.3 %collective-permute-start.50 = (bf16[2,128,2048]{2,1,0:T(8,128)(2,1)S(1)}, bf16[2,128,2048]{2,1,0:T(8,128)(2,1)S(1)}, u32[]{:S(2)}, u32[]{:S(2)}) collective-permute-start(bf16[2,128,2048]{2,1,0:T(8,128)(2,1)S(1)} %get-tuple-element.190), channel_id=1, source_target_pairs={{0,2},{2,0},{4,6},{6,4},{1,3},{3,1},{5,7},{7,5},{8,10},{10,8},{12,... | collective-permute-start | bytes 3145736 | tf_op jit(solution)/shard_map/ppermute | solution.py:26
  522.1 23.2 %collective-permute-start.51 = (bf16[2,128,2048]{2,1,0:T(8,128)(2,1)S(1)}, bf16[2,128,2048]{2,1,0:T(8,128)(2,1)S(1)}, u32[]{:S(2)}, u32[]{:S(2)}) collective-permute-start(bf16[2,128,2048]{2,1,0:T(8,128)(2,1)S(1)} %get-tuple-element.190), channel_id=1, source_target_pairs={{0,4},{2,6},{4,0},{6,2},{1,5},{3,7},{5,1},{7,3},{8,12},{10,14},{12... | collective-permute-start | bytes 3145736 | tf_op jit(solution)/shard_map/ppermute | solution.py:26
  581.4 71.6 %collective-permute-start.80 = (bf16[2048,768]{1,0:T(8,128)(2,1)}, bf16[2048,768]{1,0:T(8,128)(2,1)}, u32[]{:S(2)}, u32[]{:S(2)}) collective-permute-start(bf16[2048,768]{1,0:T(8,128)(2,1)} %convolution_convert_fusion.5), channel_id=1, source_target_pairs={{0,1},{1,0},{2,3},{3,2},{4,5},{5,4},{6,7},{7,6},{8,9},{9,8},{10,11... | collective-permute-start | bytes 9437192 | tf_op jit(solution)/shard_map/ppermute | solution.py:91
  653.0 211.0 %reduce-scatter.11.cloned.1.call-start = ((), (), s32[]{:S(2)}) async-start(), calls=%async_computation.10 | async-start | bytes 3932160 | tf_op jit(solution)/shard_map/reduce_scatter | solution.py:101
  658.3 223.0 %reduce-scatter.5.cloned.1.call-start = ((), (), s32[]{:S(2)}) async-start(), calls=%async_computation.7 | async-start | bytes 4915200 | tf_op jit(solution)/shard_map/reduce_scatter | solution.py:101
  680.4 255.9 %reduce-scatter.9.cloned.1.call-start = ((), (), s32[]{:S(2)}) async-start(), calls=%async_computation.9 | async-start | bytes 7864320 | tf_op jit(solution)/shard_map/reduce_scatter | solution.py:101
  685.0 15.8 %collective-permute-start.63 = (f32[2,2,4,320]{3,2,1,0:T(4,128)S(1)}, f32[2,2,4,320]{3,2,1,0:T(4,128)S(1)}, u32[]{:S(2)}, u32[]{:S(2)}) collective-permute-start(f32[2,2,4,320]{3,2,1,0:T(4,128)S(1)} %get-tuple-element.332), channel_id=1, source_target_pairs={{0,1},{1,0},{2,3},{3,2},{4,5},{5,4},{6,7},{7,6},{8,9},{9,8},{10,11... | collective-permute-start | bytes 61448 | tf_op jit(solution)/shard_map/ppermute | solution.py:91
  711.1 14.8 %collective-permute-start.37 = (bf16[1,128,2048]{2,1,0:T(8,128)(2,1)S(1)}, bf16[1,128,2048]{2,1,0:T(8,128)(2,1)S(1)}, u32[]{:S(2)}, u32[]{:S(2)}) collective-permute-start(bf16[1,128,2048]{2,1,0:T(8,128)(2,1)S(1)} %get-tuple-element.233), channel_id=1, source_target_pairs={{0,4},{2,6},{4,0},{6,2},{1,5},{3,7},{5,1},{7,3},{8,12},{10,14},{12... | collective-permute-start | bytes 1572872 | tf_op jit(solution)/shard_map/ppermute | solution.py:26
  712.5 14.8 %collective-permute-start.39 = (bf16[1,128,2048]{2,1,0:T(8,128)(2,1)S(1)}, bf16[1,128,2048]{2,1,0:T(8,128)(2,1)S(1)}, u32[]{:S(2)}, u32[]{:S(2)}) collective-permute-start(bf16[1,128,2048]{2,1,0:T(8,128)(2,1)S(1)} %get-tuple-element.235), channel_id=1, source_target_pairs={{0,2},{2,0},{4,6},{6,4},{1,3},{3,1},{5,7},{7,5},{8,10},{10,8},{12,... | collective-permute-start | bytes 1572872 | tf_op jit(solution)/shard_map/ppermute | solution.py:26
  720.5 16.7 %collective-permute-start.58 = (bf16[1,128,2048]{2,1,0:T(8,128)(2,1)S(1)}, bf16[1,128,2048]{2,1,0:T(8,128)(2,1)S(1)}, u32[]{:S(2)}, u32[]{:S(2)}) collective-permute-start(bf16[1,128,2048]{2,1,0:T(8,128)(2,1)S(1)} %get-tuple-element.221), channel_id=1, source_target_pairs={{0,4},{2,6},{4,0},{6,2},{1,5},{3,7},{5,1},{7,3},{8,12},{10,14},{12... | collective-permute-start | bytes 1572872 | tf_op jit(solution)/shard_map/ppermute | solution.py:26
  721.9 16.6 %collective-permute-start.60 = (bf16[1,128,2048]{2,1,0:T(8,128)(2,1)S(1)}, bf16[1,128,2048]{2,1,0:T(8,128)(2,1)S(1)}, u32[]{:S(2)}, u32[]{:S(2)}) collective-permute-start(bf16[1,128,2048]{2,1,0:T(8,128)(2,1)S(1)} %get-tuple-element.223), channel_id=1, source_target_pairs={{0,2},{2,0},{4,6},{6,4},{1,3},{3,1},{5,7},{7,5},{8,10},{10,8},{12,... | collective-permute-start | bytes 1572872 | tf_op jit(solution)/shard_map/ppermute | solution.py:26
  728.7 102.0 %collective-permute-start.40 = (bf16[2,128,2048]{2,1,0:T(8,128)(2,1)}, bf16[2,128,2048]{2,1,0:T(8,128)(2,1)}, u32[]{:S(2)}, u32[]{:S(2)}) collective-permute-start(bf16[2,128,2048]{2,1,0:T(8,128)(2,1)} %pad_maximum_fusion.24), channel_id=1, source_target_pairs={{0,4},{2,6},{4,0},{6,2},{1,5},{3,7},{5,1},{7,3},{8,12},{10,14},{12... | collective-permute-start | bytes 3145736 | tf_op jit(solution)/shard_map/ppermute | solution.py:26
  730.5 100.2 %collective-permute-start.38 = (bf16[2,128,2048]{2,1,0:T(8,128)(2,1)}, bf16[2,128,2048]{2,1,0:T(8,128)(2,1)}, u32[]{:S(2)}, u32[]{:S(2)}) collective-permute-start(bf16[2,128,2048]{2,1,0:T(8,128)(2,1)} %pad_maximum_fusion.23), channel_id=1, source_target_pairs={{0,2},{2,0},{4,6},{6,4},{1,3},{3,1},{5,7},{7,5},{8,10},{10,8},{12,... | collective-permute-start | bytes 3145736 | tf_op jit(solution)/shard_map/ppermute | solution.py:26
  739.9 98.3 %collective-permute-start.61 = (bf16[2,128,2048]{2,1,0:T(8,128)(2,1)}, bf16[2,128,2048]{2,1,0:T(8,128)(2,1)}, u32[]{:S(2)}, u32[]{:S(2)}) collective-permute-start(bf16[2,128,2048]{2,1,0:T(8,128)(2,1)} %pad_maximum_fusion.28), channel_id=1, source_target_pairs={{0,4},{2,6},{4,0},{6,2},{1,5},{3,7},{5,1},{7,3},{8,12},{10,14},{12... | collective-permute-start | bytes 3145736 | tf_op jit(solution)/shard_map/ppermute | solution.py:26
  741.8 96.5 %collective-permute-start.59 = (bf16[2,128,2048]{2,1,0:T(8,128)(2,1)}, bf16[2,128,2048]{2,1,0:T(8,128)(2,1)}, u32[]{:S(2)}, u32[]{:S(2)}) collective-permute-start(bf16[2,128,2048]{2,1,0:T(8,128)(2,1)} %pad_maximum_fusion.27), channel_id=1, source_target_pairs={{0,2},{2,0},{4,6},{6,4},{1,3},{3,1},{5,7},{7,5},{8,10},{10,8},{12,... | collective-permute-start | bytes 3145736 | tf_op jit(solution)/shard_map/ppermute | solution.py:26
  836.4 15.6 %collective-permute-start.41 = (bf16[2,128,2048]{2,1,0:T(8,128)(2,1)}, bf16[2,128,2048]{2,1,0:T(8,128)(2,1)}, u32[]{:S(2)}, u32[]{:S(2)}) collective-permute-start(bf16[2,128,2048]{2,1,0:T(8,128)(2,1)} %get-tuple-element.197), channel_id=1, source_target_pairs={{0,1},{1,0},{2,3},{3,2},{4,5},{5,4},{6,7},{7,6},{8,9},{9,8},{10,11... | collective-permute-start | bytes 3145736 | tf_op jit(solution)/shard_map/ppermute | solution.py:91
  836.5 21.9 %collective-permute-start.75 = (bf16[80,328]{1,0:T(8,128)(2,1)}, bf16[80,328]{1,0:T(8,128)(2,1)S(1)}, u32[]{:S(2)}, u32[]{:S(2)}) collective-permute-start(bf16[80,328]{1,0:T(8,128)(2,1)} %reduce-scatter.7.cloned.1.call-done), channel_id=1, source_target_pairs={{0,0},{2,8},{4,16},{6,24},{8,2},{10,10},{12,18},{14,26},{16,4},{18... | collective-permute-start | bytes 157448 | tf_op jit(solution)/shard_map/ppermute | solution.py:531
  848.4 25.4 %collective-permute-start.62 = (bf16[2,128,2048]{2,1,0:T(8,128)(2,1)}, bf16[2,128,2048]{2,1,0:T(8,128)(2,1)S(1)}, u32[]{:S(2)}, u32[]{:S(2)}) collective-permute-start(bf16[2,128,2048]{2,1,0:T(8,128)(2,1)} %get-tuple-element.186), channel_id=1, source_target_pairs={{0,1},{1,0},{2,3},{3,2},{4,5},{5,4},{6,7},{7,6},{8,9},{9,8},{10,11... | collective-permute-start | bytes 3145736 | tf_op jit(solution)/shard_map/ppermute | solution.py:91
  886.5 12.9 %collective-permute-start.72 = (bf16[128,960]{0,1:T(8,128)(2,1)S(1)}, bf16[128,960]{0,1:T(8,128)(2,1)S(1)}, u32[]{:S(2)}, u32[]{:S(2)}) collective-permute-start(bf16[128,960]{0,1:T(8,128)(2,1)S(1)} %bitcast.572), channel_id=1, source_target_pairs={{0,4},{2,6},{4,0},{6,2},{1,5},{3,7},{5,1},{7,3},{8,12},{10,14},{12... | collective-permute-start | bytes 737288 | tf_op jit(solution)/shard_map/ppermute | solution.py:26
  937.6 13.0 %collective-permute-start.77 = (bf16[128,1536]{1,0:T(8,128)(2,1)S(1)}, bf16[128,1536]{1,0:T(8,128)(2,1)S(1)}, u32[]{:S(2)}, u32[]{:S(2)}) collective-permute-start(bf16[128,1536]{1,0:T(8,128)(2,1)S(1)} %get-tuple-element.270), channel_id=1, source_target_pairs={{0,6},{2,4},{4,2},{6,0},{1,7},{3,5},{5,3},{7,1},{8,14},{10,12},{12... | collective-permute-start | bytes 1179656 | tf_op jit(solution)/shard_map/ppermute | solution.py:26
  937.7 19.4 %collective-permute-start.78 = (bf16[128,1536]{1,0:T(8,128)(2,1)S(1)}, bf16[128,1536]{1,0:T(8,128)(2,1)S(1)}, u32[]{:S(2)}, u32[]{:S(2)}) collective-permute-start(bf16[128,1536]{1,0:T(8,128)(2,1)S(1)} %get-tuple-element.269), channel_id=1, source_target_pairs={{0,4},{2,6},{4,0},{6,2},{1,5},{3,7},{5,1},{7,3},{8,12},{10,14},{12... | collective-permute-start | bytes 1179656 | tf_op jit(solution)/shard_map/ppermute | solution.py:26
  937.8 19.3 %collective-permute-start.79 = (bf16[128,1536]{1,0:T(8,128)(2,1)S(1)}, bf16[128,1536]{1,0:T(8,128)(2,1)S(1)}, u32[]{:S(2)}, u32[]{:S(2)}) collective-permute-start(bf16[128,1536]{1,0:T(8,128)(2,1)S(1)} %get-tuple-element.268), channel_id=1, source_target_pairs={{0,2},{2,0},{4,6},{6,4},{1,3},{3,1},{5,7},{7,5},{8,10},{10,8},{12,... | collective-permute-start | bytes 1179656 | tf_op jit(solution)/shard_map/ppermute | solution.py:26
  (190 other events, 2382.7 us)
Sparse Core Ops, SparseCore 0:
  51.8 76.9 all-gather.3
  130.9 126.9 all-gather.5
  356.0 62.4 all-gather.7
  653.1 22.5 reduce-scatter.6
  677.9 58.5 reduce-scatter.10
  738.7 77.8 reduce-scatter.4
  819.0 117.2 reduce-scatter.8

commit v3 on v2

--- a/solution.py
+++ b/solution.py
@@ -96,9 +96,15 @@
     return own, to_core(own)
 
 
-def collect(own, other):
-    total = (own.astype(F32) + to_core(other).astype(F32)).astype(BF16)
-    summed = lax.psum_scatter(total, "z", scatter_dimension=0, tiled=True)
+def both_cores(own, other):
+    return (own.astype(F32) + to_core(other).astype(F32)).astype(BF16)
+
+
+def sum_along_z(total):
+    return lax.psum_scatter(total, "z", scatter_dimension=0, tiled=True)
+
+
+def to_owners(summed):
     return plane_swap(summed.reshape(PLANE, -1, summed.shape[1]))
 
 
@@ -289,6 +295,7 @@
 
     first_blocks = jnp.concatenate([to_chips(w_x), to_chips(w_g), to_chips(w_o.T)], axis=2)
     first_rows = jnp.concatenate(plane_swap(first_blocks), axis=0)
+    first_rows, own_in, small = lax.optimization_barrier((first_rows, own_in, small))
     whole_in = plane_gather(own_in)
     found = [small] + [to_partner(small, bit) for bit in (1, 2, 3)]
     small = z_gather(jnp.stack(in_order(found, j_index)))
@@ -306,7 +313,7 @@
     )
     w_back = jnp.concatenate([w[:, 2 * part_width :] for w in w_first], axis=1)
     later = (w_gate, w_up, w_down)
-    later, whole_in = lax.optimization_barrier((later, whole_in))
+    later, whole_in, small = lax.optimization_barrier((later, whole_in, small))
     wide_blocks = jnp.concatenate([to_chips(later[0]), to_chips(later[1])], axis=2)
     wide_rows = jnp.concatenate(plane_swap(wide_blocks), axis=0)
     narrow_rows = jnp.concatenate(plane_swap(to_chips(later[2].T)), axis=0)
@@ -412,20 +419,14 @@
     conv_part = conv_part + jnp.einsum(
         "bdjs,bdsc->bdjc", from_state.astype(BF16), conv_here, preferred_element_type=F32
     )
-    finals = jnp.concatenate([final_part[:, :, None], conv_part], axis=2)
-    finals = jnp.concatenate(
-        [finals[..., :part_width], to_core(finals[..., part_width:])], axis=0
-    )
-    finals = jnp.where(core == 0, finals, jnp.roll(finals, n_streams, 0))
-    finals = lax.all_gather(finals, ("z", "j"), axis=0)
-    finals = finals.reshape(z_size, PLANE, all_streams_count, 2, 4, part_width)
-    finals = jnp.moveaxis(jnp.sum(finals, axis=0), 0, 3)
-    finals = finals.reshape(all_streams_count, 2, 4, half_width)
+    state_high = lax.reduce_precision(final_part, exponent_bits=8, mantissa_bits=7)
+    finals = jnp.stack([state_high, final_part - state_high], axis=2)
+    finals = jnp.concatenate([finals, conv_part], axis=2).reshape(-1, rec_width)
+    columns = finals.shape[0]
+    finals = lax.dynamic_update_slice_in_dim(
+        jnp.zeros((rec_width, halves * columns), F32), finals.T, core * columns, 1
+    )
     dp_index = z_index * PLANE + j_index
-    out_width = half_width // (z_size * PLANE)
-    finals = lax.dynamic_slice_in_dim(finals, dp_index * out_width, out_width, 3)
-    state_block = finals[:, :, 0][:, :, None]
-    conv_block = finals[:, :, 1:].astype(BF16)[:, :, :, None]
 
     states_flat = states.reshape(tokens, rec_width)
     mixed_rows = (states_flat * branch).astype(BF16)
@@ -459,9 +460,10 @@
     own_rec = (d_hidden * own_live).astype(BF16).reshape(n_streams, own_rows, model_width)
     d_rec = plane_gather(own_rec).reshape(tokens, model_width)
     d_rec, g_narrow, g_wide = lax.optimization_barrier((d_rec, g_narrow, g_wide))
-    out_wide = collect(*g_wide)
-    out_narrow = collect(*g_narrow)
+    sum_wide, sum_narrow = both_cores(*g_wide), both_cores(*g_narrow)
     d_mixed = dot(d_rec, w_back, 1, 0)
+    d_mixed, sum_wide, sum_narrow = lax.optimization_barrier((d_mixed, sum_wide, sum_narrow))
+    sum_wide = sum_along_z(sum_wide)
     g_back = dot(d_rec, mixed_rows, 0, 0).astype(BF16)
 
     grad_state = (d_mixed * branch).reshape(n_streams, n_rows, rec_width)
@@ -494,6 +496,9 @@
         "nho,hko->nhk", grad_gates, gates_all, preferred_element_type=F32
     ).reshape(tokens, rec_width)
     d_conv = (d_conv_direct + d_conv_gates).reshape(n_streams, n_rows, rec_width)
+    d_conv, sum_wide, sum_narrow = lax.optimization_barrier((d_conv, sum_wide, sum_narrow))
+    sum_narrow = sum_along_z(sum_narrow)
+    out_wide = to_owners(sum_wide)
     d_extended, g_taps, g_conv_bias = conv_back(d_conv)
     rim_grad = shifted(d_extended[:, :3].astype(BF16), -1).astype(F32)
     d_source = jnp.concatenate([d_extended[:, 3:n_rows], d_extended[:, n_rows:] + rim_grad], axis=1)
@@ -502,7 +507,7 @@
     )
     first_part = dot(d_projected, w_rec, 1, 1)
     g_rec = dot(normed_low, d_projected, 0, 0).astype(BF16)
-    out_first = collect(
+    sum_first = both_cores(
         *(
             jnp.concatenate(
                 [
@@ -522,13 +527,23 @@
             jnp.sum(entry_low.astype(F32), axis=0)[:, None],
             g_lam[:, None],
             g_gates,
+            finals,
         ],
         axis=1,
     ).astype(BF16)
-    g_small = g_small[:part_width].astype(F32) + to_core(g_small[part_width:]).astype(F32)
-    g_small = lax.psum_scatter(g_small.astype(BF16), "z", scatter_dimension=0, tiled=True)
+    sum_small = both_cores(g_small[:part_width], g_small[part_width:])
+    sum_small, sum_first, sum_narrow = lax.optimization_barrier((sum_small, sum_first, sum_narrow))
+    out_narrow = to_owners(sum_narrow)
+    sum_first = sum_along_z(sum_first)
+    out_first = to_owners(sum_first)
+    g_small = sum_along_z(sum_small)
     route = [(z * PLANE + j, j * z_size + z) for z in range(z_size) for j in range(PLANE)]
-    g_small = lax.ppermute(g_small, ("z", "j"), route).astype(F32)[None]
+    g_small = lax.ppermute(g_small, ("z", "j"), route).astype(F32)
+    g_params = g_small[None, :, :8]
+    g_gates = g_small[None, :, 8 : 8 + 2 * HEAD_DIM]
+    finals = g_small[:, 8 + 2 * HEAD_DIM :].T.reshape(all_streams_count, 2, 5, -1)
+    state_block = (finals[:, :, 0] + finals[:, :, 1])[:, :, None]
+    conv_block = finals[:, :, 2:].astype(BF16)[:, :, :, None]
 
     first_total = plane_sum(first_part, n_streams).reshape(own_tokens, model_width)
     d_input_norm, g_gain_one = norm_one_back(first_total)
@@ -549,8 +564,8 @@
         g_gains,
         flat(out_first, 0, part_width),
         flat(out_first, part_width, 2 * part_width),
-        g_small[..., :8],
-        g_small[..., 8:],
+        g_params,
+        g_gates,
         flat(out_first, 2 * part_width, 3 * part_width).T,
         flat(out_wide, 0, ff_part),
         flat(out_wide, ff_part, 2 * ff_part),

time: 975 us -> 886 us (0.909)
  blocking collectives: 85.6 us -> 0 us
  local copies, waits for them, and re-layouts: 155 us -> 133 us
  waiting for transfers between devices: 298 us -> 317 us
    all_gather x1 -> x0, blocking collectives: 85.6 us -> none  [shards(): finals = lax.all_gather(finals, ('z', 'j'), axis=0)]
    ppermute x53, waiting for transfers between devices: 175 us -> 250 us  [to_partner(): return lax.ppermute(block, 'j', [(i, i ^ bit) for i in range(PLANE)])]
    reduce_scatter x4 -> x3, waiting for transfers between devices: 34.2 us -> 0.02 us  [sum_along_z(): return lax.psum_scatter(total, 'z', scatter_dimension=0, tiled=True)]
    all_gather x3, waiting for transfers between devices: 36.6 us -> 13.1 us  [along_z(): own = lax.all_gather(block, 'z', axis=0, tiled=True)]
    unnamed x342 -> x332, local copies, waits for them, and re-layouts: 34.7 us -> 28.7 us
  transfers between devices with their start and end apart: 91 -> 90, of which waited for: 45 -> 52; matrix products, arithmetic and copies ran while one was open for 37% -> 37% of each run, Pallas kernels for 1% -> 2%
where the time goes in v3:
time: 886 us; the launch traced here: 880 us
  waiting for transfers between devices  317 us (36%)
  matrix products  157 us (18%)
  local copies, waits for them, and re-layouts  133 us (15%)
  starting transfers between devices  121 us (14%)
  other arithmetic  117 us (13%)
  between operations  17.3 us (2%)
  Pallas kernels  17.1 us (2%)
    ppermute x53, waiting for transfers between devices, to_partner(): return lax.ppermute(block, 'j', [(i, i ^ bit) for i in range(PLANE)])  250 us
    dot_general x18, matrix products, dot(): lax.dot_general(left, right, (((left_dim,), (right_dim,)), ((), ())), pre...  143 us
    ppermute x53, starting transfers between devices, to_partner(): return lax.ppermute(block, 'j', [(i, i ^ bit) for i in range(PLANE)])  73.6 us
    ppermute x8, starting transfers between devices, shifted(): lax.ppermute(block, 'z', [(i - distance, i) for i in range(size) if 0 <=...  33.3 us
    ppermute x6, waiting for transfers between devices, z_gather(): lax.ppermute(block, 'z', [(i, (i + step) % size) for i in range(size)])  33.3 us
    unnamed x332, local copies, waits for them, and re-layouts  28.7 us
  transfers between devices with their start and end apart: 90, of which 52 were waited for; matrix products, arithmetic and copies ran while one was open for 37% of the time, Pallas kernels for 2%

profile of v3, /device:TPU:0, one launch (start us, length us, event | category | flops | bytes accessed | tf_op | source)
XLA Modules:
  0.0 879.6 jit_solution(1711961580358996278)
XLA Ops:
  10.8 4.0 collective-permute-start
  34.6 22.2 %collective-permute-done.11 = bf16[2,128,2048]{2,1,0:T(8,128)(2,1)S(1)} collective-permute-done((bf16[2,128,2048]{2,1,0:T(8,128)(2,1)S(1)}, bf16[2,128,2048]{2,1,0:T(8,128)(2,1)S(1)}, u32[]{:S(2)}, u32[]{:S(2)}) %collective-permute-start.11) | collective-permute-done | bytes 1048608 | tf_op jit(solution)/shard_map/ppermute | solution.py:26
  59.4 10.2 %collective-permute-done.13 = bf16[1,128,2048]{2,1,0:T(8,128)(2,1)S(1)} collective-permute-done((bf16[1,128,2048]{2,1,0:T(8,128)(2,1)S(1)}, bf16[1,128,2048]{2,1,0:T(8,128)(2,1)S(1)}, u32[]{:S(2)}, u32[]{:S(2)}) %collective-permute-start.13) | collective-permute-done | bytes 524320 | tf_op jit(solution)/shard_map/ppermute | solution.py:26
  80.0 10.4 %collective-permute-done.33 = bf16[128,1536]{1,0:T(8,128)(2,1)S(1)} collective-permute-done((bf16[128,1536]{1,0:T(8,128)(2,1)}, bf16[128,1536]{1,0:T(8,128)(2,1)S(1)}, u32[]{:S(2)}, u32[]{:S(2)}) %collective-permute-start.33) | collective-permute-done | bytes 393248 | tf_op jit(solution)/shard_map/ppermute | solution.py:26
  97.6 6.8 all-gather.4.cloned.1.call-done
  109.4 6.5 collective-permute-done.6
  116.0 24.2 %collective-permute-done.7 = bf16[4,82,328]{2,1,0:T(8,128)(2,1)S(1)} collective-permute-done((bf16[4,82,328]{2,1,0:T(8,128)(2,1)S(1)}, bf16[4,82,328]{2,1,0:T(8,128)(2,1)S(1)}, u32[]{:S(2)}, u32[]{:S(2)}) %collective-permute-start.7) | collective-permute-done | bytes 215200 | tf_op jit(solution)/shard_map/ppermute | solution.py:116
  144.1 3.7 multiply_reduce_fusion
  151.6 4.7 fusion.158
  156.2 5.6 fusion.67
  162.1 22.2 %collective-permute-start.15 = (bf16[2,3,640]{2,1,0:T(4,128)(2,1)S(1)}, bf16[2,3,640]{2,1,0:T(4,128)(2,1)S(1)}, u32[]{:S(2)}, u32[]{:S(2)}) collective-permute-start(bf16[2,3,640]{2,1,0:T(4,128)(2,1)S(1)} %slice.607), channel_id=1, source_target_pairs={{0,8},{8,16},{16,24},{1,9},{9,17},{17,25},{2,10},{10,18},{18,26},{... | collective-permute-start | bytes 23048 | tf_op jit(solution)/shard_map/ppermute | solution.py:150
  192.5 4.2 fusion.154
  207.4 3.8 copy.453
  211.2 5.6 reshape.1533
  216.8 5.2 copy.452
  222.1 5.1 fusion.17
  227.2 8.0 shard_map.246
  266.7 9.3 %collective-permute-done.21 = bf16[1,128,2048]{2,1,0:T(8,128)(2,1)} collective-permute-done((bf16[1,128,2048]{2,1,0:T(8,128)(2,1)}, bf16[1,128,2048]{2,1,0:T(8,128)(2,1)}, u32[]{:S(2)}, u32[]{:S(2)}) %collective-permute-start.21) | collective-permute-done | bytes 524320 | tf_op jit(solution)/shard_map/ppermute | solution.py:26
  281.4 16.9 %collective-permute-done.43 = bf16[2,128,2048]{2,1,0:T(8,128)(2,1)S(1)} collective-permute-done((bf16[2,128,2048]{2,1,0:T(8,128)(2,1)S(1)}, bf16[2,128,2048]{2,1,0:T(8,128)(2,1)S(1)}, u32[]{:S(2)}, u32[]{:S(2)}) %collective-permute-start.43) | collective-permute-done | bytes 1048608 | tf_op jit(solution)/shard_map/ppermute | solution.py:26
  303.0 17.8 %collective-permute-done.24 = bf16[2,128,2048]{2,1,0:T(8,128)(2,1)S(1)} collective-permute-done((bf16[2,128,2048]{2,1,0:T(8,128)(2,1)S(1)}, bf16[2,128,2048]{2,1,0:T(8,128)(2,1)S(1)}, u32[]{:S(2)}, u32[]{:S(2)}) %collective-permute-start.24) | collective-permute-done | bytes 1048608 | tf_op jit(solution)/shard_map/ppermute | solution.py:26
  327.4 6.2 collective-permute-done.45
  334.9 18.1 %collective-permute-done.26 = bf16[2,128,2048]{2,1,0:T(8,128)(2,1)S(1)} collective-permute-done((bf16[2,128,2048]{2,1,0:T(8,128)(2,1)S(1)}, bf16[2,128,2048]{2,1,0:T(8,128)(2,1)S(1)}, u32[]{:S(2)}, u32[]{:S(2)}) %collective-permute-start.26) | collective-permute-done | bytes 1048608 | tf_op jit(solution)/shard_map/ppermute | solution.py:26
  356.5 9.3 %collective-permute-done.28 = bf16[1,128,2048]{2,1,0:T(8,128)(2,1)S(1)} collective-permute-done((bf16[1,128,2048]{2,1,0:T(8,128)(2,1)S(1)}, bf16[1,128,2048]{2,1,0:T(8,128)(2,1)S(1)}, u32[]{:S(2)}, u32[]{:S(2)}) %collective-permute-start.28) | collective-permute-done | bytes 524320 | tf_op jit(solution)/shard_map/ppermute | solution.py:26
  369.3 10.8 %fusion.171 = f32[1024,1536]{1,0:T(8,128)} fusion(bf16[1024,2048]{1,0:T(8,128)(2,1)S(1)} %bitcast.555, bf16[2048,1536]{1,0:T(8,128)(2,1)} %collective-permute-done.35), kind=kOutput, calls=%fused_computation.523 | convolution fusion | flops 6442450944 | bytes 16777216 | tf_op jit(solution)/shard_map/dot_general | solution.py:20
  380.2 6.2 all-gather.8.cloned.1.call-done
  386.4 11.9 %fusion.170 = f32[1024,1536]{1,0:T(8,128)} fusion(bf16[1024,2048]{1,0:T(8,128)(2,1)} %bitcast.556, bf16[2048,1536]{1,0:T(8,128)(2,1)} %all-gather.6.cloned.1.call-done), kind=kOutput, calls=%fused_computation.522 | convolution fusion | flops 6442450944 | bytes 16777216 | tf_op jit(solution)/shard_map/dot_general | solution.py:20
  398.3 9.2 %fusion.8 = (bf16[1024,768]{1,0:T(8,128)(2,1)}, bf16[1024,768]{1,0:T(8,128)(2,1)}, bf16[1024,768]{1,0:T(8,128)(2,1)}) fusion(f32[1024,1536]{1,0:T(8,128)} %fusion.170, bf16[1024,2048]{1,0:T(8,128)(2,1)S(1)} %bitcast.551, bf16[2048,768]{0,1:T(8,128)(2,1)S(1)} %copy-done.135), kind=kOutput, calls=%fused_computation.42 | convolution fusion | flops 3241672704 | bytes 18350080 | tf_op jit(solution)/shard_map/dot_general | solution.py:20
  407.5 9.7 %fusion.15 = (bf16[1024,768]{1,0:T(8,128)(2,1)S(1)}, bf16[1024,768]{1,0:T(8,128)(2,1)S(1)}, bf16[1024,768]{1,0:T(8,128)(2,1)}) fusion(f32[1024,1536]{1,0:T(8,128)} %fusion.171, bf16[1024,2048]{1,0:T(8,128)(2,1)S(1)} %bitcast.552, bf16[2048,768]{0,1:T(8,128)(2,1)S(1)} %collective-permute-done.36), kind=kOutput, calls=%fused_computation.49 | convolution fusion | flops 3241672704 | bytes 18350080 | tf_op jit(solution)/shard_map/dot_general | solution.py:20
  417.2 12.0 %fusion.49 = f32[1024,2048]{1,0:T(8,128)} fusion(bf16[2048,1536]{1,0:T(8,128)(2,1)} %collective-permute-done.35, bf16[1024,768]{1,0:T(8,128)(2,1)S(1)} %get-tuple-element.217, bf16[1024,768]{1,0:T(8,128)(2,1)S(1)} %get-tuple-element.216), kind=kOutput, calls=%fused_computation.145 | convolution fusion | flops 6448742400 | bytes 17825792 | tf_op jit(solution)/shard_map/dot_general | solution.py:20
  429.2 10.1 %add_convert_fusion.1 = bf16[1024,2048]{1,0:T(8,128)(2,1)S(1)} fusion(f32[1024,2048]{1,0:T(8,128)} %fusion.49, bf16[2048,1536]{1,0:T(8,128)(2,1)S(1)} %bitcast.605, bf16[1024,768]{1,0:T(8,128)(2,1)} %get-tuple-element.215, bf16[1024,768]{1,0:T(8,128)(2,1)} %get-tuple-element.214), kind=kOutput, calls=%fused_computation.4 | convolution fusion | flops 6452936704 | bytes 22020096 | tf_op jit(solution)/shard_map/dot_general | solution.py:20
  442.6 11.6 %collective-permute-done.46 = bf16[1,128,2048]{2,1,0:T(8,128)(2,1)S(1)} collective-permute-done((bf16[1,128,2048]{2,1,0:T(8,128)(2,1)S(1)}, bf16[1,128,2048]{2,1,0:T(8,128)(2,1)S(1)}, u32[]{:S(2)}, u32[]{:S(2)}) %collective-permute-start.46) | collective-permute-done | bytes 524320 | tf_op jit(solution)/shard_map/ppermute | solution.py:26
  458.6 9.3 %convolution_convert_fusion.2 = bf16[2048,1536]{1,0:T(8,128)(2,1)} fusion(bf16[1024,2048]{1,0:T(8,128)(2,1)S(1)} %bitcast.557, bf16[1024,768]{1,0:T(8,128)(2,1)S(1)} %copy-done.148, bf16[1024,768]{1,0:T(8,128)(2,1)S(1)} %copy-done.147), kind=kOutput, calls=%fused_computation.10 | convolution fusion | flops 6451888128 | bytes 13631488 | tf_op jit(solution)/shard_map/dot_general | solution.py:20
  467.9 5.1 convolution_convert_fusion.6
  473.0 7.6 collective-permute-done.49
  491.0 9.3 %convolution_convert_fusion.1 = bf16[2048,1536]{1,0:T(8,128)(2,1)} fusion(bf16[1024,2048]{1,0:T(8,128)(2,1)S(1)} %bitcast.558, bf16[1024,768]{1,0:T(8,128)(2,1)S(1)} %copy-done.146, bf16[1024,768]{1,0:T(8,128)(2,1)S(1)} %copy-done.144), kind=kOutput, calls=%fused_computation.9 | convolution fusion | flops 6451888128 | bytes 13631488 | tf_op jit(solution)/shard_map/dot_general | solution.py:20
  500.3 5.2 convolution_convert_fusion.5
  505.5 7.3 collective-permute-done.51
  517.1 6.8 collective-permute-done.53
  526.5 8.0 fusion.51
  534.5 5.4 collective-permute-done.55
  542.5 9.0 %add_convert_fusion = bf16[2048,1536]{1,0:T(8,128)(2,1)} fusion(bf16[2048,1536]{1,0:T(8,128)(2,1)} %collective-permute-done.54, bf16[2048,1536]{1,0:T(8,128)(2,1)} %convolution_convert_fusion.2), kind=kLoop, calls=%fused_computation | loop fusion | flops 12582912 | bytes 18874368 | tf_op jit(solution)/shard_map/convert_element_type | solution.py:100
  559.3 4.1 add_convert_fusion.2
  567.6 11.2 %collective-permute-done.37 = bf16[1,128,2048]{2,1,0:T(8,128)(2,1)S(1)} collective-permute-done((bf16[1,128,2048]{2,1,0:T(8,128)(2,1)S(1)}, bf16[1,128,2048]{2,1,0:T(8,128)(2,1)S(1)}, u32[]{:S(2)}, u32[]{:S(2)}) %collective-permute-start.37) | collective-permute-done | bytes 524320 | tf_op jit(solution)/shard_map/ppermute | solution.py:26
  585.1 9.1 %shard_map.247 = (f32[2,512,640]{2,1,0:T(8,128)S(1)}, f32[2,512,640]{2,1,0:T(8,128)S(1)}) custom-call(f32[2,512,640]{2,1,0:T(8,128)S(1)} %concatenate.155.keep_ref, f32[2,512,640]{2,1,0:T(8,128)S(1)} %bitcast.521), custom_call_target="tpu_custom_call" | custom-call | flops 5242880 | bytes 10485760 | tf_op jit(solution)/shard_map/pallas_call | solution.py:204
  595.8 7.3 convolution_convert_fusion.7
  611.5 6.6 fusion.52
  618.2 3.9 copy.482
  625.4 5.2 copy.487
  630.5 4.9 reshape.1543
  635.4 6.8 multiply_reduce_fusion.1
  644.0 4.0 fusion.146
  653.3 5.6 copy.488
  659.0 8.5 multiply_add_fusion.1
  667.5 5.4 fusion.145
  683.3 8.3 convolution_convert_fusion
  702.2 20.6 %collective-permute-done.38 = bf16[2,128,2048]{2,1,0:T(8,128)(2,1)} collective-permute-done((bf16[2,128,2048]{2,1,0:T(8,128)(2,1)}, bf16[2,128,2048]{2,1,0:T(8,128)(2,1)}, u32[]{:S(2)}, u32[]{:S(2)}) %collective-permute-start.38) | collective-permute-done | bytes 1048608 | tf_op jit(solution)/shard_map/ppermute | solution.py:26
  724.3 4.8 constant_dynamic-update-slice_fusion.3
  733.8 9.9 %convolution_convert_fusion.3 = bf16[1024,2048]{1,0:T(8,128)(2,1)} fusion(bf16[1024,640]{1,0:T(8,128)(2,1)} %get-tuple-element.219, bf16[1024,640]{1,0:T(8,128)(2,1)} %bitcast.566, bf16[2048,320]{0,1:T(8,128)(2,1)} %copy-done.67, bf16[2048,320]{0,1:T(8,128)(2,1)} %copy-done.65, bf16[2048,320]{0,1:T(8,128)(2,1)} %copy-done.68, bf16[2048,320]{0,1:T(8,128)(2,1)} %copy-done.66), kind=kOutput, calls=%fused_computation.27 | convolution fusion | flops 5397020672 | bytes 12058624 | tf_op jit(solution)/shard_map/dot_general | solution.py:20
  743.9 4.9 add_convert_fusion.3
  761.6 7.1 collective-permute-done.60
  773.5 4.0 collective-permute-done.77
  777.5 6.9 collective-permute-done.78
  786.2 19.6 %collective-permute-done.63 = bf16[2,128,2048]{2,1,0:T(8,128)(2,1)S(1)} collective-permute-done((bf16[2,128,2048]{2,1,0:T(8,128)(2,1)S(1)}, bf16[2,128,2048]{2,1,0:T(8,128)(2,1)S(1)}, u32[]{:S(2)}, u32[]{:S(2)}) %collective-permute-start.63) | collective-permute-done | bytes 1048608 | tf_op jit(solution)/shard_map/ppermute | solution.py:26
  849.3 9.3 %collective-permute-start.74 = (bf16[128,960]{0,1:T(8,128)(2,1)S(1)}, bf16[128,960]{0,1:T(8,128)(2,1)S(1)}, u32[]{:S(2)}, u32[]{:S(2)}) collective-permute-start(bf16[128,960]{0,1:T(8,128)(2,1)S(1)} %bitcast.579), channel_id=1, source_target_pairs={{0,6},{2,4},{4,2},{6,0},{1,7},{3,5},{5,3},{7,1},{8,14},{10,12},{12... | collective-permute-start | bytes 737288 | tf_op jit(solution)/shard_map/ppermute | solution.py:26
  (740 shorter events, 299.9 us)
Async XLA Ops:
  7.2 97.3 %all-gather.4.cloned.1.call-start = ((), (), s32[]{:S(2)}) async-start(), calls=%async_computation.4 | async-start | bytes 4915200 | tf_op jit(solution)/shard_map/all_gather | solution.py:95
  10.8 13.1 %collective-permute-start = (bf16[128,960]{0,1:T(8,128)(2,1)S(1)}, bf16[128,960]{0,1:T(8,128)(2,1)S(1)}, u32[]{:S(2)}, u32[]{:S(2)}) collective-permute-start(bf16[128,960]{0,1:T(8,128)(2,1)S(1)} %get-tuple-element.298), channel_id=1, source_target_pairs={{0,6},{2,4},{4,2},{6,0},{1,7},{3,5},{5,3},{7,1},{8,14},{10,12},{12... | collective-permute-start | bytes 737288 | tf_op jit(solution)/shard_map/ppermute | solution.py:26
  17.4 171.6 %collective-permute-start.16 = (bf16[2,2,3,320]{3,2,1,0:T(4,128)(2,1)}, bf16[2,2,3,320]{3,2,1,0:T(4,128)(2,1)}, u32[]{:S(2)}, u32[]{:S(2)}) collective-permute-start(bf16[2,2,3,320]{3,2,1,0:T(4,128)(2,1)} %copy.525), channel_id=1, source_target_pairs={{0,1},{1,0},{2,3},{3,2},{4,5},{5,4},{6,7},{7,6},{8,9},{9,8},{10,11... | collective-permute-start | bytes 23048 | tf_op jit(solution)/shard_map/ppermute | solution.py:91
  18.8 58.2 %collective-permute-start.17 = (f32[2,2,320]{2,1,0:T(2,128)}, f32[2,2,320]{2,1,0:T(2,128)}, u32[]{:S(2)}, u32[]{:S(2)}) collective-permute-start(f32[2,2,320]{2,1,0:T(2,128)} %get-tuple-element.341), channel_id=1, source_target_pairs={{0,1},{1,0},{2,3},{3,2},{4,5},{5,4},{6,7},{7,6},{8,9},{9,8},{10,11... | collective-permute-start | bytes 15368 | tf_op jit(solution)/shard_map/ppermute | solution.py:91
  27.4 212.9 %all-gather.6.cloned.1.call-start = ((), (), s32[]{:S(2)}) async-start(), calls=%async_computation.5 | async-start | bytes 7864320 | tf_op jit(solution)/shard_map/all_gather | solution.py:95
  30.6 26.7 %collective-permute-start.10 = (bf16[2,128,2048]{2,1,0:T(8,128)(2,1)S(1)}, bf16[2,128,2048]{2,1,0:T(8,128)(2,1)S(1)}, u32[]{:S(2)}, u32[]{:S(2)}) collective-permute-start(bf16[2,128,2048]{2,1,0:T(8,128)(2,1)S(1)} %get-tuple-element.43), channel_id=1, source_target_pairs={{0,2},{2,0},{4,6},{6,4},{1,3},{3,1},{5,7},{7,5},{8,10},{10,8},{12,... | collective-permute-start | bytes 3145736 | tf_op jit(solution)/shard_map/ppermute | solution.py:26
  32.1 24.7 %collective-permute-start.11 = (bf16[2,128,2048]{2,1,0:T(8,128)(2,1)S(1)}, bf16[2,128,2048]{2,1,0:T(8,128)(2,1)S(1)}, u32[]{:S(2)}, u32[]{:S(2)}) collective-permute-start(bf16[2,128,2048]{2,1,0:T(8,128)(2,1)S(1)} %get-tuple-element.43), channel_id=1, source_target_pairs={{0,4},{2,6},{4,0},{6,2},{1,5},{3,7},{5,1},{7,3},{8,12},{10,14},{12... | collective-permute-start | bytes 3145736 | tf_op jit(solution)/shard_map/ppermute | solution.py:26
  56.9 12.7 %collective-permute-start.13 = (bf16[1,128,2048]{2,1,0:T(8,128)(2,1)S(1)}, bf16[1,128,2048]{2,1,0:T(8,128)(2,1)S(1)}, u32[]{:S(2)}, u32[]{:S(2)}) collective-permute-start(bf16[1,128,2048]{2,1,0:T(8,128)(2,1)S(1)} %slice.599), channel_id=1, source_target_pairs={{0,2},{2,0},{4,6},{6,4},{1,3},{3,1},{5,7},{7,5},{8,10},{10,8},{12,... | collective-permute-start | bytes 1572872 | tf_op jit(solution)/shard_map/ppermute | solution.py:26
  57.3 12.5 %collective-permute-start.12 = (bf16[1,128,2048]{2,1,0:T(8,128)(2,1)S(1)}, bf16[1,128,2048]{2,1,0:T(8,128)(2,1)S(1)}, u32[]{:S(2)}, u32[]{:S(2)}) collective-permute-start(bf16[1,128,2048]{2,1,0:T(8,128)(2,1)S(1)} %slice.598), channel_id=1, source_target_pairs={{0,4},{2,6},{4,0},{6,2},{1,5},{3,7},{5,1},{7,3},{8,12},{10,14},{12... | collective-permute-start | bytes 1572872 | tf_op jit(solution)/shard_map/ppermute | solution.py:26
  72.2 18.3 %collective-permute-start.33 = (bf16[128,1536]{1,0:T(8,128)(2,1)}, bf16[128,1536]{1,0:T(8,128)(2,1)S(1)}, u32[]{:S(2)}, u32[]{:S(2)}) collective-permute-start(bf16[128,1536]{1,0:T(8,128)(2,1)} %get-tuple-element.284), channel_id=1, source_target_pairs={{0,4},{2,6},{4,0},{6,2},{1,5},{3,7},{5,1},{7,3},{8,12},{10,14},{12... | collective-permute-start | bytes 1179656 | tf_op jit(solution)/shard_map/ppermute | solution.py:26
  73.9 18.3 %collective-permute-start.32 = (bf16[128,1536]{1,0:T(8,128)(2,1)S(1)}, bf16[128,1536]{1,0:T(8,128)(2,1)S(1)}, u32[]{:S(2)}, u32[]{:S(2)}) collective-permute-start(bf16[128,1536]{1,0:T(8,128)(2,1)S(1)} %get-tuple-element.283), channel_id=1, source_target_pairs={{0,6},{2,4},{4,2},{6,0},{1,7},{3,5},{5,3},{7,1},{8,14},{10,12},{12... | collective-permute-start | bytes 1179656 | tf_op jit(solution)/shard_map/ppermute | solution.py:26
  75.2 17.4 %collective-permute-start.34 = (bf16[128,1536]{1,0:T(8,128)(2,1)S(1)}, bf16[128,1536]{1,0:T(8,128)(2,1)S(1)}, u32[]{:S(2)}, u32[]{:S(2)}) collective-permute-start(bf16[128,1536]{1,0:T(8,128)(2,1)S(1)} %get-tuple-element.282), channel_id=1, source_target_pairs={{0,2},{2,0},{4,6},{6,4},{1,3},{3,1},{5,7},{7,5},{8,10},{10,8},{12,... | collective-permute-start | bytes 1179656 | tf_op jit(solution)/shard_map/ppermute | solution.py:26
  78.5 15.8 %collective-permute-start.3 = (bf16[82,328]{1,0:T(8,128)(2,1)}, bf16[82,328]{1,0:T(8,128)(2,1)}, u32[]{:S(2)}, u32[]{:S(2)}) collective-permute-start(bf16[82,328]{1,0:T(8,128)(2,1)} %fusion.78), channel_id=1, source_target_pairs={{0,6},{2,4},{4,2},{6,0},{1,7},{3,5},{5,3},{7,1},{8,14},{10,12},{12... | collective-permute-start | bytes 161384 | tf_op jit(solution)/shard_map/ppermute | solution.py:26
  94.2 292.1 %all-gather.8.cloned.1.call-start = ((), (), s32[]{:S(2)}) async-start(), calls=%async_computation.6 | async-start | bytes 3932160 | tf_op jit(solution)/shard_map/all_gather | solution.py:95
  104.5 47.1 %collective-permute-start.14 = (bf16[2048,960]{0,1:T(8,128)(2,1)}, bf16[2048,960]{0,1:T(8,128)(2,1)}, u32[]{:S(2)}, u32[]{:S(2)}) collective-permute-start(bf16[2048,960]{0,1:T(8,128)(2,1)} %all-gather.4.cloned.1.call-done), channel_id=1, source_target_pairs={{0,1},{1,0},{2,3},{3,2},{4,5},{5,4},{6,7},{7,6},{8,9},{9,8},{10,11... | collective-permute-start | bytes 11796488 | tf_op jit(solution)/shard_map/ppermute | solution.py:91
  104.6 11.3 %collective-permute-start.6 = (bf16[4,82,328]{2,1,0:T(8,128)(2,1)S(1)}, bf16[4,82,328]{2,1,0:T(8,128)(2,1)S(1)}, u32[]{:S(2)}, u32[]{:S(2)}) collective-permute-start(bf16[4,82,328]{2,1,0:T(8,128)(2,1)S(1)} %get-tuple-element.320), channel_id=1, source_target_pairs={{0,8},{8,16},{16,24},{24,0},{1,9},{9,17},{17,25},{25,1},{2,10},{10... | collective-permute-start | bytes 645512 | tf_op jit(solution)/shard_map/ppermute | solution.py:116
  104.6 35.6 %collective-permute-start.7 = (bf16[4,82,328]{2,1,0:T(8,128)(2,1)S(1)}, bf16[4,82,328]{2,1,0:T(8,128)(2,1)S(1)}, u32[]{:S(2)}, u32[]{:S(2)}) collective-permute-start(bf16[4,82,328]{2,1,0:T(8,128)(2,1)S(1)} %get-tuple-element.320), channel_id=1, source_target_pairs={{0,16},{8,24},{16,0},{24,8},{1,17},{9,25},{17,1},{25,9},{2,18},{10... | collective-permute-start | bytes 645512 | tf_op jit(solution)/shard_map/ppermute | solution.py:116
  105.9 34.4 %collective-permute-start.8 = (bf16[4,82,328]{2,1,0:T(8,128)(2,1)S(1)}, bf16[4,82,328]{2,1,0:T(8,128)(2,1)S(1)}, u32[]{:S(2)}, u32[]{:S(2)}) collective-permute-start(bf16[4,82,328]{2,1,0:T(8,128)(2,1)S(1)} %get-tuple-element.320), channel_id=1, source_target_pairs={{0,24},{8,0},{16,8},{24,16},{1,25},{9,1},{17,9},{25,17},{2,26},{10... | collective-permute-start | bytes 645512 | tf_op jit(solution)/shard_map/ppermute | solution.py:116
  162.1 26.6 %collective-permute-start.15 = (bf16[2,3,640]{2,1,0:T(4,128)(2,1)S(1)}, bf16[2,3,640]{2,1,0:T(4,128)(2,1)S(1)}, u32[]{:S(2)}, u32[]{:S(2)}) collective-permute-start(bf16[2,3,640]{2,1,0:T(4,128)(2,1)S(1)} %slice.607), channel_id=1, source_target_pairs={{0,8},{8,16},{16,24},{1,9},{9,17},{17,25},{2,10},{10,18},{18,26},{... | collective-permute-start | bytes 23048 | tf_op jit(solution)/shard_map/ppermute | solution.py:150
  185.2 59.2 %collective-permute-start.29 = (bf16[128,768]{0,1:T(8,128)(2,1)}, bf16[128,768]{0,1:T(8,128)(2,1)S(1)}, u32[]{:S(2)}, u32[]{:S(2)}) collective-permute-start(bf16[128,768]{0,1:T(8,128)(2,1)} %get-tuple-element.309), channel_id=1, source_target_pairs={{0,6},{2,4},{4,2},{6,0},{1,7},{3,5},{5,3},{7,1},{8,14},{10,12},{12... | collective-permute-start | bytes 589832 | tf_op jit(solution)/shard_map/ppermute | solution.py:26
  187.6 56.8 %collective-permute-start.30 = (bf16[128,768]{0,1:T(8,128)(2,1)}, bf16[128,768]{0,1:T(8,128)(2,1)S(1)}, u32[]{:S(2)}, u32[]{:S(2)}) collective-permute-start(bf16[128,768]{0,1:T(8,128)(2,1)} %get-tuple-element.308), channel_id=1, source_target_pairs={{0,4},{2,6},{4,0},{6,2},{1,5},{3,7},{5,1},{7,3},{8,12},{10,14},{12... | collective-permute-start | bytes 589832 | tf_op jit(solution)/shard_map/ppermute | solution.py:26
  188.1 56.3 %collective-permute-start.31 = (bf16[128,768]{0,1:T(8,128)(2,1)}, bf16[128,768]{0,1:T(8,128)(2,1)}, u32[]{:S(2)}, u32[]{:S(2)}) collective-permute-start(bf16[128,768]{0,1:T(8,128)(2,1)} %get-tuple-element.307), channel_id=1, source_target_pairs={{0,2},{2,0},{4,6},{6,4},{1,3},{3,1},{5,7},{7,5},{8,10},{10,8},{12,... | collective-permute-start | bytes 589832 | tf_op jit(solution)/shard_map/ppermute | solution.py:26
  240.3 83.4 %collective-permute-start.35 = (bf16[2048,1536]{1,0:T(8,128)(2,1)}, bf16[2048,1536]{1,0:T(8,128)(2,1)}, u32[]{:S(2)}, u32[]{:S(2)}) collective-permute-start(bf16[2048,1536]{1,0:T(8,128)(2,1)} %all-gather.6.cloned.1.call-done), channel_id=1, source_target_pairs={{0,1},{1,0},{2,3},{3,2},{4,5},{5,4},{6,7},{7,6},{8,9},{9,8},{10,11... | collective-permute-start | bytes 18874376 | tf_op jit(solution)/shard_map/ppermute | solution.py:91
  260.8 15.2 %collective-permute-start.21 = (bf16[1,128,2048]{2,1,0:T(8,128)(2,1)}, bf16[1,128,2048]{2,1,0:T(8,128)(2,1)}, u32[]{:S(2)}, u32[]{:S(2)}) collective-permute-start(bf16[1,128,2048]{2,1,0:T(8,128)(2,1)} %get-tuple-element.247), channel_id=1, source_target_pairs={{0,4},{2,6},{4,0},{6,2},{1,5},{3,7},{5,1},{7,3},{8,12},{10,14},{12... | collective-permute-start | bytes 1572872 | tf_op jit(solution)/shard_map/ppermute | solution.py:26
  262.2 15.2 %collective-permute-start.23 = (bf16[1,128,2048]{2,1,0:T(8,128)(2,1)}, bf16[1,128,2048]{2,1,0:T(8,128)(2,1)}, u32[]{:S(2)}, u32[]{:S(2)}) collective-permute-start(bf16[1,128,2048]{2,1,0:T(8,128)(2,1)} %get-tuple-element.249), channel_id=1, source_target_pairs={{0,2},{2,0},{4,6},{6,4},{1,3},{3,1},{5,7},{7,5},{8,10},{10,8},{12,... | collective-permute-start | bytes 1572872 | tf_op jit(solution)/shard_map/ppermute | solution.py:26
  265.5 35.2 %collective-permute-start.42 = (bf16[2,128,2048]{2,1,0:T(8,128)(2,1)S(1)}, bf16[2,128,2048]{2,1,0:T(8,128)(2,1)S(1)}, u32[]{:S(2)}, u32[]{:S(2)}) collective-permute-start(bf16[2,128,2048]{2,1,0:T(8,128)(2,1)S(1)} %get-tuple-element.203), channel_id=1, source_target_pairs={{0,2},{2,0},{4,6},{6,4},{1,3},{3,1},{5,7},{7,5},{8,10},{10,8},{12,... | collective-permute-start | bytes 3145736 | tf_op jit(solution)/shard_map/ppermute | solution.py:26
  266.1 32.2 %collective-permute-start.43 = (bf16[2,128,2048]{2,1,0:T(8,128)(2,1)S(1)}, bf16[2,128,2048]{2,1,0:T(8,128)(2,1)S(1)}, u32[]{:S(2)}, u32[]{:S(2)}) collective-permute-start(bf16[2,128,2048]{2,1,0:T(8,128)(2,1)S(1)} %get-tuple-element.203), channel_id=1, source_target_pairs={{0,4},{2,6},{4,0},{6,2},{1,5},{3,7},{5,1},{7,3},{8,12},{10,14},{12... | collective-permute-start | bytes 3145736 | tf_op jit(solution)/shard_map/ppermute | solution.py:26
  279.2 41.6 %collective-permute-start.24 = (bf16[2,128,2048]{2,1,0:T(8,128)(2,1)S(1)}, bf16[2,128,2048]{2,1,0:T(8,128)(2,1)S(1)}, u32[]{:S(2)}, u32[]{:S(2)}) collective-permute-start(bf16[2,128,2048]{2,1,0:T(8,128)(2,1)S(1)} %pad_maximum_fusion.22), channel_id=1, source_target_pairs={{0,4},{2,6},{4,0},{6,2},{1,5},{3,7},{5,1},{7,3},{8,12},{10,14},{12... | collective-permute-start | bytes 3145736 | tf_op jit(solution)/shard_map/ppermute | solution.py:26
  279.9 42.4 %collective-permute-start.22 = (bf16[2,128,2048]{2,1,0:T(8,128)(2,1)S(1)}, bf16[2,128,2048]{2,1,0:T(8,128)(2,1)S(1)}, u32[]{:S(2)}, u32[]{:S(2)}) collective-permute-start(bf16[2,128,2048]{2,1,0:T(8,128)(2,1)S(1)} %pad_maximum_fusion.21), channel_id=1, source_target_pairs={{0,2},{2,0},{4,6},{6,4},{1,3},{3,1},{5,7},{7,5},{8,10},{10,8},{12,... | collective-permute-start | bytes 3145736 | tf_op jit(solution)/shard_map/ppermute | solution.py:26
  299.2 34.4 %collective-permute-start.45 = (bf16[1,128,2048]{2,1,0:T(8,128)(2,1)}, bf16[1,128,2048]{2,1,0:T(8,128)(2,1)}, u32[]{:S(2)}, u32[]{:S(2)}) collective-permute-start(bf16[1,128,2048]{2,1,0:T(8,128)(2,1)} %slice.641), channel_id=1, source_target_pairs={{0,2},{2,0},{4,6},{6,4},{1,3},{3,1},{5,7},{7,5},{8,10},{10,8},{12,... | collective-permute-start | bytes 1572872 | tf_op jit(solution)/shard_map/ppermute | solution.py:26
  301.5 32.1 %collective-permute-start.44 = (bf16[1,128,2048]{2,1,0:T(8,128)(2,1)}, bf16[1,128,2048]{2,1,0:T(8,128)(2,1)}, u32[]{:S(2)}, u32[]{:S(2)}) collective-permute-start(bf16[1,128,2048]{2,1,0:T(8,128)(2,1)} %slice.640), channel_id=1, source_target_pairs={{0,4},{2,6},{4,0},{6,2},{1,5},{3,7},{5,1},{7,3},{8,12},{10,14},{12... | collective-permute-start | bytes 1572872 | tf_op jit(solution)/shard_map/ppermute | solution.py:26
  323.8 343.7 %reduce-scatter.7.cloned.1.call-start = ((), (), s32[]{:S(2)}) async-start(), calls=%async_computation.7 | async-start | bytes 7864320 | tf_op jit(solution)/shard_map/reduce_scatter | solution.py:104
  324.7 29.9 %collective-permute-start.25 = (bf16[2,128,2048]{2,1,0:T(8,128)(2,1)S(1)}, bf16[2,128,2048]{2,1,0:T(8,128)(2,1)S(1)}, u32[]{:S(2)}, u32[]{:S(2)}) collective-permute-start(bf16[2,128,2048]{2,1,0:T(8,128)(2,1)S(1)} %get-tuple-element.209), channel_id=1, source_target_pairs={{0,2},{2,0},{4,6},{6,4},{1,3},{3,1},{5,7},{7,5},{8,10},{10,8},{12,... | collective-permute-start | bytes 3145736 | tf_op jit(solution)/shard_map/ppermute | solution.py:26
  326.2 26.8 %collective-permute-start.26 = (bf16[2,128,2048]{2,1,0:T(8,128)(2,1)S(1)}, bf16[2,128,2048]{2,1,0:T(8,128)(2,1)S(1)}, u32[]{:S(2)}, u32[]{:S(2)}) collective-permute-start(bf16[2,128,2048]{2,1,0:T(8,128)(2,1)S(1)} %get-tuple-element.209), channel_id=1, source_target_pairs={{0,4},{2,6},{4,0},{6,2},{1,5},{3,7},{5,1},{7,3},{8,12},{10,14},{12... | collective-permute-start | bytes 3145736 | tf_op jit(solution)/shard_map/ppermute | solution.py:26
  353.1 12.7 %collective-permute-start.28 = (bf16[1,128,2048]{2,1,0:T(8,128)(2,1)S(1)}, bf16[1,128,2048]{2,1,0:T(8,128)(2,1)S(1)}, u32[]{:S(2)}, u32[]{:S(2)}) collective-permute-start(bf16[1,128,2048]{2,1,0:T(8,128)(2,1)S(1)} %slice.635), channel_id=1, source_target_pairs={{0,2},{2,0},{4,6},{6,4},{1,3},{3,1},{5,7},{7,5},{8,10},{10,8},{12,... | collective-permute-start | bytes 1572872 | tf_op jit(solution)/shard_map/ppermute | solution.py:26
  354.7 12.4 %collective-permute-start.27 = (bf16[1,128,2048]{2,1,0:T(8,128)(2,1)S(1)}, bf16[1,128,2048]{2,1,0:T(8,128)(2,1)S(1)}, u32[]{:S(2)}, u32[]{:S(2)}) collective-permute-start(bf16[1,128,2048]{2,1,0:T(8,128)(2,1)S(1)} %slice.634), channel_id=1, source_target_pairs={{0,4},{2,6},{4,0},{6,2},{1,5},{3,7},{5,1},{7,3},{8,12},{10,14},{12... | collective-permute-start | bytes 1572872 | tf_op jit(solution)/shard_map/ppermute | solution.py:26
  386.4 21.1 %collective-permute-start.36 = (bf16[2048,768]{0,1:T(8,128)(2,1)}, bf16[2048,768]{0,1:T(8,128)(2,1)S(1)}, u32[]{:S(2)}, u32[]{:S(2)}) collective-permute-start(bf16[2048,768]{0,1:T(8,128)(2,1)} %all-gather.8.cloned.1.call-done), channel_id=1, source_target_pairs={{0,1},{1,0},{2,3},{3,2},{4,5},{5,4},{6,7},{7,6},{8,9},{9,8},{10,11... | collective-permute-start | bytes 9437192 | tf_op jit(solution)/shard_map/ppermute | solution.py:91
  439.6 14.6 %collective-permute-start.46 = (bf16[1,128,2048]{2,1,0:T(8,128)(2,1)S(1)}, bf16[1,128,2048]{2,1,0:T(8,128)(2,1)S(1)}, u32[]{:S(2)}, u32[]{:S(2)}) collective-permute-start(bf16[1,128,2048]{2,1,0:T(8,128)(2,1)S(1)} %get-tuple-element.235), channel_id=1, source_target_pairs={{0,4},{2,6},{4,0},{6,2},{1,5},{3,7},{5,1},{7,3},{8,12},{10,14},{12... | collective-permute-start | bytes 1572872 | tf_op jit(solution)/shard_map/ppermute | solution.py:26
  441.1 14.3 %collective-permute-start.48 = (bf16[1,128,2048]{2,1,0:T(8,128)(2,1)S(1)}, bf16[1,128,2048]{2,1,0:T(8,128)(2,1)S(1)}, u32[]{:S(2)}, u32[]{:S(2)}) collective-permute-start(bf16[1,128,2048]{2,1,0:T(8,128)(2,1)S(1)} %get-tuple-element.237), channel_id=1, source_target_pairs={{0,2},{2,0},{4,6},{6,4},{1,3},{3,1},{5,7},{7,5},{8,10},{10,8},{12,... | collective-permute-start | bytes 1572872 | tf_op jit(solution)/shard_map/ppermute | solution.py:26
  455.9 24.8 %collective-permute-start.49 = (bf16[2,128,2048]{2,1,0:T(8,128)(2,1)S(1)}, bf16[2,128,2048]{2,1,0:T(8,128)(2,1)S(1)}, u32[]{:S(2)}, u32[]{:S(2)}) collective-permute-start(bf16[2,128,2048]{2,1,0:T(8,128)(2,1)S(1)} %pad_maximum_fusion.26), channel_id=1, source_target_pairs={{0,4},{2,6},{4,0},{6,2},{1,5},{3,7},{5,1},{7,3},{8,12},{10,14},{12... | collective-permute-start | bytes 3145736 | tf_op jit(solution)/shard_map/ppermute | solution.py:26
  456.6 24.5 %collective-permute-start.47 = (bf16[2,128,2048]{2,1,0:T(8,128)(2,1)S(1)}, bf16[2,128,2048]{2,1,0:T(8,128)(2,1)S(1)}, u32[]{:S(2)}, u32[]{:S(2)}) collective-permute-start(bf16[2,128,2048]{2,1,0:T(8,128)(2,1)S(1)} %pad_maximum_fusion.25), channel_id=1, source_target_pairs={{0,2},{2,0},{4,6},{6,4},{1,3},{3,1},{5,7},{7,5},{8,10},{10,8},{12,... | collective-permute-start | bytes 3145736 | tf_op jit(solution)/shard_map/ppermute | solution.py:26
  488.1 25.4 %collective-permute-start.50 = (bf16[2,128,2048]{2,1,0:T(8,128)(2,1)S(1)}, bf16[2,128,2048]{2,1,0:T(8,128)(2,1)S(1)}, u32[]{:S(2)}, u32[]{:S(2)}) collective-permute-start(bf16[2,128,2048]{2,1,0:T(8,128)(2,1)S(1)} %get-tuple-element.200), channel_id=1, source_target_pairs={{0,2},{2,0},{4,6},{6,4},{1,3},{3,1},{5,7},{7,5},{8,10},{10,8},{12,... | collective-permute-start | bytes 3145736 | tf_op jit(solution)/shard_map/ppermute | solution.py:26
  489.6 23.2 %collective-permute-start.51 = (bf16[2,128,2048]{2,1,0:T(8,128)(2,1)S(1)}, bf16[2,128,2048]{2,1,0:T(8,128)(2,1)S(1)}, u32[]{:S(2)}, u32[]{:S(2)}) collective-permute-start(bf16[2,128,2048]{2,1,0:T(8,128)(2,1)S(1)} %get-tuple-element.200), channel_id=1, source_target_pairs={{0,4},{2,6},{4,0},{6,2},{1,5},{3,7},{5,1},{7,3},{8,12},{10,14},{12... | collective-permute-start | bytes 3145736 | tf_op jit(solution)/shard_map/ppermute | solution.py:26
  525.4 17.1 %collective-permute-start.54 = (bf16[2048,1536]{1,0:T(8,128)(2,1)}, bf16[2048,1536]{1,0:T(8,128)(2,1)}, u32[]{:S(2)}, u32[]{:S(2)}) collective-permute-start(bf16[2048,1536]{1,0:T(8,128)(2,1)} %convolution_convert_fusion.1), channel_id=1, source_target_pairs={{0,1},{1,0},{2,3},{3,2},{4,5},{5,4},{6,7},{7,6},{8,9},{9,8},{10,11... | collective-permute-start | bytes 18874376 | tf_op jit(solution)/shard_map/ppermute | solution.py:91
  525.4 14.5 %collective-permute-start.55 = (bf16[2048,768]{1,0:T(8,128)(2,1)}, bf16[2048,768]{1,0:T(8,128)(2,1)S(1)}, u32[]{:S(2)}, u32[]{:S(2)}) collective-permute-start(bf16[2048,768]{1,0:T(8,128)(2,1)} %convolution_convert_fusion.5), channel_id=1, source_target_pairs={{0,1},{1,0},{2,3},{3,2},{4,5},{5,4},{6,7},{7,6},{8,9},{9,8},{10,11... | collective-permute-start | bytes 9437192 | tf_op jit(solution)/shard_map/ppermute | solution.py:91
  551.5 197.2 %reduce-scatter.9.cloned.1.call-start = ((), (), s32[]{:S(2)}) async-start(), calls=%async_computation.8 | async-start | bytes 3932160 | tf_op jit(solution)/shard_map/reduce_scatter | solution.py:104
  564.5 14.2 %collective-permute-start.37 = (bf16[1,128,2048]{2,1,0:T(8,128)(2,1)S(1)}, bf16[1,128,2048]{2,1,0:T(8,128)(2,1)S(1)}, u32[]{:S(2)}, u32[]{:S(2)}) collective-permute-start(bf16[1,128,2048]{2,1,0:T(8,128)(2,1)S(1)} %get-tuple-element.241), channel_id=1, source_target_pairs={{0,4},{2,6},{4,0},{6,2},{1,5},{3,7},{5,1},{7,3},{8,12},{10,14},{12... | collective-permute-start | bytes 1572872 | tf_op jit(solution)/shard_map/ppermute | solution.py:26
  566.0 13.9 %collective-permute-start.39 = (bf16[1,128,2048]{2,1,0:T(8,128)(2,1)S(1)}, bf16[1,128,2048]{2,1,0:T(8,128)(2,1)S(1)}, u32[]{:S(2)}, u32[]{:S(2)}) collective-permute-start(bf16[1,128,2048]{2,1,0:T(8,128)(2,1)S(1)} %get-tuple-element.243), channel_id=1, source_target_pairs={{0,2},{2,0},{4,6},{6,4},{1,3},{3,1},{5,7},{7,5},{8,10},{10,8},{12,... | collective-permute-start | bytes 1572872 | tf_op jit(solution)/shard_map/ppermute | solution.py:26
  581.4 120.8 %collective-permute-start.40 = (bf16[2,128,2048]{2,1,0:T(8,128)(2,1)}, bf16[2,128,2048]{2,1,0:T(8,128)(2,1)}, u32[]{:S(2)}, u32[]{:S(2)}) collective-permute-start(bf16[2,128,2048]{2,1,0:T(8,128)(2,1)} %pad_maximum_fusion.24), channel_id=1, source_target_pairs={{0,4},{2,6},{4,0},{6,2},{1,5},{3,7},{5,1},{7,3},{8,12},{10,14},{12... | collective-permute-start | bytes 3145736 | tf_op jit(solution)/shard_map/ppermute | solution.py:26
  594.3 11.5 %collective-permute-start.58 = (f32[2,2,640]{2,0,1:T(2,128)S(1)}, f32[2,2,640]{2,0,1:T(2,128)S(1)}, u32[]{:S(2)}, u32[]{:S(2)}) collective-permute-start(f32[2,2,640]{2,0,1:T(2,128)S(1)} %pad_maximum_fusion.40), channel_id=1, source_target_pairs={{24,0},{25,1},{26,2},{27,3},{28,4},{29,5},{30,6},{31,7}} | collective-permute-start | bytes 30728 | tf_op jit(solution)/shard_map/ppermute | solution.py:150
  678.3 163.2 %reduce-scatter.13.cloned.1.call-start = ((), (), s32[]{:S(2)}) async-start(), calls=%async_computation.10 | async-start | bytes 307200
  695.8 48.1 %collective-permute-start.66 = (bf16[2048,960]{0,1:T(8,128)(2,1)}, bf16[2048,960]{0,1:T(8,128)(2,1)}, u32[]{:S(2)}, u32[]{:S(2)}) collective-permute-start(bf16[2048,960]{0,1:T(8,128)(2,1)} %pad_maximum_fusion.1), channel_id=1, source_target_pairs={{0,1},{1,0},{2,3},{3,2},{4,5},{5,4},{6,7},{7,6},{8,9},{9,8},{10,11... | collective-permute-start | bytes 11796488 | tf_op jit(solution)/shard_map/ppermute | solution.py:91
  696.9 25.9 %collective-permute-start.38 = (bf16[2,128,2048]{2,1,0:T(8,128)(2,1)}, bf16[2,128,2048]{2,1,0:T(8,128)(2,1)}, u32[]{:S(2)}, u32[]{:S(2)}) collective-permute-start(bf16[2,128,2048]{2,1,0:T(8,128)(2,1)} %pad_maximum_fusion.23), channel_id=1, source_target_pairs={{0,2},{2,0},{4,6},{6,4},{1,3},{3,1},{5,7},{7,5},{8,10},{10,8},{12,... | collective-permute-start | bytes 3145736 | tf_op jit(solution)/shard_map/ppermute | solution.py:26
  729.1 26.4 %collective-permute-start.41 = (bf16[2,128,2048]{2,1,0:T(8,128)(2,1)}, bf16[2,128,2048]{2,1,0:T(8,128)(2,1)}, u32[]{:S(2)}, u32[]{:S(2)}) collective-permute-start(bf16[2,128,2048]{2,1,0:T(8,128)(2,1)} %get-tuple-element.205), channel_id=1, source_target_pairs={{0,1},{1,0},{2,3},{3,2},{4,5},{5,4},{6,7},{7,6},{8,9},{9,8},{10,11... | collective-permute-start | bytes 3145736 | tf_op jit(solution)/shard_map/ppermute | solution.py:91
  749.6 94.9 %reduce-scatter.11.cloned.1.call-start = ((), (), s32[]{:S(2)}) async-start(), calls=%async_computation.9 | async-start | bytes 4915200 | tf_op jit(solution)/shard_map/reduce_scatter | solution.py:104
  752.5 16.3 %collective-permute-start.60 = (bf16[1,128,2048]{2,1,0:T(8,128)(2,1)}, bf16[1,128,2048]{2,1,0:T(8,128)(2,1)S(1)}, u32[]{:S(2)}, u32[]{:S(2)}) collective-permute-start(bf16[1,128,2048]{2,1,0:T(8,128)(2,1)} %get-tuple-element.229), channel_id=1, source_target_pairs={{0,4},{2,6},{4,0},{6,2},{1,5},{3,7},{5,1},{7,3},{8,12},{10,14},{12... | collective-permute-start | bytes 1572872 | tf_op jit(solution)/shard_map/ppermute | solution.py:26
  754.0 15.2 %collective-permute-start.62 = (bf16[1,128,2048]{2,1,0:T(8,128)(2,1)}, bf16[1,128,2048]{2,1,0:T(8,128)(2,1)}, u32[]{:S(2)}, u32[]{:S(2)}) collective-permute-start(bf16[1,128,2048]{2,1,0:T(8,128)(2,1)} %get-tuple-element.231), channel_id=1, source_target_pairs={{0,2},{2,0},{4,6},{6,4},{1,3},{3,1},{5,7},{7,5},{8,10},{10,8},{12,... | collective-permute-start | bytes 1572872 | tf_op jit(solution)/shard_map/ppermute | solution.py:26
  758.1 19.4 %collective-permute-start.77 = (bf16[128,1536]{1,0:T(8,128)(2,1)S(1)}, bf16[128,1536]{1,0:T(8,128)(2,1)S(1)}, u32[]{:S(2)}, u32[]{:S(2)}) collective-permute-start(bf16[128,1536]{1,0:T(8,128)(2,1)S(1)} %get-tuple-element.278), channel_id=1, source_target_pairs={{0,6},{2,4},{4,2},{6,0},{1,7},{3,5},{5,3},{7,1},{8,14},{10,12},{12... | collective-permute-start | bytes 1179656 | tf_op jit(solution)/shard_map/ppermute | solution.py:26
  758.7 25.7 %collective-permute-start.78 = (bf16[128,1536]{1,0:T(8,128)(2,1)S(1)}, bf16[128,1536]{1,0:T(8,128)(2,1)S(1)}, u32[]{:S(2)}, u32[]{:S(2)}) collective-permute-start(bf16[128,1536]{1,0:T(8,128)(2,1)S(1)} %get-tuple-element.277), channel_id=1, source_target_pairs={{0,4},{2,6},{4,0},{6,2},{1,5},{3,7},{5,1},{7,3},{8,12},{10,14},{12... | collective-permute-start | bytes 1179656 | tf_op jit(solution)/shard_map/ppermute | solution.py:26
  760.2 25.8 %collective-permute-start.79 = (bf16[128,1536]{1,0:T(8,128)(2,1)S(1)}, bf16[128,1536]{1,0:T(8,128)(2,1)S(1)}, u32[]{:S(2)}, u32[]{:S(2)}) collective-permute-start(bf16[128,1536]{1,0:T(8,128)(2,1)S(1)} %get-tuple-element.276), channel_id=1, source_target_pairs={{0,2},{2,0},{4,6},{6,4},{1,3},{3,1},{5,7},{7,5},{8,10},{10,8},{12,... | collective-permute-start | bytes 1179656 | tf_op jit(solution)/shard_map/ppermute | solution.py:26
  770.6 35.2 %collective-permute-start.63 = (bf16[2,128,2048]{2,1,0:T(8,128)(2,1)S(1)}, bf16[2,128,2048]{2,1,0:T(8,128)(2,1)S(1)}, u32[]{:S(2)}, u32[]{:S(2)}) collective-permute-start(bf16[2,128,2048]{2,1,0:T(8,128)(2,1)S(1)} %pad_maximum_fusion.28), channel_id=1, source_target_pairs={{0,4},{2,6},{4,0},{6,2},{1,5},{3,7},{5,1},{7,3},{8,12},{10,14},{12... | collective-permute-start | bytes 3145736 | tf_op jit(solution)/shard_map/ppermute | solution.py:26
  771.9 35.1 %collective-permute-start.61 = (bf16[2,128,2048]{2,1,0:T(8,128)(2,1)S(1)}, bf16[2,128,2048]{2,1,0:T(8,128)(2,1)S(1)}, u32[]{:S(2)}, u32[]{:S(2)}) collective-permute-start(bf16[2,128,2048]{2,1,0:T(8,128)(2,1)S(1)} %pad_maximum_fusion.27), channel_id=1, source_target_pairs={{0,2},{2,0},{4,6},{6,4},{1,3},{3,1},{5,7},{7,5},{8,10},{10,8},{12,... | collective-permute-start | bytes 3145736 | tf_op jit(solution)/shard_map/ppermute | solution.py:26
  813.5 19.3 %collective-permute-start.64 = (bf16[2,128,2048]{2,1,0:T(8,128)(2,1)}, bf16[2,128,2048]{2,1,0:T(8,128)(2,1)}, u32[]{:S(2)}, u32[]{:S(2)}) collective-permute-start(bf16[2,128,2048]{2,1,0:T(8,128)(2,1)} %get-tuple-element.196), channel_id=1, source_target_pairs={{0,1},{1,0},{2,3},{3,2},{4,5},{5,4},{6,7},{7,6},{8,9},{9,8},{10,11... | collective-permute-start | bytes 3145736 | tf_op jit(solution)/shard_map/ppermute | solution.py:91
  849.3 16.1 %collective-permute-start.74 = (bf16[128,960]{0,1:T(8,128)(2,1)S(1)}, bf16[128,960]{0,1:T(8,128)(2,1)S(1)}, u32[]{:S(2)}, u32[]{:S(2)}) collective-permute-start(bf16[128,960]{0,1:T(8,128)(2,1)S(1)} %bitcast.579), channel_id=1, source_target_pairs={{0,6},{2,4},{4,2},{6,0},{1,7},{3,5},{5,3},{7,1},{8,14},{10,12},{12... | collective-permute-start | bytes 737288 | tf_op jit(solution)/shard_map/ppermute | solution.py:26
  (184 other events, 2256.9 us)
Sparse Core Ops, SparseCore 0:
  27.5 76.8 all-gather.3
  106.6 126.9 all-gather.5
  323.9 62.4 all-gather.7
  551.7 110.1 reduce-scatter.6
  678.4 62.3 reduce-scatter.8
  749.8 19.2 reduce-scatter.12
  771.4 71.8 reduce-scatter.10

commit v4 on v3

--- a/solution.py
+++ b/solution.py
@@ -293,19 +293,37 @@
     tails = jnp.pad(norm_gains, ((0, 0), (0, small_width - gain_width)))
     small = jnp.concatenate([small, tails], axis=0)
 
+    small = z_gather(small)
     first_blocks = jnp.concatenate([to_chips(w_x), to_chips(w_g), to_chips(w_o.T)], axis=2)
+    first_blocks, small = lax.optimization_barrier((first_blocks, small))
     first_rows = jnp.concatenate(plane_swap(first_blocks), axis=0)
     first_rows, own_in, small = lax.optimization_barrier((first_rows, own_in, small))
+    gain_rows = jnp.broadcast_to(
+        small[:, small_rows:].reshape(1, 2 * z_size, small_width),
+        (PLANE, 2 * z_size, small_width),
+    )
+    small_blocks = small[:, :small_rows].reshape(PLANE, -1, small_width)
+    small = jnp.stack(plane_swap(jnp.concatenate([small_blocks, gain_rows], axis=1)))
     whole_in = plane_gather(own_in)
-    found = [small] + [to_partner(small, bit) for bit in (1, 2, 3)]
-    small = z_gather(jnp.stack(in_order(found, j_index)))
-    gains_all = jnp.moveaxis(small[:, :, small_rows:, :gain_width], 2, 0)
+    gains_all = small[:, part_width // PLANE :, :gain_width].reshape(PLANE, z_size, 2, gain_width)
+    gains_all = jnp.moveaxis(gains_all, (0, 1, 2), (2, 1, 0))
     gains_all = gains_all.reshape(2, model_width).astype(F32)
-    small = small[:, :, :small_rows].reshape(half_width, small_width)
-    small = lax.dynamic_slice_in_dim(small, j_index * part_width, part_width, 0)
+    small = small[:, : part_width // PLANE].reshape(PLANE, -1, small_rows, small_width)
+    small = jnp.moveaxis(small, 0, 1).reshape(part_width, small_width)
     small = jnp.concatenate([small, to_core(small)], axis=0)
     params_all = small[:, :8].astype(F32)
-    gates_all = small[:, 8:].reshape(heads_here, HEAD_DIM, 2 * HEAD_DIM)
+    head = jnp.arange(rec_width, dtype=jnp.int32) // HEAD_DIM
+    gates_all = jnp.concatenate(
+        [
+            jnp.where(
+                head[:, None] == head[None, :],
+                jnp.tile(small[:, start : start + HEAD_DIM], (1, heads_here)),
+                0.0,
+            ).astype(BF16)
+            for start in (8, 8 + HEAD_DIM)
+        ],
+        axis=1,
+    )
 
     w_first = along_z(first_rows)
     w_rec = jnp.concatenate(
@@ -313,13 +331,14 @@
     )
     w_back = jnp.concatenate([w[:, 2 * part_width :] for w in w_first], axis=1)
     later = (w_gate, w_up, w_down)
-    later, whole_in, small = lax.optimization_barrier((later, whole_in, small))
+    later, whole_in = lax.optimization_barrier((later, whole_in))
     wide_blocks = jnp.concatenate([to_chips(later[0]), to_chips(later[1])], axis=2)
     wide_rows = jnp.concatenate(plane_swap(wide_blocks), axis=0)
     narrow_rows = jnp.concatenate(plane_swap(to_chips(later[2].T)), axis=0)
     own_cot, narrow_rows = lax.optimization_barrier((own_cot, narrow_rows))
     w_wide = along_z(wide_rows)
-    narrow_rows, w_wide = lax.optimization_barrier((narrow_rows, w_wide))
+    narrow_rows, wide_own = lax.optimization_barrier((narrow_rows, w_wide[0]))
+    w_wide = (wide_own, w_wide[1])
     w_narrow = along_z(narrow_rows)
 
     def live_at(position):
@@ -382,10 +401,10 @@
         params_all[:, 4],
     )
     conv_flat = conv_value.reshape(tokens, rec_width)
-    conv_low = conv_flat.astype(BF16).reshape(tokens, heads_here, HEAD_DIM)
-    gate_mixed = jnp.einsum("nhk,hko->nho", conv_low, gates_all, preferred_element_type=F32)
-    pre_rate = gate_mixed[..., :HEAD_DIM].reshape(tokens, rec_width) + params_all[:, 5]
-    pre_entry = gate_mixed[..., HEAD_DIM:].reshape(tokens, rec_width) + params_all[:, 6]
+    conv_low = conv_flat.astype(BF16)
+    gate_mixed = dot(conv_low, gates_all, 1, 0)
+    pre_rate = gate_mixed[:, :rec_width] + params_all[:, 5]
+    pre_entry = gate_mixed[:, rec_width:] + params_all[:, 6]
     (retain, drive_term), gate_back = jax.vjp(
         gate_math, pre_rate, pre_entry, params_all[:, 7], conv_flat
     )
@@ -482,19 +501,25 @@
     )
     rate_low = d_rate.astype(BF16)
     entry_low = d_entry.astype(BF16)
-    grad_gates = jnp.concatenate(
+    grad_gates = jnp.concatenate([rate_low, entry_low], axis=1)
+    g_gates = dot(conv_low, grad_gates, 0, 0)
+    g_gates = jnp.concatenate(
         [
-            rate_low.reshape(tokens, heads_here, HEAD_DIM),
-            entry_low.reshape(tokens, heads_here, HEAD_DIM),
+            jnp.concatenate(
+                [
+                    g_gates[
+                        h * HEAD_DIM : (h + 1) * HEAD_DIM,
+                        start + h * HEAD_DIM : start + (h + 1) * HEAD_DIM,
+                    ]
+                    for start in (0, rec_width)
+                ],
+                axis=1,
+            )
+            for h in range(heads_here)
         ],
-        axis=2,
-    )
-    g_gates = jnp.einsum(
-        "nhk,nho->hko", conv_low, grad_gates, preferred_element_type=F32
-    ).reshape(rec_width, 2 * HEAD_DIM)
-    d_conv_gates = jnp.einsum(
-        "nho,hko->nhk", grad_gates, gates_all, preferred_element_type=F32
-    ).reshape(tokens, rec_width)
+        axis=0,
+    )
+    d_conv_gates = dot(grad_gates, gates_all, 1, 1)
     d_conv = (d_conv_direct + d_conv_gates).reshape(n_streams, n_rows, rec_width)
     d_conv, sum_wide, sum_narrow = lax.optimization_barrier((d_conv, sum_wide, sum_narrow))
     sum_narrow = sum_along_z(sum_narrow)

time: 886 us -> 822 us (0.928)
  local copies, waits for them, and re-layouts: 133 us -> 99 us
  starting transfers between devices: 121 us -> 101 us
  other arithmetic: 117 us -> 107 us
    ppermute x53, waiting for transfers between devices: 250 us -> 199 us  [to_partner(): return lax.ppermute(block, 'j', [(i, i ^ bit) for i in range(PLANE)])]
    all_gather x3, waiting for transfers between devices: 13.1 us -> 53.9 us  [along_z(): own = lax.all_gather(block, 'z', axis=0, tiled=True)]
    reduce_scatter x3 -> x4, waiting for transfers between devices: 0.02 us -> 40.7 us  [sum_along_z(): return lax.psum_scatter(total, 'z', scatter_dimension=0, tiled=True)]
    ppermute x6, waiting for transfers between devices: 33.3 us -> 0.02 us  [z_gather(): lax.ppermute(block, 'z', [(i, (i + step) % size) for i in range(size)])]
    reshape x8 -> x0, local copies, waits for them, and re-layouts: 31.9 us -> none  [the longest x2 10.8 us: shards(): gate_mixed[..., :HEAD_DIM].reshape(tokens, rec_width) + params_all[:, 5]]
    ppermute x8, starting transfers between devices: 33.3 us -> 16.2 us  [shifted(): lax.ppermute(block, 'z', [(i - distance, i) for i in range(size) if 0 <=...]
    mul x3 -> x0, local copies, waits for them, and re-layouts: 12.4 us -> none  [the longest x2 7.2 us: gate_math(): return (retain, factor * entry_gate * conv_value)]
    unnamed x332 -> x315, local copies, waits for them, and re-layouts: 28.7 us -> 36.6 us
  transfers between devices with their start and end apart: 90 -> 90, of which waited for: 52 -> 44; matrix products, arithmetic and copies ran while one was open for 37% -> 36% of each run, Pallas kernels for 2% -> 2%
where the time goes in v4:
time: 822 us; the launch traced here: 811 us
  waiting for transfers between devices  315 us (38%)
  matrix products  154 us (19%)
  other arithmetic  107 us (13%)
  starting transfers between devices  101 us (12%)
  local copies, waits for them, and re-layouts  99 us (12%)
  between operations  17.5 us (2%)
  Pallas kernels  16.9 us (2%)
    ppermute x53, waiting for transfers between devices, to_partner(): return lax.ppermute(block, 'j', [(i, i ^ bit) for i in range(PLANE)])  199 us
    dot_general x21, matrix products, dot(): lax.dot_general(left, right, (((left_dim,), (right_dim,)), ((), ())), pre...  146 us
    ppermute x53, starting transfers between devices, to_partner(): return lax.ppermute(block, 'j', [(i, i ^ bit) for i in range(PLANE)])  65.6 us
    all_gather x3, waiting for transfers between devices, along_z(): own = lax.all_gather(block, 'z', axis=0, tiled=True)  53.9 us
    reduce_scatter x4, waiting for transfers between devices, sum_along_z(): return lax.psum_scatter(total, 'z', scatter_dimension=0, tiled=True)  40.7 us
    unnamed x315, local copies, waits for them, and re-layouts  36.6 us
    convert_element_type x4, other arithmetic, both_cores(): return (own.astype(F32) + to_core(other).astype(F32)).astype(BF16)  17.6 us
    pallas_call x2, Pallas kernels, local_scan(): pl.pallas_call(partial(scan_kernel, backward), grid=(width // 128,), in_s...  16.9 us
  transfers between devices with their start and end apart: 90, of which 44 were waited for; matrix products, arithmetic and copies ran while one was open for 36% of the time, Pallas kernels for 2%

profile of v4, /device:TPU:0, one launch (start us, length us, event | category | flops | bytes accessed | tf_op | source)
XLA Modules:
  0.0 810.7 jit_solution(6191514561495758478)
XLA Ops:
  9.0 3.1 collective-permute-start
  25.0 4.6 collective-permute-done.3
  29.6 3.7 collective-permute-done.4
  59.3 16.7 %collective-permute-done.11 = bf16[2,128,2048]{2,1,0:T(8,128)(2,1)} collective-permute-done((bf16[2,128,2048]{2,1,0:T(8,128)(2,1)S(1)}, bf16[2,128,2048]{2,1,0:T(8,128)(2,1)}, u32[]{:S(2)}, u32[]{:S(2)}) %collective-permute-start.11) | collective-permute-done | bytes 1048608 | tf_op jit(solution)/shard_map/ppermute | solution.py:26
  81.8 28.3 %all-gather.4.cloned.1.call-done = bf16[2048,960]{0,1:T(8,128)(2,1)} async-done(((bf16[512,960]{0,1:T(8,128)(2,1)}), bf16[2048,960]{0,1:T(8,128)(2,1)}) %all-gather.4.cloned.1.call-update) | async-done | bytes 3932176 | tf_op jit(solution)/shard_map/all_gather | solution.py:95
  114.7 3.2 multiply_reduce_fusion
  121.7 3.3 fusion.1
  126.0 12.2 %collective-permute-done.33 = bf16[128,1536]{1,0:T(8,128)(2,1)S(1)} collective-permute-done((bf16[128,1536]{1,0:T(8,128)(2,1)S(1)}, bf16[128,1536]{1,0:T(8,128)(2,1)S(1)}, u32[]{:S(2)}, u32[]{:S(2)}) %collective-permute-start.33) | collective-permute-done | bytes 393248 | tf_op jit(solution)/shard_map/ppermute | solution.py:26
  147.9 6.9 fusion.74
  164.2 3.6 multiply_add_fusion.2
  172.8 3.1 bitcast_multiply_fusion.6
  176.7 7.8 shard_map.246
  188.7 5.5 collective-permute-start.20
  205.8 3.6 convolution_convert_fusion.4
  218.6 9.3 %collective-permute-done.21 = bf16[1,128,2048]{2,1,0:T(8,128)(2,1)} collective-permute-done((bf16[1,128,2048]{2,1,0:T(8,128)(2,1)}, bf16[1,128,2048]{2,1,0:T(8,128)(2,1)}, u32[]{:S(2)}, u32[]{:S(2)}) %collective-permute-start.21) | collective-permute-done | bytes 524320 | tf_op jit(solution)/shard_map/ppermute | solution.py:26
  234.3 15.9 %collective-permute-done.43 = bf16[2,128,2048]{2,1,0:T(8,128)(2,1)S(1)} collective-permute-done((bf16[2,128,2048]{2,1,0:T(8,128)(2,1)S(1)}, bf16[2,128,2048]{2,1,0:T(8,128)(2,1)S(1)}, u32[]{:S(2)}, u32[]{:S(2)}) %collective-permute-start.43) | collective-permute-done | bytes 1048608 | tf_op jit(solution)/shard_map/ppermute | solution.py:26
  255.0 19.4 %all-gather.6.cloned.1.call-done = bf16[2048,1536]{1,0:T(8,128)(2,1)} async-done(((bf16[512,1536]{1,0:T(8,128)(2,1)}), bf16[2048,1536]{1,0:T(8,128)(2,1)}) %all-gather.6.cloned.1.call-update) | async-done | bytes 6291472 | tf_op jit(solution)/shard_map/all_gather | solution.py:95
  275.4 3.3 multiply_reduce_fusion.8
  284.3 21.6 %collective-permute-done.26 = bf16[2,128,2048]{2,1,0:T(8,128)(2,1)S(1)} collective-permute-done((bf16[2,128,2048]{2,1,0:T(8,128)(2,1)S(1)}, bf16[2,128,2048]{2,1,0:T(8,128)(2,1)S(1)}, u32[]{:S(2)}, u32[]{:S(2)}) %collective-permute-start.26) | collective-permute-done | bytes 1048608 | tf_op jit(solution)/shard_map/ppermute | solution.py:26
  308.5 10.4 %collective-permute-done.28 = bf16[1,128,2048]{2,1,0:T(8,128)(2,1)S(1)} collective-permute-done((bf16[1,128,2048]{2,1,0:T(8,128)(2,1)S(1)}, bf16[1,128,2048]{2,1,0:T(8,128)(2,1)S(1)}, u32[]{:S(2)}, u32[]{:S(2)}) %collective-permute-start.28) | collective-permute-done | bytes 524320 | tf_op jit(solution)/shard_map/ppermute | solution.py:26
  321.4 10.7 %fusion.187 = f32[1024,1536]{1,0:T(8,128)} fusion(bf16[1024,2048]{1,0:T(8,128)(2,1)S(1)} %bitcast.589, bf16[2048,1536]{1,0:T(8,128)(2,1)} %all-gather.6.cloned.1.call-done), kind=kOutput, calls=%fused_computation.547 | convolution fusion | flops 6442450944 | bytes 16777216 | tf_op jit(solution)/shard_map/dot_general | solution.py:20
  332.1 6.3 all-gather.8.cloned.1.call-done
  338.4 11.5 %fusion.8 = (bf16[1024,768]{1,0:T(8,128)(2,1)S(1)}, bf16[1024,768]{1,0:T(8,128)(2,1)S(1)}, bf16[1024,768]{1,0:T(8,128)(2,1)}) fusion(f32[1024,1536]{1,0:T(8,128)} %fusion.187, bf16[1024,2048]{1,0:T(8,128)(2,1)} %bitcast.585, bf16[2048,768]{0,1:T(8,128)(2,1)} %all-gather.8.cloned.1.call-done), kind=kOutput, calls=%fused_computation.42 | convolution fusion | flops 3241672704 | bytes 18350080 | tf_op jit(solution)/shard_map/dot_general | solution.py:20
  351.6 11.0 %fusion.57 = f32[1024,2048]{1,0:T(8,128)} fusion(bf16[2048,1536]{1,0:T(8,128)(2,1)} %all-gather.6.cloned.1.call-done, bf16[1024,768]{1,0:T(8,128)(2,1)S(1)} %get-tuple-element.206, bf16[1024,768]{1,0:T(8,128)(2,1)S(1)} %get-tuple-element.205), kind=kOutput, calls=%fused_computation.154 | convolution fusion | flops 6448742400 | bytes 17825792 | tf_op jit(solution)/shard_map/dot_general | solution.py:20
  362.6 8.9 %fusion.189 = f32[1024,1536]{1,0:T(8,128)S(1)} fusion(bf16[1024,2048]{1,0:T(8,128)(2,1)S(1)} %bitcast.590, bf16[2048,1536]{1,0:T(8,128)(2,1)} %collective-permute-done.35), kind=kOutput, calls=%fused_computation.549 | convolution fusion | flops 6442450944 | bytes 16777216 | tf_op jit(solution)/shard_map/dot_general | solution.py:20
  371.5 7.4 fusion.15
  379.0 11.0 %add_convert_fusion.1 = bf16[1024,2048]{1,0:T(8,128)(2,1)S(1)} fusion(f32[1024,2048]{1,0:T(8,128)} %fusion.57, bf16[2048,1536]{1,0:T(8,128)(2,1)} %collective-permute-done.35, bf16[1024,768]{1,0:T(8,128)(2,1)} %get-tuple-element.204, bf16[1024,768]{1,0:T(8,128)(2,1)} %get-tuple-element.203), kind=kOutput, calls=%fused_computation.4 | convolution fusion | flops 6452936704 | bytes 22020096 | tf_op jit(solution)/shard_map/dot_general | solution.py:20
  393.2 11.4 %collective-permute-done.46 = bf16[1,128,2048]{2,1,0:T(8,128)(2,1)S(1)} collective-permute-done((bf16[1,128,2048]{2,1,0:T(8,128)(2,1)S(1)}, bf16[1,128,2048]{2,1,0:T(8,128)(2,1)S(1)}, u32[]{:S(2)}, u32[]{:S(2)}) %collective-permute-start.46) | collective-permute-done | bytes 524320 | tf_op jit(solution)/shard_map/ppermute | solution.py:26
  408.6 9.4 %convolution_convert_fusion.2 = bf16[2048,1536]{1,0:T(8,128)(2,1)} fusion(bf16[1024,2048]{1,0:T(8,128)(2,1)S(1)} %bitcast.591, bf16[1024,768]{1,0:T(8,128)(2,1)S(1)} %copy-done.141, bf16[1024,768]{1,0:T(8,128)(2,1)S(1)} %copy-done.139), kind=kOutput, calls=%fused_computation.10 | convolution fusion | flops 6451888128 | bytes 13631488 | tf_op jit(solution)/shard_map/dot_general | solution.py:20
  418.0 4.2 convolution_convert_fusion.6
  422.2 8.7 %collective-permute-done.49 = bf16[2,128,2048]{2,1,0:T(8,128)(2,1)S(1)} collective-permute-done((bf16[2,128,2048]{2,1,0:T(8,128)(2,1)S(1)}, bf16[2,128,2048]{2,1,0:T(8,128)(2,1)S(1)}, u32[]{:S(2)}, u32[]{:S(2)}) %collective-permute-start.49) | collective-permute-done | bytes 1048608 | tf_op jit(solution)/shard_map/ppermute | solution.py:26
  439.5 9.4 %convolution_convert_fusion.1 = bf16[2048,1536]{1,0:T(8,128)(2,1)} fusion(bf16[1024,2048]{1,0:T(8,128)(2,1)S(1)} %bitcast.592, bf16[1024,768]{1,0:T(8,128)(2,1)S(1)} %copy-done.143, bf16[1024,768]{1,0:T(8,128)(2,1)S(1)} %copy-done.142), kind=kOutput, calls=%fused_computation.9 | convolution fusion | flops 6451888128 | bytes 13631488 | tf_op jit(solution)/shard_map/dot_general | solution.py:20
  448.9 4.0 convolution_convert_fusion.5
  452.9 8.2 %collective-permute-done.51 = bf16[2,128,2048]{2,1,0:T(8,128)(2,1)S(1)} collective-permute-done((bf16[2,128,2048]{2,1,0:T(8,128)(2,1)S(1)}, bf16[2,128,2048]{2,1,0:T(8,128)(2,1)S(1)}, u32[]{:S(2)}, u32[]{:S(2)}) %collective-permute-start.51) | collective-permute-done | bytes 1048608 | tf_op jit(solution)/shard_map/ppermute | solution.py:26
  463.5 8.6 %collective-permute-done.53 = bf16[1,128,2048]{2,1,0:T(8,128)(2,1)S(1)} collective-permute-done((bf16[1,128,2048]{2,1,0:T(8,128)(2,1)S(1)}, bf16[1,128,2048]{2,1,0:T(8,128)(2,1)S(1)}, u32[]{:S(2)}, u32[]{:S(2)}) %collective-permute-start.53) | collective-permute-done | bytes 524320 | tf_op jit(solution)/shard_map/ppermute | solution.py:26
  473.2 4.9 fusion.59
  478.1 8.9 %collective-permute-done.55 = bf16[2048,768]{1,0:T(8,128)(2,1)S(1)} collective-permute-done((bf16[2048,768]{1,0:T(8,128)(2,1)S(1)}, bf16[2048,768]{1,0:T(8,128)(2,1)S(1)}, u32[]{:S(2)}, u32[]{:S(2)}) %collective-permute-start.55) | collective-permute-done | bytes 3145760 | tf_op jit(solution)/shard_map/ppermute | solution.py:91
  489.6 9.0 %add_convert_fusion = bf16[2048,1536]{1,0:T(8,128)(2,1)} fusion(bf16[2048,1536]{1,0:T(8,128)(2,1)} %collective-permute-done.54, bf16[2048,1536]{1,0:T(8,128)(2,1)} %convolution_convert_fusion.2), kind=kLoop, calls=%fused_computation | loop fusion | flops 12582912 | bytes 18874368 | tf_op jit(solution)/shard_map/convert_element_type | solution.py:100
  502.9 3.4 fusion.188
  506.4 5.3 add_convert_fusion.2
  514.9 11.3 %collective-permute-done.37 = bf16[1,128,2048]{2,1,0:T(8,128)(2,1)S(1)} collective-permute-done((bf16[1,128,2048]{2,1,0:T(8,128)(2,1)S(1)}, bf16[1,128,2048]{2,1,0:T(8,128)(2,1)S(1)}, u32[]{:S(2)}, u32[]{:S(2)}) %collective-permute-start.37) | collective-permute-done | bytes 524320 | tf_op jit(solution)/shard_map/ppermute | solution.py:26
  532.1 3.1 fusion.73
  535.2 9.1 %shard_map.247 = (f32[2,512,640]{2,1,0:T(8,128)S(1)}, f32[2,512,640]{2,1,0:T(8,128)S(1)}) custom-call(f32[2,512,640]{2,1,0:T(8,128)S(1)} %concatenate.183.keep_ref, f32[2,512,640]{2,1,0:T(8,128)S(1)} %bitcast.555), custom_call_target="tpu_custom_call" | custom-call | flops 5242880 | bytes 10485760 | tf_op jit(solution)/shard_map/pallas_call | solution.py:204
  545.7 4.3 convolution_convert_fusion.8
  552.6 3.4 collective-permute-done.56
  561.5 4.4 multiply_reduce_fusion.1
  565.9 4.0 fusion.164
  571.5 5.6 fusion.39
  577.1 31.7 %reduce-scatter.5.cloned.1.call-done = bf16[512,1536]{1,0:T(8,128)(2,1)} async-done(((bf16[2048,1536]{1,0:T(8,128)(2,1)}), bf16[512,1536]{1,0:T(8,128)(2,1)}) %reduce-scatter.5.cloned.1.call-update) | async-done | bytes 1572880 | tf_op jit(solution)/shard_map/reduce_scatter | solution.py:104
  608.9 5.4 fusion.160
  624.2 8.4 %convolution_convert_fusion = bf16[2048,1280]{0,1:T(8,128)(2,1)S(1)} fusion(bf16[1024,2048]{1,0:T(8,128)(2,1)} %copy-done.27, bf16[1024,640]{1,0:T(8,128)(2,1)S(1)} %copy-done.64, bf16[1024,640]{1,0:T(8,128)(2,1)S(1)} %bitcast.599), kind=kOutput, calls=%fused_computation.8 | convolution fusion | flops 5376573440 | bytes 12058624 | tf_op jit(solution)/shard_map/dot_general | solution.py:20
  643.6 3.7 constant_dynamic-update-slice_fusion.3
  652.7 4.0 convolution_convert_fusion.7
  661.3 9.8 %convolution_convert_fusion.3 = bf16[1024,2048]{1,0:T(8,128)(2,1)} fusion(bf16[1024,640]{1,0:T(8,128)(2,1)} %get-tuple-element.208, bf16[1024,640]{1,0:T(8,128)(2,1)} %bitcast.600, bf16[2048,320]{0,1:T(8,128)(2,1)} %copy-done.59, bf16[2048,320]{0,1:T(8,128)(2,1)} %copy-done.57, bf16[2048,320]{0,1:T(8,128)(2,1)} %get-tuple-element.248, ...), kind=kOutput, calls=%fused_computation.26 | convolution fusion | flops 5397020672 | bytes 12058624 | tf_op jit(solution)/shard_map/dot_general | solution.py:20
  671.9 5.2 add_convert_fusion.3
  677.1 5.5 reduce-scatter.7.cloned.1.call-done
  695.6 11.8 %collective-permute-done.60 = bf16[1,128,2048]{2,1,0:T(8,128)(2,1)} collective-permute-done((bf16[1,128,2048]{2,1,0:T(8,128)(2,1)}, bf16[1,128,2048]{2,1,0:T(8,128)(2,1)}, u32[]{:S(2)}, u32[]{:S(2)}) %collective-permute-start.60) | collective-permute-done | bytes 524320 | tf_op jit(solution)/shard_map/ppermute | solution.py:26
  712.3 5.1 collective-permute-done.78
  720.2 18.3 %collective-permute-done.63 = bf16[2,128,2048]{2,1,0:T(8,128)(2,1)S(1)} collective-permute-done((bf16[2,128,2048]{2,1,0:T(8,128)(2,1)S(1)}, bf16[2,128,2048]{2,1,0:T(8,128)(2,1)S(1)}, u32[]{:S(2)}, u32[]{:S(2)}) %collective-permute-start.63) | collective-permute-done | bytes 1048608 | tf_op jit(solution)/shard_map/ppermute | solution.py:26
  765.4 3.3 collective-permute-done.80
  776.0 3.4 reduce-scatter.11.cloned.1.call-done
  784.2 5.6 collective-permute-start.74
  793.5 3.2 collective-permute-done.74
  796.7 3.3 collective-permute-done.75
  (714 shorter events, 272.4 us)
Async XLA Ops:
  7.2 102.8 %all-gather.4.cloned.1.call-start = ((), (), s32[]{:S(2)}) async-start(), calls=%async_computation.4 | async-start | bytes 4915200 | tf_op jit(solution)/shard_map/all_gather | solution.py:95
  9.0 10.5 %collective-permute-start = (bf16[82,328]{1,0:T(8,128)(2,1)S(1)}, bf16[82,328]{1,0:T(8,128)(2,1)S(1)}, u32[]{:S(2)}, u32[]{:S(2)}) collective-permute-start(bf16[82,328]{1,0:T(8,128)(2,1)S(1)} %get-tuple-element.202), channel_id=1, source_target_pairs={{0,8},{8,16},{16,24},{24,0},{1,9},{9,17},{17,25},{25,1},{2,10},{10... | collective-permute-start | bytes 161384 | tf_op jit(solution)/shard_map/ppermute | solution.py:116
  19.7 9.9 %collective-permute-start.3 = (bf16[128,960]{0,1:T(8,128)(2,1)S(1)}, bf16[128,960]{0,1:T(8,128)(2,1)S(1)}, u32[]{:S(2)}, u32[]{:S(2)}) collective-permute-start(bf16[128,960]{0,1:T(8,128)(2,1)S(1)} %get-tuple-element.297), channel_id=1, source_target_pairs={{0,6},{2,4},{4,2},{6,0},{1,7},{3,5},{5,3},{7,1},{8,14},{10,12},{12... | collective-permute-start | bytes 737288 | tf_op jit(solution)/shard_map/ppermute | solution.py:26
  22.3 11.1 %collective-permute-start.4 = (bf16[128,960]{0,1:T(8,128)(2,1)S(1)}, bf16[128,960]{0,1:T(8,128)(2,1)S(1)}, u32[]{:S(2)}, u32[]{:S(2)}) collective-permute-start(bf16[128,960]{0,1:T(8,128)(2,1)S(1)} %get-tuple-element.296), channel_id=1, source_target_pairs={{0,4},{2,6},{4,0},{6,2},{1,5},{3,7},{5,1},{7,3},{8,12},{10,14},{12... | collective-permute-start | bytes 737288 | tf_op jit(solution)/shard_map/ppermute | solution.py:26
  22.8 10.6 %collective-permute-start.5 = (bf16[128,960]{0,1:T(8,128)(2,1)S(1)}, bf16[128,960]{0,1:T(8,128)(2,1)S(1)}, u32[]{:S(2)}, u32[]{:S(2)}) collective-permute-start(bf16[128,960]{0,1:T(8,128)(2,1)S(1)} %get-tuple-element.295), channel_id=1, source_target_pairs={{0,2},{2,0},{4,6},{6,4},{1,3},{3,1},{5,7},{7,5},{8,10},{10,8},{12,... | collective-permute-start | bytes 737288 | tf_op jit(solution)/shard_map/ppermute | solution.py:26
  34.5 239.8 %all-gather.6.cloned.1.call-start = ((), (), s32[]{:S(2)}) async-start(), calls=%async_computation.5 | async-start | bytes 7864320 | tf_op jit(solution)/shard_map/all_gather | solution.py:95
  36.0 124.5 %collective-permute-start.16 = (bf16[2,2,3,320]{3,2,1,0:T(4,128)(2,1)}, bf16[2,2,3,320]{3,2,1,0:T(4,128)(2,1)}, u32[]{:S(2)}, u32[]{:S(2)}) collective-permute-start(bf16[2,2,3,320]{3,2,1,0:T(4,128)(2,1)} %copy.442), channel_id=1, source_target_pairs={{0,1},{1,0},{2,3},{3,2},{4,5},{5,4},{6,7},{7,6},{8,9},{9,8},{10,11... | collective-permute-start | bytes 23048 | tf_op jit(solution)/shard_map/ppermute | solution.py:91
  47.3 31.6 %collective-permute-start.10 = (bf16[2,128,2048]{2,1,0:T(8,128)(2,1)S(1)}, bf16[2,128,2048]{2,1,0:T(8,128)(2,1)S(1)}, u32[]{:S(2)}, u32[]{:S(2)}) collective-permute-start(bf16[2,128,2048]{2,1,0:T(8,128)(2,1)S(1)} %get-tuple-element.46), channel_id=1, source_target_pairs={{0,2},{2,0},{4,6},{6,4},{1,3},{3,1},{5,7},{7,5},{8,10},{10,8},{12,... | collective-permute-start | bytes 3145736 | tf_op jit(solution)/shard_map/ppermute | solution.py:26
  51.9 24.1 %collective-permute-start.11 = (bf16[2,128,2048]{2,1,0:T(8,128)(2,1)S(1)}, bf16[2,128,2048]{2,1,0:T(8,128)(2,1)}, u32[]{:S(2)}, u32[]{:S(2)}) collective-permute-start(bf16[2,128,2048]{2,1,0:T(8,128)(2,1)S(1)} %get-tuple-element.46), channel_id=1, source_target_pairs={{0,4},{2,6},{4,0},{6,2},{1,5},{3,7},{5,1},{7,3},{8,12},{10,14},{12... | collective-permute-start | bytes 3145736 | tf_op jit(solution)/shard_map/ppermute | solution.py:26
  77.9 34.5 %collective-permute-start.13 = (bf16[1,128,2048]{2,1,0:T(8,128)(2,1)}, bf16[1,128,2048]{2,1,0:T(8,128)(2,1)}, u32[]{:S(2)}, u32[]{:S(2)}) collective-permute-start(bf16[1,128,2048]{2,1,0:T(8,128)(2,1)} %slice.647), channel_id=1, source_target_pairs={{0,2},{2,0},{4,6},{6,4},{1,3},{3,1},{5,7},{7,5},{8,10},{10,8},{12,... | collective-permute-start | bytes 1572872 | tf_op jit(solution)/shard_map/ppermute | solution.py:26
  79.7 32.7 %collective-permute-start.12 = (bf16[1,128,2048]{2,1,0:T(8,128)(2,1)}, bf16[1,128,2048]{2,1,0:T(8,128)(2,1)}, u32[]{:S(2)}, u32[]{:S(2)}) collective-permute-start(bf16[1,128,2048]{2,1,0:T(8,128)(2,1)} %slice.646), channel_id=1, source_target_pairs={{0,4},{2,6},{4,0},{6,2},{1,5},{3,7},{5,1},{7,3},{8,12},{10,14},{12... | collective-permute-start | bytes 1572872 | tf_op jit(solution)/shard_map/ppermute | solution.py:26
  110.0 34.7 %collective-permute-start.14 = (bf16[2048,960]{0,1:T(8,128)(2,1)}, bf16[2048,960]{0,1:T(8,128)(2,1)S(1)}, u32[]{:S(2)}, u32[]{:S(2)}) collective-permute-start(bf16[2048,960]{0,1:T(8,128)(2,1)} %all-gather.4.cloned.1.call-done), channel_id=1, source_target_pairs={{0,1},{1,0},{2,3},{3,2},{4,5},{5,4},{6,7},{7,6},{8,9},{9,8},{10,11... | collective-permute-start | bytes 11796488 | tf_op jit(solution)/shard_map/ppermute | solution.py:91
  118.2 20.0 %collective-permute-start.33 = (bf16[128,1536]{1,0:T(8,128)(2,1)S(1)}, bf16[128,1536]{1,0:T(8,128)(2,1)S(1)}, u32[]{:S(2)}, u32[]{:S(2)}) collective-permute-start(bf16[128,1536]{1,0:T(8,128)(2,1)S(1)} %get-tuple-element.283), channel_id=1, source_target_pairs={{0,4},{2,6},{4,0},{6,2},{1,5},{3,7},{5,1},{7,3},{8,12},{10,14},{12... | collective-permute-start | bytes 1179656 | tf_op jit(solution)/shard_map/ppermute | solution.py:26
  119.7 20.9 %collective-permute-start.32 = (bf16[128,1536]{1,0:T(8,128)(2,1)S(1)}, bf16[128,1536]{1,0:T(8,128)(2,1)S(1)}, u32[]{:S(2)}, u32[]{:S(2)}) collective-permute-start(bf16[128,1536]{1,0:T(8,128)(2,1)S(1)} %get-tuple-element.282), channel_id=1, source_target_pairs={{0,6},{2,4},{4,2},{6,0},{1,7},{3,5},{5,3},{7,1},{8,14},{10,12},{12... | collective-permute-start | bytes 1179656 | tf_op jit(solution)/shard_map/ppermute | solution.py:26
  121.2 20.0 %collective-permute-start.34 = (bf16[128,1536]{1,0:T(8,128)(2,1)S(1)}, bf16[128,1536]{1,0:T(8,128)(2,1)S(1)}, u32[]{:S(2)}, u32[]{:S(2)}) collective-permute-start(bf16[128,1536]{1,0:T(8,128)(2,1)S(1)} %get-tuple-element.281), channel_id=1, source_target_pairs={{0,2},{2,0},{4,6},{6,4},{1,3},{3,1},{5,7},{7,5},{8,10},{10,8},{12,... | collective-permute-start | bytes 1179656 | tf_op jit(solution)/shard_map/ppermute | solution.py:26
  138.2 56.0 %collective-permute-start.29 = (bf16[128,768]{0,1:T(8,128)(2,1)}, bf16[128,768]{0,1:T(8,128)(2,1)}, u32[]{:S(2)}, u32[]{:S(2)}) collective-permute-start(bf16[128,768]{0,1:T(8,128)(2,1)} %get-tuple-element.308), channel_id=1, source_target_pairs={{0,6},{2,4},{4,2},{6,0},{1,7},{3,5},{5,3},{7,1},{8,14},{10,12},{12... | collective-permute-start | bytes 589832 | tf_op jit(solution)/shard_map/ppermute | solution.py:26
  140.6 53.6 %collective-permute-start.30 = (bf16[128,768]{0,1:T(8,128)(2,1)}, bf16[128,768]{0,1:T(8,128)(2,1)}, u32[]{:S(2)}, u32[]{:S(2)}) collective-permute-start(bf16[128,768]{0,1:T(8,128)(2,1)} %get-tuple-element.307), channel_id=1, source_target_pairs={{0,4},{2,6},{4,0},{6,2},{1,5},{3,7},{5,1},{7,3},{8,12},{10,14},{12... | collective-permute-start | bytes 589832 | tf_op jit(solution)/shard_map/ppermute | solution.py:26
  141.1 53.0 %collective-permute-start.31 = (bf16[128,768]{0,1:T(8,128)(2,1)}, bf16[128,768]{0,1:T(8,128)(2,1)}, u32[]{:S(2)}, u32[]{:S(2)}) collective-permute-start(bf16[128,768]{0,1:T(8,128)(2,1)} %get-tuple-element.306), channel_id=1, source_target_pairs={{0,2},{2,0},{4,6},{6,4},{1,3},{3,1},{5,7},{7,5},{8,10},{10,8},{12,... | collective-permute-start | bytes 589832 | tf_op jit(solution)/shard_map/ppermute | solution.py:26
  160.0 178.4 %all-gather.8.cloned.1.call-start = ((), (), s32[]{:S(2)}) async-start(), calls=%async_computation.6 | async-start | bytes 3932160 | tf_op jit(solution)/shard_map/all_gather | solution.py:95
  188.7 11.3 %collective-permute-start.20 = (f32[2,2,640]{2,1,0:T(2,128)S(1)}, f32[2,2,640]{2,1,0:T(2,128)S(1)}, u32[]{:S(2)}, u32[]{:S(2)}) collective-permute-start(f32[2,2,640]{2,1,0:T(2,128)S(1)} %pad_maximum_fusion.43), channel_id=1, source_target_pairs={{0,24},{1,25},{2,26},{3,27},{4,28},{5,29},{6,30},{7,31}} | collective-permute-start | bytes 30728 | tf_op jit(solution)/shard_map/ppermute | solution.py:150
  212.7 15.2 %collective-permute-start.21 = (bf16[1,128,2048]{2,1,0:T(8,128)(2,1)}, bf16[1,128,2048]{2,1,0:T(8,128)(2,1)}, u32[]{:S(2)}, u32[]{:S(2)}) collective-permute-start(bf16[1,128,2048]{2,1,0:T(8,128)(2,1)} %get-tuple-element.238), channel_id=1, source_target_pairs={{0,4},{2,6},{4,0},{6,2},{1,5},{3,7},{5,1},{7,3},{8,12},{10,14},{12... | collective-permute-start | bytes 1572872 | tf_op jit(solution)/shard_map/ppermute | solution.py:26
  214.1 15.2 %collective-permute-start.23 = (bf16[1,128,2048]{2,1,0:T(8,128)(2,1)}, bf16[1,128,2048]{2,1,0:T(8,128)(2,1)}, u32[]{:S(2)}, u32[]{:S(2)}) collective-permute-start(bf16[1,128,2048]{2,1,0:T(8,128)(2,1)} %get-tuple-element.240), channel_id=1, source_target_pairs={{0,2},{2,0},{4,6},{6,4},{1,3},{3,1},{5,7},{7,5},{8,10},{10,8},{12,... | collective-permute-start | bytes 1572872 | tf_op jit(solution)/shard_map/ppermute | solution.py:26
  216.5 35.2 %collective-permute-start.42 = (bf16[2,128,2048]{2,1,0:T(8,128)(2,1)S(1)}, bf16[2,128,2048]{2,1,0:T(8,128)(2,1)S(1)}, u32[]{:S(2)}, u32[]{:S(2)}) collective-permute-start(bf16[2,128,2048]{2,1,0:T(8,128)(2,1)S(1)} %get-tuple-element.192), channel_id=1, source_target_pairs={{0,2},{2,0},{4,6},{6,4},{1,3},{3,1},{5,7},{7,5},{8,10},{10,8},{12,... | collective-permute-start | bytes 3145736 | tf_op jit(solution)/shard_map/ppermute | solution.py:26
  218.0 32.2 %collective-permute-start.43 = (bf16[2,128,2048]{2,1,0:T(8,128)(2,1)S(1)}, bf16[2,128,2048]{2,1,0:T(8,128)(2,1)S(1)}, u32[]{:S(2)}, u32[]{:S(2)}) collective-permute-start(bf16[2,128,2048]{2,1,0:T(8,128)(2,1)S(1)} %get-tuple-element.192), channel_id=1, source_target_pairs={{0,4},{2,6},{4,0},{6,2},{1,5},{3,7},{5,1},{7,3},{8,12},{10,14},{12... | collective-permute-start | bytes 3145736 | tf_op jit(solution)/shard_map/ppermute | solution.py:26
  232.3 42.2 %collective-permute-start.24 = (bf16[2,128,2048]{2,1,0:T(8,128)(2,1)}, bf16[2,128,2048]{2,1,0:T(8,128)(2,1)S(1)}, u32[]{:S(2)}, u32[]{:S(2)}) collective-permute-start(bf16[2,128,2048]{2,1,0:T(8,128)(2,1)} %pad_maximum_fusion.25), channel_id=1, source_target_pairs={{0,4},{2,6},{4,0},{6,2},{1,5},{3,7},{5,1},{7,3},{8,12},{10,14},{12... | collective-permute-start | bytes 3145736 | tf_op jit(solution)/shard_map/ppermute | solution.py:26
  233.9 41.5 %collective-permute-start.22 = (bf16[2,128,2048]{2,1,0:T(8,128)(2,1)}, bf16[2,128,2048]{2,1,0:T(8,128)(2,1)}, u32[]{:S(2)}, u32[]{:S(2)}) collective-permute-start(bf16[2,128,2048]{2,1,0:T(8,128)(2,1)} %pad_maximum_fusion.24), channel_id=1, source_target_pairs={{0,2},{2,0},{4,6},{6,4},{1,3},{3,1},{5,7},{7,5},{8,10},{10,8},{12,... | collective-permute-start | bytes 3145736 | tf_op jit(solution)/shard_map/ppermute | solution.py:26
  251.1 31.8 %collective-permute-start.45 = (bf16[1,128,2048]{2,1,0:T(8,128)(2,1)}, bf16[1,128,2048]{2,1,0:T(8,128)(2,1)}, u32[]{:S(2)}, u32[]{:S(2)}) collective-permute-start(bf16[1,128,2048]{2,1,0:T(8,128)(2,1)} %slice.688), channel_id=1, source_target_pairs={{0,2},{2,0},{4,6},{6,4},{1,3},{3,1},{5,7},{7,5},{8,10},{10,8},{12,... | collective-permute-start | bytes 1572872 | tf_op jit(solution)/shard_map/ppermute | solution.py:26
  253.5 29.4 %collective-permute-start.44 = (bf16[1,128,2048]{2,1,0:T(8,128)(2,1)}, bf16[1,128,2048]{2,1,0:T(8,128)(2,1)}, u32[]{:S(2)}, u32[]{:S(2)}) collective-permute-start(bf16[1,128,2048]{2,1,0:T(8,128)(2,1)} %slice.687), channel_id=1, source_target_pairs={{0,4},{2,6},{4,0},{6,2},{1,5},{3,7},{5,1},{7,3},{8,12},{10,14},{12... | collective-permute-start | bytes 1572872 | tf_op jit(solution)/shard_map/ppermute | solution.py:26
  274.4 334.4 %reduce-scatter.5.cloned.1.call-start = ((), (), s32[]{:S(2)}) async-start(), calls=%async_computation.7 | async-start | bytes 7864320 | tf_op jit(solution)/shard_map/reduce_scatter | solution.py:104
  279.6 27.0 %collective-permute-start.25 = (bf16[2,128,2048]{2,1,0:T(8,128)(2,1)S(1)}, bf16[2,128,2048]{2,1,0:T(8,128)(2,1)S(1)}, u32[]{:S(2)}, u32[]{:S(2)}) collective-permute-start(bf16[2,128,2048]{2,1,0:T(8,128)(2,1)S(1)} %get-tuple-element.198), channel_id=1, source_target_pairs={{0,2},{2,0},{4,6},{6,4},{1,3},{3,1},{5,7},{7,5},{8,10},{10,8},{12,... | collective-permute-start | bytes 3145736 | tf_op jit(solution)/shard_map/ppermute | solution.py:26
  281.1 24.8 %collective-permute-start.26 = (bf16[2,128,2048]{2,1,0:T(8,128)(2,1)S(1)}, bf16[2,128,2048]{2,1,0:T(8,128)(2,1)S(1)}, u32[]{:S(2)}, u32[]{:S(2)}) collective-permute-start(bf16[2,128,2048]{2,1,0:T(8,128)(2,1)S(1)} %get-tuple-element.198), channel_id=1, source_target_pairs={{0,4},{2,6},{4,0},{6,2},{1,5},{3,7},{5,1},{7,3},{8,12},{10,14},{12... | collective-permute-start | bytes 3145736 | tf_op jit(solution)/shard_map/ppermute | solution.py:26
  284.3 78.3 %collective-permute-start.35 = (bf16[2048,1536]{1,0:T(8,128)(2,1)}, bf16[2048,1536]{1,0:T(8,128)(2,1)}, u32[]{:S(2)}, u32[]{:S(2)}) collective-permute-start(bf16[2048,1536]{1,0:T(8,128)(2,1)} %all-gather.6.cloned.1.call-done), channel_id=1, source_target_pairs={{0,1},{1,0},{2,3},{3,2},{4,5},{5,4},{6,7},{7,6},{8,9},{9,8},{10,11... | collective-permute-start | bytes 18874376 | tf_op jit(solution)/shard_map/ppermute | solution.py:91
  306.0 12.8 %collective-permute-start.28 = (bf16[1,128,2048]{2,1,0:T(8,128)(2,1)S(1)}, bf16[1,128,2048]{2,1,0:T(8,128)(2,1)S(1)}, u32[]{:S(2)}, u32[]{:S(2)}) collective-permute-start(bf16[1,128,2048]{2,1,0:T(8,128)(2,1)S(1)} %slice.682), channel_id=1, source_target_pairs={{0,2},{2,0},{4,6},{6,4},{1,3},{3,1},{5,7},{7,5},{8,10},{10,8},{12,... | collective-permute-start | bytes 1572872 | tf_op jit(solution)/shard_map/ppermute | solution.py:26
  306.6 12.6 %collective-permute-start.27 = (bf16[1,128,2048]{2,1,0:T(8,128)(2,1)S(1)}, bf16[1,128,2048]{2,1,0:T(8,128)(2,1)S(1)}, u32[]{:S(2)}, u32[]{:S(2)}) collective-permute-start(bf16[1,128,2048]{2,1,0:T(8,128)(2,1)S(1)} %slice.681), channel_id=1, source_target_pairs={{0,4},{2,6},{4,0},{6,2},{1,5},{3,7},{5,1},{7,3},{8,12},{10,14},{12... | collective-permute-start | bytes 1572872 | tf_op jit(solution)/shard_map/ppermute | solution.py:26
  338.4 33.1 %collective-permute-start.36 = (bf16[2048,768]{0,1:T(8,128)(2,1)}, bf16[2048,768]{0,1:T(8,128)(2,1)S(1)}, u32[]{:S(2)}, u32[]{:S(2)}) collective-permute-start(bf16[2048,768]{0,1:T(8,128)(2,1)} %all-gather.8.cloned.1.call-done), channel_id=1, source_target_pairs={{0,1},{1,0},{2,3},{3,2},{4,5},{5,4},{6,7},{7,6},{8,9},{9,8},{10,11... | collective-permute-start | bytes 9437192 | tf_op jit(solution)/shard_map/ppermute | solution.py:91
  390.2 14.4 %collective-permute-start.46 = (bf16[1,128,2048]{2,1,0:T(8,128)(2,1)S(1)}, bf16[1,128,2048]{2,1,0:T(8,128)(2,1)S(1)}, u32[]{:S(2)}, u32[]{:S(2)}) collective-permute-start(bf16[1,128,2048]{2,1,0:T(8,128)(2,1)S(1)} %get-tuple-element.226), channel_id=1, source_target_pairs={{0,4},{2,6},{4,0},{6,2},{1,5},{3,7},{5,1},{7,3},{8,12},{10,14},{12... | collective-permute-start | bytes 1572872 | tf_op jit(solution)/shard_map/ppermute | solution.py:26
  391.7 14.1 %collective-permute-start.48 = (bf16[1,128,2048]{2,1,0:T(8,128)(2,1)S(1)}, bf16[1,128,2048]{2,1,0:T(8,128)(2,1)S(1)}, u32[]{:S(2)}, u32[]{:S(2)}) collective-permute-start(bf16[1,128,2048]{2,1,0:T(8,128)(2,1)S(1)} %get-tuple-element.228), channel_id=1, source_target_pairs={{0,2},{2,0},{4,6},{6,4},{1,3},{3,1},{5,7},{7,5},{8,10},{10,8},{12,... | collective-permute-start | bytes 1572872 | tf_op jit(solution)/shard_map/ppermute | solution.py:26
  406.3 24.5 %collective-permute-start.49 = (bf16[2,128,2048]{2,1,0:T(8,128)(2,1)S(1)}, bf16[2,128,2048]{2,1,0:T(8,128)(2,1)S(1)}, u32[]{:S(2)}, u32[]{:S(2)}) collective-permute-start(bf16[2,128,2048]{2,1,0:T(8,128)(2,1)S(1)} %pad_maximum_fusion.29), channel_id=1, source_target_pairs={{0,4},{2,6},{4,0},{6,2},{1,5},{3,7},{5,1},{7,3},{8,12},{10,14},{12... | collective-permute-start | bytes 3145736 | tf_op jit(solution)/shard_map/ppermute | solution.py:26
  407.1 24.3 %collective-permute-start.47 = (bf16[2,128,2048]{2,1,0:T(8,128)(2,1)S(1)}, bf16[2,128,2048]{2,1,0:T(8,128)(2,1)S(1)}, u32[]{:S(2)}, u32[]{:S(2)}) collective-permute-start(bf16[2,128,2048]{2,1,0:T(8,128)(2,1)S(1)} %pad_maximum_fusion.28), channel_id=1, source_target_pairs={{0,2},{2,0},{4,6},{6,4},{1,3},{3,1},{5,7},{7,5},{8,10},{10,8},{12,... | collective-permute-start | bytes 3145736 | tf_op jit(solution)/shard_map/ppermute | solution.py:26
  436.6 25.2 %collective-permute-start.50 = (bf16[2,128,2048]{2,1,0:T(8,128)(2,1)S(1)}, bf16[2,128,2048]{2,1,0:T(8,128)(2,1)S(1)}, u32[]{:S(2)}, u32[]{:S(2)}) collective-permute-start(bf16[2,128,2048]{2,1,0:T(8,128)(2,1)S(1)} %get-tuple-element.189), channel_id=1, source_target_pairs={{0,2},{2,0},{4,6},{6,4},{1,3},{3,1},{5,7},{7,5},{8,10},{10,8},{12,... | collective-permute-start | bytes 3145736 | tf_op jit(solution)/shard_map/ppermute | solution.py:26
  438.0 23.1 %collective-permute-start.51 = (bf16[2,128,2048]{2,1,0:T(8,128)(2,1)S(1)}, bf16[2,128,2048]{2,1,0:T(8,128)(2,1)S(1)}, u32[]{:S(2)}, u32[]{:S(2)}) collective-permute-start(bf16[2,128,2048]{2,1,0:T(8,128)(2,1)S(1)} %get-tuple-element.189), channel_id=1, source_target_pairs={{0,4},{2,6},{4,0},{6,2},{1,5},{3,7},{5,1},{7,3},{8,12},{10,14},{12... | collective-permute-start | bytes 3145736 | tf_op jit(solution)/shard_map/ppermute | solution.py:26
  461.1 11.0 %collective-permute-start.53 = (bf16[1,128,2048]{2,1,0:T(8,128)(2,1)S(1)}, bf16[1,128,2048]{2,1,0:T(8,128)(2,1)S(1)}, u32[]{:S(2)}, u32[]{:S(2)}) collective-permute-start(bf16[1,128,2048]{2,1,0:T(8,128)(2,1)S(1)} %slice.691), channel_id=1, source_target_pairs={{0,2},{2,0},{4,6},{6,4},{1,3},{3,1},{5,7},{7,5},{8,10},{10,8},{12,... | collective-permute-start | bytes 1572872 | tf_op jit(solution)/shard_map/ppermute | solution.py:26
  461.8 10.7 %collective-permute-start.52 = (bf16[1,128,2048]{2,1,0:T(8,128)(2,1)S(1)}, bf16[1,128,2048]{2,1,0:T(8,128)(2,1)S(1)}, u32[]{:S(2)}, u32[]{:S(2)}) collective-permute-start(bf16[1,128,2048]{2,1,0:T(8,128)(2,1)S(1)} %slice.690), channel_id=1, source_target_pairs={{0,4},{2,6},{4,0},{6,2},{1,5},{3,7},{5,1},{7,3},{8,12},{10,14},{12... | collective-permute-start | bytes 1572872 | tf_op jit(solution)/shard_map/ppermute | solution.py:26
  472.6 17.0 %collective-permute-start.54 = (bf16[2048,1536]{1,0:T(8,128)(2,1)}, bf16[2048,1536]{1,0:T(8,128)(2,1)}, u32[]{:S(2)}, u32[]{:S(2)}) collective-permute-start(bf16[2048,1536]{1,0:T(8,128)(2,1)} %convolution_convert_fusion.1), channel_id=1, source_target_pairs={{0,1},{1,0},{2,3},{3,2},{4,5},{5,4},{6,7},{7,6},{8,9},{9,8},{10,11... | collective-permute-start | bytes 18874376 | tf_op jit(solution)/shard_map/ppermute | solution.py:91
  472.7 14.3 %collective-permute-start.55 = (bf16[2048,768]{1,0:T(8,128)(2,1)S(1)}, bf16[2048,768]{1,0:T(8,128)(2,1)S(1)}, u32[]{:S(2)}, u32[]{:S(2)}) collective-permute-start(bf16[2048,768]{1,0:T(8,128)(2,1)S(1)} %convolution_convert_fusion.5), channel_id=1, source_target_pairs={{0,1},{1,0},{2,3},{3,2},{4,5},{5,4},{6,7},{7,6},{8,9},{9,8},{10,11... | collective-permute-start | bytes 9437192 | tf_op jit(solution)/shard_map/ppermute | solution.py:91
  498.6 184.0 %reduce-scatter.7.cloned.1.call-start = ((), (), s32[]{:S(2)}) async-start(), calls=%async_computation.8 | async-start | bytes 3932160 | tf_op jit(solution)/shard_map/reduce_scatter | solution.py:104
  512.0 14.3 %collective-permute-start.37 = (bf16[1,128,2048]{2,1,0:T(8,128)(2,1)S(1)}, bf16[1,128,2048]{2,1,0:T(8,128)(2,1)S(1)}, u32[]{:S(2)}, u32[]{:S(2)}) collective-permute-start(bf16[1,128,2048]{2,1,0:T(8,128)(2,1)S(1)} %get-tuple-element.232), channel_id=1, source_target_pairs={{0,4},{2,6},{4,0},{6,2},{1,5},{3,7},{5,1},{7,3},{8,12},{10,14},{12... | collective-permute-start | bytes 1572872 | tf_op jit(solution)/shard_map/ppermute | solution.py:26
  513.4 13.9 %collective-permute-start.39 = (bf16[1,128,2048]{2,1,0:T(8,128)(2,1)S(1)}, bf16[1,128,2048]{2,1,0:T(8,128)(2,1)S(1)}, u32[]{:S(2)}, u32[]{:S(2)}) collective-permute-start(bf16[1,128,2048]{2,1,0:T(8,128)(2,1)S(1)} %get-tuple-element.234), channel_id=1, source_target_pairs={{0,2},{2,0},{4,6},{6,4},{1,3},{3,1},{5,7},{7,5},{8,10},{10,8},{12,... | collective-permute-start | bytes 1572872 | tf_op jit(solution)/shard_map/ppermute | solution.py:26
  528.8 114.6 %collective-permute-start.40 = (bf16[2,128,2048]{2,1,0:T(8,128)(2,1)}, bf16[2,128,2048]{2,1,0:T(8,128)(2,1)}, u32[]{:S(2)}, u32[]{:S(2)}) collective-permute-start(bf16[2,128,2048]{2,1,0:T(8,128)(2,1)} %pad_maximum_fusion.27), channel_id=1, source_target_pairs={{0,4},{2,6},{4,0},{6,2},{1,5},{3,7},{5,1},{7,3},{8,12},{10,14},{12... | collective-permute-start | bytes 3145736 | tf_op jit(solution)/shard_map/ppermute | solution.py:26
  530.5 112.8 %collective-permute-start.38 = (bf16[2,128,2048]{2,1,0:T(8,128)(2,1)}, bf16[2,128,2048]{2,1,0:T(8,128)(2,1)}, u32[]{:S(2)}, u32[]{:S(2)}) collective-permute-start(bf16[2,128,2048]{2,1,0:T(8,128)(2,1)} %pad_maximum_fusion.26), channel_id=1, source_target_pairs={{0,2},{2,0},{4,6},{6,4},{1,3},{3,1},{5,7},{7,5},{8,10},{10,8},{12,... | collective-permute-start | bytes 3145736 | tf_op jit(solution)/shard_map/ppermute | solution.py:26
  619.7 153.4 %reduce-scatter.9.cloned.1.call-start = ((), (), s32[]{:S(2)}) async-start(), calls=%async_computation.9 | async-start | bytes 307200 | tf_op jit(solution)/shard_map/reduce_scatter | solution.py:104
  637.1 34.8 %collective-permute-start.66 = (bf16[2048,960]{0,1:T(8,128)(2,1)}, bf16[2048,960]{0,1:T(8,128)(2,1)}, u32[]{:S(2)}, u32[]{:S(2)}) collective-permute-start(bf16[2048,960]{0,1:T(8,128)(2,1)} %pad_maximum_fusion.1), channel_id=1, source_target_pairs={{0,1},{1,0},{2,3},{3,2},{4,5},{5,4},{6,7},{7,6},{8,9},{9,8},{10,11... | collective-permute-start | bytes 11796488 | tf_op jit(solution)/shard_map/ppermute | solution.py:91
  648.7 39.7 %collective-permute-start.41 = (bf16[2,128,2048]{2,1,0:T(8,128)(2,1)}, bf16[2,128,2048]{2,1,0:T(8,128)(2,1)}, u32[]{:S(2)}, u32[]{:S(2)}) collective-permute-start(bf16[2,128,2048]{2,1,0:T(8,128)(2,1)} %get-tuple-element.194), channel_id=1, source_target_pairs={{0,1},{1,0},{2,3},{3,2},{4,5},{5,4},{6,7},{7,6},{8,9},{9,8},{10,11... | collective-permute-start | bytes 3145736 | tf_op jit(solution)/shard_map/ppermute | solution.py:91
  682.7 96.8 %reduce-scatter.11.cloned.1.call-start = ((), (), s32[]{:S(2)}) async-start(), calls=%async_computation.10 | async-start | bytes 4915200 | tf_op jit(solution)/shard_map/reduce_scatter | solution.py:104
  685.4 22.0 %collective-permute-start.60 = (bf16[1,128,2048]{2,1,0:T(8,128)(2,1)}, bf16[1,128,2048]{2,1,0:T(8,128)(2,1)}, u32[]{:S(2)}, u32[]{:S(2)}) collective-permute-start(bf16[1,128,2048]{2,1,0:T(8,128)(2,1)} %get-tuple-element.220), channel_id=1, source_target_pairs={{0,4},{2,6},{4,0},{6,2},{1,5},{3,7},{5,1},{7,3},{8,12},{10,14},{12... | collective-permute-start | bytes 1572872 | tf_op jit(solution)/shard_map/ppermute | solution.py:26
  686.9 20.6 %collective-permute-start.62 = (bf16[1,128,2048]{2,1,0:T(8,128)(2,1)}, bf16[1,128,2048]{2,1,0:T(8,128)(2,1)}, u32[]{:S(2)}, u32[]{:S(2)}) collective-permute-start(bf16[1,128,2048]{2,1,0:T(8,128)(2,1)} %get-tuple-element.222), channel_id=1, source_target_pairs={{0,2},{2,0},{4,6},{6,4},{1,3},{3,1},{5,7},{7,5},{8,10},{10,8},{12,... | collective-permute-start | bytes 1572872 | tf_op jit(solution)/shard_map/ppermute | solution.py:26
  692.1 20.2 %collective-permute-start.77 = (bf16[128,1536]{1,0:T(8,128)(2,1)S(1)}, bf16[128,1536]{1,0:T(8,128)(2,1)S(1)}, u32[]{:S(2)}, u32[]{:S(2)}) collective-permute-start(bf16[128,1536]{1,0:T(8,128)(2,1)S(1)} %get-tuple-element.277), channel_id=1, source_target_pairs={{0,6},{2,4},{4,2},{6,0},{1,7},{3,5},{5,3},{7,1},{8,14},{10,12},{12... | collective-permute-start | bytes 1179656 | tf_op jit(solution)/shard_map/ppermute | solution.py:26
  693.1 24.2 %collective-permute-start.78 = (bf16[128,1536]{1,0:T(8,128)(2,1)S(1)}, bf16[128,1536]{1,0:T(8,128)(2,1)S(1)}, u32[]{:S(2)}, u32[]{:S(2)}) collective-permute-start(bf16[128,1536]{1,0:T(8,128)(2,1)S(1)} %get-tuple-element.276), channel_id=1, source_target_pairs={{0,4},{2,6},{4,0},{6,2},{1,5},{3,7},{5,1},{7,3},{8,12},{10,14},{12... | collective-permute-start | bytes 1179656 | tf_op jit(solution)/shard_map/ppermute | solution.py:26
  694.1 24.7 %collective-permute-start.79 = (bf16[128,1536]{1,0:T(8,128)(2,1)S(1)}, bf16[128,1536]{1,0:T(8,128)(2,1)S(1)}, u32[]{:S(2)}, u32[]{:S(2)}) collective-permute-start(bf16[128,1536]{1,0:T(8,128)(2,1)S(1)} %get-tuple-element.275), channel_id=1, source_target_pairs={{0,2},{2,0},{4,6},{6,4},{1,3},{3,1},{5,7},{7,5},{8,10},{10,8},{12,... | collective-permute-start | bytes 1179656 | tf_op jit(solution)/shard_map/ppermute | solution.py:26
  709.1 29.4 %collective-permute-start.63 = (bf16[2,128,2048]{2,1,0:T(8,128)(2,1)S(1)}, bf16[2,128,2048]{2,1,0:T(8,128)(2,1)S(1)}, u32[]{:S(2)}, u32[]{:S(2)}) collective-permute-start(bf16[2,128,2048]{2,1,0:T(8,128)(2,1)S(1)} %pad_maximum_fusion.31), channel_id=1, source_target_pairs={{0,4},{2,6},{4,0},{6,2},{1,5},{3,7},{5,1},{7,3},{8,12},{10,14},{12... | collective-permute-start | bytes 3145736 | tf_op jit(solution)/shard_map/ppermute | solution.py:26
  710.7 29.0 %collective-permute-start.61 = (bf16[2,128,2048]{2,1,0:T(8,128)(2,1)S(1)}, bf16[2,128,2048]{2,1,0:T(8,128)(2,1)S(1)}, u32[]{:S(2)}, u32[]{:S(2)}) collective-permute-start(bf16[2,128,2048]{2,1,0:T(8,128)(2,1)S(1)} %pad_maximum_fusion.30), channel_id=1, source_target_pairs={{0,2},{2,0},{4,6},{6,4},{1,3},{3,1},{5,7},{7,5},{8,10},{10,8},{12,... | collective-permute-start | bytes 3145736 | tf_op jit(solution)/shard_map/ppermute | solution.py:26
  746.1 17.7 %collective-permute-start.64 = (bf16[2,128,2048]{2,1,0:T(8,128)(2,1)}, bf16[2,128,2048]{2,1,0:T(8,128)(2,1)}, u32[]{:S(2)}, u32[]{:S(2)}) collective-permute-start(bf16[2,128,2048]{2,1,0:T(8,128)(2,1)} %get-tuple-element.183), channel_id=1, source_target_pairs={{0,1},{1,0},{2,3},{3,2},{4,5},{5,4},{6,7},{7,6},{8,9},{9,8},{10,11... | collective-permute-start | bytes 3145736 | tf_op jit(solution)/shard_map/ppermute | solution.py:91
  784.2 12.5 %collective-permute-start.74 = (bf16[128,960]{0,1:T(8,128)(2,1)S(1)}, bf16[128,960]{0,1:T(8,128)(2,1)S(1)}, u32[]{:S(2)}, u32[]{:S(2)}) collective-permute-start(bf16[128,960]{0,1:T(8,128)(2,1)S(1)} %bitcast.611), channel_id=1, source_target_pairs={{0,6},{2,4},{4,2},{6,0},{1,7},{3,5},{5,3},{7,1},{8,14},{10,12},{12... | collective-permute-start | bytes 737288 | tf_op jit(solution)/shard_map/ppermute | solution.py:26
  789.8 10.2 %collective-permute-start.75 = (bf16[128,960]{0,1:T(8,128)(2,1)S(1)}, bf16[128,960]{0,1:T(8,128)(2,1)S(1)}, u32[]{:S(2)}, u32[]{:S(2)}) collective-permute-start(bf16[128,960]{0,1:T(8,128)(2,1)S(1)} %bitcast.612), channel_id=1, source_target_pairs={{0,4},{2,6},{4,0},{6,2},{1,5},{3,7},{5,1},{7,3},{8,12},{10,14},{12... | collective-permute-start | bytes 737288 | tf_op jit(solution)/shard_map/ppermute | solution.py:26
  (177 other events, 2872.5 us)
Sparse Core Ops, SparseCore 0:
  34.6 75.3 all-gather.3
  160.1 114.1 all-gather.5
  275.9 62.3 all-gather.7
  498.8 110.0 reduce-scatter.4
  619.8 62.8 reduce-scatter.6
  685.3 19.6 reduce-scatter.8
  707.4 71.9 reduce-scatter.10

commit v5 on v4

--- a/solution.py
+++ b/solution.py
@@ -56,22 +56,34 @@
     return whole.reshape(streams, PLANE * rows, width)
 
 
-def plane_sum(part, streams):
+def plane_sum_first(part, streams):
     mine = lax.axis_index("j")
-    width = part.shape[-1]
-    part = part.astype(BF16).reshape(streams, PLANE, -1, width)
+    part = part.astype(BF16).reshape(streams, PLANE, -1, part.shape[-1])
+    far = at(part, mine ^ 3, 1)
     half = streams // 2
-    far = at(part, mine ^ 3, 1)
-    via_x = to_partner(far[:half], 1).astype(F32)
-    via_y = to_partner(far[half:], 2).astype(F32)
+    return part, to_partner(far[:half], 1), to_partner(far[half:], 2)
+
+
+def plane_sum_second(state):
+    part, via_x, via_y = state
+    mine = lax.axis_index("j")
+    half = via_x.shape[0]
     for_x = at(part, mine ^ 1, 1)
     for_y = at(part, mine ^ 2, 1)
-    for_x = jnp.concatenate([for_x[:half], (for_x[half:] + via_y).astype(BF16)], axis=0)
-    for_y = jnp.concatenate([(for_y[:half] + via_x).astype(BF16), for_y[half:]], axis=0)
+    for_x = jnp.concatenate(
+        [for_x[:half], (for_x[half:].astype(F32) + via_y.astype(F32)).astype(BF16)], axis=0
+    )
+    for_y = jnp.concatenate(
+        [(for_y[:half].astype(F32) + via_x.astype(F32)).astype(BF16), for_y[half:]], axis=0
+    )
     from_x = to_partner(for_x, 1)
     from_y = to_partner(for_y, 2)
     own = at(part, mine, 1)
     return own.astype(F32) + from_x.astype(F32) + from_y.astype(F32)
+
+
+def plane_sum(part, streams):
+    return plane_sum_second(plane_sum_first(part, streams))
 
 
 def plane_swap(blocks):
@@ -102,6 +114,16 @@
 
 def sum_along_z(total):
     return lax.psum_scatter(total, "z", scatter_dimension=0, tiled=True)
+
+
+def sent_along_z(total):
+    size, mine = lax.axis_size("z"), lax.axis_index("z")
+    rows = total.reshape(size, -1, total.shape[1])
+    result = at(rows, mine, 0).astype(F32)
+    for step in range(1, size):
+        route = [(i, (i + step) % size) for i in range(size)]
+        result += lax.ppermute(at(rows, (mine + step) % size, 0), "z", route).astype(F32)
+    return result
 
 
 def to_owners(summed):
@@ -293,11 +315,11 @@
     tails = jnp.pad(norm_gains, ((0, 0), (0, small_width - gain_width)))
     small = jnp.concatenate([small, tails], axis=0)
 
+    first_blocks = jnp.concatenate([to_chips(w_x), to_chips(w_g), to_chips(w_o.T)], axis=2)
+    first_rows = jnp.concatenate(plane_swap(first_blocks), axis=0)
     small = z_gather(small)
-    first_blocks = jnp.concatenate([to_chips(w_x), to_chips(w_g), to_chips(w_o.T)], axis=2)
-    first_blocks, small = lax.optimization_barrier((first_blocks, small))
-    first_rows = jnp.concatenate(plane_swap(first_blocks), axis=0)
-    first_rows, own_in, small = lax.optimization_barrier((first_rows, own_in, small))
+    later = (w_gate, w_up, w_down)
+    first_rows, own_in, small, later = lax.optimization_barrier((first_rows, own_in, small, later))
     gain_rows = jnp.broadcast_to(
         small[:, small_rows:].reshape(1, 2 * z_size, small_width),
         (PLANE, 2 * z_size, small_width),
@@ -325,21 +347,10 @@
         axis=1,
     )
 
-    w_first = along_z(first_rows)
-    w_rec = jnp.concatenate(
-        [w[:, p * part_width : (p + 1) * part_width] for p in (0, 1) for w in w_first], axis=1
-    )
-    w_back = jnp.concatenate([w[:, 2 * part_width :] for w in w_first], axis=1)
-    later = (w_gate, w_up, w_down)
-    later, whole_in = lax.optimization_barrier((later, whole_in))
     wide_blocks = jnp.concatenate([to_chips(later[0]), to_chips(later[1])], axis=2)
     wide_rows = jnp.concatenate(plane_swap(wide_blocks), axis=0)
     narrow_rows = jnp.concatenate(plane_swap(to_chips(later[2].T)), axis=0)
     own_cot, narrow_rows = lax.optimization_barrier((own_cot, narrow_rows))
-    w_wide = along_z(wide_rows)
-    narrow_rows, wide_own = lax.optimization_barrier((narrow_rows, w_wide[0]))
-    w_wide = (wide_own, w_wide[1])
-    w_narrow = along_z(narrow_rows)
 
     def live_at(position):
         second_start = spans[:, 0:1]
@@ -364,6 +375,15 @@
     normed_low = rms_norm(
         whole_in.reshape(tokens, model_width).astype(F32), gains_all[0]
     ).astype(BF16)
+    first_own, normed_low, wide_rows = lax.optimization_barrier(
+        (lax.all_gather(first_rows, "z", axis=0, tiled=True), normed_low, wide_rows)
+    )
+    wide_own = lax.all_gather(wide_rows, "z", axis=0, tiled=True)
+    w_first = (first_own, to_core(first_own))
+    w_rec = jnp.concatenate(
+        [w[:, p * part_width : (p + 1) * part_width] for p in (0, 1) for w in w_first], axis=1
+    )
+    w_back = jnp.concatenate([w[:, 2 * part_width :] for w in w_first], axis=1)
     projected = dot(normed_low, w_rec, 1, 0)
     source_rows = projected[:, :rec_width].astype(BF16).reshape(n_streams, n_rows, rec_width)
     branch, branch_back = jax.vjp(jax.nn.gelu, projected[:, rec_width:])
@@ -450,38 +470,48 @@
     states_flat = states.reshape(tokens, rec_width)
     mixed_rows = (states_flat * branch).astype(BF16)
     rec_part = dot(mixed_rows, w_back, 1, 1)
-    rec_total = plane_sum(rec_part, n_streams).reshape(own_tokens, model_width)
+    rec_total, wide_own, narrow_rows = lax.optimization_barrier(
+        (plane_sum(rec_part, n_streams), wide_own, narrow_rows)
+    )
+    rec_total = rec_total.reshape(own_tokens, model_width)
+    w_wide = (wide_own, to_core(wide_own))
+    w_narrow = along_z(narrow_rows)
     hidden_one = flat_in + own_live * rec_total
     normed_two, norm_two_back = jax.vjp(rms_norm, hidden_one, gains_all[1])
     own_second = normed_two.astype(BF16).reshape(n_streams, own_rows, model_width)
     second_low = plane_gather(own_second).reshape(tokens, model_width)
 
-    down_part = second_part = 0.0
-    g_narrow, g_wide = [], []
+    second_part = 0.0
+    hidden, g_narrow, g_wide = [], [], []
     for h in range(halves):
         both = dot(second_low, w_wide[h], 1, 0)
         activated, mix_back = jax.vjp(mix_gelu, both[:, :ff_part], both[:, ff_part:])
         act_low = activated.astype(BF16)
-        down_part = down_part + dot(act_low, w_narrow[h], 1, 1)
+        hidden.append((act_low, mix_back))
+        g_narrow.append(dot(d_down, act_low, 0, 0).astype(BF16))
+    sum_narrow = both_cores(*g_narrow)
+    for h, (act_low, mix_back) in enumerate(hidden):
         d_act = dot(d_down, w_narrow[h], 1, 0)
         d_both = jnp.concatenate([d.astype(BF16) for d in mix_back(d_act)], axis=1)
         second_part = second_part + dot(d_both, w_wide[h], 1, 1)
-        g_narrow.append(dot(d_down, act_low, 0, 0).astype(BF16))
         g_wide.append(dot(second_low, d_both, 0, 0).astype(BF16))
-
-    mlp_total = plane_sum(down_part, n_streams).reshape(own_tokens, model_width)
-    out_flat = (hidden_one + own_live * mlp_total).astype(BF16)
-    output = all_streams(out_flat.reshape(n_streams, own_rows, model_width))
+    second_part, sum_narrow = lax.optimization_barrier((second_part, sum_narrow))
+    sum_narrow = sum_along_z(sum_narrow)
 
     second_total = plane_sum(second_part, n_streams).reshape(own_tokens, model_width)
     d_hidden_norm, g_gain_two = norm_two_back(second_total)
     d_hidden = d_out + d_hidden_norm
     own_rec = (d_hidden * own_live).astype(BF16).reshape(n_streams, own_rows, model_width)
     d_rec = plane_gather(own_rec).reshape(tokens, model_width)
-    d_rec, g_narrow, g_wide = lax.optimization_barrier((d_rec, g_narrow, g_wide))
-    sum_wide, sum_narrow = both_cores(*g_wide), both_cores(*g_narrow)
+    d_rec, g_wide, sum_narrow = lax.optimization_barrier((d_rec, g_wide, sum_narrow))
+    sum_wide = both_cores(*g_wide)
     d_mixed = dot(d_rec, w_back, 1, 0)
-    d_mixed, sum_wide, sum_narrow = lax.optimization_barrier((d_mixed, sum_wide, sum_narrow))
+    acts = [act_low for act_low, _ in hidden]
+    d_mixed, sum_wide, sum_narrow, acts = lax.optimization_barrier(
+        (d_mixed, sum_wide, sum_narrow, acts)
+    )
+    down_part = sum(dot(act_low, w, 1, 1) for act_low, w in zip(acts, w_narrow))
+    mlp_sum = plane_sum_first(down_part, n_streams)
     sum_wide = sum_along_z(sum_wide)
     g_back = dot(d_rec, mixed_rows, 0, 0).astype(BF16)
 
@@ -489,6 +519,9 @@
     branch_low = branch_back(d_mixed * states_flat)[0].astype(BF16)
     next_keep = jnp.concatenate([retain_eff[:, 1:], jnp.ones_like(retain_eff[:, :1])], axis=1)
     later_keep, later_sum = local_scan(next_keep, grad_state, True)
+    later_sum, mlp_sum = lax.optimization_barrier((later_sum, mlp_sum))
+    mlp_sum = plane_sum_second(mlp_sum)
+    out_narrow = to_owners(sum_narrow)
     carried_grad = entering(
         retain_eff[:, 0] * later_keep[:, 0], retain_eff[:, 0] * later_sum[:, 0], True
     )
@@ -519,11 +552,13 @@
         ],
         axis=0,
     )
+    grad_gates, mlp_total, out_narrow = lax.optimization_barrier((grad_gates, mlp_sum, out_narrow))
+    mlp_total = mlp_total.reshape(own_tokens, model_width)
+    out_flat = (hidden_one + own_live * mlp_total).astype(BF16)
+    output = all_streams(out_flat.reshape(n_streams, own_rows, model_width))
+
     d_conv_gates = dot(grad_gates, gates_all, 1, 1)
     d_conv = (d_conv_direct + d_conv_gates).reshape(n_streams, n_rows, rec_width)
-    d_conv, sum_wide, sum_narrow = lax.optimization_barrier((d_conv, sum_wide, sum_narrow))
-    sum_narrow = sum_along_z(sum_narrow)
-    out_wide = to_owners(sum_wide)
     d_extended, g_taps, g_conv_bias = conv_back(d_conv)
     rim_grad = shifted(d_extended[:, :3].astype(BF16), -1).astype(F32)
     d_source = jnp.concatenate([d_extended[:, 3:n_rows], d_extended[:, n_rows:] + rim_grad], axis=1)
@@ -557,13 +592,13 @@
         axis=1,
     ).astype(BF16)
     sum_small = both_cores(g_small[:part_width], g_small[part_width:])
-    sum_small, sum_first, sum_narrow = lax.optimization_barrier((sum_small, sum_first, sum_narrow))
-    out_narrow = to_owners(sum_narrow)
+    first_part, sum_first, sum_wide = lax.optimization_barrier((first_part, sum_first, sum_wide))
+    out_wide = to_owners(sum_wide)
     sum_first = sum_along_z(sum_first)
     out_first = to_owners(sum_first)
-    g_small = sum_along_z(sum_small)
+    g_small = sent_along_z(sum_small)
     route = [(z * PLANE + j, j * z_size + z) for z in range(z_size) for j in range(PLANE)]
-    g_small = lax.ppermute(g_small, ("z", "j"), route).astype(F32)
+    g_small = lax.ppermute(g_small.astype(BF16), ("z", "j"), route).astype(F32)
     g_params = g_small[None, :, :8]
     g_gates = g_small[None, :, 8 : 8 + 2 * HEAD_DIM]
     finals = g_small[:, 8 + 2 * HEAD_DIM :].T.reshape(all_streams_count, 2, 5, -1)

time: 822 us -> 782 us (0.951)
  waiting for transfers between devices: 315 us -> 245 us
  matrix products: 154 us -> 166 us
  local copies, waits for them, and re-layouts: 99 us -> 111 us
  starting transfers between devices: 101 us -> 110 us
    all_gather x3 -> x1, waiting for transfers between devices: 53.9 us -> 11.5 us  [along_z(): own = lax.all_gather(block, 'z', axis=0, tiled=True)]
    reduce_scatter x4 -> x3, waiting for transfers between devices: 40.7 us -> 0.02 us  [sum_along_z(): return lax.psum_scatter(total, 'z', scatter_dimension=0, tiled=True)]
    ppermute x53, waiting for transfers between devices: 199 us -> 218 us  [to_partner(): return lax.ppermute(block, 'j', [(i, i ^ bit) for i in range(PLANE)])]
    dot_general x21, matrix products: 146 us -> 159 us  [dot(): lax.dot_general(left, right, (((left_dim,), (right_dim,)), ((), ())), pre...]
    ppermute x12, waiting for transfers between devices: 9.65 us -> 0.03 us  [to_core(): return lax.ppermute(block, 'c', [(0, 1), (1, 0)])]
    convert_element_type x4 -> x3, other arithmetic: 17.6 us -> 14.1 us  [both_cores(): return (own.astype(F32) + to_core(other).astype(F32)).astype(BF16)]
    unnamed x315 -> x349, local copies, waits for them, and re-layouts: 36.6 us -> 35.3 us
  transfers between devices with their start and end apart: 90 -> 92, of which waited for: 44 -> 43; matrix products, arithmetic and copies ran while one was open for 36% -> 41% of each run, Pallas kernels for 2% -> 2%
where the time goes in v5:
time: 782 us; the launch traced here: 771 us
  waiting for transfers between devices  245 us (31%)
  matrix products  166 us (21%)
  local copies, waits for them, and re-layouts  111 us (14%)
  starting transfers between devices  110 us (14%)
  other arithmetic  105 us (13%)
  between operations  17.3 us (2%)
  Pallas kernels  16.9 us (2%)
    ppermute x53, waiting for transfers between devices, to_partner(): return lax.ppermute(block, 'j', [(i, i ^ bit) for i in range(PLANE)])  218 us
    dot_general x21, matrix products, dot(): lax.dot_general(left, right, (((left_dim,), (right_dim,)), ((), ())), pre...  159 us
    ppermute x53, starting transfers between devices, to_partner(): return lax.ppermute(block, 'j', [(i, i ^ bit) for i in range(PLANE)])  70 us
    unnamed x349, local copies, waits for them, and re-layouts  35.3 us
    pallas_call x2, Pallas kernels, local_scan(): pl.pallas_call(partial(scan_kernel, backward), grid=(width // 128,), in_s...  16.9 us
    ppermute x8, starting transfers between devices, shifted(): lax.ppermute(block, 'z', [(i - distance, i) for i in range(size) if 0 <=...  16.4 us
  transfers between devices with their start and end apart: 92, of which 43 were waited for; matrix products, arithmetic and copies ran while one was open for 41% of the time, Pallas kernels for 2%

profile of v5, /device:TPU:0, one launch (start us, length us, event | category | flops | bytes accessed | tf_op | source)
XLA Modules:
  0.0 770.7 jit_solution(6435451164862245543)
XLA Ops:
  9.8 3.0 collective-permute-start.3
  32.5 2.8 collective-permute-done.1
  51.7 8.7 %collective-permute-done.14 = bf16[128,1536]{1,0:T(8,128)(2,1)S(1)} collective-permute-done((bf16[128,1536]{1,0:T(8,128)(2,1)S(1)}, bf16[128,1536]{1,0:T(8,128)(2,1)S(1)}, u32[]{:S(2)}, u32[]{:S(2)}) %collective-permute-start.14) | collective-permute-done | bytes 393248 | tf_op jit(solution)/shard_map/ppermute | solution.py:26
  60.9 4.5 collective-permute-done.15
  70.5 17.5 %collective-permute-done.10 = bf16[2,128,2048]{2,1,0:T(8,128)(2,1)S(1)} collective-permute-done((bf16[2,128,2048]{2,1,0:T(8,128)(2,1)S(1)}, bf16[2,128,2048]{2,1,0:T(8,128)(2,1)S(1)}, u32[]{:S(2)}, u32[]{:S(2)}) %collective-permute-start.10) | collective-permute-done | bytes 1048608 | tf_op jit(solution)/shard_map/ppermute | solution.py:26
  88.6 2.8 collective-permute-done.11
  95.1 6.8 collective-permute-done.12
  105.1 3.1 multiply_reduce_fusion
  108.2 5.2 fusion.1
  127.6 3.6 fusion.169
  131.2 4.5 fusion.170
  135.7 5.6 fusion.70
  145.5 2.9 collective-permute-start.18
  154.4 2.8 multiply_add_fusion.2
  161.3 3.1 bitcast_multiply_fusion.6
  165.2 7.8 %shard_map.246 = (f32[2,512,640]{2,1,0:T(8,128)S(1)}, f32[2,512,640]{2,1,0:T(8,128)S(1)}) custom-call(f32[2,512,640]{2,1,0:T(8,128)S(1)} %get-tuple-element.275.keep_ref, f32[2,512,640]{2,1,0:T(8,128)S(1)} %get-tuple-element.274.add_ref), custom_call_target="tpu_custom_call" | custom-call | flops 5242880 | bytes 10485760 | tf_op jit(solution)/shard_map/pallas_call | solution.py:226
  177.2 3.6 collective-permute-start.23
  183.5 2.9 collective-permute-start.22
  191.8 3.6 convolution_convert_fusion.3
  204.5 9.3 %collective-permute-done.24 = bf16[1,128,2048]{2,1,0:T(8,128)(2,1)} collective-permute-done((bf16[1,128,2048]{2,1,0:T(8,128)(2,1)}, bf16[1,128,2048]{2,1,0:T(8,128)(2,1)}, u32[]{:S(2)}, u32[]{:S(2)}) %collective-permute-start.24) | collective-permute-done | bytes 524320 | tf_op jit(solution)/shard_map/ppermute | solution.py:26
  219.5 18.4 %collective-permute-done.31 = bf16[2,128,2048]{2,1,0:T(8,128)(2,1)S(1)} collective-permute-done((bf16[2,128,2048]{2,1,0:T(8,128)(2,1)S(1)}, bf16[2,128,2048]{2,1,0:T(8,128)(2,1)S(1)}, u32[]{:S(2)}, u32[]{:S(2)}) %collective-permute-start.31) | collective-permute-done | bytes 1048608 | tf_op jit(solution)/shard_map/ppermute | solution.py:26
  243.5 16.8 %collective-permute-done.25 = bf16[2,128,2048]{2,1,0:T(8,128)(2,1)S(1)} collective-permute-done((bf16[2,128,2048]{2,1,0:T(8,128)(2,1)S(1)}, bf16[2,128,2048]{2,1,0:T(8,128)(2,1)S(1)}, u32[]{:S(2)}, u32[]{:S(2)}) %collective-permute-start.25) | collective-permute-done | bytes 1048608 | tf_op jit(solution)/shard_map/ppermute | solution.py:26
  263.3 2.8 multiply_reduce_fusion.8
  271.8 20.8 %collective-permute-done.35 = bf16[2,128,2048]{2,1,0:T(8,128)(2,1)S(1)} collective-permute-done((bf16[2,128,2048]{2,1,0:T(8,128)(2,1)S(1)}, bf16[2,128,2048]{2,1,0:T(8,128)(2,1)S(1)}, u32[]{:S(2)}, u32[]{:S(2)}) %collective-permute-start.35) | collective-permute-done | bytes 1048608 | tf_op jit(solution)/shard_map/ppermute | solution.py:26
  296.1 10.2 %collective-permute-done.37 = bf16[1,128,2048]{2,1,0:T(8,128)(2,1)S(1)} collective-permute-done((bf16[1,128,2048]{2,1,0:T(8,128)(2,1)S(1)}, bf16[1,128,2048]{2,1,0:T(8,128)(2,1)S(1)}, u32[]{:S(2)}, u32[]{:S(2)}) %collective-permute-start.37) | collective-permute-done | bytes 524320 | tf_op jit(solution)/shard_map/ppermute | solution.py:26
  309.9 8.9 %fusion.183 = f32[1024,1536]{0,1:T(8,128)} fusion(bf16[1024,2048]{1,0:T(8,128)(2,1)S(1)} %bitcast.582, bf16[2048,1536]{1,0:T(8,128)(2,1)S(1)} %bitcast.635), kind=kOutput, calls=%fused_computation.549 | convolution fusion | flops 6442450944 | bytes 16777216 | tf_op jit(solution)/shard_map/dot_general | solution.py:20
  318.8 11.5 %all-gather.8.cloned.1.call-done = bf16[2048,768]{0,1:T(8,128)(2,1)} async-done(((bf16[512,768]{0,1:T(8,128)(2,1)}), bf16[2048,768]{0,1:T(8,128)(2,1)}) %all-gather.8.cloned.1.call-update) | async-done | bytes 3145744 | tf_op jit(solution)/shard_map/all_gather | solution.py:107
  330.3 12.3 %fusion.8 = (bf16[1024,768]{0,1:T(8,128)(2,1)}, bf16[1024,768]{0,1:T(8,128)(2,1)}, bf16[1024,768]{0,1:T(8,128)(2,1)S(1)}) fusion(f32[1024,1536]{0,1:T(8,128)} %fusion.183, bf16[1024,2048]{1,0:T(8,128)(2,1)} %bitcast.578, bf16[2048,768]{0,1:T(8,128)(2,1)} %all-gather.8.cloned.1.call-done), kind=kOutput, calls=%fused_computation.41 | convolution fusion | flops 3241672704 | bytes 18350080 | tf_op jit(solution)/shard_map/dot_general | solution.py:20
  342.6 11.1 %fusion.184 = f32[1024,1536]{0,1:T(8,128)} fusion(bf16[1024,2048]{1,0:T(8,128)(2,1)S(1)} %bitcast.583, bf16[2048,1536]{1,0:T(8,128)(2,1)} %collective-permute-done.40), kind=kOutput, calls=%fused_computation.550 | convolution fusion | flops 6442450944 | bytes 16777216 | tf_op jit(solution)/shard_map/dot_general | solution.py:20
  353.8 10.3 %fusion.15 = (bf16[1024,768]{0,1:T(8,128)(2,1)S(1)}, bf16[1024,768]{0,1:T(8,128)(2,1)}, bf16[1024,768]{0,1:T(8,128)(2,1)S(1)}) fusion(f32[1024,1536]{0,1:T(8,128)} %fusion.184, bf16[1024,2048]{1,0:T(8,128)(2,1)S(1)} %bitcast.579, bf16[2048,768]{0,1:T(8,128)(2,1)S(1)} %collective-permute-done.39), kind=kOutput, calls=%fused_computation.48 | convolution fusion | flops 3241672704 | bytes 18350080 | tf_op jit(solution)/shard_map/dot_general | solution.py:20
  364.1 3.8 convolution_convert_fusion.4
  368.5 10.2 %fusion.53 = f32[1024,2048]{1,0:T(8,128)} fusion(bf16[2048,1536]{1,0:T(8,128)(2,1)S(1)} %bitcast.637, bf16[1024,768]{0,1:T(8,128)(2,1)} %get-tuple-element.227, bf16[1024,768]{0,1:T(8,128)(2,1)S(1)} %copy-done.154), kind=kOutput, calls=%fused_computation.150 | convolution fusion | flops 6448742400 | bytes 17825792 | tf_op jit(solution)/shard_map/dot_general | solution.py:20
  378.7 12.4 %convolution_add_fusion = bf16[1024,2048]{1,0:T(8,128)(2,1)} fusion(f32[1024,2048]{1,0:T(8,128)} %fusion.53, bf16[2048,1536]{1,0:T(8,128)(2,1)} %collective-permute-done.40, bf16[1024,768]{0,1:T(8,128)(2,1)S(1)} %copy-done.152, bf16[1024,768]{0,1:T(8,128)(2,1)S(1)} %get-tuple-element.224), kind=kOutput, calls=%fused_computation.25 | convolution fusion | flops 6452936704 | bytes 22020096 | tf_op jit(solution)/shard_map/dot_general | solution.py:20
  391.1 5.2 add_convert_fusion.3
  402.0 11.2 %collective-permute-done.42 = bf16[1,128,2048]{2,1,0:T(8,128)(2,1)} collective-permute-done((bf16[1,128,2048]{2,1,0:T(8,128)(2,1)}, bf16[1,128,2048]{2,1,0:T(8,128)(2,1)}, u32[]{:S(2)}, u32[]{:S(2)}) %collective-permute-start.42) | collective-permute-done | bytes 524320 | tf_op jit(solution)/shard_map/ppermute | solution.py:26
  418.8 9.7 %convolution_convert_fusion.2 = bf16[2048,1536]{1,0:T(8,128)(2,1)} fusion(bf16[1024,2048]{1,0:T(8,128)(2,1)S(1)} %bitcast.584, bf16[1024,768]{0,1:T(8,128)(2,1)S(1)} %copy-done.156, bf16[1024,768]{0,1:T(8,128)(2,1)S(1)} %copy-done.155), kind=kOutput, calls=%fused_computation.9 | convolution fusion | flops 6451888128 | bytes 13631488 | tf_op jit(solution)/shard_map/dot_general | solution.py:20
  428.5 12.0 %collective-permute-done.43 = bf16[2,128,2048]{2,1,0:T(8,128)(2,1)S(1)} collective-permute-done((bf16[2,128,2048]{2,1,0:T(8,128)(2,1)S(1)}, bf16[2,128,2048]{2,1,0:T(8,128)(2,1)S(1)}, u32[]{:S(2)}, u32[]{:S(2)}) %collective-permute-start.43) | collective-permute-done | bytes 1048608 | tf_op jit(solution)/shard_map/ppermute | solution.py:26
  449.8 10.0 %convolution_convert_fusion.1 = bf16[2048,1536]{1,0:T(8,128)(2,1)} fusion(bf16[1024,2048]{1,0:T(8,128)(2,1)S(1)} %bitcast.585, bf16[1024,768]{0,1:T(8,128)(2,1)S(1)} %copy-done.153, bf16[1024,768]{0,1:T(8,128)(2,1)S(1)} %copy-done.151), kind=kOutput, calls=%fused_computation.8 | convolution fusion | flops 6451888128 | bytes 13631488 | tf_op jit(solution)/shard_map/dot_general | solution.py:20
  459.8 11.7 %collective-permute-done.46 = bf16[2,128,2048]{2,1,0:T(8,128)(2,1)S(1)} collective-permute-done((bf16[2,128,2048]{2,1,0:T(8,128)(2,1)S(1)}, bf16[2,128,2048]{2,1,0:T(8,128)(2,1)S(1)}, u32[]{:S(2)}, u32[]{:S(2)}) %collective-permute-start.46) | collective-permute-done | bytes 1048608 | tf_op jit(solution)/shard_map/ppermute | solution.py:26
  477.1 5.9 collective-permute-done.48
  490.2 7.2 fusion.55
  497.5 6.6 convolution_convert_fusion.7
  504.1 9.1 %add_convert_fusion = bf16[2048,1536]{1,0:T(8,128)(2,1)} fusion(bf16[2048,1536]{1,0:T(8,128)(2,1)} %collective-permute-done.50, bf16[2048,1536]{1,0:T(8,128)(2,1)} %convolution_convert_fusion.2), kind=kLoop, calls=%fused_computation | loop fusion | flops 12582912 | bytes 18874368 | tf_op jit(solution)/shard_map/convert_element_type | solution.py:112
  520.4 6.4 fusion.185
  526.8 5.5 add_convert_fusion.1
  535.7 3.6 fusion.25
  543.0 9.1 %shard_map.247 = (f32[2,512,640]{2,1,0:T(8,128)S(1)}, f32[2,512,640]{2,1,0:T(8,128)S(1)}) custom-call(f32[2,512,640]{2,1,0:T(8,128)S(1)} %copy-done.4, f32[2,512,640]{2,1,0:T(8,128)S(1)} %bitcast.556), custom_call_target="tpu_custom_call" | custom-call | flops 5242880 | bytes 10485760 | tf_op jit(solution)/shard_map/pallas_call | solution.py:226
  562.1 3.6 collective-permute-done.55
  569.0 4.4 multiply_reduce_fusion.1
  573.4 4.0 fusion.161
  580.0 4.1 collective-permute-done.56
  586.9 7.5 multiply_reduce_fusion.5
  599.7 3.9 collective-permute-done.62
  604.8 6.1 convolution_convert_fusion
  620.0 4.0 convolution_convert_fusion.6
  639.6 9.8 %fusion.54 = bf16[1024,2048]{1,0:T(8,128)(2,1)} fusion(bf16[1024,640]{1,0:T(8,128)(2,1)} %get-tuple-element.228, bf16[1024,640]{1,0:T(8,128)(2,1)} %bitcast.596, bf16[2048,320]{0,1:T(8,128)(2,1)} %copy-done.64, bf16[2048,320]{0,1:T(8,128)(2,1)} %copy-done.62, bf16[2048,320]{0,1:T(8,128)(2,1)} %copy-done.65, bf16[2048,320]{0,1:T(8,128)(2,1)} %copy-done.63), kind=kOutput, calls=%fused_computation.151 | convolution fusion | flops 5394923520 | bytes 12058624 | tf_op jit(solution)/shard_map/dot_general | solution.py:20
  652.6 5.0 add_convert_fusion.2
  663.4 5.9 collective-permute-start.64
  669.3 3.4 collective-permute-start.66
  682.0 3.8 collective-permute-done.66
  693.8 5.3 collective-permute-done.84
  699.1 3.5 collective-permute-done.85
  703.9 20.0 %collective-permute-done.65 = bf16[2,128,2048]{2,1,0:T(8,128)(2,1)S(1)} collective-permute-done((bf16[2,128,2048]{2,1,0:T(8,128)(2,1)S(1)}, bf16[2,128,2048]{2,1,0:T(8,128)(2,1)S(1)}, u32[]{:S(2)}, u32[]{:S(2)}) %collective-permute-start.65) | collective-permute-done | bytes 1048608 | tf_op jit(solution)/shard_map/ppermute | solution.py:26
  750.9 4.7 collective-permute-done.80
  (761 shorter events, 287.4 us)
Async XLA Ops:
  7.2 106.2 %all-gather.4.cloned.1.call-start = ((), (), s32[]{:S(2)}) async-start(), calls=%async_computation.3 | async-start | bytes 4915200 | tf_op jit(solution)/shard_map/all_gather | solution.py:379
  9.8 20.6 %collective-permute-start.3 = (bf16[82,328]{1,0:T(8,128)(2,1)}, bf16[82,328]{1,0:T(8,128)(2,1)S(1)}, u32[]{:S(2)}, u32[]{:S(2)}) collective-permute-start(bf16[82,328]{1,0:T(8,128)(2,1)} %get-tuple-element.223), channel_id=1, source_target_pairs={{0,8},{8,16},{16,24},{24,0},{1,9},{9,17},{17,25},{25,1},{2,10},{10... | collective-permute-start | bytes 161384 | tf_op jit(solution)/shard_map/ppermute | solution.py:138
  12.8 18.1 %collective-permute-start.4 = (bf16[82,328]{1,0:T(8,128)(2,1)}, bf16[82,328]{1,0:T(8,128)(2,1)}, u32[]{:S(2)}, u32[]{:S(2)}) collective-permute-start(bf16[82,328]{1,0:T(8,128)(2,1)} %get-tuple-element.223), channel_id=1, source_target_pairs={{0,16},{8,24},{16,0},{24,8},{1,17},{9,25},{17,1},{25,9},{2,18},{10... | collective-permute-start | bytes 161384 | tf_op jit(solution)/shard_map/ppermute | solution.py:138
  15.4 16.5 %collective-permute-start.5 = (bf16[82,328]{1,0:T(8,128)(2,1)}, bf16[82,328]{1,0:T(8,128)(2,1)S(1)}, u32[]{:S(2)}, u32[]{:S(2)}) collective-permute-start(bf16[82,328]{1,0:T(8,128)(2,1)} %get-tuple-element.223), channel_id=1, source_target_pairs={{0,24},{8,0},{16,8},{24,16},{1,25},{9,1},{17,9},{25,17},{2,26},{10... | collective-permute-start | bytes 161384 | tf_op jit(solution)/shard_map/ppermute | solution.py:138
  30.9 120.8 %collective-permute-start.19 = (bf16[2,2,3,320]{3,2,1,0:T(4,128)(2,1)}, bf16[2,2,3,320]{3,2,1,0:T(4,128)(2,1)S(1)}, u32[]{:S(2)}, u32[]{:S(2)}) collective-permute-start(bf16[2,2,3,320]{3,2,1,0:T(4,128)(2,1)} %copy.456), channel_id=1, source_target_pairs={{0,1},{1,0},{2,3},{3,2},{4,5},{5,4},{6,7},{7,6},{8,9},{9,8},{10,11... | collective-permute-start | bytes 23048 | tf_op jit(solution)/shard_map/ppermute | solution.py:103
  31.9 87.3 %collective-permute-start.20 = (f32[2,2,320]{2,1,0:T(2,128)}, f32[2,2,320]{2,1,0:T(2,128)S(1)}, u32[]{:S(2)}, u32[]{:S(2)}) collective-permute-start(f32[2,2,320]{2,1,0:T(2,128)} %get-tuple-element.368), channel_id=1, source_target_pairs={{0,1},{1,0},{2,3},{3,2},{4,5},{5,4},{6,7},{7,6},{8,9},{9,8},{10,11... | collective-permute-start | bytes 15368 | tf_op jit(solution)/shard_map/ppermute | solution.py:103
  39.2 224.1 %all-gather.6.cloned.1.call-start = ((), (), s32[]{:S(2)}) async-start(), calls=%async_computation.4 | async-start | bytes 7864320 | tf_op jit(solution)/shard_map/all_gather | solution.py:381
  47.4 13.0 %collective-permute-start.14 = (bf16[128,1536]{1,0:T(8,128)(2,1)S(1)}, bf16[128,1536]{1,0:T(8,128)(2,1)S(1)}, u32[]{:S(2)}, u32[]{:S(2)}) collective-permute-start(bf16[128,1536]{1,0:T(8,128)(2,1)S(1)} %get-tuple-element.303), channel_id=1, source_target_pairs={{0,6},{2,4},{4,2},{6,0},{1,7},{3,5},{5,3},{7,1},{8,14},{10,12},{12... | collective-permute-start | bytes 1179656 | tf_op jit(solution)/shard_map/ppermute | solution.py:26
  49.0 16.4 %collective-permute-start.15 = (bf16[128,1536]{1,0:T(8,128)(2,1)S(1)}, bf16[128,1536]{1,0:T(8,128)(2,1)S(1)}, u32[]{:S(2)}, u32[]{:S(2)}) collective-permute-start(bf16[128,1536]{1,0:T(8,128)(2,1)S(1)} %get-tuple-element.304), channel_id=1, source_target_pairs={{0,4},{2,6},{4,0},{6,2},{1,5},{3,7},{5,1},{7,3},{8,12},{10,14},{12... | collective-permute-start | bytes 1179656 | tf_op jit(solution)/shard_map/ppermute | solution.py:26
  49.4 19.4 %collective-permute-start.16 = (bf16[128,1536]{1,0:T(8,128)(2,1)S(1)}, bf16[128,1536]{1,0:T(8,128)(2,1)S(1)}, u32[]{:S(2)}, u32[]{:S(2)}) collective-permute-start(bf16[128,1536]{1,0:T(8,128)(2,1)S(1)} %get-tuple-element.302), channel_id=1, source_target_pairs={{0,2},{2,0},{4,6},{6,4},{1,3},{3,1},{5,7},{7,5},{8,10},{10,8},{12,... | collective-permute-start | bytes 1179656 | tf_op jit(solution)/shard_map/ppermute | solution.py:26
  60.4 27.6 %collective-permute-start.10 = (bf16[2,128,2048]{2,1,0:T(8,128)(2,1)S(1)}, bf16[2,128,2048]{2,1,0:T(8,128)(2,1)S(1)}, u32[]{:S(2)}, u32[]{:S(2)}) collective-permute-start(bf16[2,128,2048]{2,1,0:T(8,128)(2,1)S(1)} %constant_dynamic-slice_fusion.20), channel_id=1, source_target_pairs={{0,2},{2,0},{4,6},{6,4},{1,3},{3,1},{5,7},{7,5},{8,10},{10,8},{12,... | collective-permute-start | bytes 3145736 | tf_op jit(solution)/shard_map/ppermute | solution.py:26
  65.4 26.0 %collective-permute-start.11 = (bf16[2,128,2048]{2,1,0:T(8,128)(2,1)S(1)}, bf16[2,128,2048]{2,1,0:T(8,128)(2,1)S(1)}, u32[]{:S(2)}, u32[]{:S(2)}) collective-permute-start(bf16[2,128,2048]{2,1,0:T(8,128)(2,1)S(1)} %constant_dynamic-slice_fusion.20), channel_id=1, source_target_pairs={{0,4},{2,6},{4,0},{6,2},{1,5},{3,7},{5,1},{7,3},{8,12},{10,14},{12... | collective-permute-start | bytes 3145736 | tf_op jit(solution)/shard_map/ppermute | solution.py:26
  88.1 13.8 %collective-permute-start.12 = (bf16[1,128,2048]{2,1,0:T(8,128)(2,1)S(1)}, bf16[1,128,2048]{2,1,0:T(8,128)(2,1)S(1)}, u32[]{:S(2)}, u32[]{:S(2)}) collective-permute-start(bf16[1,128,2048]{2,1,0:T(8,128)(2,1)S(1)} %slice.646), channel_id=1, source_target_pairs={{0,4},{2,6},{4,0},{6,2},{1,5},{3,7},{5,1},{7,3},{8,12},{10,14},{12... | collective-permute-start | bytes 1572872 | tf_op jit(solution)/shard_map/ppermute | solution.py:26
  91.5 12.5 %collective-permute-start.13 = (bf16[1,128,2048]{2,1,0:T(8,128)(2,1)S(1)}, bf16[1,128,2048]{2,1,0:T(8,128)(2,1)S(1)}, u32[]{:S(2)}, u32[]{:S(2)}) collective-permute-start(bf16[1,128,2048]{2,1,0:T(8,128)(2,1)S(1)} %slice.647), channel_id=1, source_target_pairs={{0,2},{2,0},{4,6},{6,4},{1,3},{3,1},{5,7},{7,5},{8,10},{10,8},{12,... | collective-permute-start | bytes 1572872 | tf_op jit(solution)/shard_map/ppermute | solution.py:26
  113.4 17.8 %collective-permute-start.17 = (bf16[2048,960]{0,1:T(8,128)(2,1)}, bf16[2048,960]{0,1:T(8,128)(2,1)}, u32[]{:S(2)}, u32[]{:S(2)}) collective-permute-start(bf16[2048,960]{0,1:T(8,128)(2,1)} %all-gather.4.cloned.1.call-done), channel_id=1, source_target_pairs={{0,1},{1,0},{2,3},{3,2},{4,5},{5,4},{6,7},{7,6},{8,9},{9,8},{10,11... | collective-permute-start | bytes 11796488 | tf_op jit(solution)/shard_map/ppermute | solution.py:103
  122.7 58.0 %collective-permute-start.28 = (bf16[128,768]{0,1:T(8,128)(2,1)}, bf16[128,768]{0,1:T(8,128)(2,1)S(1)}, u32[]{:S(2)}, u32[]{:S(2)}) collective-permute-start(bf16[128,768]{0,1:T(8,128)(2,1)} %get-tuple-element.329), channel_id=1, source_target_pairs={{0,6},{2,4},{4,2},{6,0},{1,7},{3,5},{5,3},{7,1},{8,14},{10,12},{12... | collective-permute-start | bytes 589832 | tf_op jit(solution)/shard_map/ppermute | solution.py:26
  124.9 55.9 %collective-permute-start.29 = (bf16[128,768]{0,1:T(8,128)(2,1)}, bf16[128,768]{0,1:T(8,128)(2,1)S(1)}, u32[]{:S(2)}, u32[]{:S(2)}) collective-permute-start(bf16[128,768]{0,1:T(8,128)(2,1)} %get-tuple-element.328), channel_id=1, source_target_pairs={{0,4},{2,6},{4,0},{6,2},{1,5},{3,7},{5,1},{7,3},{8,12},{10,14},{12... | collective-permute-start | bytes 589832 | tf_op jit(solution)/shard_map/ppermute | solution.py:26
  125.6 55.2 %collective-permute-start.30 = (bf16[128,768]{0,1:T(8,128)(2,1)}, bf16[128,768]{0,1:T(8,128)(2,1)}, u32[]{:S(2)}, u32[]{:S(2)}) collective-permute-start(bf16[128,768]{0,1:T(8,128)(2,1)} %get-tuple-element.327), channel_id=1, source_target_pairs={{0,2},{2,0},{4,6},{6,4},{1,3},{3,1},{5,7},{7,5},{8,10},{10,8},{12,... | collective-permute-start | bytes 589832 | tf_op jit(solution)/shard_map/ppermute | solution.py:26
  149.9 180.4 %all-gather.8.cloned.1.call-start = ((), (), s32[]{:S(2)}) async-start(), calls=%async_computation.5 | async-start | bytes 3932160 | tf_op jit(solution)/shard_map/all_gather | solution.py:107
  198.6 15.2 %collective-permute-start.24 = (bf16[1,128,2048]{2,1,0:T(8,128)(2,1)}, bf16[1,128,2048]{2,1,0:T(8,128)(2,1)}, u32[]{:S(2)}, u32[]{:S(2)}) collective-permute-start(bf16[1,128,2048]{2,1,0:T(8,128)(2,1)} %get-tuple-element.259), channel_id=1, source_target_pairs={{0,4},{2,6},{4,0},{6,2},{1,5},{3,7},{5,1},{7,3},{8,12},{10,14},{12... | collective-permute-start | bytes 1572872 | tf_op jit(solution)/shard_map/ppermute | solution.py:26
  200.3 15.2 %collective-permute-start.26 = (bf16[1,128,2048]{2,1,0:T(8,128)(2,1)}, bf16[1,128,2048]{2,1,0:T(8,128)(2,1)}, u32[]{:S(2)}, u32[]{:S(2)}) collective-permute-start(bf16[1,128,2048]{2,1,0:T(8,128)(2,1)} %get-tuple-element.261), channel_id=1, source_target_pairs={{0,2},{2,0},{4,6},{6,4},{1,3},{3,1},{5,7},{7,5},{8,10},{10,8},{12,... | collective-permute-start | bytes 1572872 | tf_op jit(solution)/shard_map/ppermute | solution.py:26
  203.6 34.3 %collective-permute-start.31 = (bf16[2,128,2048]{2,1,0:T(8,128)(2,1)S(1)}, bf16[2,128,2048]{2,1,0:T(8,128)(2,1)S(1)}, u32[]{:S(2)}, u32[]{:S(2)}) collective-permute-start(bf16[2,128,2048]{2,1,0:T(8,128)(2,1)S(1)} %get-tuple-element.217), channel_id=1, source_target_pairs={{0,2},{2,0},{4,6},{6,4},{1,3},{3,1},{5,7},{7,5},{8,10},{10,8},{12,... | collective-permute-start | bytes 3145736 | tf_op jit(solution)/shard_map/ppermute | solution.py:26
  204.2 35.8 %collective-permute-start.32 = (bf16[2,128,2048]{2,1,0:T(8,128)(2,1)S(1)}, bf16[2,128,2048]{2,1,0:T(8,128)(2,1)S(1)}, u32[]{:S(2)}, u32[]{:S(2)}) collective-permute-start(bf16[2,128,2048]{2,1,0:T(8,128)(2,1)S(1)} %get-tuple-element.217), channel_id=1, source_target_pairs={{0,4},{2,6},{4,0},{6,2},{1,5},{3,7},{5,1},{7,3},{8,12},{10,14},{12... | collective-permute-start | bytes 3145736 | tf_op jit(solution)/shard_map/ppermute | solution.py:26
  217.2 43.1 %collective-permute-start.25 = (bf16[2,128,2048]{2,1,0:T(8,128)(2,1)S(1)}, bf16[2,128,2048]{2,1,0:T(8,128)(2,1)S(1)}, u32[]{:S(2)}, u32[]{:S(2)}) collective-permute-start(bf16[2,128,2048]{2,1,0:T(8,128)(2,1)S(1)} %pad_maximum_fusion.20), channel_id=1, source_target_pairs={{0,2},{2,0},{4,6},{6,4},{1,3},{3,1},{5,7},{7,5},{8,10},{10,8},{12,... | collective-permute-start | bytes 3145736 | tf_op jit(solution)/shard_map/ppermute | solution.py:26
  218.9 41.5 %collective-permute-start.27 = (bf16[2,128,2048]{2,1,0:T(8,128)(2,1)S(1)}, bf16[2,128,2048]{2,1,0:T(8,128)(2,1)S(1)}, u32[]{:S(2)}, u32[]{:S(2)}) collective-permute-start(bf16[2,128,2048]{2,1,0:T(8,128)(2,1)S(1)} %pad_maximum_fusion.21), channel_id=1, source_target_pairs={{0,4},{2,6},{4,0},{6,2},{1,5},{3,7},{5,1},{7,3},{8,12},{10,14},{12... | collective-permute-start | bytes 3145736 | tf_op jit(solution)/shard_map/ppermute | solution.py:26
  239.7 30.7 %collective-permute-start.33 = (bf16[1,128,2048]{2,1,0:T(8,128)(2,1)}, bf16[1,128,2048]{2,1,0:T(8,128)(2,1)}, u32[]{:S(2)}, u32[]{:S(2)}) collective-permute-start(bf16[1,128,2048]{2,1,0:T(8,128)(2,1)} %slice.678), channel_id=1, source_target_pairs={{0,4},{2,6},{4,0},{6,2},{1,5},{3,7},{5,1},{7,3},{8,12},{10,14},{12... | collective-permute-start | bytes 1572872 | tf_op jit(solution)/shard_map/ppermute | solution.py:26
  241.8 28.5 %collective-permute-start.34 = (bf16[1,128,2048]{2,1,0:T(8,128)(2,1)}, bf16[1,128,2048]{2,1,0:T(8,128)(2,1)}, u32[]{:S(2)}, u32[]{:S(2)}) collective-permute-start(bf16[1,128,2048]{2,1,0:T(8,128)(2,1)} %slice.679), channel_id=1, source_target_pairs={{0,2},{2,0},{4,6},{6,4},{1,3},{3,1},{5,7},{7,5},{8,10},{10,8},{12,... | collective-permute-start | bytes 1572872 | tf_op jit(solution)/shard_map/ppermute | solution.py:26
  266.1 76.5 %collective-permute-start.40 = (bf16[2048,1536]{1,0:T(8,128)(2,1)}, bf16[2048,1536]{1,0:T(8,128)(2,1)}, u32[]{:S(2)}, u32[]{:S(2)}) collective-permute-start(bf16[2048,1536]{1,0:T(8,128)(2,1)} %all-gather.6.cloned.1.call-done), channel_id=1, source_target_pairs={{0,1},{1,0},{2,3},{3,2},{4,5},{5,4},{6,7},{7,6},{8,9},{9,8},{10,11... | collective-permute-start | bytes 18874376 | tf_op jit(solution)/shard_map/ppermute | solution.py:103
  266.1 217.9 %reduce-scatter.4.cloned.1.call-start = ((), (), s32[]{:S(2)}) async-start(), calls=%async_computation.6 | async-start | bytes 3932160 | tf_op jit(solution)/shard_map/reduce_scatter | solution.py:116
  267.0 25.6 %collective-permute-start.35 = (bf16[2,128,2048]{2,1,0:T(8,128)(2,1)S(1)}, bf16[2,128,2048]{2,1,0:T(8,128)(2,1)S(1)}, u32[]{:S(2)}, u32[]{:S(2)}) collective-permute-start(bf16[2,128,2048]{2,1,0:T(8,128)(2,1)S(1)} %get-tuple-element.215), channel_id=1, source_target_pairs={{0,2},{2,0},{4,6},{6,4},{1,3},{3,1},{5,7},{7,5},{8,10},{10,8},{12,... | collective-permute-start | bytes 3145736 | tf_op jit(solution)/shard_map/ppermute | solution.py:26
  268.6 25.7 %collective-permute-start.36 = (bf16[2,128,2048]{2,1,0:T(8,128)(2,1)S(1)}, bf16[2,128,2048]{2,1,0:T(8,128)(2,1)S(1)}, u32[]{:S(2)}, u32[]{:S(2)}) collective-permute-start(bf16[2,128,2048]{2,1,0:T(8,128)(2,1)S(1)} %get-tuple-element.215), channel_id=1, source_target_pairs={{0,4},{2,6},{4,0},{6,2},{1,5},{3,7},{5,1},{7,3},{8,12},{10,14},{12... | collective-permute-start | bytes 3145736 | tf_op jit(solution)/shard_map/ppermute | solution.py:26
  292.7 13.7 %collective-permute-start.37 = (bf16[1,128,2048]{2,1,0:T(8,128)(2,1)S(1)}, bf16[1,128,2048]{2,1,0:T(8,128)(2,1)S(1)}, u32[]{:S(2)}, u32[]{:S(2)}) collective-permute-start(bf16[1,128,2048]{2,1,0:T(8,128)(2,1)S(1)} %slice.681), channel_id=1, source_target_pairs={{0,4},{2,6},{4,0},{6,2},{1,5},{3,7},{5,1},{7,3},{8,12},{10,14},{12... | collective-permute-start | bytes 1572872 | tf_op jit(solution)/shard_map/ppermute | solution.py:26
  294.3 13.4 %collective-permute-start.38 = (bf16[1,128,2048]{2,1,0:T(8,128)(2,1)S(1)}, bf16[1,128,2048]{2,1,0:T(8,128)(2,1)S(1)}, u32[]{:S(2)}, u32[]{:S(2)}) collective-permute-start(bf16[1,128,2048]{2,1,0:T(8,128)(2,1)S(1)} %slice.682), channel_id=1, source_target_pairs={{0,2},{2,0},{4,6},{6,4},{1,3},{3,1},{5,7},{7,5},{8,10},{10,8},{12,... | collective-permute-start | bytes 1572872 | tf_op jit(solution)/shard_map/ppermute | solution.py:26
  330.3 23.5 %collective-permute-start.39 = (bf16[2048,768]{0,1:T(8,128)(2,1)}, bf16[2048,768]{0,1:T(8,128)(2,1)S(1)}, u32[]{:S(2)}, u32[]{:S(2)}) collective-permute-start(bf16[2048,768]{0,1:T(8,128)(2,1)} %all-gather.8.cloned.1.call-done), channel_id=1, source_target_pairs={{0,1},{1,0},{2,3},{3,2},{4,5},{5,4},{6,7},{7,6},{8,9},{9,8},{10,11... | collective-permute-start | bytes 9437192 | tf_op jit(solution)/shard_map/ppermute | solution.py:103
  367.9 23.2 %collective-permute-start.41 = (bf16[2048,768]{1,0:T(8,128)(2,1)S(1)}, bf16[2048,768]{1,0:T(8,128)(2,1)S(1)}, u32[]{:S(2)}, u32[]{:S(2)}) collective-permute-start(bf16[2048,768]{1,0:T(8,128)(2,1)S(1)} %convolution_convert_fusion.4), channel_id=1, source_target_pairs={{0,1},{1,0},{2,3},{3,2},{4,5},{5,4},{6,7},{7,6},{8,9},{9,8},{10,11... | collective-permute-start | bytes 9437192 | tf_op jit(solution)/shard_map/ppermute | solution.py:103
  398.9 14.2 %collective-permute-start.42 = (bf16[1,128,2048]{2,1,0:T(8,128)(2,1)}, bf16[1,128,2048]{2,1,0:T(8,128)(2,1)}, u32[]{:S(2)}, u32[]{:S(2)}) collective-permute-start(bf16[1,128,2048]{2,1,0:T(8,128)(2,1)} %get-tuple-element.253), channel_id=1, source_target_pairs={{0,4},{2,6},{4,0},{6,2},{1,5},{3,7},{5,1},{7,3},{8,12},{10,14},{12... | collective-permute-start | bytes 1572872 | tf_op jit(solution)/shard_map/ppermute | solution.py:26
  400.4 13.9 %collective-permute-start.44 = (bf16[1,128,2048]{2,1,0:T(8,128)(2,1)}, bf16[1,128,2048]{2,1,0:T(8,128)(2,1)}, u32[]{:S(2)}, u32[]{:S(2)}) collective-permute-start(bf16[1,128,2048]{2,1,0:T(8,128)(2,1)} %get-tuple-element.255), channel_id=1, source_target_pairs={{0,2},{2,0},{4,6},{6,4},{1,3},{3,1},{5,7},{7,5},{8,10},{10,8},{12,... | collective-permute-start | bytes 1572872 | tf_op jit(solution)/shard_map/ppermute | solution.py:26
  401.9 255.7 %reduce-scatter.6.cloned.1.call-start = ((), (), s32[]{:S(2)}) async-start(), calls=%async_computation.7 | async-start | bytes 7864320 | tf_op jit(solution)/shard_map/reduce_scatter | solution.py:116
  416.5 24.0 %collective-permute-start.43 = (bf16[2,128,2048]{2,1,0:T(8,128)(2,1)S(1)}, bf16[2,128,2048]{2,1,0:T(8,128)(2,1)S(1)}, u32[]{:S(2)}, u32[]{:S(2)}) collective-permute-start(bf16[2,128,2048]{2,1,0:T(8,128)(2,1)S(1)} %pad_maximum_fusion.22), channel_id=1, source_target_pairs={{0,2},{2,0},{4,6},{6,4},{1,3},{3,1},{5,7},{7,5},{8,10},{10,8},{12,... | collective-permute-start | bytes 3145736 | tf_op jit(solution)/shard_map/ppermute | solution.py:26
  418.2 23.7 %collective-permute-start.45 = (bf16[2,128,2048]{2,1,0:T(8,128)(2,1)S(1)}, bf16[2,128,2048]{2,1,0:T(8,128)(2,1)S(1)}, u32[]{:S(2)}, u32[]{:S(2)}) collective-permute-start(bf16[2,128,2048]{2,1,0:T(8,128)(2,1)S(1)} %pad_maximum_fusion.23), channel_id=1, source_target_pairs={{0,4},{2,6},{4,0},{6,2},{1,5},{3,7},{5,1},{7,3},{8,12},{10,14},{12... | collective-permute-start | bytes 3145736 | tf_op jit(solution)/shard_map/ppermute | solution.py:26
  448.7 22.9 %collective-permute-start.46 = (bf16[2,128,2048]{2,1,0:T(8,128)(2,1)S(1)}, bf16[2,128,2048]{2,1,0:T(8,128)(2,1)S(1)}, u32[]{:S(2)}, u32[]{:S(2)}) collective-permute-start(bf16[2,128,2048]{2,1,0:T(8,128)(2,1)S(1)} %get-tuple-element.212), channel_id=1, source_target_pairs={{0,2},{2,0},{4,6},{6,4},{1,3},{3,1},{5,7},{7,5},{8,10},{10,8},{12,... | collective-permute-start | bytes 3145736 | tf_op jit(solution)/shard_map/ppermute | solution.py:26
  449.2 23.2 %collective-permute-start.47 = (bf16[2,128,2048]{2,1,0:T(8,128)(2,1)S(1)}, bf16[2,128,2048]{2,1,0:T(8,128)(2,1)S(1)}, u32[]{:S(2)}, u32[]{:S(2)}) collective-permute-start(bf16[2,128,2048]{2,1,0:T(8,128)(2,1)S(1)} %get-tuple-element.212), channel_id=1, source_target_pairs={{0,4},{2,6},{4,0},{6,2},{1,5},{3,7},{5,1},{7,3},{8,12},{10,14},{12... | collective-permute-start | bytes 3145736 | tf_op jit(solution)/shard_map/ppermute | solution.py:26
  484.1 20.1 %collective-permute-start.50 = (bf16[2048,1536]{1,0:T(8,128)(2,1)}, bf16[2048,1536]{1,0:T(8,128)(2,1)}, u32[]{:S(2)}, u32[]{:S(2)}) collective-permute-start(bf16[2048,1536]{1,0:T(8,128)(2,1)} %convolution_convert_fusion.1), channel_id=1, source_target_pairs={{0,1},{1,0},{2,3},{3,2},{4,5},{5,4},{6,7},{7,6},{8,9},{9,8},{10,11... | collective-permute-start | bytes 18874376 | tf_op jit(solution)/shard_map/ppermute | solution.py:103
  515.3 36.8 %collective-permute-start.58 = (bf16[128,768]{0,1:T(8,128)(2,1)}, bf16[128,768]{0,1:T(8,128)(2,1)}, u32[]{:S(2)}, u32[]{:S(2)}) collective-permute-start(bf16[128,768]{0,1:T(8,128)(2,1)} %bitcast.611), channel_id=1, source_target_pairs={{0,6},{2,4},{4,2},{6,0},{1,7},{3,5},{5,3},{7,1},{8,14},{10,12},{12... | collective-permute-start | bytes 589832 | tf_op jit(solution)/shard_map/ppermute | solution.py:26
  517.7 34.4 %collective-permute-start.59 = (bf16[128,768]{0,1:T(8,128)(2,1)}, bf16[128,768]{0,1:T(8,128)(2,1)}, u32[]{:S(2)}, u32[]{:S(2)}) collective-permute-start(bf16[128,768]{0,1:T(8,128)(2,1)} %bitcast.141), channel_id=1, source_target_pairs={{0,4},{2,6},{4,0},{6,2},{1,5},{3,7},{5,1},{7,3},{8,12},{10,14},{12... | collective-permute-start | bytes 589832 | tf_op jit(solution)/shard_map/ppermute | solution.py:26
  519.8 32.2 %collective-permute-start.60 = (bf16[128,768]{0,1:T(8,128)(2,1)}, bf16[128,768]{0,1:T(8,128)(2,1)}, u32[]{:S(2)}, u32[]{:S(2)}) collective-permute-start(bf16[128,768]{0,1:T(8,128)(2,1)} %bitcast.142), channel_id=1, source_target_pairs={{0,2},{2,0},{4,6},{6,4},{1,3},{3,1},{5,7},{7,5},{8,10},{10,8},{12,... | collective-permute-start | bytes 589832 | tf_op jit(solution)/shard_map/ppermute | solution.py:26
  533.6 20.5 %collective-permute-start.51 = (bf16[1,128,2048]{2,1,0:T(8,128)(2,1)}, bf16[1,128,2048]{2,1,0:T(8,128)(2,1)S(1)}, u32[]{:S(2)}, u32[]{:S(2)}) collective-permute-start(bf16[1,128,2048]{2,1,0:T(8,128)(2,1)} %get-tuple-element.251), channel_id=1, source_target_pairs={{0,2},{2,0},{4,6},{6,4},{1,3},{3,1},{5,7},{7,5},{8,10},{10,8},{12,... | collective-permute-start | bytes 1572872 | tf_op jit(solution)/shard_map/ppermute | solution.py:26
  535.0 19.2 %collective-permute-start.52 = (bf16[1,128,2048]{2,1,0:T(8,128)(2,1)}, bf16[1,128,2048]{2,1,0:T(8,128)(2,1)}, u32[]{:S(2)}, u32[]{:S(2)}) collective-permute-start(bf16[1,128,2048]{2,1,0:T(8,128)(2,1)} %get-tuple-element.250), channel_id=1, source_target_pairs={{0,4},{2,6},{4,0},{6,2},{1,5},{3,7},{5,1},{7,3},{8,12},{10,14},{12... | collective-permute-start | bytes 1572872 | tf_op jit(solution)/shard_map/ppermute | solution.py:26
  539.4 202.3 %reduce-scatter.8.cloned.1.call-start = ((), (), s32[]{:S(2)}) async-start(), calls=%async_computation.8 | async-start | bytes 4915200 | tf_op jit(solution)/shard_map/reduce_scatter | solution.py:116
  559.8 24.3 %collective-permute-start.56 = (bf16[2,128,2048]{2,1,0:T(8,128)(2,1)S(1)}, bf16[2,128,2048]{2,1,0:T(8,128)(2,1)S(1)}, u32[]{:S(2)}, u32[]{:S(2)}) collective-permute-start(bf16[2,128,2048]{2,1,0:T(8,128)(2,1)S(1)} %pad_maximum_fusion.24), channel_id=1, source_target_pairs={{0,2},{2,0},{4,6},{6,4},{1,3},{3,1},{5,7},{7,5},{8,10},{10,8},{12,... | collective-permute-start | bytes 3145736 | tf_op jit(solution)/shard_map/ppermute | solution.py:26
  561.0 24.0 %collective-permute-start.57 = (bf16[2,128,2048]{2,1,0:T(8,128)(2,1)S(1)}, bf16[2,128,2048]{2,1,0:T(8,128)(2,1)S(1)}, u32[]{:S(2)}, u32[]{:S(2)}) collective-permute-start(bf16[2,128,2048]{2,1,0:T(8,128)(2,1)S(1)} %pad_maximum_fusion.25), channel_id=1, source_target_pairs={{0,4},{2,6},{4,0},{6,2},{1,5},{3,7},{5,1},{7,3},{8,12},{10,14},{12... | collective-permute-start | bytes 3145736 | tf_op jit(solution)/shard_map/ppermute | solution.py:26
  615.0 37.6 %collective-permute-start.63 = (bf16[2048,960]{0,1:T(8,128)(2,1)}, bf16[2048,960]{0,1:T(8,128)(2,1)}, u32[]{:S(2)}, u32[]{:S(2)}) collective-permute-start(bf16[2048,960]{0,1:T(8,128)(2,1)} %pad_maximum_fusion.1), channel_id=1, source_target_pairs={{0,1},{1,0},{2,3},{3,2},{4,5},{5,4},{6,7},{7,6},{8,9},{9,8},{10,11... | collective-permute-start | bytes 11796488 | tf_op jit(solution)/shard_map/ppermute | solution.py:103
  633.0 41.7 %collective-permute-start.61 = (bf16[2,128,2048]{2,1,0:T(8,128)(2,1)}, bf16[2,128,2048]{2,1,0:T(8,128)(2,1)}, u32[]{:S(2)}, u32[]{:S(2)}) collective-permute-start(bf16[2,128,2048]{2,1,0:T(8,128)(2,1)} %get-tuple-element.208), channel_id=1, source_target_pairs={{0,1},{1,0},{2,3},{3,2},{4,5},{5,4},{6,7},{7,6},{8,9},{9,8},{10,11... | collective-permute-start | bytes 3145736 | tf_op jit(solution)/shard_map/ppermute | solution.py:103
  634.4 15.2 %collective-permute-start.70 = (bf16[80,368]{0,1:T(8,128)(2,1)S(1)}, bf16[80,368]{0,1:T(8,128)(2,1)S(1)}, u32[]{:S(2)}, u32[]{:S(2)}) collective-permute-start(bf16[80,368]{0,1:T(8,128)(2,1)S(1)} %bitcast.624), channel_id=1, source_target_pairs={{0,8},{8,16},{16,24},{24,0},{1,9},{9,17},{17,25},{25,1},{2,10},{10... | collective-permute-start | bytes 176648 | tf_op jit(solution)/shard_map/ppermute | solution.py:125
  635.2 16.5 %collective-permute-start.71 = (bf16[80,368]{0,1:T(8,128)(2,1)S(1)}, bf16[80,368]{0,1:T(8,128)(2,1)S(1)}, u32[]{:S(2)}, u32[]{:S(2)}) collective-permute-start(bf16[80,368]{0,1:T(8,128)(2,1)S(1)} %bitcast.625), channel_id=1, source_target_pairs={{0,16},{8,24},{16,0},{24,8},{1,17},{9,25},{17,1},{25,9},{2,18},{10... | collective-permute-start | bytes 176648 | tf_op jit(solution)/shard_map/ppermute | solution.py:125
  637.8 14.1 %collective-permute-start.72 = (bf16[80,368]{0,1:T(8,128)(2,1)S(1)}, bf16[80,368]{0,1:T(8,128)(2,1)S(1)}, u32[]{:S(2)}, u32[]{:S(2)}) collective-permute-start(bf16[80,368]{0,1:T(8,128)(2,1)S(1)} %bitcast.626), channel_id=1, source_target_pairs={{0,24},{8,0},{16,8},{24,16},{1,25},{9,1},{17,9},{25,17},{2,26},{10... | collective-permute-start | bytes 176648 | tf_op jit(solution)/shard_map/ppermute | solution.py:125
  663.4 18.6 %collective-permute-start.64 = (bf16[1,128,2048]{2,1,0:T(8,128)(2,1)}, bf16[1,128,2048]{2,1,0:T(8,128)(2,1)}, u32[]{:S(2)}, u32[]{:S(2)}) collective-permute-start(bf16[1,128,2048]{2,1,0:T(8,128)(2,1)} %get-tuple-element.241), channel_id=1, source_target_pairs={{0,4},{2,6},{4,0},{6,2},{1,5},{3,7},{5,1},{7,3},{8,12},{10,14},{12... | collective-permute-start | bytes 1572872 | tf_op jit(solution)/shard_map/ppermute | solution.py:26
  669.3 16.5 %collective-permute-start.66 = (bf16[1,128,2048]{2,1,0:T(8,128)(2,1)}, bf16[1,128,2048]{2,1,0:T(8,128)(2,1)}, u32[]{:S(2)}, u32[]{:S(2)}) collective-permute-start(bf16[1,128,2048]{2,1,0:T(8,128)(2,1)} %get-tuple-element.243), channel_id=1, source_target_pairs={{0,2},{2,0},{4,6},{6,4},{1,3},{3,1},{5,7},{7,5},{8,10},{10,8},{12,... | collective-permute-start | bytes 1572872 | tf_op jit(solution)/shard_map/ppermute | solution.py:26
  678.5 15.3 %collective-permute-start.83 = (bf16[128,1536]{1,0:T(8,128)(2,1)S(1)}, bf16[128,1536]{1,0:T(8,128)(2,1)S(1)}, u32[]{:S(2)}, u32[]{:S(2)}) collective-permute-start(bf16[128,1536]{1,0:T(8,128)(2,1)S(1)} %get-tuple-element.298), channel_id=1, source_target_pairs={{0,6},{2,4},{4,2},{6,0},{1,7},{3,5},{5,3},{7,1},{8,14},{10,12},{12... | collective-permute-start | bytes 1179656 | tf_op jit(solution)/shard_map/ppermute | solution.py:26
  678.5 20.5 %collective-permute-start.84 = (bf16[128,1536]{1,0:T(8,128)(2,1)S(1)}, bf16[128,1536]{1,0:T(8,128)(2,1)S(1)}, u32[]{:S(2)}, u32[]{:S(2)}) collective-permute-start(bf16[128,1536]{1,0:T(8,128)(2,1)S(1)} %get-tuple-element.297), channel_id=1, source_target_pairs={{0,4},{2,6},{4,0},{6,2},{1,5},{3,7},{5,1},{7,3},{8,12},{10,14},{12... | collective-permute-start | bytes 1179656 | tf_op jit(solution)/shard_map/ppermute | solution.py:26
  680.0 22.7 %collective-permute-start.85 = (bf16[128,1536]{1,0:T(8,128)(2,1)S(1)}, bf16[128,1536]{1,0:T(8,128)(2,1)S(1)}, u32[]{:S(2)}, u32[]{:S(2)}) collective-permute-start(bf16[128,1536]{1,0:T(8,128)(2,1)S(1)} %get-tuple-element.296), channel_id=1, source_target_pairs={{0,2},{2,0},{4,6},{6,4},{1,3},{3,1},{5,7},{7,5},{8,10},{10,8},{12,... | collective-permute-start | bytes 1179656 | tf_op jit(solution)/shard_map/ppermute | solution.py:26
  687.5 36.4 %collective-permute-start.65 = (bf16[2,128,2048]{2,1,0:T(8,128)(2,1)S(1)}, bf16[2,128,2048]{2,1,0:T(8,128)(2,1)S(1)}, u32[]{:S(2)}, u32[]{:S(2)}) collective-permute-start(bf16[2,128,2048]{2,1,0:T(8,128)(2,1)S(1)} %pad_maximum_fusion.26), channel_id=1, source_target_pairs={{0,2},{2,0},{4,6},{6,4},{1,3},{3,1},{5,7},{7,5},{8,10},{10,8},{12,... | collective-permute-start | bytes 3145736 | tf_op jit(solution)/shard_map/ppermute | solution.py:26
  689.8 34.1 %collective-permute-start.67 = (bf16[2,128,2048]{2,1,0:T(8,128)(2,1)S(1)}, bf16[2,128,2048]{2,1,0:T(8,128)(2,1)S(1)}, u32[]{:S(2)}, u32[]{:S(2)}) collective-permute-start(bf16[2,128,2048]{2,1,0:T(8,128)(2,1)S(1)} %pad_maximum_fusion.27), channel_id=1, source_target_pairs={{0,4},{2,6},{4,0},{6,2},{1,5},{3,7},{5,1},{7,3},{8,12},{10,14},{12... | collective-permute-start | bytes 3145736 | tf_op jit(solution)/shard_map/ppermute | solution.py:26
  730.8 18.8 %collective-permute-start.68 = (bf16[2,128,2048]{2,1,0:T(8,128)(2,1)}, bf16[2,128,2048]{2,1,0:T(8,128)(2,1)}, u32[]{:S(2)}, u32[]{:S(2)}) collective-permute-start(bf16[2,128,2048]{2,1,0:T(8,128)(2,1)} %get-tuple-element.204), channel_id=1, source_target_pairs={{0,1},{1,0},{2,3},{3,2},{4,5},{5,4},{6,7},{7,6},{8,9},{9,8},{10,11... | collective-permute-start | bytes 3145736 | tf_op jit(solution)/shard_map/ppermute | solution.py:103
  (196 other events, 2119.4 us)
Sparse Core Ops, SparseCore 0:
  39.3 73.8 all-gather.3
  150.0 113.2 all-gather.5
  266.3 63.9 all-gather.7
  402.0 57.1 reduce-scatter.3
  539.6 115.5 reduce-scatter.5
  657.8 78.0 reduce-scatter.7

commit v6 on v5

--- a/solution.py
+++ b/solution.py
@@ -40,12 +40,15 @@
     return [jnp.where(high, found[k ^ 2], found[k]) for k in range(PLANE)]
 
 
-def plane_gather(own):
+def plane_gather_first(own):
+    return own, to_partner(own, 1), to_partner(own, 2)
+
+
+def plane_gather_second(state):
+    own, from_x, from_y = state
     mine = lax.axis_index("j")
     streams, rows, width = own.shape
     half = streams // 2
-    from_x = to_partner(own, 1)
-    from_y = to_partner(own, 2)
     first = to_partner(from_x[:half], 2)
     second = to_partner(from_y[half:], 1)
     whole = jnp.zeros((streams, PLANE, rows, width), own.dtype)
@@ -56,6 +59,10 @@
     return whole.reshape(streams, PLANE * rows, width)
 
 
+def plane_gather(own):
+    return plane_gather_second(plane_gather_first(own))
+
+
 def plane_sum_first(part, streams):
     mine = lax.axis_index("j")
     part = part.astype(BF16).reshape(streams, PLANE, -1, part.shape[-1])
@@ -140,14 +147,14 @@
     return whole
 
 
-def sum_of_all(array):
+def sum_of_chip_plane(array):
     for axis, pairs in (
         ("c", [(0, 1), (1, 0)]),
         ("j", [(i, i ^ 1) for i in range(PLANE)]),
         ("j", [(i, i ^ 2) for i in range(PLANE)]),
     ):
         array = array + lax.ppermute(array, axis, pairs)
-    return jnp.sum(z_gather(array), axis=0)
+    return array
 
 
 def with_other_core(array, dim):
@@ -252,8 +259,92 @@
     return (retain, factor * entry_gate * conv_value)
 
 
-def mix_gelu(gate_value, up_value):
-    return jax.nn.gelu(gate_value) * up_value
+def mlp_kernel(
+    in_ref, down_ref, gate_w, up_w, narrow_w, act_ref, both_ref, second_ref, out_ref, *totals
+):
+    half, tile = pl.program_id(1), pl.program_id(2)
+    first = (half == 0) & (tile == 0)
+    last = (half == pl.num_programs(1) - 1) & (tile == pl.num_programs(2) - 1)
+    second_total, out_total = totals
+    wide = gate_w.shape[2]
+    hidden = wide * pl.num_programs(2)
+
+    def times(left, right, left_dim, right_dim):
+        return dot(left, right, left_dim, right_dim)
+
+    rows = in_ref[0]
+    gate = times(rows, gate_w[0], 1, 0)
+    up = times(rows, up_w[0], 1, 0)
+    d_act = times(down_ref[0], narrow_w[0], 1, 0)
+    scale = 0.7978845608028654
+    square = gate * gate
+    bent = jnp.tanh(scale * (gate + 0.044715 * square * gate))
+    gelu = 0.5 * gate * (1.0 + bent)
+    slope = 0.5 * (1.0 + bent) + (0.5 * scale) * gate * (1.0 - bent * bent) * (
+        1.0 + 0.134145 * square
+    )
+    act = (gelu * up).astype(BF16)
+    d_gate = (d_act * up * slope).astype(BF16)
+    d_up = (d_act * gelu).astype(BF16)
+    act_ref[0] = act
+    place = pl.multiple_of(tile * wide, wide)
+    both_ref[0, :, pl.ds(place, wide)] = d_gate
+    both_ref[0, :, pl.ds(pl.multiple_of(hidden + place, wide), wide)] = d_up
+    second = times(d_gate, gate_w[0], 1, 1) + times(d_up, up_w[0], 1, 1)
+    out = times(act, narrow_w[0], 1, 1)
+
+    @pl.when(first)
+    def _():
+        second_total[...] = second
+        out_total[...] = out
+
+    @pl.when(jnp.logical_not(first))
+    def _():
+        second_total[...] += second
+        out_total[...] += out
+
+    @pl.when(last)
+    def _():
+        second_ref[0] = second_total[...].astype(BF16)
+        out_ref[0] = out_total[...].astype(BF16)
+
+
+def mlp(second_low, d_down, weights, tiles):
+    streams, rows, width = second_low.shape
+    halves, _, columns = weights.shape
+    hidden = columns // 3
+    wide = hidden // tiles
+    token_block = pl.BlockSpec((1, rows, width), lambda s, h, t: (s, 0, 0))
+    weight_blocks = [
+        pl.BlockSpec((1, width, wide), lambda s, h, t, k=k: (h, 0, k * tiles + t)) for k in range(3)
+    ]
+    return pl.pallas_call(
+        mlp_kernel,
+        grid=(streams, halves, tiles),
+        in_specs=[token_block, token_block, *weight_blocks],
+        out_specs=[
+            pl.BlockSpec((1, rows, wide), lambda s, h, t: (h, s, t)),
+            pl.BlockSpec((1, rows, 2 * hidden), lambda s, h, t: (h, s, 0)),
+            token_block,
+            token_block,
+        ],
+        out_shape=[
+            jax.ShapeDtypeStruct((halves, streams * rows, hidden), BF16),
+            jax.ShapeDtypeStruct((halves, streams * rows, 2 * hidden), BF16),
+            jax.ShapeDtypeStruct(second_low.shape, BF16),
+            jax.ShapeDtypeStruct(second_low.shape, BF16),
+        ],
+        scratch_shapes=[pltpu.VMEM((rows, width), F32), pltpu.VMEM((rows, width), F32)],
+        compiler_params=pltpu.CompilerParams(
+            vmem_limit_bytes=60 * 1024 * 1024,
+            dimension_semantics=("arbitrary", "arbitrary", "arbitrary"),
+        ),
+        cost_estimate=pl.CostEstimate(
+            flops=12 * streams * rows * width * hidden * halves,
+            bytes_accessed=40 * 1024 * 1024,
+            transcendentals=streams * rows * hidden * halves,
+        ),
+    )(second_low, d_down, weights, weights, weights)
 
 
 def convolve(extended, conv_taps, conv_bias, fill_values, insides):
@@ -326,7 +417,8 @@
     )
     small_blocks = small[:, :small_rows].reshape(PLANE, -1, small_width)
     small = jnp.stack(plane_swap(jnp.concatenate([small_blocks, gain_rows], axis=1)))
-    whole_in = plane_gather(own_in)
+    in_state, later = lax.optimization_barrier((plane_gather_first(own_in), later))
+    whole_in = plane_gather_second(in_state)
     gains_all = small[:, part_width // PLANE :, :gain_width].reshape(PLANE, z_size, 2, gain_width)
     gains_all = jnp.moveaxis(gains_all, (0, 1, 2), (2, 1, 0))
     gains_all = gains_all.reshape(2, model_width).astype(F32)
@@ -347,10 +439,11 @@
         axis=1,
     )
 
-    wide_blocks = jnp.concatenate([to_chips(later[0]), to_chips(later[1])], axis=2)
-    wide_rows = jnp.concatenate(plane_swap(wide_blocks), axis=0)
-    narrow_rows = jnp.concatenate(plane_swap(to_chips(later[2].T)), axis=0)
-    own_cot, narrow_rows = lax.optimization_barrier((own_cot, narrow_rows))
+    later_blocks = jnp.concatenate(
+        [to_chips(later[0]), to_chips(later[1]), to_chips(later[2].T)], axis=2
+    )
+    later_rows = jnp.concatenate(plane_swap(later_blocks), axis=0)
+    own_cot, later_rows = lax.optimization_barrier((own_cot, later_rows))
 
     def live_at(position):
         second_start = spans[:, 0:1]
@@ -368,17 +461,17 @@
 
     d_out = own_cot.reshape(own_tokens, model_width).astype(F32)
     own_down = (d_out * own_live).astype(BF16).reshape(n_streams, own_rows, model_width)
-    d_down = plane_gather(own_down).reshape(tokens, model_width)
+    d_down = plane_gather(own_down)
 
     flat_in = own_in.reshape(own_tokens, model_width).astype(F32)
     _, norm_one_back = jax.vjp(rms_norm, flat_in, gains_all[0])
     normed_low = rms_norm(
         whole_in.reshape(tokens, model_width).astype(F32), gains_all[0]
     ).astype(BF16)
-    first_own, normed_low, wide_rows = lax.optimization_barrier(
-        (lax.all_gather(first_rows, "z", axis=0, tiled=True), normed_low, wide_rows)
-    )
-    wide_own = lax.all_gather(wide_rows, "z", axis=0, tiled=True)
+    first_own, normed_low, later_rows = lax.optimization_barrier(
+        (lax.all_gather(first_rows, "z", axis=0, tiled=True), normed_low, later_rows)
+    )
+    w_later = lax.all_gather(later_rows, ("c", "z"), axis=0)
     w_first = (first_own, to_core(first_own))
     w_rec = jnp.concatenate(
         [w[:, p * part_width : (p + 1) * part_width] for p in (0, 1) for w in w_first], axis=1
@@ -470,61 +563,48 @@
     states_flat = states.reshape(tokens, rec_width)
     mixed_rows = (states_flat * branch).astype(BF16)
     rec_part = dot(mixed_rows, w_back, 1, 1)
-    rec_total, wide_own, narrow_rows = lax.optimization_barrier(
-        (plane_sum(rec_part, n_streams), wide_own, narrow_rows)
-    )
-    rec_total = rec_total.reshape(own_tokens, model_width)
-    w_wide = (wide_own, to_core(wide_own))
-    w_narrow = along_z(narrow_rows)
+    rec_total = plane_sum(rec_part, n_streams).reshape(own_tokens, model_width)
     hidden_one = flat_in + own_live * rec_total
     normed_two, norm_two_back = jax.vjp(rms_norm, hidden_one, gains_all[1])
     own_second = normed_two.astype(BF16).reshape(n_streams, own_rows, model_width)
-    second_low = plane_gather(own_second).reshape(tokens, model_width)
-
-    second_part = 0.0
-    hidden, g_narrow, g_wide = [], [], []
-    for h in range(halves):
-        both = dot(second_low, w_wide[h], 1, 0)
-        activated, mix_back = jax.vjp(mix_gelu, both[:, :ff_part], both[:, ff_part:])
-        act_low = activated.astype(BF16)
-        hidden.append((act_low, mix_back))
-        g_narrow.append(dot(d_down, act_low, 0, 0).astype(BF16))
-    sum_narrow = both_cores(*g_narrow)
-    for h, (act_low, mix_back) in enumerate(hidden):
-        d_act = dot(d_down, w_narrow[h], 1, 0)
-        d_both = jnp.concatenate([d.astype(BF16) for d in mix_back(d_act)], axis=1)
-        second_part = second_part + dot(d_both, w_wide[h], 1, 1)
-        g_wide.append(dot(second_low, d_both, 0, 0).astype(BF16))
-    second_part, sum_narrow = lax.optimization_barrier((second_part, sum_narrow))
-    sum_narrow = sum_along_z(sum_narrow)
+    second_state, w_later = lax.optimization_barrier((plane_gather_first(own_second), w_later))
+    second_low = plane_gather_second(second_state)
+    w_later = w_later.reshape(halves, model_width, 3 * ff_part)
+    acts, d_both, second_part, down_part = mlp(second_low, d_down, w_later, 1)
+    second_low = second_low.reshape(tokens, model_width)
+    d_down = d_down.reshape(tokens, model_width)
+
+    def mine_and_other(array):
+        return at(array, core, 0), at(array, 1 - core, 0)
+
+    g_narrow = [dot(d_down, act, 0, 0).astype(BF16) for act in mine_and_other(acts)]
+    g_wide = [dot(second_low, d, 0, 0).astype(BF16) for d in mine_and_other(d_both)]
+    sum_narrow = sum_along_z(both_cores(*g_narrow))
 
     second_total = plane_sum(second_part, n_streams).reshape(own_tokens, model_width)
     d_hidden_norm, g_gain_two = norm_two_back(second_total)
     d_hidden = d_out + d_hidden_norm
     own_rec = (d_hidden * own_live).astype(BF16).reshape(n_streams, own_rows, model_width)
     d_rec = plane_gather(own_rec).reshape(tokens, model_width)
-    d_rec, g_wide, sum_narrow = lax.optimization_barrier((d_rec, g_wide, sum_narrow))
-    sum_wide = both_cores(*g_wide)
+    d_rec, sum_wide, sum_narrow = lax.optimization_barrier(
+        (d_rec, both_cores(*g_wide), sum_narrow)
+    )
+    sum_wide = sum_along_z(sum_wide)
     d_mixed = dot(d_rec, w_back, 1, 0)
-    acts = [act_low for act_low, _ in hidden]
-    d_mixed, sum_wide, sum_narrow, acts = lax.optimization_barrier(
-        (d_mixed, sum_wide, sum_narrow, acts)
-    )
-    down_part = sum(dot(act_low, w, 1, 1) for act_low, w in zip(acts, w_narrow))
+    d_mixed, down_part = lax.optimization_barrier((d_mixed, down_part))
     mlp_sum = plane_sum_first(down_part, n_streams)
-    sum_wide = sum_along_z(sum_wide)
     g_back = dot(d_rec, mixed_rows, 0, 0).astype(BF16)
 
     grad_state = (d_mixed * branch).reshape(n_streams, n_rows, rec_width)
     branch_low = branch_back(d_mixed * states_flat)[0].astype(BF16)
     next_keep = jnp.concatenate([retain_eff[:, 1:], jnp.ones_like(retain_eff[:, :1])], axis=1)
     later_keep, later_sum = local_scan(next_keep, grad_state, True)
-    later_sum, mlp_sum = lax.optimization_barrier((later_sum, mlp_sum))
+    carried_grad = entering(
+        retain_eff[:, 0] * later_keep[:, 0], retain_eff[:, 0] * later_sum[:, 0], True
+    )
+    carried_grad, mlp_sum = lax.optimization_barrier((carried_grad, mlp_sum))
     mlp_sum = plane_sum_second(mlp_sum)
     out_narrow = to_owners(sum_narrow)
-    carried_grad = entering(
-        retain_eff[:, 0] * later_keep[:, 0], retain_eff[:, 0] * later_sum[:, 0], True
-    )
     adjoint = later_sum + later_keep * carried_grad[:, None]
     state_prev = jnp.concatenate([state_before[:, None], states[:, :-1]], axis=1)
     state_prev = jnp.where(reset_rows, carried, state_prev)
@@ -535,6 +615,42 @@
     rate_low = d_rate.astype(BF16)
     entry_low = d_entry.astype(BF16)
     grad_gates = jnp.concatenate([rate_low, entry_low], axis=1)
+    d_conv_gates = dot(grad_gates, gates_all, 1, 1)
+    d_conv = (d_conv_direct + d_conv_gates).reshape(n_streams, n_rows, rec_width)
+    d_extended, g_taps, g_conv_bias = conv_back(d_conv)
+    rim_grad = shifted(d_extended[:, :3].astype(BF16), -1).astype(F32)
+    d_source = jnp.concatenate([d_extended[:, 3:n_rows], d_extended[:, n_rows:] + rim_grad], axis=1)
+    d_projected = jnp.concatenate(
+        [d_source.reshape(tokens, rec_width).astype(BF16), branch_low], axis=1
+    )
+    d_projected, sum_wide, mlp_total, out_narrow = lax.optimization_barrier(
+        (d_projected, sum_wide, mlp_sum, out_narrow)
+    )
+    mlp_total = mlp_total.reshape(own_tokens, model_width)
+    out_flat = (hidden_one + own_live * mlp_total).astype(BF16)
+    output = all_streams(out_flat.reshape(n_streams, own_rows, model_width))
+
+    g_rec = dot(normed_low, d_projected, 0, 0).astype(BF16)
+    mine, other = (
+        jnp.concatenate(
+            [
+                g[:, start + h * part_width : start + (h + 1) * part_width]
+                for g, start in ((g_rec, 0), (g_rec, rec_width), (g_back, 0))
+            ],
+            axis=1,
+        )
+        for h in range(halves)
+    )
+    sum_first = both_cores(mine, other)
+    sum_first, d_projected, grad_gates = lax.optimization_barrier(
+        (sum_first, d_projected, grad_gates)
+    )
+    sum_first = sum_along_z(sum_first)
+    first_part = dot(d_projected, w_rec, 1, 1)
+    whole_flat = whole_in.reshape(tokens, model_width).astype(F32)
+    whole_factor = lax.rsqrt(jnp.mean(whole_flat * whole_flat, axis=-1, keepdims=True) + EPSILON)
+    g_gain_one = jnp.sum(first_part * whole_flat * whole_factor, axis=0)
+    g_gains = sum_of_chip_plane(jnp.stack([g_gain_one, g_gain_two]))
     g_gates = dot(conv_low, grad_gates, 0, 0)
     g_gates = jnp.concatenate(
         [
@@ -552,33 +668,6 @@
         ],
         axis=0,
     )
-    grad_gates, mlp_total, out_narrow = lax.optimization_barrier((grad_gates, mlp_sum, out_narrow))
-    mlp_total = mlp_total.reshape(own_tokens, model_width)
-    out_flat = (hidden_one + own_live * mlp_total).astype(BF16)
-    output = all_streams(out_flat.reshape(n_streams, own_rows, model_width))
-
-    d_conv_gates = dot(grad_gates, gates_all, 1, 1)
-    d_conv = (d_conv_direct + d_conv_gates).reshape(n_streams, n_rows, rec_width)
-    d_extended, g_taps, g_conv_bias = conv_back(d_conv)
-    rim_grad = shifted(d_extended[:, :3].astype(BF16), -1).astype(F32)
-    d_source = jnp.concatenate([d_extended[:, 3:n_rows], d_extended[:, n_rows:] + rim_grad], axis=1)
-    d_projected = jnp.concatenate(
-        [d_source.reshape(tokens, rec_width).astype(BF16), branch_low], axis=1
-    )
-    first_part = dot(d_projected, w_rec, 1, 1)
-    g_rec = dot(normed_low, d_projected, 0, 0).astype(BF16)
-    sum_first = both_cores(
-        *(
-            jnp.concatenate(
-                [
-                    g[:, start + h * part_width : start + (h + 1) * part_width]
-                    for g, start in ((g_rec, 0), (g_rec, rec_width), (g_back, 0))
-                ],
-                axis=1,
-            )
-            for h in range(halves)
-        )
-    )
     g_small = jnp.concatenate(
         [
             g_taps,
@@ -592,9 +681,8 @@
         axis=1,
     ).astype(BF16)
     sum_small = both_cores(g_small[:part_width], g_small[part_width:])
-    first_part, sum_first, sum_wide = lax.optimization_barrier((first_part, sum_first, sum_wide))
-    out_wide = to_owners(sum_wide)
-    sum_first = sum_along_z(sum_first)
+    sum_first, sum_small, g_gains = lax.optimization_barrier((sum_first, sum_small, g_gains))
+    g_gains = jnp.sum(z_gather(g_gains), axis=0)
     out_first = to_owners(sum_first)
     g_small = sent_along_z(sum_small)
     route = [(z * PLANE + j, j * z_size + z) for z in range(z_size) for j in range(PLANE)]
@@ -605,12 +693,13 @@
     state_block = (finals[:, :, 0] + finals[:, :, 1])[:, :, None]
     conv_block = finals[:, :, 2:].astype(BF16)[:, :, :, None]
 
-    first_total = plane_sum(first_part, n_streams).reshape(own_tokens, model_width)
-    d_input_norm, g_gain_one = norm_one_back(first_total)
+    first_total, sum_wide = lax.optimization_barrier((plane_sum(first_part, n_streams), sum_wide))
+    first_total = first_total.reshape(own_tokens, model_width)
+    out_wide = to_owners(sum_wide)
+    d_input_norm = norm_one_back(first_total)[0]
     input_grad = all_streams(
         (d_hidden + d_input_norm).astype(BF16).reshape(n_streams, own_rows, model_width)
     )
-    g_gains = sum_of_all(jnp.stack([g_gain_one, g_gain_two]))
     g_gains = lax.dynamic_slice_in_dim(g_gains, dp_index * gain_width, gain_width, 1)
 
     def flat(blocks, start, stop):

time: 782 us -> 771 us (0.986)
  matrix products: 166 us -> 95.5 us
  Pallas kernels: 16.9 us -> 70.9 us
  starting transfers between devices: 110 us -> 96.7 us
  local copies, waits for them, and re-layouts: 111 us -> 121 us
  other arithmetic: 105 us -> 113 us
    dot_general x21 -> x13, matrix products: 159 us -> 88.9 us  [dot(): lax.dot_general(left, right, (((left_dim,), (right_dim,)), ((), ())), pre...]
    pallas_call x0 -> x1, Pallas kernels: none -> 54.1 us  [mlp(): pl.pallas_call(mlp_kernel, grid=(streams, halves, tiles), in_specs=[token...]
    reduce_scatter x3, waiting for transfers between devices: 0.02 us -> 30.6 us  [sum_along_z(): return lax.psum_scatter(total, 'z', scatter_dimension=0, tiled=True)]
    ppermute x53 -> x50, waiting for transfers between devices: 218 us -> 189 us  [to_partner(): return lax.ppermute(block, 'j', [(i, i ^ bit) for i in range(PLANE)])]
    ppermute x3, waiting for transfers between devices: 3.31 us -> 19.5 us  [sum_of_chip_plane(): array = array + lax.ppermute(array, axis, pairs)]
    unnamed x349 -> x281, local copies, waits for them, and re-layouts: 35.3 us -> 21.4 us
    ppermute x53 -> x50, starting transfers between devices: 70 us -> 57.4 us  [to_partner(): return lax.ppermute(block, 'j', [(i, i ^ bit) for i in range(PLANE)])]
    all_gather x2 -> x1, waiting for transfers between devices: 12.6 us -> 0.21 us  [shards(): w_later = lax.all_gather(later_rows, ('c', 'z'), axis=0)]
  transfers between devices with their start and end apart: 92 -> 86, of which waited for: 43 -> 36; matrix products, arithmetic and copies ran while one was open for 41% -> 37% of each run, Pallas kernels for 2% -> 2%
where the time goes in v6:
time: 771 us; the launch traced here: 762 us
  waiting for transfers between devices  248 us (32%)
  local copies, waits for them, and re-layouts  121 us (16%)
  other arithmetic  113 us (15%)
  starting transfers between devices  96.7 us (13%)
  matrix products  95.5 us (12%)
  Pallas kernels  70.9 us (9%)
  between operations  17 us (2%)
    ppermute x50, waiting for transfers between devices, to_partner(): return lax.ppermute(block, 'j', [(i, i ^ bit) for i in range(PLANE)])  189 us
    dot_general x13, matrix products, dot(): lax.dot_general(left, right, (((left_dim,), (right_dim,)), ((), ())), pre...  88.9 us
    ppermute x50, starting transfers between devices, to_partner(): return lax.ppermute(block, 'j', [(i, i ^ bit) for i in range(PLANE)])  57.4 us
    pallas_call x1, Pallas kernels, mlp(): pl.pallas_call(mlp_kernel, grid=(streams, halves, tiles), in_specs=[token...  54.1 us
    reduce_scatter x3, waiting for transfers between devices, sum_along_z(): return lax.psum_scatter(total, 'z', scatter_dimension=0, tiled=True)  30.6 us
    unnamed x281, local copies, waits for them, and re-layouts  21.4 us
    ppermute x3, waiting for transfers between devices, sum_of_chip_plane(): array = array + lax.ppermute(array, axis, pairs)  19.5 us
    dynamic_update_slice x17, local copies, waits for them, and re-layouts, put(): return lax.dynamic_update_index_in_dim(whole, block, index, axis)  17.8 us
  transfers between devices with their start and end apart: 86, of which 36 were waited for; matrix products, arithmetic and copies ran while one was open for 37% of the time, Pallas kernels for 2%

profile of v6, /device:TPU:0, one launch (start us, length us, event | category | flops | bytes accessed | tf_op | source)
XLA Modules:
  0.0 762.3 jit_solution(8194034913958704240)
XLA Ops:
  9.8 3.0 collective-permute-start.3
  12.8 2.6 collective-permute-start.4
  22.0 2.4 collective-permute-start
  26.7 5.4 collective-permute-done
  32.1 3.2 collective-permute-done.1
  46.1 19.9 %collective-permute-done.6 = bf16[88,328]{1,0:T(8,128)(2,1)S(1)} collective-permute-done((bf16[88,328]{1,0:T(8,128)(2,1)S(1)}, bf16[88,328]{1,0:T(8,128)(2,1)S(1)}, u32[]{:S(2)}, u32[]{:S(2)}) %collective-permute-start.6) | collective-permute-done | bytes 57760 | tf_op jit(solution)/shard_map/ppermute | solution.py:26
  88.7 2.6 broadcast.852.clone
  95.9 19.0 %collective-permute-done.12 = bf16[1,128,2048]{2,1,0:T(8,128)(2,1)} collective-permute-done((bf16[1,128,2048]{2,1,0:T(8,128)(2,1)}, bf16[1,128,2048]{2,1,0:T(8,128)(2,1)}, u32[]{:S(2)}, u32[]{:S(2)}) %collective-permute-start.12) | collective-permute-done | bytes 524320 | tf_op jit(solution)/shard_map/ppermute | solution.py:26
  117.3 3.1 fusion
  120.4 5.2 fusion.2
  133.8 5.0 collective-permute-done.9
  139.7 3.7 fusion.154
  143.4 4.5 fusion.155
  147.9 5.6 fusion.65
  153.8 3.0 collective-permute-start.18
  160.7 2.8 multiply_add_fusion.2
  166.0 3.1 bitcast_multiply_fusion.7
  169.9 7.8 %shard_map.246 = (f32[2,512,640]{2,1,0:T(8,128)S(1)}, f32[2,512,640]{2,1,0:T(8,128)S(1)}) custom-call(f32[2,512,640]{2,1,0:T(8,128)S(1)} %get-tuple-element.289.keep_ref, f32[2,512,640]{2,1,0:T(8,128)S(1)} %get-tuple-element.288.add_ref), custom_call_target="tpu_custom_call" | custom-call | flops 5242880 | bytes 10485760 | tf_op jit(solution)/shard_map/pallas_call | solution.py:233
  181.8 4.1 collective-permute-start.23
  187.3 2.9 collective-permute-start.22
  191.2 2.9 multiply_add_fusion.1
  194.1 4.0 fusion.33
  198.2 3.6 convolution_convert_fusion.3
  210.1 6.9 collective-permute-done.24
  222.1 17.9 %collective-permute-done.32 = bf16[2,128,2048]{2,1,0:T(8,128)(2,1)} collective-permute-done((bf16[2,128,2048]{2,1,0:T(8,128)(2,1)}, bf16[2,128,2048]{2,1,0:T(8,128)(2,1)}, u32[]{:S(2)}, u32[]{:S(2)}) %collective-permute-start.32) | collective-permute-done | bytes 1048608 | tf_op jit(solution)/shard_map/ppermute | solution.py:26
  244.4 18.1 %collective-permute-done.25 = bf16[2,128,2048]{2,1,0:T(8,128)(2,1)} collective-permute-done((bf16[2,128,2048]{2,1,0:T(8,128)(2,1)}, bf16[2,128,2048]{2,1,0:T(8,128)(2,1)}, u32[]{:S(2)}, u32[]{:S(2)}) %collective-permute-start.25) | collective-permute-done | bytes 1048608 | tf_op jit(solution)/shard_map/ppermute | solution.py:26
  262.5 2.8 multiply_reduce_fusion.7
  273.8 19.7 %collective-permute-done.28 = bf16[2,128,2048]{2,1,0:T(8,128)(2,1)S(1)} collective-permute-done((bf16[2,128,2048]{2,1,0:T(8,128)(2,1)S(1)}, bf16[2,128,2048]{2,1,0:T(8,128)(2,1)S(1)}, u32[]{:S(2)}, u32[]{:S(2)}) %collective-permute-start.28) | collective-permute-done | bytes 1048608 | tf_op jit(solution)/shard_map/ppermute | solution.py:26
  299.9 2.5 broadcast.852.clone.1
  306.9 3.0 collective-permute-done.30
  313.3 54.1 %shard_map.247 = (bf16[2,1024,768]{2,1,0:T(8,128)(2,1)}, bf16[2,1024,1536]{2,1,0:T(8,128)(2,1)}, bf16[2,512,2048]{2,1,0:T(8,128)(2,1)}, bf16[2,512,2048]{2,1,0:T(8,128)(2,1)}) custom-call(bf16[2,512,2048]{2,1,0:T(8,128)(2,1)} %bitcast.90.in_ref, bf16[2,512,2048]{2,1,0:T(8,128)(2,1)} %bitcast.560, bf16[2,2048,2304]{2,1,0:T(8,128)(2,1)} %bitcast.614, ...), custom_call_target="tpu_custom_call" | custom-call | flops 38654705664 | bytes 41943040 | tf_op jit(solution)/shard_map/pallas_call | solution.py:321
  367.4 8.0 %convolution_convert_fusion.4 = bf16[2048,768]{1,0:T(8,128)(2,1)} fusion(bf16[1024,2048]{1,0:T(8,128)(2,1)} %bitcast.561, bf16[2,1024,768]{2,1,0:T(8,128)(2,1)} %get-tuple-element.91, s32[]{:T(128)S(6)} %select_n.658), kind=kOutput, calls=%fused_computation.28 | convolution fusion | flops 3222798336 | bytes 8912900 | tf_op jit(solution)/shard_map/dot_general | solution.py:20
  378.7 11.0 %convolution_convert_fusion.1 = bf16[2048,1536]{1,0:T(8,128)(2,1)} fusion(bf16[1024,2048]{1,0:T(8,128)(2,1)} %bitcast.118, bf16[2,1024,1536]{2,1,0:T(8,128)(2,1)S(1)} %bitcast.618, s32[]{:T(128)S(6)} %select_n.658), kind=kOutput, calls=%fused_computation.11 | convolution fusion | flops 6445596672 | bytes 13631492 | tf_op jit(solution)/shard_map/dot_general | solution.py:20
  398.7 6.9 add_convert_fusion.2
  405.8 13.6 %collective-permute-done.37 = bf16[2,128,2048]{2,1,0:T(8,128)(2,1)} collective-permute-done((bf16[2,128,2048]{2,1,0:T(8,128)(2,1)}, bf16[2,128,2048]{2,1,0:T(8,128)(2,1)}, u32[]{:S(2)}, u32[]{:S(2)}) %collective-permute-start.37) | collective-permute-done | bytes 1048608 | tf_op jit(solution)/shard_map/ppermute | solution.py:26
  421.8 3.3 multiply_reduce_fusion.5
  425.1 2.4 broadcast.852
  428.0 4.9 bitcast_dynamic-update-slice_fusion.2
  436.7 19.8 %collective-permute-done.40 = bf16[2,128,2048]{2,1,0:T(8,128)(2,1)} collective-permute-done((bf16[2,128,2048]{2,1,0:T(8,128)(2,1)}, bf16[2,128,2048]{2,1,0:T(8,128)(2,1)}, u32[]{:S(2)}, u32[]{:S(2)}) %collective-permute-start.40) | collective-permute-done | bytes 1048608 | tf_op jit(solution)/shard_map/ppermute | solution.py:26
  465.3 3.5 collective-permute-done.42
  471.9 12.0 %add_convert_fusion = bf16[2048,1536]{1,0:T(8,128)(2,1)} fusion(bf16[2048,1536]{1,0:T(8,128)(2,1)} %collective-permute-done.44, bf16[1024,2048]{1,0:T(8,128)(2,1)} %bitcast.118, bf16[2,1024,1536]{2,1,0:T(8,128)(2,1)S(1)} %bitcast.620, s32[]{:T(128)S(6)} %select_n.657), kind=kOutput, calls=%fused_computation | convolution fusion | flops 6458179584 | bytes 19922948 | tf_op jit(solution)/shard_map/dot_general | solution.py:20
  484.6 6.2 fusion.45
  490.9 4.4 fusion.63
  495.2 9.1 %shard_map.248 = (f32[2,512,640]{2,1,0:T(8,128)S(1)}, f32[2,512,640]{2,1,0:T(8,128)S(1)}) custom-call(f32[2,512,640]{2,1,0:T(8,128)S(1)} %copy-done.2, f32[2,512,640]{2,1,0:T(8,128)S(1)} %bitcast.545), custom_call_target="tpu_custom_call" | custom-call | flops 5242880 | bytes 10485760 | tf_op jit(solution)/shard_map/pallas_call | solution.py:233
  510.9 5.1 convolution_convert_fusion.7
  535.4 4.4 multiply_reduce_fusion
  539.8 4.0 fusion.147
  544.0 7.8 %multiply_reduce_fusion.4 = (f32[640]{0:T(1024)S(1)}, f32[640]{0:T(1024)S(1)}, f32[640]{0:T(1024)S(1)}, f32[640]{0:T(1024)S(1)}, f32[1024,640]{1,0:T(8,128)S(1)}) fusion(f32[2,512,640]{2,1,0:T(8,128)} %get-tuple-element.405, f32[2,512,640]{2,1,0:T(8,128)S(1)} %copy-done.27, f32[2,512,640]{2,1,0:T(8,128)S(1)} %copy-done.25, ...), kind=kOutput, calls=%fused_computation.86 | convolution fusion | flops 1700656640 | bytes 25249280 | tf_op jit(solution)/shard_map/dot_general | solution.py:20
  561.6 3.7 fusion.41
  565.4 28.1 %reduce-scatter.6.cloned.1.call-done = bf16[512,1536]{1,0:T(8,128)(2,1)} async-done(((bf16[2048,1536]{1,0:T(8,128)(2,1)}), bf16[512,1536]{1,0:T(8,128)(2,1)}) %reduce-scatter.6.cloned.1.call-update) | async-done | bytes 1572880 | tf_op jit(solution)/shard_map/reduce_scatter | solution.py:123
  593.5 8.5 %convolution_convert_fusion = bf16[2048,1280]{0,1:T(8,128)(2,1)S(1)} fusion(bf16[1024,2048]{1,0:T(8,128)(2,1)} %fusion.2, bf16[1024,1280]{1,0:T(8,128)(2,1)} %pad_maximum_fusion.4), kind=kOutput, calls=%fused_computation.10 | convolution fusion | flops 5371330560 | bytes 12058624 | tf_op jit(solution)/shard_map/dot_general | solution.py:20
  610.5 2.6 dynamic_update_slice.114
  630.7 5.0 add_convert_fusion.1
  635.7 8.5 %fusion.4 = (f32[2048]{0:T(1024)S(1)}, bf16[1024,2048]{1,0:T(8,128)(2,1)S(1)}) fusion(bf16[2,4,128,2048]{3,2,1,0:T(8,128)(2,1)} %fusion.51, f32[1024]{0:T(1024)S(1)} %bitcast.611, bf16[1024,1280]{1,0:T(8,128)(2,1)S(1)} %copy-done.54, bf16[2048,320]{0,1:T(8,128)(2,1)} %copy-done.71, bf16[2048,320]{0,1:T(8,128)(2,1)} %copy-done.69, ...), kind=kOutput, calls=%fused_computation.8 | convolution fusion | flops 5400164352 | bytes 16265216 | tf_op jit(solution)/shard_map/dot_general | solution.py:20
  650.8 3.2 convolution_convert_fusion.6
  654.9 7.5 collective-permute-done.59
  674.9 19.5 %collective-permute-done.67 = f32[2,2048]{1,0:T(2,128)S(1)} collective-permute-done((f32[2,2048]{1,0:T(2,128)S(1)}, f32[2,2048]{1,0:T(2,128)S(1)}, u32[]{:S(2)}, u32[]{:S(2)}) %collective-permute-start.67) | collective-permute-done | bytes 16416 | tf_op jit(solution)/shard_map/ppermute | solution.py:156
  694.5 2.6 fusion.40
  704.5 5.8 collective-permute-done.78
  710.2 5.3 collective-permute-done.79
  719.5 2.4 reduce-scatter.8.cloned.1.call-done
  724.9 2.7 collective-permute-start.74
  730.7 3.3 collective-permute-start.70
  744.8 2.9 collective-permute-done.75
  (673 shorter events, 262.6 us)
Async XLA Ops:
  7.2 121.6 %all-gather.4.cloned.1.call-start = ((), (), s32[]{:S(2)}) async-start(), calls=%async_computation.3 | async-start | bytes 4915200 | tf_op jit(solution)/shard_map/all_gather | solution.py:472
  9.8 15.4 %collective-permute-start.3 = (bf16[82,328]{1,0:T(8,128)(2,1)}, bf16[82,328]{1,0:T(8,128)(2,1)}, u32[]{:S(2)}, u32[]{:S(2)}) collective-permute-start(bf16[82,328]{1,0:T(8,128)(2,1)} %get-tuple-element.241), channel_id=1, source_target_pairs={{0,8},{8,16},{16,24},{24,0},{1,9},{9,17},{17,25},{25,1},{2,10},{10... | collective-permute-start | bytes 161384 | tf_op jit(solution)/shard_map/ppermute | solution.py:145
  12.8 13.9 %collective-permute-start.4 = (bf16[82,328]{1,0:T(8,128)(2,1)}, bf16[82,328]{1,0:T(8,128)(2,1)S(1)}, u32[]{:S(2)}, u32[]{:S(2)}) collective-permute-start(bf16[82,328]{1,0:T(8,128)(2,1)} %get-tuple-element.241), channel_id=1, source_target_pairs={{0,16},{8,24},{16,0},{24,8},{1,17},{9,25},{17,1},{25,9},{2,18},{10... | collective-permute-start | bytes 161384 | tf_op jit(solution)/shard_map/ppermute | solution.py:145
  37.6 30.9 %collective-permute-start.10 = (bf16[2,128,2048]{2,1,0:T(8,128)(2,1)S(1)}, bf16[2,128,2048]{2,1,0:T(8,128)(2,1)S(1)}, u32[]{:S(2)}, u32[]{:S(2)}) collective-permute-start(bf16[2,128,2048]{2,1,0:T(8,128)(2,1)S(1)} %constant_dynamic-slice_fusion.24), channel_id=1, source_target_pairs={{0,2},{2,0},{4,6},{6,4},{1,3},{3,1},{5,7},{7,5},{8,10},{10,8},{12,... | collective-permute-start | bytes 3145736 | tf_op jit(solution)/shard_map/ppermute | solution.py:26
  39.1 30.4 %collective-permute-start.11 = (bf16[2,128,2048]{2,1,0:T(8,128)(2,1)S(1)}, bf16[2,128,2048]{2,1,0:T(8,128)(2,1)}, u32[]{:S(2)}, u32[]{:S(2)}) collective-permute-start(bf16[2,128,2048]{2,1,0:T(8,128)(2,1)S(1)} %constant_dynamic-slice_fusion.24), channel_id=1, source_target_pairs={{0,4},{2,6},{4,0},{6,2},{1,5},{3,7},{5,1},{7,3},{8,12},{10,14},{12... | collective-permute-start | bytes 3145736 | tf_op jit(solution)/shard_map/ppermute | solution.py:26
  40.1 25.9 %collective-permute-start.6 = (bf16[88,328]{1,0:T(8,128)(2,1)S(1)}, bf16[88,328]{1,0:T(8,128)(2,1)S(1)}, u32[]{:S(2)}, u32[]{:S(2)}) collective-permute-start(bf16[88,328]{1,0:T(8,128)(2,1)S(1)} %get-tuple-element.355), channel_id=1, source_target_pairs={{0,6},{2,4},{4,2},{6,0},{1,7},{3,5},{5,3},{7,1},{8,14},{10,12},{12... | collective-permute-start | bytes 173192 | tf_op jit(solution)/shard_map/ppermute | solution.py:26
  41.3 25.5 %collective-permute-start.7 = (bf16[88,328]{1,0:T(8,128)(2,1)S(1)}, bf16[88,328]{1,0:T(8,128)(2,1)S(1)}, u32[]{:S(2)}, u32[]{:S(2)}) collective-permute-start(bf16[88,328]{1,0:T(8,128)(2,1)S(1)} %get-tuple-element.356), channel_id=1, source_target_pairs={{0,4},{2,6},{4,0},{6,2},{1,5},{3,7},{5,1},{7,3},{8,12},{10,14},{12... | collective-permute-start | bytes 173192 | tf_op jit(solution)/shard_map/ppermute | solution.py:26
  42.8 24.6 %collective-permute-start.8 = (bf16[88,328]{1,0:T(8,128)(2,1)S(1)}, bf16[88,328]{1,0:T(8,128)(2,1)}, u32[]{:S(2)}, u32[]{:S(2)}) collective-permute-start(bf16[88,328]{1,0:T(8,128)(2,1)S(1)} %get-tuple-element.354), channel_id=1, source_target_pairs={{0,2},{2,0},{4,6},{6,4},{1,3},{3,1},{5,7},{7,5},{8,10},{10,8},{12,... | collective-permute-start | bytes 173192 | tf_op jit(solution)/shard_map/ppermute | solution.py:26
  43.7 251.0 %all-gather.6.cloned.1.call-start = ((), (), s32[]{:S(2)}) async-start(), calls=%async_computation.7 | async-start | bytes 21233664 | tf_op jit(solution)/shard_map/all_gather | solution.py:474
  76.2 49.4 %collective-permute-start.14 = (bf16[128,2304]{1,0:T(8,128)(2,1)}, bf16[128,2304]{1,0:T(8,128)(2,1)}, u32[]{:S(2)}, u32[]{:S(2)}) collective-permute-start(bf16[128,2304]{1,0:T(8,128)(2,1)} %bitcast.584), channel_id=1, source_target_pairs={{0,6},{2,4},{4,2},{6,0},{1,7},{3,5},{5,3},{7,1},{8,14},{10,12},{12... | collective-permute-start | bytes 1769480 | tf_op jit(solution)/shard_map/ppermute | solution.py:26
  79.8 45.8 %collective-permute-start.15 = (bf16[128,2304]{1,0:T(8,128)(2,1)}, bf16[128,2304]{1,0:T(8,128)(2,1)}, u32[]{:S(2)}, u32[]{:S(2)}) collective-permute-start(bf16[128,2304]{1,0:T(8,128)(2,1)} %bitcast.585), channel_id=1, source_target_pairs={{0,4},{2,6},{4,0},{6,2},{1,5},{3,7},{5,1},{7,3},{8,12},{10,14},{12... | collective-permute-start | bytes 1769480 | tf_op jit(solution)/shard_map/ppermute | solution.py:26
  82.4 43.2 %collective-permute-start.16 = (bf16[128,2304]{1,0:T(8,128)(2,1)}, bf16[128,2304]{1,0:T(8,128)(2,1)}, u32[]{:S(2)}, u32[]{:S(2)}) collective-permute-start(bf16[128,2304]{1,0:T(8,128)(2,1)} %bitcast.586), channel_id=1, source_target_pairs={{0,2},{2,0},{4,6},{6,4},{1,3},{3,1},{5,7},{7,5},{8,10},{10,8},{12,... | collective-permute-start | bytes 1769480 | tf_op jit(solution)/shard_map/ppermute | solution.py:26
  84.8 30.2 %collective-permute-start.12 = (bf16[1,128,2048]{2,1,0:T(8,128)(2,1)}, bf16[1,128,2048]{2,1,0:T(8,128)(2,1)}, u32[]{:S(2)}, u32[]{:S(2)}) collective-permute-start(bf16[1,128,2048]{2,1,0:T(8,128)(2,1)} %slice.487), channel_id=1, source_target_pairs={{0,4},{2,6},{4,0},{6,2},{1,5},{3,7},{5,1},{7,3},{8,12},{10,14},{12... | collective-permute-start | bytes 1572872 | tf_op jit(solution)/shard_map/ppermute | solution.py:26
  87.0 28.0 %collective-permute-start.13 = (bf16[1,128,2048]{2,1,0:T(8,128)(2,1)}, bf16[1,128,2048]{2,1,0:T(8,128)(2,1)}, u32[]{:S(2)}, u32[]{:S(2)}) collective-permute-start(bf16[1,128,2048]{2,1,0:T(8,128)(2,1)} %slice.488), channel_id=1, source_target_pairs={{0,2},{2,0},{4,6},{6,4},{1,3},{3,1},{5,7},{7,5},{8,10},{10,8},{12,... | collective-permute-start | bytes 1572872 | tf_op jit(solution)/shard_map/ppermute | solution.py:26
  128.9 355.1 %reduce-scatter.4.cloned.1.call-start = ((), (), s32[]{:S(2)}) async-start(), calls=%async_computation.4 | async-start | bytes 3932160 | tf_op jit(solution)/shard_map/reduce_scatter | solution.py:123
  130.0 28.2 %collective-permute-start.19 = (bf16[2,2,3,320]{3,2,1,0:T(4,128)(2,1)S(1)}, bf16[2,2,3,320]{3,2,1,0:T(4,128)(2,1)S(1)}, u32[]{:S(2)}, u32[]{:S(2)}) collective-permute-start(bf16[2,2,3,320]{3,2,1,0:T(4,128)(2,1)S(1)} %copy.465), channel_id=1, source_target_pairs={{0,1},{1,0},{2,3},{3,2},{4,5},{5,4},{6,7},{7,6},{8,9},{9,8},{10,11... | collective-permute-start | bytes 23048 | tf_op jit(solution)/shard_map/ppermute | solution.py:110
  131.4 12.0 %collective-permute-start.17 = (bf16[2048,960]{0,1:T(8,128)(2,1)}, bf16[2048,960]{0,1:T(8,128)(2,1)}, u32[]{:S(2)}, u32[]{:S(2)}) collective-permute-start(bf16[2048,960]{0,1:T(8,128)(2,1)} %all-gather.4.cloned.1.call-done), channel_id=1, source_target_pairs={{0,1},{1,0},{2,3},{3,2},{4,5},{5,4},{6,7},{7,6},{8,9},{9,8},{10,11... | collective-permute-start | bytes 11796488 | tf_op jit(solution)/shard_map/ppermute | solution.py:110
  202.1 14.9 %collective-permute-start.24 = (bf16[1,128,2048]{2,1,0:T(8,128)(2,1)S(1)}, bf16[1,128,2048]{2,1,0:T(8,128)(2,1)S(1)}, u32[]{:S(2)}, u32[]{:S(2)}) collective-permute-start(bf16[1,128,2048]{2,1,0:T(8,128)(2,1)S(1)} %get-tuple-element.273), channel_id=1, source_target_pairs={{0,4},{2,6},{4,0},{6,2},{1,5},{3,7},{5,1},{7,3},{8,12},{10,14},{12... | collective-permute-start | bytes 1572872 | tf_op jit(solution)/shard_map/ppermute | solution.py:26
  202.6 14.9 %collective-permute-start.26 = (bf16[1,128,2048]{2,1,0:T(8,128)(2,1)S(1)}, bf16[1,128,2048]{2,1,0:T(8,128)(2,1)S(1)}, u32[]{:S(2)}, u32[]{:S(2)}) collective-permute-start(bf16[1,128,2048]{2,1,0:T(8,128)(2,1)S(1)} %get-tuple-element.275), channel_id=1, source_target_pairs={{0,2},{2,0},{4,6},{6,4},{1,3},{3,1},{5,7},{7,5},{8,10},{10,8},{12,... | collective-permute-start | bytes 1572872 | tf_op jit(solution)/shard_map/ppermute | solution.py:26
  207.9 32.1 %collective-permute-start.32 = (bf16[2,128,2048]{2,1,0:T(8,128)(2,1)}, bf16[2,128,2048]{2,1,0:T(8,128)(2,1)}, u32[]{:S(2)}, u32[]{:S(2)}) collective-permute-start(bf16[2,128,2048]{2,1,0:T(8,128)(2,1)} %get-tuple-element.237), channel_id=1, source_target_pairs={{0,2},{2,0},{4,6},{6,4},{1,3},{3,1},{5,7},{7,5},{8,10},{10,8},{12,... | collective-permute-start | bytes 3145736 | tf_op jit(solution)/shard_map/ppermute | solution.py:26
  208.5 34.3 %collective-permute-start.33 = (bf16[2,128,2048]{2,1,0:T(8,128)(2,1)}, bf16[2,128,2048]{2,1,0:T(8,128)(2,1)}, u32[]{:S(2)}, u32[]{:S(2)}) collective-permute-start(bf16[2,128,2048]{2,1,0:T(8,128)(2,1)} %get-tuple-element.237), channel_id=1, source_target_pairs={{0,4},{2,6},{4,0},{6,2},{1,5},{3,7},{5,1},{7,3},{8,12},{10,14},{12... | collective-permute-start | bytes 3145736 | tf_op jit(solution)/shard_map/ppermute | solution.py:26
  218.9 43.6 %collective-permute-start.25 = (bf16[2,128,2048]{2,1,0:T(8,128)(2,1)}, bf16[2,128,2048]{2,1,0:T(8,128)(2,1)}, u32[]{:S(2)}, u32[]{:S(2)}) collective-permute-start(bf16[2,128,2048]{2,1,0:T(8,128)(2,1)} %pad_maximum_fusion.13), channel_id=1, source_target_pairs={{0,2},{2,0},{4,6},{6,4},{1,3},{3,1},{5,7},{7,5},{8,10},{10,8},{12,... | collective-permute-start | bytes 3145736 | tf_op jit(solution)/shard_map/ppermute | solution.py:26
  221.5 41.1 %collective-permute-start.27 = (bf16[2,128,2048]{2,1,0:T(8,128)(2,1)}, bf16[2,128,2048]{2,1,0:T(8,128)(2,1)}, u32[]{:S(2)}, u32[]{:S(2)}) collective-permute-start(bf16[2,128,2048]{2,1,0:T(8,128)(2,1)} %pad_maximum_fusion.14), channel_id=1, source_target_pairs={{0,4},{2,6},{4,0},{6,2},{1,5},{3,7},{5,1},{7,3},{8,12},{10,14},{12... | collective-permute-start | bytes 3145736 | tf_op jit(solution)/shard_map/ppermute | solution.py:26
  241.1 32.1 %collective-permute-start.34 = (bf16[1,128,2048]{2,1,0:T(8,128)(2,1)S(1)}, bf16[1,128,2048]{2,1,0:T(8,128)(2,1)S(1)}, u32[]{:S(2)}, u32[]{:S(2)}) collective-permute-start(bf16[1,128,2048]{2,1,0:T(8,128)(2,1)S(1)} %slice.661), channel_id=1, source_target_pairs={{0,4},{2,6},{4,0},{6,2},{1,5},{3,7},{5,1},{7,3},{8,12},{10,14},{12... | collective-permute-start | bytes 1572872 | tf_op jit(solution)/shard_map/ppermute | solution.py:26
  243.9 29.7 %collective-permute-start.35 = (bf16[1,128,2048]{2,1,0:T(8,128)(2,1)S(1)}, bf16[1,128,2048]{2,1,0:T(8,128)(2,1)S(1)}, u32[]{:S(2)}, u32[]{:S(2)}) collective-permute-start(bf16[1,128,2048]{2,1,0:T(8,128)(2,1)S(1)} %slice.662), channel_id=1, source_target_pairs={{0,2},{2,0},{4,6},{6,4},{1,3},{3,1},{5,7},{7,5},{8,10},{10,8},{12,... | collective-permute-start | bytes 1572872 | tf_op jit(solution)/shard_map/ppermute | solution.py:26
  266.9 26.5 %collective-permute-start.28 = (bf16[2,128,2048]{2,1,0:T(8,128)(2,1)S(1)}, bf16[2,128,2048]{2,1,0:T(8,128)(2,1)S(1)}, u32[]{:S(2)}, u32[]{:S(2)}) collective-permute-start(bf16[2,128,2048]{2,1,0:T(8,128)(2,1)S(1)} %multiply_convert_fusion.1), channel_id=1, source_target_pairs={{0,2},{2,0},{4,6},{6,4},{1,3},{3,1},{5,7},{7,5},{8,10},{10,8},{12,... | collective-permute-start | bytes 3145736 | tf_op jit(solution)/shard_map/ppermute | solution.py:26
  268.5 26.0 %collective-permute-start.29 = (bf16[2,128,2048]{2,1,0:T(8,128)(2,1)S(1)}, bf16[2,128,2048]{2,1,0:T(8,128)(2,1)}, u32[]{:S(2)}, u32[]{:S(2)}) collective-permute-start(bf16[2,128,2048]{2,1,0:T(8,128)(2,1)S(1)} %multiply_convert_fusion.1), channel_id=1, source_target_pairs={{0,4},{2,6},{4,0},{6,2},{1,5},{3,7},{5,1},{7,3},{8,12},{10,14},{12... | collective-permute-start | bytes 3145736 | tf_op jit(solution)/shard_map/ppermute | solution.py:26
  295.8 14.2 %collective-permute-start.30 = (bf16[1,128,2048]{2,1,0:T(8,128)(2,1)S(1)}, bf16[1,128,2048]{2,1,0:T(8,128)(2,1)S(1)}, u32[]{:S(2)}, u32[]{:S(2)}) collective-permute-start(bf16[1,128,2048]{2,1,0:T(8,128)(2,1)S(1)} %slice.536), channel_id=1, source_target_pairs={{0,4},{2,6},{4,0},{6,2},{1,5},{3,7},{5,1},{7,3},{8,12},{10,14},{12... | collective-permute-start | bytes 1572872 | tf_op jit(solution)/shard_map/ppermute | solution.py:26
  298.4 13.9 %collective-permute-start.31 = (bf16[1,128,2048]{2,1,0:T(8,128)(2,1)S(1)}, bf16[1,128,2048]{2,1,0:T(8,128)(2,1)S(1)}, u32[]{:S(2)}, u32[]{:S(2)}) collective-permute-start(bf16[1,128,2048]{2,1,0:T(8,128)(2,1)S(1)} %slice.537), channel_id=1, source_target_pairs={{0,2},{2,0},{4,6},{6,4},{1,3},{3,1},{5,7},{7,5},{8,10},{10,8},{12,... | collective-permute-start | bytes 1572872 | tf_op jit(solution)/shard_map/ppermute | solution.py:26
  375.4 23.2 %collective-permute-start.45 = (bf16[2048,768]{1,0:T(8,128)(2,1)}, bf16[2048,768]{1,0:T(8,128)(2,1)}, u32[]{:S(2)}, u32[]{:S(2)}) collective-permute-start(bf16[2048,768]{1,0:T(8,128)(2,1)} %convolution_convert_fusion.4), channel_id=1, source_target_pairs={{0,1},{1,0},{2,3},{3,2},{4,5},{5,4},{6,7},{7,6},{8,9},{9,8},{10,11... | collective-permute-start | bytes 9437192 | tf_op jit(solution)/shard_map/ppermute | solution.py:110
  376.6 14.7 %collective-permute-start.36 = (bf16[1,128,2048]{2,1,0:T(8,128)(2,1)}, bf16[1,128,2048]{2,1,0:T(8,128)(2,1)}, u32[]{:S(2)}, u32[]{:S(2)}) collective-permute-start(bf16[1,128,2048]{2,1,0:T(8,128)(2,1)} %get-tuple-element.267), channel_id=1, source_target_pairs={{0,4},{2,6},{4,0},{6,2},{1,5},{3,7},{5,1},{7,3},{8,12},{10,14},{12... | collective-permute-start | bytes 1572872 | tf_op jit(solution)/shard_map/ppermute | solution.py:26
  377.3 14.4 %collective-permute-start.38 = (bf16[1,128,2048]{2,1,0:T(8,128)(2,1)}, bf16[1,128,2048]{2,1,0:T(8,128)(2,1)}, u32[]{:S(2)}, u32[]{:S(2)}) collective-permute-start(bf16[1,128,2048]{2,1,0:T(8,128)(2,1)} %get-tuple-element.269), channel_id=1, source_target_pairs={{0,2},{2,0},{4,6},{6,4},{1,3},{3,1},{5,7},{7,5},{8,10},{10,8},{12,... | collective-permute-start | bytes 1572872 | tf_op jit(solution)/shard_map/ppermute | solution.py:26
  389.7 82.2 %collective-permute-start.44 = (bf16[2048,1536]{1,0:T(8,128)(2,1)}, bf16[2048,1536]{1,0:T(8,128)(2,1)}, u32[]{:S(2)}, u32[]{:S(2)}) collective-permute-start(bf16[2048,1536]{1,0:T(8,128)(2,1)} %convolution_convert_fusion.1), channel_id=1, source_target_pairs={{0,1},{1,0},{2,3},{3,2},{4,5},{5,4},{6,7},{7,6},{8,9},{9,8},{10,11... | collective-permute-start | bytes 18874376 | tf_op jit(solution)/shard_map/ppermute | solution.py:110
  394.7 24.8 %collective-permute-start.37 = (bf16[2,128,2048]{2,1,0:T(8,128)(2,1)}, bf16[2,128,2048]{2,1,0:T(8,128)(2,1)}, u32[]{:S(2)}, u32[]{:S(2)}) collective-permute-start(bf16[2,128,2048]{2,1,0:T(8,128)(2,1)} %pad_maximum_fusion.15), channel_id=1, source_target_pairs={{0,2},{2,0},{4,6},{6,4},{1,3},{3,1},{5,7},{7,5},{8,10},{10,8},{12,... | collective-permute-start | bytes 3145736 | tf_op jit(solution)/shard_map/ppermute | solution.py:26
  397.2 24.6 %collective-permute-start.39 = (bf16[2,128,2048]{2,1,0:T(8,128)(2,1)}, bf16[2,128,2048]{2,1,0:T(8,128)(2,1)}, u32[]{:S(2)}, u32[]{:S(2)}) collective-permute-start(bf16[2,128,2048]{2,1,0:T(8,128)(2,1)} %pad_maximum_fusion.16), channel_id=1, source_target_pairs={{0,4},{2,6},{4,0},{6,2},{1,5},{3,7},{5,1},{7,3},{8,12},{10,14},{12... | collective-permute-start | bytes 3145736 | tf_op jit(solution)/shard_map/ppermute | solution.py:26
  405.6 187.9 %reduce-scatter.6.cloned.1.call-start = ((), (), s32[]{:S(2)}) async-start(), calls=%async_computation.5 | async-start | bytes 7864320 | tf_op jit(solution)/shard_map/reduce_scatter | solution.py:123
  432.9 23.6 %collective-permute-start.40 = (bf16[2,128,2048]{2,1,0:T(8,128)(2,1)}, bf16[2,128,2048]{2,1,0:T(8,128)(2,1)}, u32[]{:S(2)}, u32[]{:S(2)}) collective-permute-start(bf16[2,128,2048]{2,1,0:T(8,128)(2,1)} %get-tuple-element.234), channel_id=1, source_target_pairs={{0,2},{2,0},{4,6},{6,4},{1,3},{3,1},{5,7},{7,5},{8,10},{10,8},{12,... | collective-permute-start | bytes 3145736 | tf_op jit(solution)/shard_map/ppermute | solution.py:26
  433.4 25.5 %collective-permute-start.41 = (bf16[2,128,2048]{2,1,0:T(8,128)(2,1)}, bf16[2,128,2048]{2,1,0:T(8,128)(2,1)}, u32[]{:S(2)}, u32[]{:S(2)}) collective-permute-start(bf16[2,128,2048]{2,1,0:T(8,128)(2,1)} %get-tuple-element.234), channel_id=1, source_target_pairs={{0,4},{2,6},{4,0},{6,2},{1,5},{3,7},{5,1},{7,3},{8,12},{10,14},{12... | collective-permute-start | bytes 3145736 | tf_op jit(solution)/shard_map/ppermute | solution.py:26
  483.9 238.0 %reduce-scatter.8.cloned.1.call-start = ((), (), s32[]{:S(2)}) async-start(), calls=%async_computation.6 | async-start | bytes 4915200 | tf_op jit(solution)/shard_map/reduce_scatter | solution.py:123
  504.4 18.9 %collective-permute-start.46 = (f32[2,2,640]{2,1,0:T(2,128)S(1)}, f32[2,2,640]{2,1,0:T(2,128)S(1)}, u32[]{:S(2)}, u32[]{:S(2)}) collective-permute-start(f32[2,2,640]{2,1,0:T(2,128)S(1)} %copy.415), channel_id=1, source_target_pairs={{8,0},{16,8},{24,16},{9,1},{17,9},{25,17},{10,2},{18,10},{26,18},{... | collective-permute-start | bytes 30728 | tf_op jit(solution)/shard_map/ppermute | solution.py:179
  505.7 18.6 %collective-permute-start.47 = (f32[2,2,640]{2,1,0:T(2,128)S(1)}, f32[2,2,640]{2,1,0:T(2,128)S(1)}, u32[]{:S(2)}, u32[]{:S(2)}) collective-permute-start(f32[2,2,640]{2,1,0:T(2,128)S(1)} %copy.415), channel_id=1, source_target_pairs={{16,0},{24,8},{17,1},{25,9},{18,2},{26,10},{19,3},{27,11},{20,4},{... | collective-permute-start | bytes 30728 | tf_op jit(solution)/shard_map/ppermute | solution.py:179
  507.0 14.1 %collective-permute-start.48 = (f32[2,2,640]{2,0,1:T(2,128)S(1)}, f32[2,2,640]{2,0,1:T(2,128)S(1)}, u32[]{:S(2)}, u32[]{:S(2)}) collective-permute-start(f32[2,2,640]{2,0,1:T(2,128)S(1)} %pad_maximum_fusion.32), channel_id=1, source_target_pairs={{24,0},{25,1},{26,2},{27,3},{28,4},{29,5},{30,6},{31,7}} | collective-permute-start | bytes 30728 | tf_op jit(solution)/shard_map/ppermute | solution.py:179
  509.6 15.1 %collective-permute-start.49 = (bf16[1,128,2048]{2,1,0:T(8,128)(2,1)S(1)}, bf16[1,128,2048]{2,1,0:T(8,128)(2,1)S(1)}, u32[]{:S(2)}, u32[]{:S(2)}) collective-permute-start(bf16[1,128,2048]{2,1,0:T(8,128)(2,1)S(1)} %get-tuple-element.265), channel_id=1, source_target_pairs={{0,2},{2,0},{4,6},{6,4},{1,3},{3,1},{5,7},{7,5},{8,10},{10,8},{12,... | collective-permute-start | bytes 1572872 | tf_op jit(solution)/shard_map/ppermute | solution.py:26
  510.2 14.5 %collective-permute-start.50 = (bf16[1,128,2048]{2,1,0:T(8,128)(2,1)S(1)}, bf16[1,128,2048]{2,1,0:T(8,128)(2,1)}, u32[]{:S(2)}, u32[]{:S(2)}) collective-permute-start(bf16[1,128,2048]{2,1,0:T(8,128)(2,1)S(1)} %get-tuple-element.264), channel_id=1, source_target_pairs={{0,4},{2,6},{4,0},{6,2},{1,5},{3,7},{5,1},{7,3},{8,12},{10,14},{12... | collective-permute-start | bytes 1572872 | tf_op jit(solution)/shard_map/ppermute | solution.py:26
  521.1 32.8 %collective-permute-start.54 = (bf16[128,768]{0,1:T(8,128)(2,1)}, bf16[128,768]{0,1:T(8,128)(2,1)}, u32[]{:S(2)}, u32[]{:S(2)}) collective-permute-start(bf16[128,768]{0,1:T(8,128)(2,1)} %bitcast.149), channel_id=1, source_target_pairs={{0,6},{2,4},{4,2},{6,0},{1,7},{3,5},{5,3},{7,1},{8,14},{10,12},{12... | collective-permute-start | bytes 589832 | tf_op jit(solution)/shard_map/ppermute | solution.py:26
  523.3 32.0 %collective-permute-start.55 = (bf16[128,768]{0,1:T(8,128)(2,1)}, bf16[128,768]{0,1:T(8,128)(2,1)}, u32[]{:S(2)}, u32[]{:S(2)}) collective-permute-start(bf16[128,768]{0,1:T(8,128)(2,1)} %bitcast.150), channel_id=1, source_target_pairs={{0,4},{2,6},{4,0},{6,2},{1,5},{3,7},{5,1},{7,3},{8,12},{10,14},{12... | collective-permute-start | bytes 589832 | tf_op jit(solution)/shard_map/ppermute | solution.py:26
  524.3 31.1 %collective-permute-start.56 = (bf16[128,768]{0,1:T(8,128)(2,1)}, bf16[128,768]{0,1:T(8,128)(2,1)}, u32[]{:S(2)}, u32[]{:S(2)}) collective-permute-start(bf16[128,768]{0,1:T(8,128)(2,1)} %bitcast.151), channel_id=1, source_target_pairs={{0,2},{2,0},{4,6},{6,4},{1,3},{3,1},{5,7},{7,5},{8,10},{10,8},{12,... | collective-permute-start | bytes 589832 | tf_op jit(solution)/shard_map/ppermute | solution.py:26
  528.2 33.5 %collective-permute-start.52 = (bf16[2,128,2048]{2,1,0:T(8,128)(2,1)S(1)}, bf16[2,128,2048]{2,1,0:T(8,128)(2,1)}, u32[]{:S(2)}, u32[]{:S(2)}) collective-permute-start(bf16[2,128,2048]{2,1,0:T(8,128)(2,1)S(1)} %pad_maximum_fusion.17), channel_id=1, source_target_pairs={{0,2},{2,0},{4,6},{6,4},{1,3},{3,1},{5,7},{7,5},{8,10},{10,8},{12,... | collective-permute-start | bytes 3145736 | tf_op jit(solution)/shard_map/ppermute | solution.py:26
  531.0 30.7 %collective-permute-start.53 = (bf16[2,128,2048]{2,1,0:T(8,128)(2,1)}, bf16[2,128,2048]{2,1,0:T(8,128)(2,1)}, u32[]{:S(2)}, u32[]{:S(2)}) collective-permute-start(bf16[2,128,2048]{2,1,0:T(8,128)(2,1)} %pad_maximum_fusion.18), channel_id=1, source_target_pairs={{0,4},{2,6},{4,0},{6,2},{1,5},{3,7},{5,1},{7,3},{8,12},{10,14},{12... | collective-permute-start | bytes 3145736 | tf_op jit(solution)/shard_map/ppermute | solution.py:26
  606.4 23.6 %collective-permute-start.58 = (bf16[2048,960]{0,1:T(8,128)(2,1)}, bf16[2048,960]{0,1:T(8,128)(2,1)}, u32[]{:S(2)}, u32[]{:S(2)}) collective-permute-start(bf16[2048,960]{0,1:T(8,128)(2,1)} %pad_maximum_fusion.1), channel_id=1, source_target_pairs={{0,1},{1,0},{2,3},{3,2},{4,5},{5,4},{6,7},{7,6},{8,9},{9,8},{10,11... | collective-permute-start | bytes 11796488 | tf_op jit(solution)/shard_map/ppermute | solution.py:110
  627.8 45.7 %collective-permute-start.57 = (bf16[2,128,2048]{2,1,0:T(8,128)(2,1)}, bf16[2,128,2048]{2,1,0:T(8,128)(2,1)}, u32[]{:S(2)}, u32[]{:S(2)}) collective-permute-start(bf16[2,128,2048]{2,1,0:T(8,128)(2,1)} %get-tuple-element.228), channel_id=1, source_target_pairs={{0,1},{1,0},{2,3},{3,2},{4,5},{5,4},{6,7},{7,6},{8,9},{9,8},{10,11... | collective-permute-start | bytes 3145736 | tf_op jit(solution)/shard_map/ppermute | solution.py:110
  647.4 15.1 %collective-permute-start.59 = (bf16[1,128,2048]{2,1,0:T(8,128)(2,1)}, bf16[1,128,2048]{2,1,0:T(8,128)(2,1)}, u32[]{:S(2)}, u32[]{:S(2)}) collective-permute-start(bf16[1,128,2048]{2,1,0:T(8,128)(2,1)} %get-tuple-element.255), channel_id=1, source_target_pairs={{0,4},{2,6},{4,0},{6,2},{1,5},{3,7},{5,1},{7,3},{8,12},{10,14},{12... | collective-permute-start | bytes 1572872 | tf_op jit(solution)/shard_map/ppermute | solution.py:26
  648.9 15.0 %collective-permute-start.61 = (bf16[1,128,2048]{2,1,0:T(8,128)(2,1)}, bf16[1,128,2048]{2,1,0:T(8,128)(2,1)}, u32[]{:S(2)}, u32[]{:S(2)}) collective-permute-start(bf16[1,128,2048]{2,1,0:T(8,128)(2,1)} %get-tuple-element.257), channel_id=1, source_target_pairs={{0,2},{2,0},{4,6},{6,4},{1,3},{3,1},{5,7},{7,5},{8,10},{10,8},{12,... | collective-permute-start | bytes 1572872 | tf_op jit(solution)/shard_map/ppermute | solution.py:26
  654.3 17.6 %collective-permute-start.66 = (f32[2,2048]{1,0:T(2,128)S(1)}, f32[2,2048]{1,0:T(2,128)S(1)}, u32[]{:S(2)}, u32[]{:S(2)}) collective-permute-start(f32[2,2048]{1,0:T(2,128)S(1)} %fusion.143), channel_id=1, source_target_pairs={{0,2},{2,0},{4,6},{6,4},{1,3},{3,1},{5,7},{7,5},{8,10},{10,8},{12,... | collective-permute-start | bytes 49160 | tf_op jit(solution)/shard_map/ppermute | solution.py:156
  666.9 27.6 %collective-permute-start.60 = (bf16[2,128,2048]{2,1,0:T(8,128)(2,1)}, bf16[2,128,2048]{2,1,0:T(8,128)(2,1)}, u32[]{:S(2)}, u32[]{:S(2)}) collective-permute-start(bf16[2,128,2048]{2,1,0:T(8,128)(2,1)} %pad_maximum_fusion.19), channel_id=1, source_target_pairs={{0,2},{2,0},{4,6},{6,4},{1,3},{3,1},{5,7},{7,5},{8,10},{10,8},{12,... | collective-permute-start | bytes 3145736 | tf_op jit(solution)/shard_map/ppermute | solution.py:26
  669.4 25.1 %collective-permute-start.62 = (bf16[2,128,2048]{2,1,0:T(8,128)(2,1)}, bf16[2,128,2048]{2,1,0:T(8,128)(2,1)}, u32[]{:S(2)}, u32[]{:S(2)}) collective-permute-start(bf16[2,128,2048]{2,1,0:T(8,128)(2,1)} %pad_maximum_fusion.20), channel_id=1, source_target_pairs={{0,4},{2,6},{4,0},{6,2},{1,5},{3,7},{5,1},{7,3},{8,12},{10,14},{12... | collective-permute-start | bytes 3145736 | tf_op jit(solution)/shard_map/ppermute | solution.py:26
  671.9 22.5 %collective-permute-start.64 = (bf16[320,368]{1,0:T(8,128)(2,1)S(1)}, bf16[320,368]{1,0:T(8,128)(2,1)S(1)}, u32[]{:S(2)}, u32[]{:S(2)}) collective-permute-start(bf16[320,368]{1,0:T(8,128)(2,1)S(1)} %slice.691), channel_id=1, source_target_pairs={{0,1},{1,0},{2,3},{3,2},{4,5},{5,4},{6,7},{7,6},{8,9},{9,8},{10,11... | collective-permute-start | bytes 706568 | tf_op jit(solution)/shard_map/ppermute | solution.py:110
  672.0 22.4 %collective-permute-start.67 = (f32[2,2048]{1,0:T(2,128)S(1)}, f32[2,2048]{1,0:T(2,128)S(1)}, u32[]{:S(2)}, u32[]{:S(2)}) collective-permute-start(f32[2,2048]{1,0:T(2,128)S(1)} %fusion.184), channel_id=1, source_target_pairs={{0,4},{2,6},{4,0},{6,2},{1,5},{3,7},{5,1},{7,3},{8,12},{10,14},{12... | collective-permute-start | bytes 49160 | tf_op jit(solution)/shard_map/ppermute | solution.py:156
  697.2 13.0 %collective-permute-start.78 = (bf16[128,1536]{1,0:T(8,128)(2,1)S(1)}, bf16[128,1536]{1,0:T(8,128)(2,1)S(1)}, u32[]{:S(2)}, u32[]{:S(2)}) collective-permute-start(bf16[128,1536]{1,0:T(8,128)(2,1)S(1)} %get-tuple-element.320), channel_id=1, source_target_pairs={{0,6},{2,4},{4,2},{6,0},{1,7},{3,5},{5,3},{7,1},{8,14},{10,12},{12... | collective-permute-start | bytes 1179656 | tf_op jit(solution)/shard_map/ppermute | solution.py:26
  697.9 17.6 %collective-permute-start.79 = (bf16[128,1536]{1,0:T(8,128)(2,1)S(1)}, bf16[128,1536]{1,0:T(8,128)(2,1)S(1)}, u32[]{:S(2)}, u32[]{:S(2)}) collective-permute-start(bf16[128,1536]{1,0:T(8,128)(2,1)S(1)} %get-tuple-element.319), channel_id=1, source_target_pairs={{0,4},{2,6},{4,0},{6,2},{1,5},{3,7},{5,1},{7,3},{8,12},{10,14},{12... | collective-permute-start | bytes 1179656 | tf_op jit(solution)/shard_map/ppermute | solution.py:26
  699.3 16.2 %collective-permute-start.80 = (bf16[128,1536]{1,0:T(8,128)(2,1)S(1)}, bf16[128,1536]{1,0:T(8,128)(2,1)S(1)}, u32[]{:S(2)}, u32[]{:S(2)}) collective-permute-start(bf16[128,1536]{1,0:T(8,128)(2,1)S(1)} %get-tuple-element.318), channel_id=1, source_target_pairs={{0,2},{2,0},{4,6},{6,4},{1,3},{3,1},{5,7},{7,5},{8,10},{10,8},{12,... | collective-permute-start | bytes 1179656 | tf_op jit(solution)/shard_map/ppermute | solution.py:26
  704.5 13.9 %collective-permute-start.63 = (bf16[2,128,2048]{2,1,0:T(8,128)(2,1)S(1)}, bf16[2,128,2048]{2,1,0:T(8,128)(2,1)S(1)}, u32[]{:S(2)}, u32[]{:S(2)}) collective-permute-start(bf16[2,128,2048]{2,1,0:T(8,128)(2,1)S(1)} %get-tuple-element.226), channel_id=1, source_target_pairs={{0,1},{1,0},{2,3},{3,2},{4,5},{5,4},{6,7},{7,6},{8,9},{9,8},{10,11... | collective-permute-start | bytes 3145736 | tf_op jit(solution)/shard_map/ppermute | solution.py:110
  723.2 13.3 %collective-permute-start.73 = (f32[2,2048]{1,0:T(2,128)S(1)}, f32[2,2048]{1,0:T(2,128)S(1)}, u32[]{:S(2)}, u32[]{:S(2)}) collective-permute-start(f32[2,2048]{1,0:T(2,128)S(1)} %add.761), channel_id=1, source_target_pairs={{0,16},{8,24},{16,0},{24,8},{1,17},{9,25},{17,1},{25,9},{2,18},{10... | collective-permute-start | bytes 49160 | tf_op jit(solution)/shard_map/ppermute | solution.py:145
  724.9 14.4 %collective-permute-start.74 = (f32[2,2048]{1,0:T(2,128)S(1)}, f32[2,2048]{1,0:T(2,128)S(1)}, u32[]{:S(2)}, u32[]{:S(2)}) collective-permute-start(f32[2,2048]{1,0:T(2,128)S(1)} %add.761), channel_id=1, source_target_pairs={{0,24},{8,0},{16,8},{24,16},{1,25},{9,1},{17,9},{25,17},{2,26},{10... | collective-permute-start | bytes 49160 | tf_op jit(solution)/shard_map/ppermute | solution.py:145
  (156 other events, 1549.2 us)
Sparse Core Ops, SparseCore 0:
  43.8 73.5 all-gather.3
  129.0 165.6 all-gather.5
  405.7 57.6 reduce-scatter.3
  484.1 109.3 reduce-scatter.5
  650.5 71.3 reduce-scatter.7

commit v7 on v6

--- a/solution.py
+++ b/solution.py
@@ -461,7 +461,7 @@
 
     d_out = own_cot.reshape(own_tokens, model_width).astype(F32)
     own_down = (d_out * own_live).astype(BF16).reshape(n_streams, own_rows, model_width)
-    d_down = plane_gather(own_down)
+    down_state = plane_gather_first(own_down)
 
     flat_in = own_in.reshape(own_tokens, model_width).astype(F32)
     _, norm_one_back = jax.vjp(rms_norm, flat_in, gains_all[0])
@@ -477,6 +477,7 @@
         [w[:, p * part_width : (p + 1) * part_width] for p in (0, 1) for w in w_first], axis=1
     )
     w_back = jnp.concatenate([w[:, 2 * part_width :] for w in w_first], axis=1)
+    w_rec, down_state = lax.optimization_barrier((w_rec, down_state))
     projected = dot(normed_low, w_rec, 1, 0)
     source_rows = projected[:, :rec_width].astype(BF16).reshape(n_streams, n_rows, rec_width)
     branch, branch_back = jax.vjp(jax.nn.gelu, projected[:, rec_width:])
@@ -562,13 +563,13 @@
 
     states_flat = states.reshape(tokens, rec_width)
     mixed_rows = (states_flat * branch).astype(BF16)
+    mixed_rows, d_down = lax.optimization_barrier((mixed_rows, plane_gather_second(down_state)))
     rec_part = dot(mixed_rows, w_back, 1, 1)
     rec_total = plane_sum(rec_part, n_streams).reshape(own_tokens, model_width)
     hidden_one = flat_in + own_live * rec_total
     normed_two, norm_two_back = jax.vjp(rms_norm, hidden_one, gains_all[1])
     own_second = normed_two.astype(BF16).reshape(n_streams, own_rows, model_width)
-    second_state, w_later = lax.optimization_barrier((plane_gather_first(own_second), w_later))
-    second_low = plane_gather_second(second_state)
+    second_low, w_later = lax.optimization_barrier((plane_gather(own_second), w_later))
     w_later = w_later.reshape(halves, model_width, 3 * ff_part)
     acts, d_both, second_part, down_part = mlp(second_low, d_down, w_later, 1)
     second_low = second_low.reshape(tokens, model_width)

time: 771 us -> 763 us (0.990)
  local copies, waits for them, and re-layouts: 121 us -> 113 us
    concatenate x0 -> x1, other arithmetic: none -> 10 us  [shards(): jnp.concatenate([w[:, p * part_width:(p + 1) * part_width] for p in (0, 1...]
    unnamed x281 -> x263, local copies, waits for them, and re-layouts: 21.4 us -> 20.8 us
  transfers between devices with their start and end apart: 86 -> 86, of which waited for: 36 -> 37; matrix products, arithmetic and copies ran while one was open for 37% -> 37% of each run, Pallas kernels for 2% -> 2%
where the time goes in v7:
time: 763 us; the launch traced here: 755 us
  waiting for transfers between devices  247 us (32%)
  other arithmetic  115 us (15%)
  local copies, waits for them, and re-layouts  113 us (15%)
  starting transfers between devices  98.5 us (13%)
  matrix products  93.2 us (12%)
  Pallas kernels  70.7 us (9%)
  between operations  16.9 us (2%)
    ppermute x50, waiting for transfers between devices, to_partner(): return lax.ppermute(block, 'j', [(i, i ^ bit) for i in range(PLANE)])  187 us
    dot_general x13, matrix products, dot(): lax.dot_general(left, right, (((left_dim,), (right_dim,)), ((), ())), pre...  86.5 us
    ppermute x50, starting transfers between devices, to_partner(): return lax.ppermute(block, 'j', [(i, i ^ bit) for i in range(PLANE)])  56.8 us
    pallas_call x1, Pallas kernels, mlp(): pl.pallas_call(mlp_kernel, grid=(streams, halves, tiles), in_specs=[token...  53.8 us
    reduce_scatter x3, waiting for transfers between devices, sum_along_z(): return lax.psum_scatter(total, 'z', scatter_dimension=0, tiled=True)  31.2 us
    unnamed x263, local copies, waits for them, and re-layouts  20.8 us
    ppermute x3, waiting for transfers between devices, sum_of_chip_plane(): array = array + lax.ppermute(array, axis, pairs)  19.5 us
    ppermute x8, starting transfers between devices, shifted(): lax.ppermute(block, 'z', [(i - distance, i) for i in range(size) if 0 <=...  19.2 us
  transfers between devices with their start and end apart: 86, of which 37 were waited for; matrix products, arithmetic and copies ran while one was open for 37% of the time, Pallas kernels for 2%

profile of v7, /device:TPU:0, one launch (start us, length us, event | category | flops | bytes accessed | tf_op | source)
XLA Modules:
  0.0 754.7 jit_solution(16941310780794289797)
XLA Ops:
  9.8 3.0 collective-permute-start.3
  12.8 2.6 collective-permute-start.4
  22.0 2.4 collective-permute-start
  26.7 5.4 collective-permute-done
  32.1 3.2 collective-permute-done.1
  47.3 18.7 %collective-permute-done.6 = bf16[88,328]{1,0:T(8,128)(2,1)S(1)} collective-permute-done((bf16[88,328]{1,0:T(8,128)(2,1)}, bf16[88,328]{1,0:T(8,128)(2,1)S(1)}, u32[]{:S(2)}, u32[]{:S(2)}) %collective-permute-start.6) | collective-permute-done | bytes 57760 | tf_op jit(solution)/shard_map/ppermute | solution.py:26
  91.7 2.5 broadcast.860.clone
  99.9 18.0 %collective-permute-done.12 = bf16[1,128,2048]{2,1,0:T(8,128)(2,1)} collective-permute-done((bf16[1,128,2048]{2,1,0:T(8,128)(2,1)}, bf16[1,128,2048]{2,1,0:T(8,128)(2,1)}, u32[]{:S(2)}, u32[]{:S(2)}) %collective-permute-start.12) | collective-permute-done | bytes 524320 | tf_op jit(solution)/shard_map/ppermute | solution.py:26
  120.2 3.1 fusion
  123.3 5.3 fusion.2
  136.6 6.1 collective-permute-done.9
  147.2 3.1 fusion.150
  150.3 10.0 %pad_maximum_fusion = bf16[2048,1280]{0,1:T(8,128)(2,1)S(1)} fusion(bf16[2048,320]{0,1:T(8,128)(2,1)S(1)} %get-tuple-element.290, bf16[2048,320]{0,1:T(8,128)(2,1)S(1)} %get-tuple-element.287, bf16[2048,320]{0,1:T(8,128)(2,1)S(1)} %get-tuple-element.291, bf16[2048,320]{0,1:T(8,128)(2,1)S(1)} %get-tuple-element.288), kind=kLoop, calls=%fused_computation.14 | loop fusion | flops 20971520 | bytes 10485760 | tf_op jit(solution)/shard_map/concatenate | solution.py:476
  160.4 9.4 %collective-permute-done.18 = bf16[2,128,2048]{2,1,0:T(8,128)(2,1)S(1)} collective-permute-done((bf16[2,128,2048]{2,1,0:T(8,128)(2,1)S(1)}, bf16[2,128,2048]{2,1,0:T(8,128)(2,1)S(1)}, u32[]{:S(2)}, u32[]{:S(2)}) %collective-permute-start.18) | collective-permute-done | bytes 1048608 | tf_op jit(solution)/shard_map/ppermute | solution.py:26
  170.1 5.7 fusion.162
  176.0 2.7 collective-permute-start.20
  182.4 2.8 multiply_add_fusion.2
  187.7 3.1 bitcast_multiply_fusion.7
  191.6 7.8 %shard_map.246 = (f32[2,512,640]{2,1,0:T(8,128)S(1)}, f32[2,512,640]{2,1,0:T(8,128)S(1)}) custom-call(f32[2,512,640]{2,1,0:T(8,128)S(1)} %get-tuple-element.297.keep_ref, f32[2,512,640]{2,1,0:T(8,128)S(1)} %get-tuple-element.296.add_ref), custom_call_target="tpu_custom_call" | custom-call | flops 5242880 | bytes 10485760 | tf_op jit(solution)/shard_map/pallas_call | solution.py:233
  203.5 5.0 collective-permute-start.25
  213.2 4.9 collective-permute-start.24
  223.9 3.6 convolution_convert_fusion.3
  229.9 10.5 %collective-permute-done.28 = bf16[1,128,2048]{2,1,0:T(8,128)(2,1)S(1)} collective-permute-done((bf16[1,128,2048]{2,1,0:T(8,128)(2,1)S(1)}, bf16[1,128,2048]{2,1,0:T(8,128)(2,1)S(1)}, u32[]{:S(2)}, u32[]{:S(2)}) %collective-permute-start.28) | collective-permute-done | bytes 524320 | tf_op jit(solution)/shard_map/ppermute | solution.py:26
  244.2 20.0 %collective-permute-done.29 = bf16[2,128,2048]{2,1,0:T(8,128)(2,1)S(1)} collective-permute-done((bf16[2,128,2048]{2,1,0:T(8,128)(2,1)S(1)}, bf16[2,128,2048]{2,1,0:T(8,128)(2,1)S(1)}, u32[]{:S(2)}, u32[]{:S(2)}) %collective-permute-start.29) | collective-permute-done | bytes 1048608 | tf_op jit(solution)/shard_map/ppermute | solution.py:26
  272.8 20.0 %collective-permute-done.32 = bf16[2,128,2048]{2,1,0:T(8,128)(2,1)} collective-permute-done((bf16[2,128,2048]{2,1,0:T(8,128)(2,1)}, bf16[2,128,2048]{2,1,0:T(8,128)(2,1)}, u32[]{:S(2)}, u32[]{:S(2)}) %collective-permute-start.32) | collective-permute-done | bytes 1048608 | tf_op jit(solution)/shard_map/ppermute | solution.py:26
  301.7 2.8 collective-permute-done.34
  306.2 53.8 %shard_map.247 = (bf16[2,1024,768]{2,1,0:T(8,128)(2,1)}, bf16[2,1024,1536]{2,1,0:T(8,128)(2,1)}, bf16[2,512,2048]{2,1,0:T(8,128)(2,1)}, bf16[2,512,2048]{2,1,0:T(8,128)(2,1)}) custom-call(bf16[2,512,2048]{2,1,0:T(8,128)(2,1)} %bitcast.562, bf16[2,512,2048]{2,1,0:T(8,128)(2,1)} %bitcast.565, bf16[2,2048,2304]{2,1,0:T(8,128)(2,1)} %bitcast.619, ...), custom_call_target="tpu_custom_call" | custom-call | flops 38654705664 | bytes 41943040 | tf_op jit(solution)/shard_map/pallas_call | solution.py:321
  360.1 8.0 %convolution_convert_fusion.4 = bf16[2048,768]{1,0:T(8,128)(2,1)} fusion(bf16[1024,2048]{1,0:T(8,128)(2,1)} %bitcast.566, bf16[2,1024,768]{2,1,0:T(8,128)(2,1)} %get-tuple-element.99, s32[]{:T(128)S(6)} %select_n.658), kind=kOutput, calls=%fused_computation.28 | convolution fusion | flops 3222798336 | bytes 8912900 | tf_op jit(solution)/shard_map/dot_general | solution.py:20
  371.5 9.1 %convolution_convert_fusion.1 = bf16[2048,1536]{1,0:T(8,128)(2,1)} fusion(bf16[1024,2048]{1,0:T(8,128)(2,1)S(1)} %bitcast.563, bf16[2,1024,1536]{2,1,0:T(8,128)(2,1)S(1)} %bitcast.623, s32[]{:T(128)S(6)} %select_n.658), kind=kOutput, calls=%fused_computation.11 | convolution fusion | flops 6445596672 | bytes 13631492 | tf_op jit(solution)/shard_map/dot_general | solution.py:20
  380.6 3.4 collective-permute-done.36
  390.9 6.9 add_convert_fusion.2
  398.0 14.7 %collective-permute-done.37 = bf16[2,128,2048]{2,1,0:T(8,128)(2,1)} collective-permute-done((bf16[2,128,2048]{2,1,0:T(8,128)(2,1)}, bf16[2,128,2048]{2,1,0:T(8,128)(2,1)}, u32[]{:S(2)}, u32[]{:S(2)}) %collective-permute-start.37) | collective-permute-done | bytes 1048608 | tf_op jit(solution)/shard_map/ppermute | solution.py:26
  414.4 3.3 multiply_reduce_fusion.5
  417.8 2.5 broadcast.860
  420.6 4.9 bitcast_dynamic-update-slice_fusion.2
  429.3 19.7 %collective-permute-done.40 = bf16[2,128,2048]{2,1,0:T(8,128)(2,1)} collective-permute-done((bf16[2,128,2048]{2,1,0:T(8,128)(2,1)}, bf16[2,128,2048]{2,1,0:T(8,128)(2,1)}, u32[]{:S(2)}, u32[]{:S(2)}) %collective-permute-start.40) | collective-permute-done | bytes 1048608 | tf_op jit(solution)/shard_map/ppermute | solution.py:26
  455.5 2.5 bitcast_dynamic-update-slice_fusion
  458.0 3.3 collective-permute-done.42
  464.2 10.8 %add_convert_fusion = bf16[2048,1536]{1,0:T(8,128)(2,1)} fusion(bf16[2048,1536]{1,0:T(8,128)(2,1)} %collective-permute-done.44, bf16[1024,2048]{1,0:T(8,128)(2,1)S(1)} %bitcast.564, bf16[2,1024,1536]{2,1,0:T(8,128)(2,1)S(1)} %bitcast.625, s32[]{:T(128)S(6)} %select_n.657), kind=kOutput, calls=%fused_computation | convolution fusion | flops 6458179584 | bytes 19922948 | tf_op jit(solution)/shard_map/dot_general | solution.py:20
  475.7 6.2 fusion.45
  481.9 4.4 fusion.63
  486.3 9.1 %shard_map.248 = (f32[2,512,640]{2,1,0:T(8,128)S(1)}, f32[2,512,640]{2,1,0:T(8,128)S(1)}) custom-call(f32[2,512,640]{2,1,0:T(8,128)S(1)} %copy-done.2, f32[2,512,640]{2,1,0:T(8,128)S(1)} %bitcast.547), custom_call_target="tpu_custom_call" | custom-call | flops 5242880 | bytes 10485760 | tf_op jit(solution)/shard_map/pallas_call | solution.py:233
  502.8 5.1 convolution_convert_fusion.7
  526.4 4.4 multiply_reduce_fusion
  530.8 4.0 fusion.143
  535.0 7.9 %multiply_reduce_fusion.4 = (f32[640]{0:T(1024)S(1)}, f32[640]{0:T(1024)S(1)}, f32[640]{0:T(1024)S(1)}, f32[640]{0:T(1024)S(1)}, f32[1024,640]{1,0:T(8,128)S(1)}) fusion(f32[2,512,640]{2,1,0:T(8,128)} %get-tuple-element.413, f32[2,512,640]{2,1,0:T(8,128)S(1)} %copy-done.25, f32[2,512,640]{2,1,0:T(8,128)S(1)} %copy-done.23, ...), kind=kOutput, calls=%fused_computation.86 | convolution fusion | flops 1700656640 | bytes 25249280 | tf_op jit(solution)/shard_map/dot_general | solution.py:20
  552.7 3.7 fusion.41
  556.4 28.8 %reduce-scatter.6.cloned.1.call-done = bf16[512,1536]{1,0:T(8,128)(2,1)} async-done(((bf16[2048,1536]{1,0:T(8,128)(2,1)}), bf16[512,1536]{1,0:T(8,128)(2,1)}) %reduce-scatter.6.cloned.1.call-update) | async-done | bytes 1572880 | tf_op jit(solution)/shard_map/reduce_scatter | solution.py:123
  585.2 8.5 %convolution_convert_fusion = bf16[2048,1280]{0,1:T(8,128)(2,1)S(1)} fusion(bf16[1024,2048]{1,0:T(8,128)(2,1)} %fusion.2, bf16[1024,1280]{1,0:T(8,128)(2,1)} %pad_maximum_fusion.4), kind=kOutput, calls=%fused_computation.10 | convolution fusion | flops 5371330560 | bytes 12058624 | tf_op jit(solution)/shard_map/dot_general | solution.py:20
  602.2 2.6 dynamic_update_slice.114
  622.5 4.9 add_convert_fusion.1
  627.4 9.3 %fusion.4 = (f32[2048]{0:T(1024)S(1)}, bf16[1024,2048]{1,0:T(8,128)(2,1)S(1)}) fusion(bf16[2,4,128,2048]{3,2,1,0:T(8,128)(2,1)} %fusion.51, f32[1024]{0:T(1024)S(1)} %bitcast.616, bf16[1024,1280]{1,0:T(8,128)(2,1)S(1)} %copy-done.52, bf16[2048,1280]{0,1:T(8,128)(2,1)} %copy-done.37), kind=kOutput, calls=%fused_computation.8 | convolution fusion | flops 5379192832 | bytes 16265216 | tf_op jit(solution)/shard_map/dot_general | solution.py:20
  643.3 3.2 convolution_convert_fusion.6
  647.4 7.5 collective-permute-done.59
  667.4 19.5 %collective-permute-done.67 = f32[2,2048]{1,0:T(2,128)S(1)} collective-permute-done((f32[2,2048]{1,0:T(2,128)S(1)}, f32[2,2048]{1,0:T(2,128)S(1)}, u32[]{:S(2)}, u32[]{:S(2)}) %collective-permute-start.67) | collective-permute-done | bytes 16416 | tf_op jit(solution)/shard_map/ppermute | solution.py:156
  687.0 2.6 fusion.40
  696.9 5.8 collective-permute-done.78
  702.7 5.3 collective-permute-done.79
  712.0 2.3 reduce-scatter.8.cloned.1.call-done
  717.3 2.7 collective-permute-start.74
  723.1 3.3 collective-permute-start.70
  728.9 2.4 collective-permute-start.75
  737.2 2.9 collective-permute-done.75
  740.1 2.4 collective-permute-done.76
  (656 shorter events, 254.5 us)
Async XLA Ops:
  7.2 124.7 %all-gather.4.cloned.1.call-start = ((), (), s32[]{:S(2)}) async-start(), calls=%async_computation.3 | async-start | bytes 4915200 | tf_op jit(solution)/shard_map/all_gather | solution.py:472
  9.8 15.4 %collective-permute-start.3 = (bf16[82,328]{1,0:T(8,128)(2,1)}, bf16[82,328]{1,0:T(8,128)(2,1)}, u32[]{:S(2)}, u32[]{:S(2)}) collective-permute-start(bf16[82,328]{1,0:T(8,128)(2,1)} %get-tuple-element.249), channel_id=1, source_target_pairs={{0,8},{8,16},{16,24},{24,0},{1,9},{9,17},{17,25},{25,1},{2,10},{10... | collective-permute-start | bytes 161384 | tf_op jit(solution)/shard_map/ppermute | solution.py:145
  12.8 13.9 %collective-permute-start.4 = (bf16[82,328]{1,0:T(8,128)(2,1)}, bf16[82,328]{1,0:T(8,128)(2,1)S(1)}, u32[]{:S(2)}, u32[]{:S(2)}) collective-permute-start(bf16[82,328]{1,0:T(8,128)(2,1)} %get-tuple-element.249), channel_id=1, source_target_pairs={{0,16},{8,24},{16,0},{24,8},{1,17},{9,25},{17,1},{25,9},{2,18},{10... | collective-permute-start | bytes 161384 | tf_op jit(solution)/shard_map/ppermute | solution.py:145
  37.6 30.9 %collective-permute-start.10 = (bf16[2,128,2048]{2,1,0:T(8,128)(2,1)S(1)}, bf16[2,128,2048]{2,1,0:T(8,128)(2,1)S(1)}, u32[]{:S(2)}, u32[]{:S(2)}) collective-permute-start(bf16[2,128,2048]{2,1,0:T(8,128)(2,1)S(1)} %constant_dynamic-slice_fusion.24), channel_id=1, source_target_pairs={{0,2},{2,0},{4,6},{6,4},{1,3},{3,1},{5,7},{7,5},{8,10},{10,8},{12,... | collective-permute-start | bytes 3145736 | tf_op jit(solution)/shard_map/ppermute | solution.py:26
  39.1 31.0 %collective-permute-start.11 = (bf16[2,128,2048]{2,1,0:T(8,128)(2,1)S(1)}, bf16[2,128,2048]{2,1,0:T(8,128)(2,1)}, u32[]{:S(2)}, u32[]{:S(2)}) collective-permute-start(bf16[2,128,2048]{2,1,0:T(8,128)(2,1)S(1)} %constant_dynamic-slice_fusion.24), channel_id=1, source_target_pairs={{0,4},{2,6},{4,0},{6,2},{1,5},{3,7},{5,1},{7,3},{8,12},{10,14},{12... | collective-permute-start | bytes 3145736 | tf_op jit(solution)/shard_map/ppermute | solution.py:26
  42.4 23.6 %collective-permute-start.6 = (bf16[88,328]{1,0:T(8,128)(2,1)}, bf16[88,328]{1,0:T(8,128)(2,1)S(1)}, u32[]{:S(2)}, u32[]{:S(2)}) collective-permute-start(bf16[88,328]{1,0:T(8,128)(2,1)} %get-tuple-element.363), channel_id=1, source_target_pairs={{0,6},{2,4},{4,2},{6,0},{1,7},{3,5},{5,3},{7,1},{8,14},{10,12},{12... | collective-permute-start | bytes 173192 | tf_op jit(solution)/shard_map/ppermute | solution.py:26
  43.6 23.3 %collective-permute-start.7 = (bf16[88,328]{1,0:T(8,128)(2,1)}, bf16[88,328]{1,0:T(8,128)(2,1)S(1)}, u32[]{:S(2)}, u32[]{:S(2)}) collective-permute-start(bf16[88,328]{1,0:T(8,128)(2,1)} %get-tuple-element.364), channel_id=1, source_target_pairs={{0,4},{2,6},{4,0},{6,2},{1,5},{3,7},{5,1},{7,3},{8,12},{10,14},{12... | collective-permute-start | bytes 173192 | tf_op jit(solution)/shard_map/ppermute | solution.py:26
  45.1 22.4 %collective-permute-start.8 = (bf16[88,328]{1,0:T(8,128)(2,1)}, bf16[88,328]{1,0:T(8,128)(2,1)}, u32[]{:S(2)}, u32[]{:S(2)}) collective-permute-start(bf16[88,328]{1,0:T(8,128)(2,1)} %get-tuple-element.362), channel_id=1, source_target_pairs={{0,2},{2,0},{4,6},{6,4},{1,3},{3,1},{5,7},{7,5},{8,10},{10,8},{12,... | collective-permute-start | bytes 173192 | tf_op jit(solution)/shard_map/ppermute | solution.py:26
  45.9 260.3 %all-gather.6.cloned.1.call-start = ((), (), s32[]{:S(2)}) async-start(), calls=%async_computation.7 | async-start | bytes 21233664 | tf_op jit(solution)/shard_map/all_gather | solution.py:474
  79.1 49.5 %collective-permute-start.14 = (bf16[128,2304]{1,0:T(8,128)(2,1)}, bf16[128,2304]{1,0:T(8,128)(2,1)}, u32[]{:S(2)}, u32[]{:S(2)}) collective-permute-start(bf16[128,2304]{1,0:T(8,128)(2,1)} %bitcast.589), channel_id=1, source_target_pairs={{0,6},{2,4},{4,2},{6,0},{1,7},{3,5},{5,3},{7,1},{8,14},{10,12},{12... | collective-permute-start | bytes 1769480 | tf_op jit(solution)/shard_map/ppermute | solution.py:26
  82.8 45.9 %collective-permute-start.15 = (bf16[128,2304]{1,0:T(8,128)(2,1)}, bf16[128,2304]{1,0:T(8,128)(2,1)}, u32[]{:S(2)}, u32[]{:S(2)}) collective-permute-start(bf16[128,2304]{1,0:T(8,128)(2,1)} %bitcast.590), channel_id=1, source_target_pairs={{0,4},{2,6},{4,0},{6,2},{1,5},{3,7},{5,1},{7,3},{8,12},{10,14},{12... | collective-permute-start | bytes 1769480 | tf_op jit(solution)/shard_map/ppermute | solution.py:26
  85.3 43.3 %collective-permute-start.16 = (bf16[128,2304]{1,0:T(8,128)(2,1)}, bf16[128,2304]{1,0:T(8,128)(2,1)}, u32[]{:S(2)}, u32[]{:S(2)}) collective-permute-start(bf16[128,2304]{1,0:T(8,128)(2,1)} %bitcast.591), channel_id=1, source_target_pairs={{0,2},{2,0},{4,6},{6,4},{1,3},{3,1},{5,7},{7,5},{8,10},{10,8},{12,... | collective-permute-start | bytes 1769480 | tf_op jit(solution)/shard_map/ppermute | solution.py:26
  87.7 30.2 %collective-permute-start.12 = (bf16[1,128,2048]{2,1,0:T(8,128)(2,1)}, bf16[1,128,2048]{2,1,0:T(8,128)(2,1)}, u32[]{:S(2)}, u32[]{:S(2)}) collective-permute-start(bf16[1,128,2048]{2,1,0:T(8,128)(2,1)} %slice.487), channel_id=1, source_target_pairs={{0,4},{2,6},{4,0},{6,2},{1,5},{3,7},{5,1},{7,3},{8,12},{10,14},{12... | collective-permute-start | bytes 1572872 | tf_op jit(solution)/shard_map/ppermute | solution.py:26
  89.9 28.0 %collective-permute-start.13 = (bf16[1,128,2048]{2,1,0:T(8,128)(2,1)}, bf16[1,128,2048]{2,1,0:T(8,128)(2,1)}, u32[]{:S(2)}, u32[]{:S(2)}) collective-permute-start(bf16[1,128,2048]{2,1,0:T(8,128)(2,1)} %slice.488), channel_id=1, source_target_pairs={{0,2},{2,0},{4,6},{6,4},{1,3},{3,1},{5,7},{7,5},{8,10},{10,8},{12,... | collective-permute-start | bytes 1572872 | tf_op jit(solution)/shard_map/ppermute | solution.py:26
  131.9 343.1 %reduce-scatter.4.cloned.1.call-start = ((), (), s32[]{:S(2)}) async-start(), calls=%async_computation.4 | async-start | bytes 3932160 | tf_op jit(solution)/shard_map/reduce_scatter | solution.py:123
  133.0 46.9 %collective-permute-start.21 = (bf16[2,2,3,320]{3,2,1,0:T(4,128)(2,1)S(1)}, bf16[2,2,3,320]{3,2,1,0:T(4,128)(2,1)S(1)}, u32[]{:S(2)}, u32[]{:S(2)}) collective-permute-start(bf16[2,2,3,320]{3,2,1,0:T(4,128)(2,1)S(1)} %copy.465), channel_id=1, source_target_pairs={{0,1},{1,0},{2,3},{3,2},{4,5},{5,4},{6,7},{7,6},{8,9},{9,8},{10,11... | collective-permute-start | bytes 23048 | tf_op jit(solution)/shard_map/ppermute | solution.py:110
  135.1 12.1 %collective-permute-start.17 = (bf16[2048,960]{0,1:T(8,128)(2,1)}, bf16[2048,960]{0,1:T(8,128)(2,1)}, u32[]{:S(2)}, u32[]{:S(2)}) collective-permute-start(bf16[2048,960]{0,1:T(8,128)(2,1)} %all-gather.4.cloned.1.call-done), channel_id=1, source_target_pairs={{0,1},{1,0},{2,3},{3,2},{4,5},{5,4},{6,7},{7,6},{8,9},{9,8},{10,11... | collective-permute-start | bytes 11796488 | tf_op jit(solution)/shard_map/ppermute | solution.py:110
  144.5 25.3 %collective-permute-start.18 = (bf16[2,128,2048]{2,1,0:T(8,128)(2,1)S(1)}, bf16[2,128,2048]{2,1,0:T(8,128)(2,1)S(1)}, u32[]{:S(2)}, u32[]{:S(2)}) collective-permute-start(bf16[2,128,2048]{2,1,0:T(8,128)(2,1)S(1)} %fusion.35), channel_id=1, source_target_pairs={{0,2},{2,0},{4,6},{6,4},{1,3},{3,1},{5,7},{7,5},{8,10},{10,8},{12,... | collective-permute-start | bytes 3145736 | tf_op jit(solution)/shard_map/ppermute | solution.py:26
  145.2 24.9 %collective-permute-start.19 = (bf16[2,128,2048]{2,1,0:T(8,128)(2,1)S(1)}, bf16[2,128,2048]{2,1,0:T(8,128)(2,1)S(1)}, u32[]{:S(2)}, u32[]{:S(2)}) collective-permute-start(bf16[2,128,2048]{2,1,0:T(8,128)(2,1)S(1)} %fusion.35), channel_id=1, source_target_pairs={{0,4},{2,6},{4,0},{6,2},{1,5},{3,7},{5,1},{7,3},{8,12},{10,14},{12... | collective-permute-start | bytes 3145736 | tf_op jit(solution)/shard_map/ppermute | solution.py:26
  203.5 14.6 %collective-permute-start.25 = (f32[2,2,640]{2,1,0:T(2,128)S(1)}, f32[2,2,640]{2,1,0:T(2,128)S(1)}, u32[]{:S(2)}, u32[]{:S(2)}) collective-permute-start(f32[2,2,640]{2,1,0:T(2,128)S(1)} %pad_maximum_fusion.29), channel_id=1, source_target_pairs={{0,24},{1,25},{2,26},{3,27},{4,28},{5,29},{6,30},{7,31}} | collective-permute-start | bytes 30728 | tf_op jit(solution)/shard_map/ppermute | solution.py:179
  208.7 13.7 %collective-permute-start.26 = (bf16[1,128,2048]{2,1,0:T(8,128)(2,1)S(1)}, bf16[1,128,2048]{2,1,0:T(8,128)(2,1)S(1)}, u32[]{:S(2)}, u32[]{:S(2)}) collective-permute-start(bf16[1,128,2048]{2,1,0:T(8,128)(2,1)S(1)} %slice.522), channel_id=1, source_target_pairs={{0,4},{2,6},{4,0},{6,2},{1,5},{3,7},{5,1},{7,3},{8,12},{10,14},{12... | collective-permute-start | bytes 1572872 | tf_op jit(solution)/shard_map/ppermute | solution.py:26
  210.4 13.4 %collective-permute-start.27 = (bf16[1,128,2048]{2,1,0:T(8,128)(2,1)S(1)}, bf16[1,128,2048]{2,1,0:T(8,128)(2,1)S(1)}, u32[]{:S(2)}, u32[]{:S(2)}) collective-permute-start(bf16[1,128,2048]{2,1,0:T(8,128)(2,1)S(1)} %slice.523), channel_id=1, source_target_pairs={{0,2},{2,0},{4,6},{6,4},{1,3},{3,1},{5,7},{7,5},{8,10},{10,8},{12,... | collective-permute-start | bytes 1572872 | tf_op jit(solution)/shard_map/ppermute | solution.py:26
  227.8 12.6 %collective-permute-start.28 = (bf16[1,128,2048]{2,1,0:T(8,128)(2,1)S(1)}, bf16[1,128,2048]{2,1,0:T(8,128)(2,1)S(1)}, u32[]{:S(2)}, u32[]{:S(2)}) collective-permute-start(bf16[1,128,2048]{2,1,0:T(8,128)(2,1)S(1)} %get-tuple-element.281), channel_id=1, source_target_pairs={{0,4},{2,6},{4,0},{6,2},{1,5},{3,7},{5,1},{7,3},{8,12},{10,14},{12... | collective-permute-start | bytes 1572872 | tf_op jit(solution)/shard_map/ppermute | solution.py:26
  228.3 12.5 %collective-permute-start.30 = (bf16[1,128,2048]{2,1,0:T(8,128)(2,1)S(1)}, bf16[1,128,2048]{2,1,0:T(8,128)(2,1)S(1)}, u32[]{:S(2)}, u32[]{:S(2)}) collective-permute-start(bf16[1,128,2048]{2,1,0:T(8,128)(2,1)S(1)} %get-tuple-element.283), channel_id=1, source_target_pairs={{0,2},{2,0},{4,6},{6,4},{1,3},{3,1},{5,7},{7,5},{8,10},{10,8},{12,... | collective-permute-start | bytes 1572872 | tf_op jit(solution)/shard_map/ppermute | solution.py:26
  241.3 22.9 %collective-permute-start.29 = (bf16[2,128,2048]{2,1,0:T(8,128)(2,1)S(1)}, bf16[2,128,2048]{2,1,0:T(8,128)(2,1)S(1)}, u32[]{:S(2)}, u32[]{:S(2)}) collective-permute-start(bf16[2,128,2048]{2,1,0:T(8,128)(2,1)S(1)} %pad_maximum_fusion.13), channel_id=1, source_target_pairs={{0,2},{2,0},{4,6},{6,4},{1,3},{3,1},{5,7},{7,5},{8,10},{10,8},{12,... | collective-permute-start | bytes 3145736 | tf_op jit(solution)/shard_map/ppermute | solution.py:26
  242.9 22.5 %collective-permute-start.31 = (bf16[2,128,2048]{2,1,0:T(8,128)(2,1)S(1)}, bf16[2,128,2048]{2,1,0:T(8,128)(2,1)S(1)}, u32[]{:S(2)}, u32[]{:S(2)}) collective-permute-start(bf16[2,128,2048]{2,1,0:T(8,128)(2,1)S(1)} %pad_maximum_fusion.14), channel_id=1, source_target_pairs={{0,4},{2,6},{4,0},{6,2},{1,5},{3,7},{5,1},{7,3},{8,12},{10,14},{12... | collective-permute-start | bytes 3145736 | tf_op jit(solution)/shard_map/ppermute | solution.py:26
  270.9 22.0 %collective-permute-start.32 = (bf16[2,128,2048]{2,1,0:T(8,128)(2,1)}, bf16[2,128,2048]{2,1,0:T(8,128)(2,1)}, u32[]{:S(2)}, u32[]{:S(2)}) collective-permute-start(bf16[2,128,2048]{2,1,0:T(8,128)(2,1)} %get-tuple-element.245), channel_id=1, source_target_pairs={{0,2},{2,0},{4,6},{6,4},{1,3},{3,1},{5,7},{7,5},{8,10},{10,8},{12,... | collective-permute-start | bytes 3145736 | tf_op jit(solution)/shard_map/ppermute | solution.py:26
  271.5 23.3 %collective-permute-start.33 = (bf16[2,128,2048]{2,1,0:T(8,128)(2,1)}, bf16[2,128,2048]{2,1,0:T(8,128)(2,1)}, u32[]{:S(2)}, u32[]{:S(2)}) collective-permute-start(bf16[2,128,2048]{2,1,0:T(8,128)(2,1)} %get-tuple-element.245), channel_id=1, source_target_pairs={{0,4},{2,6},{4,0},{6,2},{1,5},{3,7},{5,1},{7,3},{8,12},{10,14},{12... | collective-permute-start | bytes 3145736 | tf_op jit(solution)/shard_map/ppermute | solution.py:26
  368.1 22.7 %collective-permute-start.45 = (bf16[2048,768]{1,0:T(8,128)(2,1)}, bf16[2048,768]{1,0:T(8,128)(2,1)}, u32[]{:S(2)}, u32[]{:S(2)}) collective-permute-start(bf16[2048,768]{1,0:T(8,128)(2,1)} %convolution_convert_fusion.4), channel_id=1, source_target_pairs={{0,1},{1,0},{2,3},{3,2},{4,5},{5,4},{6,7},{7,6},{8,9},{9,8},{10,11... | collective-permute-start | bytes 9437192 | tf_op jit(solution)/shard_map/ppermute | solution.py:110
  369.3 14.6 %collective-permute-start.36 = (bf16[1,128,2048]{2,1,0:T(8,128)(2,1)}, bf16[1,128,2048]{2,1,0:T(8,128)(2,1)}, u32[]{:S(2)}, u32[]{:S(2)}) collective-permute-start(bf16[1,128,2048]{2,1,0:T(8,128)(2,1)} %get-tuple-element.275), channel_id=1, source_target_pairs={{0,4},{2,6},{4,0},{6,2},{1,5},{3,7},{5,1},{7,3},{8,12},{10,14},{12... | collective-permute-start | bytes 1572872 | tf_op jit(solution)/shard_map/ppermute | solution.py:26
  370.6 14.4 %collective-permute-start.38 = (bf16[1,128,2048]{2,1,0:T(8,128)(2,1)}, bf16[1,128,2048]{2,1,0:T(8,128)(2,1)}, u32[]{:S(2)}, u32[]{:S(2)}) collective-permute-start(bf16[1,128,2048]{2,1,0:T(8,128)(2,1)} %get-tuple-element.277), channel_id=1, source_target_pairs={{0,2},{2,0},{4,6},{6,4},{1,3},{3,1},{5,7},{7,5},{8,10},{10,8},{12,... | collective-permute-start | bytes 1572872 | tf_op jit(solution)/shard_map/ppermute | solution.py:26
  380.6 83.6 %collective-permute-start.44 = (bf16[2048,1536]{1,0:T(8,128)(2,1)}, bf16[2048,1536]{1,0:T(8,128)(2,1)}, u32[]{:S(2)}, u32[]{:S(2)}) collective-permute-start(bf16[2048,1536]{1,0:T(8,128)(2,1)} %convolution_convert_fusion.1), channel_id=1, source_target_pairs={{0,1},{1,0},{2,3},{3,2},{4,5},{5,4},{6,7},{7,6},{8,9},{9,8},{10,11... | collective-permute-start | bytes 18874376 | tf_op jit(solution)/shard_map/ppermute | solution.py:110
  387.9 24.8 %collective-permute-start.37 = (bf16[2,128,2048]{2,1,0:T(8,128)(2,1)}, bf16[2,128,2048]{2,1,0:T(8,128)(2,1)}, u32[]{:S(2)}, u32[]{:S(2)}) collective-permute-start(bf16[2,128,2048]{2,1,0:T(8,128)(2,1)} %pad_maximum_fusion.15), channel_id=1, source_target_pairs={{0,2},{2,0},{4,6},{6,4},{1,3},{3,1},{5,7},{7,5},{8,10},{10,8},{12,... | collective-permute-start | bytes 3145736 | tf_op jit(solution)/shard_map/ppermute | solution.py:26
  389.9 24.5 %collective-permute-start.39 = (bf16[2,128,2048]{2,1,0:T(8,128)(2,1)}, bf16[2,128,2048]{2,1,0:T(8,128)(2,1)}, u32[]{:S(2)}, u32[]{:S(2)}) collective-permute-start(bf16[2,128,2048]{2,1,0:T(8,128)(2,1)} %pad_maximum_fusion.16), channel_id=1, source_target_pairs={{0,4},{2,6},{4,0},{6,2},{1,5},{3,7},{5,1},{7,3},{8,12},{10,14},{12... | collective-permute-start | bytes 3145736 | tf_op jit(solution)/shard_map/ppermute | solution.py:26
  397.8 187.5 %reduce-scatter.6.cloned.1.call-start = ((), (), s32[]{:S(2)}) async-start(), calls=%async_computation.5 | async-start | bytes 7864320 | tf_op jit(solution)/shard_map/reduce_scatter | solution.py:123
  425.5 23.5 %collective-permute-start.40 = (bf16[2,128,2048]{2,1,0:T(8,128)(2,1)}, bf16[2,128,2048]{2,1,0:T(8,128)(2,1)}, u32[]{:S(2)}, u32[]{:S(2)}) collective-permute-start(bf16[2,128,2048]{2,1,0:T(8,128)(2,1)} %get-tuple-element.242), channel_id=1, source_target_pairs={{0,2},{2,0},{4,6},{6,4},{1,3},{3,1},{5,7},{7,5},{8,10},{10,8},{12,... | collective-permute-start | bytes 3145736 | tf_op jit(solution)/shard_map/ppermute | solution.py:26
  426.6 24.5 %collective-permute-start.41 = (bf16[2,128,2048]{2,1,0:T(8,128)(2,1)}, bf16[2,128,2048]{2,1,0:T(8,128)(2,1)}, u32[]{:S(2)}, u32[]{:S(2)}) collective-permute-start(bf16[2,128,2048]{2,1,0:T(8,128)(2,1)} %get-tuple-element.242), channel_id=1, source_target_pairs={{0,4},{2,6},{4,0},{6,2},{1,5},{3,7},{5,1},{7,3},{8,12},{10,14},{12... | collective-permute-start | bytes 3145736 | tf_op jit(solution)/shard_map/ppermute | solution.py:26
  475.0 239.4 %reduce-scatter.8.cloned.1.call-start = ((), (), s32[]{:S(2)}) async-start(), calls=%async_computation.6 | async-start | bytes 4915200 | tf_op jit(solution)/shard_map/reduce_scatter | solution.py:123
  495.4 18.9 %collective-permute-start.46 = (f32[2,2,640]{2,1,0:T(2,128)S(1)}, f32[2,2,640]{2,1,0:T(2,128)S(1)}, u32[]{:S(2)}, u32[]{:S(2)}) collective-permute-start(f32[2,2,640]{2,1,0:T(2,128)S(1)} %copy.415), channel_id=1, source_target_pairs={{8,0},{16,8},{24,16},{9,1},{17,9},{25,17},{10,2},{18,10},{26,18},{... | collective-permute-start | bytes 30728 | tf_op jit(solution)/shard_map/ppermute | solution.py:179
  496.7 18.8 %collective-permute-start.47 = (f32[2,2,640]{2,1,0:T(2,128)S(1)}, f32[2,2,640]{2,1,0:T(2,128)S(1)}, u32[]{:S(2)}, u32[]{:S(2)}) collective-permute-start(f32[2,2,640]{2,1,0:T(2,128)S(1)} %copy.415), channel_id=1, source_target_pairs={{16,0},{24,8},{17,1},{25,9},{18,2},{26,10},{19,3},{27,11},{20,4},{... | collective-permute-start | bytes 30728 | tf_op jit(solution)/shard_map/ppermute | solution.py:179
  498.0 15.0 %collective-permute-start.48 = (f32[2,2,640]{2,0,1:T(2,128)S(1)}, f32[2,2,640]{2,0,1:T(2,128)S(1)}, u32[]{:S(2)}, u32[]{:S(2)}) collective-permute-start(f32[2,2,640]{2,0,1:T(2,128)S(1)} %pad_maximum_fusion.30), channel_id=1, source_target_pairs={{24,0},{25,1},{26,2},{27,3},{28,4},{29,5},{30,6},{31,7}} | collective-permute-start | bytes 30728 | tf_op jit(solution)/shard_map/ppermute | solution.py:179
  500.6 16.0 %collective-permute-start.49 = (bf16[1,128,2048]{2,1,0:T(8,128)(2,1)S(1)}, bf16[1,128,2048]{2,1,0:T(8,128)(2,1)S(1)}, u32[]{:S(2)}, u32[]{:S(2)}) collective-permute-start(bf16[1,128,2048]{2,1,0:T(8,128)(2,1)S(1)} %get-tuple-element.273), channel_id=1, source_target_pairs={{0,2},{2,0},{4,6},{6,4},{1,3},{3,1},{5,7},{7,5},{8,10},{10,8},{12,... | collective-permute-start | bytes 1572872 | tf_op jit(solution)/shard_map/ppermute | solution.py:26
  501.5 15.1 %collective-permute-start.50 = (bf16[1,128,2048]{2,1,0:T(8,128)(2,1)S(1)}, bf16[1,128,2048]{2,1,0:T(8,128)(2,1)}, u32[]{:S(2)}, u32[]{:S(2)}) collective-permute-start(bf16[1,128,2048]{2,1,0:T(8,128)(2,1)S(1)} %get-tuple-element.272), channel_id=1, source_target_pairs={{0,4},{2,6},{4,0},{6,2},{1,5},{3,7},{5,1},{7,3},{8,12},{10,14},{12... | collective-permute-start | bytes 1572872 | tf_op jit(solution)/shard_map/ppermute | solution.py:26
  513.0 31.8 %collective-permute-start.54 = (bf16[128,768]{0,1:T(8,128)(2,1)}, bf16[128,768]{0,1:T(8,128)(2,1)}, u32[]{:S(2)}, u32[]{:S(2)}) collective-permute-start(bf16[128,768]{0,1:T(8,128)(2,1)} %bitcast.149), channel_id=1, source_target_pairs={{0,6},{2,4},{4,2},{6,0},{1,7},{3,5},{5,3},{7,1},{8,14},{10,12},{12... | collective-permute-start | bytes 589832 | tf_op jit(solution)/shard_map/ppermute | solution.py:26
  514.3 32.0 %collective-permute-start.55 = (bf16[128,768]{0,1:T(8,128)(2,1)}, bf16[128,768]{0,1:T(8,128)(2,1)}, u32[]{:S(2)}, u32[]{:S(2)}) collective-permute-start(bf16[128,768]{0,1:T(8,128)(2,1)} %bitcast.150), channel_id=1, source_target_pairs={{0,4},{2,6},{4,0},{6,2},{1,5},{3,7},{5,1},{7,3},{8,12},{10,14},{12... | collective-permute-start | bytes 589832 | tf_op jit(solution)/shard_map/ppermute | solution.py:26
  515.5 30.9 %collective-permute-start.56 = (bf16[128,768]{0,1:T(8,128)(2,1)}, bf16[128,768]{0,1:T(8,128)(2,1)}, u32[]{:S(2)}, u32[]{:S(2)}) collective-permute-start(bf16[128,768]{0,1:T(8,128)(2,1)} %bitcast.151), channel_id=1, source_target_pairs={{0,2},{2,0},{4,6},{6,4},{1,3},{3,1},{5,7},{7,5},{8,10},{10,8},{12,... | collective-permute-start | bytes 589832 | tf_op jit(solution)/shard_map/ppermute | solution.py:26
  520.2 32.5 %collective-permute-start.52 = (bf16[2,128,2048]{2,1,0:T(8,128)(2,1)S(1)}, bf16[2,128,2048]{2,1,0:T(8,128)(2,1)}, u32[]{:S(2)}, u32[]{:S(2)}) collective-permute-start(bf16[2,128,2048]{2,1,0:T(8,128)(2,1)S(1)} %pad_maximum_fusion.17), channel_id=1, source_target_pairs={{0,2},{2,0},{4,6},{6,4},{1,3},{3,1},{5,7},{7,5},{8,10},{10,8},{12,... | collective-permute-start | bytes 3145736 | tf_op jit(solution)/shard_map/ppermute | solution.py:26
  522.2 30.5 %collective-permute-start.53 = (bf16[2,128,2048]{2,1,0:T(8,128)(2,1)}, bf16[2,128,2048]{2,1,0:T(8,128)(2,1)}, u32[]{:S(2)}, u32[]{:S(2)}) collective-permute-start(bf16[2,128,2048]{2,1,0:T(8,128)(2,1)} %pad_maximum_fusion.18), channel_id=1, source_target_pairs={{0,4},{2,6},{4,0},{6,2},{1,5},{3,7},{5,1},{7,3},{8,12},{10,14},{12... | collective-permute-start | bytes 3145736 | tf_op jit(solution)/shard_map/ppermute | solution.py:26
  598.1 23.7 %collective-permute-start.58 = (bf16[2048,960]{0,1:T(8,128)(2,1)}, bf16[2048,960]{0,1:T(8,128)(2,1)}, u32[]{:S(2)}, u32[]{:S(2)}) collective-permute-start(bf16[2048,960]{0,1:T(8,128)(2,1)} %pad_maximum_fusion.1), channel_id=1, source_target_pairs={{0,1},{1,0},{2,3},{3,2},{4,5},{5,4},{6,7},{7,6},{8,9},{9,8},{10,11... | collective-permute-start | bytes 11796488 | tf_op jit(solution)/shard_map/ppermute | solution.py:110
  619.5 46.5 %collective-permute-start.57 = (bf16[2,128,2048]{2,1,0:T(8,128)(2,1)}, bf16[2,128,2048]{2,1,0:T(8,128)(2,1)}, u32[]{:S(2)}, u32[]{:S(2)}) collective-permute-start(bf16[2,128,2048]{2,1,0:T(8,128)(2,1)} %get-tuple-element.236), channel_id=1, source_target_pairs={{0,1},{1,0},{2,3},{3,2},{4,5},{5,4},{6,7},{7,6},{8,9},{9,8},{10,11... | collective-permute-start | bytes 3145736 | tf_op jit(solution)/shard_map/ppermute | solution.py:110
  639.9 15.1 %collective-permute-start.59 = (bf16[1,128,2048]{2,1,0:T(8,128)(2,1)}, bf16[1,128,2048]{2,1,0:T(8,128)(2,1)}, u32[]{:S(2)}, u32[]{:S(2)}) collective-permute-start(bf16[1,128,2048]{2,1,0:T(8,128)(2,1)} %get-tuple-element.263), channel_id=1, source_target_pairs={{0,4},{2,6},{4,0},{6,2},{1,5},{3,7},{5,1},{7,3},{8,12},{10,14},{12... | collective-permute-start | bytes 1572872 | tf_op jit(solution)/shard_map/ppermute | solution.py:26
  641.4 15.0 %collective-permute-start.61 = (bf16[1,128,2048]{2,1,0:T(8,128)(2,1)}, bf16[1,128,2048]{2,1,0:T(8,128)(2,1)}, u32[]{:S(2)}, u32[]{:S(2)}) collective-permute-start(bf16[1,128,2048]{2,1,0:T(8,128)(2,1)} %get-tuple-element.265), channel_id=1, source_target_pairs={{0,2},{2,0},{4,6},{6,4},{1,3},{3,1},{5,7},{7,5},{8,10},{10,8},{12,... | collective-permute-start | bytes 1572872 | tf_op jit(solution)/shard_map/ppermute | solution.py:26
  646.8 17.6 %collective-permute-start.66 = (f32[2,2048]{1,0:T(2,128)S(1)}, f32[2,2048]{1,0:T(2,128)S(1)}, u32[]{:S(2)}, u32[]{:S(2)}) collective-permute-start(f32[2,2048]{1,0:T(2,128)S(1)} %fusion.139), channel_id=1, source_target_pairs={{0,2},{2,0},{4,6},{6,4},{1,3},{3,1},{5,7},{7,5},{8,10},{10,8},{12,... | collective-permute-start | bytes 49160 | tf_op jit(solution)/shard_map/ppermute | solution.py:156
  659.4 27.6 %collective-permute-start.60 = (bf16[2,128,2048]{2,1,0:T(8,128)(2,1)}, bf16[2,128,2048]{2,1,0:T(8,128)(2,1)}, u32[]{:S(2)}, u32[]{:S(2)}) collective-permute-start(bf16[2,128,2048]{2,1,0:T(8,128)(2,1)} %pad_maximum_fusion.19), channel_id=1, source_target_pairs={{0,2},{2,0},{4,6},{6,4},{1,3},{3,1},{5,7},{7,5},{8,10},{10,8},{12,... | collective-permute-start | bytes 3145736 | tf_op jit(solution)/shard_map/ppermute | solution.py:26
  661.9 25.1 %collective-permute-start.62 = (bf16[2,128,2048]{2,1,0:T(8,128)(2,1)}, bf16[2,128,2048]{2,1,0:T(8,128)(2,1)}, u32[]{:S(2)}, u32[]{:S(2)}) collective-permute-start(bf16[2,128,2048]{2,1,0:T(8,128)(2,1)} %pad_maximum_fusion.20), channel_id=1, source_target_pairs={{0,4},{2,6},{4,0},{6,2},{1,5},{3,7},{5,1},{7,3},{8,12},{10,14},{12... | collective-permute-start | bytes 3145736 | tf_op jit(solution)/shard_map/ppermute | solution.py:26
  664.3 22.5 %collective-permute-start.64 = (bf16[320,368]{1,0:T(8,128)(2,1)S(1)}, bf16[320,368]{1,0:T(8,128)(2,1)S(1)}, u32[]{:S(2)}, u32[]{:S(2)}) collective-permute-start(bf16[320,368]{1,0:T(8,128)(2,1)S(1)} %slice.691), channel_id=1, source_target_pairs={{0,1},{1,0},{2,3},{3,2},{4,5},{5,4},{6,7},{7,6},{8,9},{9,8},{10,11... | collective-permute-start | bytes 706568 | tf_op jit(solution)/shard_map/ppermute | solution.py:110
  664.5 22.4 %collective-permute-start.67 = (f32[2,2048]{1,0:T(2,128)S(1)}, f32[2,2048]{1,0:T(2,128)S(1)}, u32[]{:S(2)}, u32[]{:S(2)}) collective-permute-start(f32[2,2048]{1,0:T(2,128)S(1)} %fusion.181), channel_id=1, source_target_pairs={{0,4},{2,6},{4,0},{6,2},{1,5},{3,7},{5,1},{7,3},{8,12},{10,14},{12... | collective-permute-start | bytes 49160 | tf_op jit(solution)/shard_map/ppermute | solution.py:156
  689.7 13.0 %collective-permute-start.78 = (bf16[128,1536]{1,0:T(8,128)(2,1)S(1)}, bf16[128,1536]{1,0:T(8,128)(2,1)S(1)}, u32[]{:S(2)}, u32[]{:S(2)}) collective-permute-start(bf16[128,1536]{1,0:T(8,128)(2,1)S(1)} %get-tuple-element.328), channel_id=1, source_target_pairs={{0,6},{2,4},{4,2},{6,0},{1,7},{3,5},{5,3},{7,1},{8,14},{10,12},{12... | collective-permute-start | bytes 1179656 | tf_op jit(solution)/shard_map/ppermute | solution.py:26
  690.4 17.6 %collective-permute-start.79 = (bf16[128,1536]{1,0:T(8,128)(2,1)S(1)}, bf16[128,1536]{1,0:T(8,128)(2,1)S(1)}, u32[]{:S(2)}, u32[]{:S(2)}) collective-permute-start(bf16[128,1536]{1,0:T(8,128)(2,1)S(1)} %get-tuple-element.327), channel_id=1, source_target_pairs={{0,4},{2,6},{4,0},{6,2},{1,5},{3,7},{5,1},{7,3},{8,12},{10,14},{12... | collective-permute-start | bytes 1179656 | tf_op jit(solution)/shard_map/ppermute | solution.py:26
  691.8 16.3 %collective-permute-start.80 = (bf16[128,1536]{1,0:T(8,128)(2,1)S(1)}, bf16[128,1536]{1,0:T(8,128)(2,1)S(1)}, u32[]{:S(2)}, u32[]{:S(2)}) collective-permute-start(bf16[128,1536]{1,0:T(8,128)(2,1)S(1)} %get-tuple-element.326), channel_id=1, source_target_pairs={{0,2},{2,0},{4,6},{6,4},{1,3},{3,1},{5,7},{7,5},{8,10},{10,8},{12,... | collective-permute-start | bytes 1179656 | tf_op jit(solution)/shard_map/ppermute | solution.py:26
  696.9 14.0 %collective-permute-start.63 = (bf16[2,128,2048]{2,1,0:T(8,128)(2,1)S(1)}, bf16[2,128,2048]{2,1,0:T(8,128)(2,1)S(1)}, u32[]{:S(2)}, u32[]{:S(2)}) collective-permute-start(bf16[2,128,2048]{2,1,0:T(8,128)(2,1)S(1)} %get-tuple-element.234), channel_id=1, source_target_pairs={{0,1},{1,0},{2,3},{3,2},{4,5},{5,4},{6,7},{7,6},{8,9},{9,8},{10,11... | collective-permute-start | bytes 3145736 | tf_op jit(solution)/shard_map/ppermute | solution.py:110
  715.7 13.3 %collective-permute-start.73 = (f32[2,2048]{1,0:T(2,128)S(1)}, f32[2,2048]{1,0:T(2,128)S(1)}, u32[]{:S(2)}, u32[]{:S(2)}) collective-permute-start(f32[2,2048]{1,0:T(2,128)S(1)} %add.762), channel_id=1, source_target_pairs={{0,16},{8,24},{16,0},{24,8},{1,17},{9,25},{17,1},{25,9},{2,18},{10... | collective-permute-start | bytes 49160 | tf_op jit(solution)/shard_map/ppermute | solution.py:145
  717.3 14.4 %collective-permute-start.74 = (f32[2,2048]{1,0:T(2,128)S(1)}, f32[2,2048]{1,0:T(2,128)S(1)}, u32[]{:S(2)}, u32[]{:S(2)}) collective-permute-start(f32[2,2048]{1,0:T(2,128)S(1)} %add.762), channel_id=1, source_target_pairs={{0,24},{8,0},{16,8},{24,16},{1,25},{9,1},{17,9},{25,17},{2,26},{10... | collective-permute-start | bytes 49160 | tf_op jit(solution)/shard_map/ppermute | solution.py:145
  732.6 12.0 %collective-permute-start.77 = (bf16[128,960]{0,1:T(8,128)(2,1)S(1)}, bf16[128,960]{0,1:T(8,128)(2,1)S(1)}, u32[]{:S(2)}, u32[]{:S(2)}) collective-permute-start(bf16[128,960]{0,1:T(8,128)(2,1)S(1)} %bitcast.593), channel_id=1, source_target_pairs={{0,2},{2,0},{4,6},{6,4},{1,3},{3,1},{5,7},{7,5},{8,10},{10,8},{12,... | collective-permute-start | bytes 737288 | tf_op jit(solution)/shard_map/ppermute | solution.py:26
  (147 other events, 1871.4 us)
Sparse Core Ops, SparseCore 0:
  46.0 73.5 all-gather.3
  132.0 165.7 all-gather.5
  397.9 58.1 reduce-scatter.3
  475.1 110.0 reduce-scatter.5
  643.0 71.3 reduce-scatter.7

commit v8 on v7

--- a/solution.py
+++ b/solution.py
@@ -472,12 +472,12 @@
         (lax.all_gather(first_rows, "z", axis=0, tiled=True), normed_low, later_rows)
     )
     w_later = lax.all_gather(later_rows, ("c", "z"), axis=0)
-    w_first = (first_own, to_core(first_own))
+    first_other, down_state = lax.optimization_barrier((to_core(first_own), down_state))
+    w_first = (first_own, first_other)
     w_rec = jnp.concatenate(
         [w[:, p * part_width : (p + 1) * part_width] for p in (0, 1) for w in w_first], axis=1
     )
     w_back = jnp.concatenate([w[:, 2 * part_width :] for w in w_first], axis=1)
-    w_rec, down_state = lax.optimization_barrier((w_rec, down_state))
     projected = dot(normed_low, w_rec, 1, 0)
     source_rows = projected[:, :rec_width].astype(BF16).reshape(n_streams, n_rows, rec_width)
     branch, branch_back = jax.vjp(jax.nn.gelu, projected[:, rec_width:])

time: 763 us -> 765 us (level)
  starting transfers between devices: 98.5 us -> 110 us
  other arithmetic: 115 us -> 105 us
    ppermute x8, starting transfers between devices: 19.2 us -> 31.6 us  [shifted(): lax.ppermute(block, 'z', [(i - distance, i) for i in range(size) if 0 <=...]
    concatenate x1 -> x0, other arithmetic: 10 us -> none  [shards(): jnp.concatenate([w[:, p * part_width:(p + 1) * part_width] for p in (0, 1...]
    unnamed x263 -> x269, local copies, waits for them, and re-layouts: 20.8 us -> 22.4 us
  transfers between devices with their start and end apart: 86 -> 86, of which waited for: 37 -> 34; matrix products, arithmetic and copies ran while one was open for 37% -> 35% of each run, Pallas kernels for 2% -> 2%
where the time goes in v8:
time: 765 us; the launch traced here: 760 us
  waiting for transfers between devices  249 us (33%)
  local copies, waits for them, and re-layouts  116 us (15%)
  starting transfers between devices  110 us (14%)
  other arithmetic  105 us (14%)
  matrix products  92.4 us (12%)
  Pallas kernels  70.7 us (9%)
  between operations  16.9 us (2%)
    ppermute x50, waiting for transfers between devices, to_partner(): return lax.ppermute(block, 'j', [(i, i ^ bit) for i in range(PLANE)])  193 us
    dot_general x13, matrix products, dot(): lax.dot_general(left, right, (((left_dim,), (right_dim,)), ((), ())), pre...  85.7 us
    ppermute x50, starting transfers between devices, to_partner(): return lax.ppermute(block, 'j', [(i, i ^ bit) for i in range(PLANE)])  55.7 us
    pallas_call x1, Pallas kernels, mlp(): pl.pallas_call(mlp_kernel, grid=(streams, halves, tiles), in_specs=[token...  53.9 us
    ppermute x8, starting transfers between devices, shifted(): lax.ppermute(block, 'z', [(i - distance, i) for i in range(size) if 0 <=...  31.6 us
    reduce_scatter x3, waiting for transfers between devices, sum_along_z(): return lax.psum_scatter(total, 'z', scatter_dimension=0, tiled=True)  29.9 us
    unnamed x269, local copies, waits for them, and re-layouts  22.4 us
    ppermute x3, waiting for transfers between devices, sum_of_chip_plane(): array = array + lax.ppermute(array, axis, pairs)  19.5 us
  transfers between devices with their start and end apart: 86, of which 34 were waited for; matrix products, arithmetic and copies ran while one was open for 35% of the time, Pallas kernels for 2%

profile of v8, /device:TPU:0, one launch (start us, length us, event | category | flops | bytes accessed | tf_op | source)
XLA Modules:
  0.0 759.7 jit_solution(10729943417873155722)
XLA Ops:
  9.8 3.0 collective-permute-start.3
  12.8 2.6 collective-permute-start.4
  22.0 2.4 collective-permute-start
  26.7 5.4 collective-permute-done
  32.1 3.2 collective-permute-done.1
  47.3 18.7 %collective-permute-done.6 = bf16[88,328]{1,0:T(8,128)(2,1)S(1)} collective-permute-done((bf16[88,328]{1,0:T(8,128)(2,1)}, bf16[88,328]{1,0:T(8,128)(2,1)S(1)}, u32[]{:S(2)}, u32[]{:S(2)}) %collective-permute-start.6) | collective-permute-done | bytes 57760 | tf_op jit(solution)/shard_map/ppermute | solution.py:26
  91.7 2.6 broadcast.860.clone
  100.0 18.0 %collective-permute-done.12 = bf16[1,128,2048]{2,1,0:T(8,128)(2,1)} collective-permute-done((bf16[1,128,2048]{2,1,0:T(8,128)(2,1)}, bf16[1,128,2048]{2,1,0:T(8,128)(2,1)}, u32[]{:S(2)}, u32[]{:S(2)}) %collective-permute-start.12) | collective-permute-done | bytes 524320 | tf_op jit(solution)/shard_map/ppermute | solution.py:26
  120.2 3.1 fusion
  123.3 5.2 fusion.2
  138.9 3.7 collective-permute-done.9
  145.7 16.6 %collective-permute-done.18 = bf16[2,128,2048]{2,1,0:T(8,128)(2,1)S(1)} collective-permute-done((bf16[2,128,2048]{2,1,0:T(8,128)(2,1)S(1)}, bf16[2,128,2048]{2,1,0:T(8,128)(2,1)S(1)}, u32[]{:S(2)}, u32[]{:S(2)}) %collective-permute-start.18) | collective-permute-done | bytes 1048608 | tf_op jit(solution)/shard_map/ppermute | solution.py:26
  162.7 3.6 fusion.154
  166.3 5.6 fusion.65
  172.1 3.0 collective-permute-start.20
  179.0 2.8 multiply_add_fusion.2
  184.2 3.1 bitcast_multiply_fusion.7
  188.1 7.8 %shard_map.246 = (f32[2,512,640]{2,1,0:T(8,128)S(1)}, f32[2,512,640]{2,1,0:T(8,128)S(1)}) custom-call(f32[2,512,640]{2,1,0:T(8,128)S(1)} %get-tuple-element.297.keep_ref, f32[2,512,640]{2,1,0:T(8,128)S(1)} %get-tuple-element.296.add_ref), custom_call_target="tpu_custom_call" | custom-call | flops 5242880 | bytes 10485760 | tf_op jit(solution)/shard_map/pallas_call | solution.py:233
  200.0 8.3 %collective-permute-start.25 = (f32[2,2,640]{2,1,0:T(2,128)S(1)}, f32[2,2,640]{2,1,0:T(2,128)S(1)}, u32[]{:S(2)}, u32[]{:S(2)}) collective-permute-start(f32[2,2,640]{2,1,0:T(2,128)S(1)} %pad_maximum_fusion.31), channel_id=1, source_target_pairs={{0,24},{1,25},{2,26},{3,27},{4,28},{5,29},{6,30},{7,31}} | collective-permute-start | bytes 30728 | tf_op jit(solution)/shard_map/ppermute | solution.py:179
  212.9 13.8 %collective-permute-start.24 = (f32[2,2,640]{2,1,0:T(2,128)S(1)}, f32[2,2,640]{2,1,0:T(2,128)S(1)}, u32[]{:S(2)}, u32[]{:S(2)}) collective-permute-start(f32[2,2,640]{2,1,0:T(2,128)S(1)} %pad_maximum_fusion.31), channel_id=1, source_target_pairs={{0,16},{8,24},{1,17},{9,25},{2,18},{10,26},{3,19},{11,27},{4,20},{... | collective-permute-start | bytes 30728 | tf_op jit(solution)/shard_map/ppermute | solution.py:179
  230.3 3.6 convolution_convert_fusion.3
  235.4 10.7 %collective-permute-done.28 = bf16[1,128,2048]{2,1,0:T(8,128)(2,1)S(1)} collective-permute-done((bf16[1,128,2048]{2,1,0:T(8,128)(2,1)S(1)}, bf16[1,128,2048]{2,1,0:T(8,128)(2,1)S(1)}, u32[]{:S(2)}, u32[]{:S(2)}) %collective-permute-start.28) | collective-permute-done | bytes 524320 | tf_op jit(solution)/shard_map/ppermute | solution.py:26
  250.3 20.7 %collective-permute-done.29 = bf16[2,128,2048]{2,1,0:T(8,128)(2,1)S(1)} collective-permute-done((bf16[2,128,2048]{2,1,0:T(8,128)(2,1)S(1)}, bf16[2,128,2048]{2,1,0:T(8,128)(2,1)S(1)}, u32[]{:S(2)}, u32[]{:S(2)}) %collective-permute-start.29) | collective-permute-done | bytes 1048608 | tf_op jit(solution)/shard_map/ppermute | solution.py:26
  278.8 20.3 %collective-permute-done.32 = bf16[2,128,2048]{2,1,0:T(8,128)(2,1)} collective-permute-done((bf16[2,128,2048]{2,1,0:T(8,128)(2,1)}, bf16[2,128,2048]{2,1,0:T(8,128)(2,1)}, u32[]{:S(2)}, u32[]{:S(2)}) %collective-permute-start.32) | collective-permute-done | bytes 1048608 | tf_op jit(solution)/shard_map/ppermute | solution.py:26
  303.4 2.4 bitcast_dynamic-update-slice_fusion.4
  308.0 3.1 collective-permute-done.34
  312.8 53.9 %shard_map.247 = (bf16[2,1024,768]{2,1,0:T(8,128)(2,1)}, bf16[2,1024,1536]{2,1,0:T(8,128)(2,1)}, bf16[2,512,2048]{2,1,0:T(8,128)(2,1)}, bf16[2,512,2048]{2,1,0:T(8,128)(2,1)}) custom-call(bf16[2,512,2048]{2,1,0:T(8,128)(2,1)} %bitcast.560, bf16[2,512,2048]{2,1,0:T(8,128)(2,1)} %bitcast.563, bf16[2,2048,2304]{2,1,0:T(8,128)(2,1)} %bitcast.617, ...), custom_call_target="tpu_custom_call" | custom-call | flops 38654705664 | bytes 41943040 | tf_op jit(solution)/shard_map/pallas_call | solution.py:321
  366.7 8.0 %convolution_convert_fusion.4 = bf16[2048,768]{1,0:T(8,128)(2,1)} fusion(bf16[1024,2048]{1,0:T(8,128)(2,1)} %bitcast.564, bf16[2,1024,768]{2,1,0:T(8,128)(2,1)} %get-tuple-element.99, s32[]{:T(128)S(6)} %select_n.658), kind=kOutput, calls=%fused_computation.28 | convolution fusion | flops 3222798336 | bytes 8912900 | tf_op jit(solution)/shard_map/dot_general | solution.py:20
  378.2 9.1 %convolution_convert_fusion.1 = bf16[2048,1536]{1,0:T(8,128)(2,1)} fusion(bf16[1024,2048]{1,0:T(8,128)(2,1)S(1)} %bitcast.561, bf16[2,1024,1536]{2,1,0:T(8,128)(2,1)S(1)} %bitcast.621, s32[]{:T(128)S(6)} %select_n.658), kind=kOutput, calls=%fused_computation.11 | convolution fusion | flops 6445596672 | bytes 13631492 | tf_op jit(solution)/shard_map/dot_general | solution.py:20
  387.3 3.3 collective-permute-done.36
  397.7 6.9 add_convert_fusion.2
  404.8 14.5 %collective-permute-done.37 = bf16[2,128,2048]{2,1,0:T(8,128)(2,1)} collective-permute-done((bf16[2,128,2048]{2,1,0:T(8,128)(2,1)}, bf16[2,128,2048]{2,1,0:T(8,128)(2,1)}, u32[]{:S(2)}, u32[]{:S(2)}) %collective-permute-start.37) | collective-permute-done | bytes 1048608 | tf_op jit(solution)/shard_map/ppermute | solution.py:26
  421.1 3.3 multiply_reduce_fusion.5
  424.5 2.5 broadcast.860
  427.2 4.9 bitcast_dynamic-update-slice_fusion.2
  436.1 19.7 %collective-permute-done.40 = bf16[2,128,2048]{2,1,0:T(8,128)(2,1)} collective-permute-done((bf16[2,128,2048]{2,1,0:T(8,128)(2,1)}, bf16[2,128,2048]{2,1,0:T(8,128)(2,1)}, u32[]{:S(2)}, u32[]{:S(2)}) %collective-permute-start.40) | collective-permute-done | bytes 1048608 | tf_op jit(solution)/shard_map/ppermute | solution.py:26
  462.3 2.5 bitcast_dynamic-update-slice_fusion
  464.8 3.4 collective-permute-done.42
  470.9 10.8 %add_convert_fusion = bf16[2048,1536]{1,0:T(8,128)(2,1)} fusion(bf16[2048,1536]{1,0:T(8,128)(2,1)} %collective-permute-done.44, bf16[1024,2048]{1,0:T(8,128)(2,1)S(1)} %bitcast.562, bf16[2,1024,1536]{2,1,0:T(8,128)(2,1)S(1)} %bitcast.623, s32[]{:T(128)S(6)} %select_n.657), kind=kOutput, calls=%fused_computation | convolution fusion | flops 6458179584 | bytes 19922948 | tf_op jit(solution)/shard_map/dot_general | solution.py:20
  482.4 6.2 fusion.45
  488.7 4.4 fusion.63
  493.0 9.1 %shard_map.248 = (f32[2,512,640]{2,1,0:T(8,128)S(1)}, f32[2,512,640]{2,1,0:T(8,128)S(1)}) custom-call(f32[2,512,640]{2,1,0:T(8,128)S(1)} %copy-done.2, f32[2,512,640]{2,1,0:T(8,128)S(1)} %bitcast.545), custom_call_target="tpu_custom_call" | custom-call | flops 5242880 | bytes 10485760 | tf_op jit(solution)/shard_map/pallas_call | solution.py:233
  509.6 5.1 convolution_convert_fusion.7
  533.1 4.4 multiply_reduce_fusion
  537.5 4.0 fusion.147
  541.7 7.9 %multiply_reduce_fusion.4 = (f32[640]{0:T(1024)S(1)}, f32[640]{0:T(1024)S(1)}, f32[640]{0:T(1024)S(1)}, f32[640]{0:T(1024)S(1)}, f32[1024,640]{1,0:T(8,128)S(1)}) fusion(f32[2,512,640]{2,1,0:T(8,128)} %get-tuple-element.413, f32[2,512,640]{2,1,0:T(8,128)S(1)} %copy-done.25, f32[2,512,640]{2,1,0:T(8,128)S(1)} %copy-done.23, ...), kind=kOutput, calls=%fused_computation.86 | convolution fusion | flops 1700656640 | bytes 25249280 | tf_op jit(solution)/shard_map/dot_general | solution.py:20
  559.6 3.7 fusion.41
  563.4 27.5 %reduce-scatter.6.cloned.1.call-done = bf16[512,1536]{1,0:T(8,128)(2,1)} async-done(((bf16[2048,1536]{1,0:T(8,128)(2,1)}), bf16[512,1536]{1,0:T(8,128)(2,1)}) %reduce-scatter.6.cloned.1.call-update) | async-done | bytes 1572880 | tf_op jit(solution)/shard_map/reduce_scatter | solution.py:123
  590.8 8.5 %convolution_convert_fusion = bf16[2048,1280]{0,1:T(8,128)(2,1)S(1)} fusion(bf16[1024,2048]{1,0:T(8,128)(2,1)} %fusion.2, bf16[1024,1280]{1,0:T(8,128)(2,1)} %pad_maximum_fusion.4), kind=kOutput, calls=%fused_computation.10 | convolution fusion | flops 5371330560 | bytes 12058624 | tf_op jit(solution)/shard_map/dot_general | solution.py:20
  607.9 2.6 dynamic_update_slice.114
  628.1 5.0 add_convert_fusion.1
  633.1 8.5 %fusion.4 = (f32[2048]{0:T(1024)S(1)}, bf16[1024,2048]{1,0:T(8,128)(2,1)S(1)}) fusion(bf16[2,4,128,2048]{3,2,1,0:T(8,128)(2,1)} %fusion.51, f32[1024]{0:T(1024)S(1)} %bitcast.614, bf16[1024,1280]{1,0:T(8,128)(2,1)S(1)} %copy-done.51, bf16[2048,320]{0,1:T(8,128)(2,1)} %copy-done.66, bf16[2048,320]{0,1:T(8,128)(2,1)} %copy-done.64, ...), kind=kOutput, calls=%fused_computation.8 | convolution fusion | flops 5400164352 | bytes 16265216 | tf_op jit(solution)/shard_map/dot_general | solution.py:20
  648.2 3.2 convolution_convert_fusion.6
  652.3 7.5 collective-permute-done.59
  672.3 19.5 %collective-permute-done.67 = f32[2,2048]{1,0:T(2,128)S(1)} collective-permute-done((f32[2,2048]{1,0:T(2,128)S(1)}, f32[2,2048]{1,0:T(2,128)S(1)}, u32[]{:S(2)}, u32[]{:S(2)}) %collective-permute-start.67) | collective-permute-done | bytes 16416 | tf_op jit(solution)/shard_map/ppermute | solution.py:156
  691.9 2.6 fusion.40
  701.9 5.8 collective-permute-done.78
  707.6 5.3 collective-permute-done.79
  716.9 2.4 reduce-scatter.8.cloned.1.call-done
  722.3 2.7 collective-permute-start.74
  728.0 3.3 collective-permute-start.70
  733.9 2.4 collective-permute-start.75
  742.2 2.9 collective-permute-done.75
  745.1 2.4 collective-permute-done.76
  (661 shorter events, 250.1 us)
Async XLA Ops:
  7.2 124.6 %all-gather.4.cloned.1.call-start = ((), (), s32[]{:S(2)}) async-start(), calls=%async_computation.3 | async-start | bytes 4915200 | tf_op jit(solution)/shard_map/all_gather | solution.py:472
  9.8 15.4 %collective-permute-start.3 = (bf16[82,328]{1,0:T(8,128)(2,1)}, bf16[82,328]{1,0:T(8,128)(2,1)}, u32[]{:S(2)}, u32[]{:S(2)}) collective-permute-start(bf16[82,328]{1,0:T(8,128)(2,1)} %get-tuple-element.249), channel_id=1, source_target_pairs={{0,8},{8,16},{16,24},{24,0},{1,9},{9,17},{17,25},{25,1},{2,10},{10... | collective-permute-start | bytes 161384 | tf_op jit(solution)/shard_map/ppermute | solution.py:145
  12.8 13.9 %collective-permute-start.4 = (bf16[82,328]{1,0:T(8,128)(2,1)}, bf16[82,328]{1,0:T(8,128)(2,1)S(1)}, u32[]{:S(2)}, u32[]{:S(2)}) collective-permute-start(bf16[82,328]{1,0:T(8,128)(2,1)} %get-tuple-element.249), channel_id=1, source_target_pairs={{0,16},{8,24},{16,0},{24,8},{1,17},{9,25},{17,1},{25,9},{2,18},{10... | collective-permute-start | bytes 161384 | tf_op jit(solution)/shard_map/ppermute | solution.py:145
  37.6 30.9 %collective-permute-start.10 = (bf16[2,128,2048]{2,1,0:T(8,128)(2,1)S(1)}, bf16[2,128,2048]{2,1,0:T(8,128)(2,1)S(1)}, u32[]{:S(2)}, u32[]{:S(2)}) collective-permute-start(bf16[2,128,2048]{2,1,0:T(8,128)(2,1)S(1)} %constant_dynamic-slice_fusion.24), channel_id=1, source_target_pairs={{0,2},{2,0},{4,6},{6,4},{1,3},{3,1},{5,7},{7,5},{8,10},{10,8},{12,... | collective-permute-start | bytes 3145736 | tf_op jit(solution)/shard_map/ppermute | solution.py:26
  39.1 31.0 %collective-permute-start.11 = (bf16[2,128,2048]{2,1,0:T(8,128)(2,1)S(1)}, bf16[2,128,2048]{2,1,0:T(8,128)(2,1)}, u32[]{:S(2)}, u32[]{:S(2)}) collective-permute-start(bf16[2,128,2048]{2,1,0:T(8,128)(2,1)S(1)} %constant_dynamic-slice_fusion.24), channel_id=1, source_target_pairs={{0,4},{2,6},{4,0},{6,2},{1,5},{3,7},{5,1},{7,3},{8,12},{10,14},{12... | collective-permute-start | bytes 3145736 | tf_op jit(solution)/shard_map/ppermute | solution.py:26
  42.4 23.6 %collective-permute-start.6 = (bf16[88,328]{1,0:T(8,128)(2,1)}, bf16[88,328]{1,0:T(8,128)(2,1)S(1)}, u32[]{:S(2)}, u32[]{:S(2)}) collective-permute-start(bf16[88,328]{1,0:T(8,128)(2,1)} %get-tuple-element.363), channel_id=1, source_target_pairs={{0,6},{2,4},{4,2},{6,0},{1,7},{3,5},{5,3},{7,1},{8,14},{10,12},{12... | collective-permute-start | bytes 173192 | tf_op jit(solution)/shard_map/ppermute | solution.py:26
  43.6 23.3 %collective-permute-start.7 = (bf16[88,328]{1,0:T(8,128)(2,1)}, bf16[88,328]{1,0:T(8,128)(2,1)S(1)}, u32[]{:S(2)}, u32[]{:S(2)}) collective-permute-start(bf16[88,328]{1,0:T(8,128)(2,1)} %get-tuple-element.364), channel_id=1, source_target_pairs={{0,4},{2,6},{4,0},{6,2},{1,5},{3,7},{5,1},{7,3},{8,12},{10,14},{12... | collective-permute-start | bytes 173192 | tf_op jit(solution)/shard_map/ppermute | solution.py:26
  45.1 22.4 %collective-permute-start.8 = (bf16[88,328]{1,0:T(8,128)(2,1)}, bf16[88,328]{1,0:T(8,128)(2,1)}, u32[]{:S(2)}, u32[]{:S(2)}) collective-permute-start(bf16[88,328]{1,0:T(8,128)(2,1)} %get-tuple-element.362), channel_id=1, source_target_pairs={{0,2},{2,0},{4,6},{6,4},{1,3},{3,1},{5,7},{7,5},{8,10},{10,8},{12,... | collective-permute-start | bytes 173192 | tf_op jit(solution)/shard_map/ppermute | solution.py:26
  45.9 266.9 %all-gather.6.cloned.1.call-start = ((), (), s32[]{:S(2)}) async-start(), calls=%async_computation.7 | async-start | bytes 21233664 | tf_op jit(solution)/shard_map/all_gather | solution.py:474
  79.1 49.4 %collective-permute-start.14 = (bf16[128,2304]{1,0:T(8,128)(2,1)}, bf16[128,2304]{1,0:T(8,128)(2,1)}, u32[]{:S(2)}, u32[]{:S(2)}) collective-permute-start(bf16[128,2304]{1,0:T(8,128)(2,1)} %bitcast.587), channel_id=1, source_target_pairs={{0,6},{2,4},{4,2},{6,0},{1,7},{3,5},{5,3},{7,1},{8,14},{10,12},{12... | collective-permute-start | bytes 1769480 | tf_op jit(solution)/shard_map/ppermute | solution.py:26
  82.8 45.8 %collective-permute-start.15 = (bf16[128,2304]{1,0:T(8,128)(2,1)}, bf16[128,2304]{1,0:T(8,128)(2,1)}, u32[]{:S(2)}, u32[]{:S(2)}) collective-permute-start(bf16[128,2304]{1,0:T(8,128)(2,1)} %bitcast.588), channel_id=1, source_target_pairs={{0,4},{2,6},{4,0},{6,2},{1,5},{3,7},{5,1},{7,3},{8,12},{10,14},{12... | collective-permute-start | bytes 1769480 | tf_op jit(solution)/shard_map/ppermute | solution.py:26
  85.3 43.2 %collective-permute-start.16 = (bf16[128,2304]{1,0:T(8,128)(2,1)}, bf16[128,2304]{1,0:T(8,128)(2,1)}, u32[]{:S(2)}, u32[]{:S(2)}) collective-permute-start(bf16[128,2304]{1,0:T(8,128)(2,1)} %bitcast.589), channel_id=1, source_target_pairs={{0,2},{2,0},{4,6},{6,4},{1,3},{3,1},{5,7},{7,5},{8,10},{10,8},{12,... | collective-permute-start | bytes 1769480 | tf_op jit(solution)/shard_map/ppermute | solution.py:26
  87.7 30.2 %collective-permute-start.12 = (bf16[1,128,2048]{2,1,0:T(8,128)(2,1)}, bf16[1,128,2048]{2,1,0:T(8,128)(2,1)}, u32[]{:S(2)}, u32[]{:S(2)}) collective-permute-start(bf16[1,128,2048]{2,1,0:T(8,128)(2,1)} %slice.487), channel_id=1, source_target_pairs={{0,4},{2,6},{4,0},{6,2},{1,5},{3,7},{5,1},{7,3},{8,12},{10,14},{12... | collective-permute-start | bytes 1572872 | tf_op jit(solution)/shard_map/ppermute | solution.py:26
  89.9 28.0 %collective-permute-start.13 = (bf16[1,128,2048]{2,1,0:T(8,128)(2,1)}, bf16[1,128,2048]{2,1,0:T(8,128)(2,1)}, u32[]{:S(2)}, u32[]{:S(2)}) collective-permute-start(bf16[1,128,2048]{2,1,0:T(8,128)(2,1)} %slice.488), channel_id=1, source_target_pairs={{0,2},{2,0},{4,6},{6,4},{1,3},{3,1},{5,7},{7,5},{8,10},{10,8},{12,... | collective-permute-start | bytes 1572872 | tf_op jit(solution)/shard_map/ppermute | solution.py:26
  131.8 349.9 %reduce-scatter.4.cloned.1.call-start = ((), (), s32[]{:S(2)}) async-start(), calls=%async_computation.4 | async-start | bytes 3932160 | tf_op jit(solution)/shard_map/reduce_scatter | solution.py:123
  132.9 43.5 %collective-permute-start.21 = (bf16[2,2,3,320]{3,2,1,0:T(4,128)(2,1)S(1)}, bf16[2,2,3,320]{3,2,1,0:T(4,128)(2,1)S(1)}, u32[]{:S(2)}, u32[]{:S(2)}) collective-permute-start(bf16[2,2,3,320]{3,2,1,0:T(4,128)(2,1)S(1)} %copy.465), channel_id=1, source_target_pairs={{0,1},{1,0},{2,3},{3,2},{4,5},{5,4},{6,7},{7,6},{8,9},{9,8},{10,11... | collective-permute-start | bytes 23048 | tf_op jit(solution)/shard_map/ppermute | solution.py:110
  135.1 27.6 %collective-permute-start.17 = (bf16[2048,960]{0,1:T(8,128)(2,1)}, bf16[2048,960]{0,1:T(8,128)(2,1)}, u32[]{:S(2)}, u32[]{:S(2)}) collective-permute-start(bf16[2048,960]{0,1:T(8,128)(2,1)} %all-gather.4.cloned.1.call-done), channel_id=1, source_target_pairs={{0,1},{1,0},{2,3},{3,2},{4,5},{5,4},{6,7},{7,6},{8,9},{9,8},{10,11... | collective-permute-start | bytes 11796488 | tf_op jit(solution)/shard_map/ppermute | solution.py:110
  136.8 25.5 %collective-permute-start.18 = (bf16[2,128,2048]{2,1,0:T(8,128)(2,1)S(1)}, bf16[2,128,2048]{2,1,0:T(8,128)(2,1)S(1)}, u32[]{:S(2)}, u32[]{:S(2)}) collective-permute-start(bf16[2,128,2048]{2,1,0:T(8,128)(2,1)S(1)} %fusion.35), channel_id=1, source_target_pairs={{0,2},{2,0},{4,6},{6,4},{1,3},{3,1},{5,7},{7,5},{8,10},{10,8},{12,... | collective-permute-start | bytes 3145736 | tf_op jit(solution)/shard_map/ppermute | solution.py:26
  137.5 25.1 %collective-permute-start.19 = (bf16[2,128,2048]{2,1,0:T(8,128)(2,1)S(1)}, bf16[2,128,2048]{2,1,0:T(8,128)(2,1)S(1)}, u32[]{:S(2)}, u32[]{:S(2)}) collective-permute-start(bf16[2,128,2048]{2,1,0:T(8,128)(2,1)S(1)} %fusion.35), channel_id=1, source_target_pairs={{0,4},{2,6},{4,0},{6,2},{1,5},{3,7},{5,1},{7,3},{8,12},{10,14},{12... | collective-permute-start | bytes 3145736 | tf_op jit(solution)/shard_map/ppermute | solution.py:26
  200.0 26.6 %collective-permute-start.25 = (f32[2,2,640]{2,1,0:T(2,128)S(1)}, f32[2,2,640]{2,1,0:T(2,128)S(1)}, u32[]{:S(2)}, u32[]{:S(2)}) collective-permute-start(f32[2,2,640]{2,1,0:T(2,128)S(1)} %pad_maximum_fusion.31), channel_id=1, source_target_pairs={{0,24},{1,25},{2,26},{3,27},{4,28},{5,29},{6,30},{7,31}} | collective-permute-start | bytes 30728 | tf_op jit(solution)/shard_map/ppermute | solution.py:179
  208.5 20.0 %collective-permute-start.26 = (bf16[1,128,2048]{2,1,0:T(8,128)(2,1)S(1)}, bf16[1,128,2048]{2,1,0:T(8,128)(2,1)S(1)}, u32[]{:S(2)}, u32[]{:S(2)}) collective-permute-start(bf16[1,128,2048]{2,1,0:T(8,128)(2,1)S(1)} %slice.522), channel_id=1, source_target_pairs={{0,4},{2,6},{4,0},{6,2},{1,5},{3,7},{5,1},{7,3},{8,12},{10,14},{12... | collective-permute-start | bytes 1572872 | tf_op jit(solution)/shard_map/ppermute | solution.py:26
  210.3 18.2 %collective-permute-start.27 = (bf16[1,128,2048]{2,1,0:T(8,128)(2,1)S(1)}, bf16[1,128,2048]{2,1,0:T(8,128)(2,1)S(1)}, u32[]{:S(2)}, u32[]{:S(2)}) collective-permute-start(bf16[1,128,2048]{2,1,0:T(8,128)(2,1)S(1)} %slice.523), channel_id=1, source_target_pairs={{0,2},{2,0},{4,6},{6,4},{1,3},{3,1},{5,7},{7,5},{8,10},{10,8},{12,... | collective-permute-start | bytes 1572872 | tf_op jit(solution)/shard_map/ppermute | solution.py:26
  211.6 15.1 %collective-permute-start.23 = (f32[2,2,640]{2,1,0:T(2,128)S(1)}, f32[2,2,640]{2,1,0:T(2,128)S(1)}, u32[]{:S(2)}, u32[]{:S(2)}) collective-permute-start(f32[2,2,640]{2,1,0:T(2,128)S(1)} %pad_maximum_fusion.31), channel_id=1, source_target_pairs={{0,8},{8,16},{16,24},{1,9},{9,17},{17,25},{2,10},{10,18},{18,26},{... | collective-permute-start | bytes 30728 | tf_op jit(solution)/shard_map/ppermute | solution.py:179
  212.9 13.8 %collective-permute-start.24 = (f32[2,2,640]{2,1,0:T(2,128)S(1)}, f32[2,2,640]{2,1,0:T(2,128)S(1)}, u32[]{:S(2)}, u32[]{:S(2)}) collective-permute-start(f32[2,2,640]{2,1,0:T(2,128)S(1)} %pad_maximum_fusion.31), channel_id=1, source_target_pairs={{0,16},{8,24},{1,17},{9,25},{2,18},{10,26},{3,19},{11,27},{4,20},{... | collective-permute-start | bytes 30728 | tf_op jit(solution)/shard_map/ppermute | solution.py:179
  235.1 12.5 %collective-permute-start.30 = (bf16[1,128,2048]{2,1,0:T(8,128)(2,1)S(1)}, bf16[1,128,2048]{2,1,0:T(8,128)(2,1)S(1)}, u32[]{:S(2)}, u32[]{:S(2)}) collective-permute-start(bf16[1,128,2048]{2,1,0:T(8,128)(2,1)S(1)} %get-tuple-element.283), channel_id=1, source_target_pairs={{0,2},{2,0},{4,6},{6,4},{1,3},{3,1},{5,7},{7,5},{8,10},{10,8},{12,... | collective-permute-start | bytes 1572872 | tf_op jit(solution)/shard_map/ppermute | solution.py:26
  248.0 23.0 %collective-permute-start.29 = (bf16[2,128,2048]{2,1,0:T(8,128)(2,1)S(1)}, bf16[2,128,2048]{2,1,0:T(8,128)(2,1)S(1)}, u32[]{:S(2)}, u32[]{:S(2)}) collective-permute-start(bf16[2,128,2048]{2,1,0:T(8,128)(2,1)S(1)} %pad_maximum_fusion.13), channel_id=1, source_target_pairs={{0,2},{2,0},{4,6},{6,4},{1,3},{3,1},{5,7},{7,5},{8,10},{10,8},{12,... | collective-permute-start | bytes 3145736 | tf_op jit(solution)/shard_map/ppermute | solution.py:26
  248.7 22.8 %collective-permute-start.31 = (bf16[2,128,2048]{2,1,0:T(8,128)(2,1)S(1)}, bf16[2,128,2048]{2,1,0:T(8,128)(2,1)S(1)}, u32[]{:S(2)}, u32[]{:S(2)}) collective-permute-start(bf16[2,128,2048]{2,1,0:T(8,128)(2,1)S(1)} %pad_maximum_fusion.14), channel_id=1, source_target_pairs={{0,4},{2,6},{4,0},{6,2},{1,5},{3,7},{5,1},{7,3},{8,12},{10,14},{12... | collective-permute-start | bytes 3145736 | tf_op jit(solution)/shard_map/ppermute | solution.py:26
  276.8 22.2 %collective-permute-start.32 = (bf16[2,128,2048]{2,1,0:T(8,128)(2,1)}, bf16[2,128,2048]{2,1,0:T(8,128)(2,1)}, u32[]{:S(2)}, u32[]{:S(2)}) collective-permute-start(bf16[2,128,2048]{2,1,0:T(8,128)(2,1)} %get-tuple-element.245), channel_id=1, source_target_pairs={{0,2},{2,0},{4,6},{6,4},{1,3},{3,1},{5,7},{7,5},{8,10},{10,8},{12,... | collective-permute-start | bytes 3145736 | tf_op jit(solution)/shard_map/ppermute | solution.py:26
  278.2 23.1 %collective-permute-start.33 = (bf16[2,128,2048]{2,1,0:T(8,128)(2,1)}, bf16[2,128,2048]{2,1,0:T(8,128)(2,1)}, u32[]{:S(2)}, u32[]{:S(2)}) collective-permute-start(bf16[2,128,2048]{2,1,0:T(8,128)(2,1)} %get-tuple-element.245), channel_id=1, source_target_pairs={{0,4},{2,6},{4,0},{6,2},{1,5},{3,7},{5,1},{7,3},{8,12},{10,14},{12... | collective-permute-start | bytes 3145736 | tf_op jit(solution)/shard_map/ppermute | solution.py:26
  374.8 22.9 %collective-permute-start.45 = (bf16[2048,768]{1,0:T(8,128)(2,1)}, bf16[2048,768]{1,0:T(8,128)(2,1)}, u32[]{:S(2)}, u32[]{:S(2)}) collective-permute-start(bf16[2048,768]{1,0:T(8,128)(2,1)} %convolution_convert_fusion.4), channel_id=1, source_target_pairs={{0,1},{1,0},{2,3},{3,2},{4,5},{5,4},{6,7},{7,6},{8,9},{9,8},{10,11... | collective-permute-start | bytes 9437192 | tf_op jit(solution)/shard_map/ppermute | solution.py:110
  376.0 14.6 %collective-permute-start.36 = (bf16[1,128,2048]{2,1,0:T(8,128)(2,1)}, bf16[1,128,2048]{2,1,0:T(8,128)(2,1)}, u32[]{:S(2)}, u32[]{:S(2)}) collective-permute-start(bf16[1,128,2048]{2,1,0:T(8,128)(2,1)} %get-tuple-element.275), channel_id=1, source_target_pairs={{0,4},{2,6},{4,0},{6,2},{1,5},{3,7},{5,1},{7,3},{8,12},{10,14},{12... | collective-permute-start | bytes 1572872 | tf_op jit(solution)/shard_map/ppermute | solution.py:26
  377.1 14.4 %collective-permute-start.38 = (bf16[1,128,2048]{2,1,0:T(8,128)(2,1)}, bf16[1,128,2048]{2,1,0:T(8,128)(2,1)}, u32[]{:S(2)}, u32[]{:S(2)}) collective-permute-start(bf16[1,128,2048]{2,1,0:T(8,128)(2,1)} %get-tuple-element.277), channel_id=1, source_target_pairs={{0,2},{2,0},{4,6},{6,4},{1,3},{3,1},{5,7},{7,5},{8,10},{10,8},{12,... | collective-permute-start | bytes 1572872 | tf_op jit(solution)/shard_map/ppermute | solution.py:26
  387.3 83.6 %collective-permute-start.44 = (bf16[2048,1536]{1,0:T(8,128)(2,1)}, bf16[2048,1536]{1,0:T(8,128)(2,1)}, u32[]{:S(2)}, u32[]{:S(2)}) collective-permute-start(bf16[2048,1536]{1,0:T(8,128)(2,1)} %convolution_convert_fusion.1), channel_id=1, source_target_pairs={{0,1},{1,0},{2,3},{3,2},{4,5},{5,4},{6,7},{7,6},{8,9},{9,8},{10,11... | collective-permute-start | bytes 18874376 | tf_op jit(solution)/shard_map/ppermute | solution.py:110
  394.6 24.8 %collective-permute-start.37 = (bf16[2,128,2048]{2,1,0:T(8,128)(2,1)}, bf16[2,128,2048]{2,1,0:T(8,128)(2,1)}, u32[]{:S(2)}, u32[]{:S(2)}) collective-permute-start(bf16[2,128,2048]{2,1,0:T(8,128)(2,1)} %pad_maximum_fusion.15), channel_id=1, source_target_pairs={{0,2},{2,0},{4,6},{6,4},{1,3},{3,1},{5,7},{7,5},{8,10},{10,8},{12,... | collective-permute-start | bytes 3145736 | tf_op jit(solution)/shard_map/ppermute | solution.py:26
  396.7 24.5 %collective-permute-start.39 = (bf16[2,128,2048]{2,1,0:T(8,128)(2,1)}, bf16[2,128,2048]{2,1,0:T(8,128)(2,1)}, u32[]{:S(2)}, u32[]{:S(2)}) collective-permute-start(bf16[2,128,2048]{2,1,0:T(8,128)(2,1)} %pad_maximum_fusion.16), channel_id=1, source_target_pairs={{0,4},{2,6},{4,0},{6,2},{1,5},{3,7},{5,1},{7,3},{8,12},{10,14},{12... | collective-permute-start | bytes 3145736 | tf_op jit(solution)/shard_map/ppermute | solution.py:26
  404.6 186.3 %reduce-scatter.6.cloned.1.call-start = ((), (), s32[]{:S(2)}) async-start(), calls=%async_computation.5 | async-start | bytes 7864320 | tf_op jit(solution)/shard_map/reduce_scatter | solution.py:123
  432.1 23.7 %collective-permute-start.40 = (bf16[2,128,2048]{2,1,0:T(8,128)(2,1)}, bf16[2,128,2048]{2,1,0:T(8,128)(2,1)}, u32[]{:S(2)}, u32[]{:S(2)}) collective-permute-start(bf16[2,128,2048]{2,1,0:T(8,128)(2,1)} %get-tuple-element.242), channel_id=1, source_target_pairs={{0,2},{2,0},{4,6},{6,4},{1,3},{3,1},{5,7},{7,5},{8,10},{10,8},{12,... | collective-permute-start | bytes 3145736 | tf_op jit(solution)/shard_map/ppermute | solution.py:26
  433.2 24.7 %collective-permute-start.41 = (bf16[2,128,2048]{2,1,0:T(8,128)(2,1)}, bf16[2,128,2048]{2,1,0:T(8,128)(2,1)}, u32[]{:S(2)}, u32[]{:S(2)}) collective-permute-start(bf16[2,128,2048]{2,1,0:T(8,128)(2,1)} %get-tuple-element.242), channel_id=1, source_target_pairs={{0,4},{2,6},{4,0},{6,2},{1,5},{3,7},{5,1},{7,3},{8,12},{10,14},{12... | collective-permute-start | bytes 3145736 | tf_op jit(solution)/shard_map/ppermute | solution.py:26
  481.7 237.6 %reduce-scatter.8.cloned.1.call-start = ((), (), s32[]{:S(2)}) async-start(), calls=%async_computation.6 | async-start | bytes 4915200 | tf_op jit(solution)/shard_map/reduce_scatter | solution.py:123
  502.2 18.9 %collective-permute-start.46 = (f32[2,2,640]{2,1,0:T(2,128)S(1)}, f32[2,2,640]{2,1,0:T(2,128)S(1)}, u32[]{:S(2)}, u32[]{:S(2)}) collective-permute-start(f32[2,2,640]{2,1,0:T(2,128)S(1)} %copy.415), channel_id=1, source_target_pairs={{8,0},{16,8},{24,16},{9,1},{17,9},{25,17},{10,2},{18,10},{26,18},{... | collective-permute-start | bytes 30728 | tf_op jit(solution)/shard_map/ppermute | solution.py:179
  503.5 19.0 %collective-permute-start.47 = (f32[2,2,640]{2,1,0:T(2,128)S(1)}, f32[2,2,640]{2,1,0:T(2,128)S(1)}, u32[]{:S(2)}, u32[]{:S(2)}) collective-permute-start(f32[2,2,640]{2,1,0:T(2,128)S(1)} %copy.415), channel_id=1, source_target_pairs={{16,0},{24,8},{17,1},{25,9},{18,2},{26,10},{19,3},{27,11},{20,4},{... | collective-permute-start | bytes 30728 | tf_op jit(solution)/shard_map/ppermute | solution.py:179
  504.8 14.9 %collective-permute-start.48 = (f32[2,2,640]{2,0,1:T(2,128)S(1)}, f32[2,2,640]{2,0,1:T(2,128)S(1)}, u32[]{:S(2)}, u32[]{:S(2)}) collective-permute-start(f32[2,2,640]{2,0,1:T(2,128)S(1)} %pad_maximum_fusion.32), channel_id=1, source_target_pairs={{24,0},{25,1},{26,2},{27,3},{28,4},{29,5},{30,6},{31,7}} | collective-permute-start | bytes 30728 | tf_op jit(solution)/shard_map/ppermute | solution.py:179
  507.4 16.0 %collective-permute-start.49 = (bf16[1,128,2048]{2,1,0:T(8,128)(2,1)S(1)}, bf16[1,128,2048]{2,1,0:T(8,128)(2,1)S(1)}, u32[]{:S(2)}, u32[]{:S(2)}) collective-permute-start(bf16[1,128,2048]{2,1,0:T(8,128)(2,1)S(1)} %get-tuple-element.273), channel_id=1, source_target_pairs={{0,2},{2,0},{4,6},{6,4},{1,3},{3,1},{5,7},{7,5},{8,10},{10,8},{12,... | collective-permute-start | bytes 1572872 | tf_op jit(solution)/shard_map/ppermute | solution.py:26
  508.3 15.0 %collective-permute-start.50 = (bf16[1,128,2048]{2,1,0:T(8,128)(2,1)S(1)}, bf16[1,128,2048]{2,1,0:T(8,128)(2,1)}, u32[]{:S(2)}, u32[]{:S(2)}) collective-permute-start(bf16[1,128,2048]{2,1,0:T(8,128)(2,1)S(1)} %get-tuple-element.272), channel_id=1, source_target_pairs={{0,4},{2,6},{4,0},{6,2},{1,5},{3,7},{5,1},{7,3},{8,12},{10,14},{12... | collective-permute-start | bytes 1572872 | tf_op jit(solution)/shard_map/ppermute | solution.py:26
  519.7 31.9 %collective-permute-start.54 = (bf16[128,768]{0,1:T(8,128)(2,1)}, bf16[128,768]{0,1:T(8,128)(2,1)}, u32[]{:S(2)}, u32[]{:S(2)}) collective-permute-start(bf16[128,768]{0,1:T(8,128)(2,1)} %bitcast.149), channel_id=1, source_target_pairs={{0,6},{2,4},{4,2},{6,0},{1,7},{3,5},{5,3},{7,1},{8,14},{10,12},{12... | collective-permute-start | bytes 589832 | tf_op jit(solution)/shard_map/ppermute | solution.py:26
  521.1 32.0 %collective-permute-start.55 = (bf16[128,768]{0,1:T(8,128)(2,1)}, bf16[128,768]{0,1:T(8,128)(2,1)}, u32[]{:S(2)}, u32[]{:S(2)}) collective-permute-start(bf16[128,768]{0,1:T(8,128)(2,1)} %bitcast.150), channel_id=1, source_target_pairs={{0,4},{2,6},{4,0},{6,2},{1,5},{3,7},{5,1},{7,3},{8,12},{10,14},{12... | collective-permute-start | bytes 589832 | tf_op jit(solution)/shard_map/ppermute | solution.py:26
  522.5 30.6 %collective-permute-start.56 = (bf16[128,768]{0,1:T(8,128)(2,1)}, bf16[128,768]{0,1:T(8,128)(2,1)}, u32[]{:S(2)}, u32[]{:S(2)}) collective-permute-start(bf16[128,768]{0,1:T(8,128)(2,1)} %bitcast.151), channel_id=1, source_target_pairs={{0,2},{2,0},{4,6},{6,4},{1,3},{3,1},{5,7},{7,5},{8,10},{10,8},{12,... | collective-permute-start | bytes 589832 | tf_op jit(solution)/shard_map/ppermute | solution.py:26
  526.8 32.8 %collective-permute-start.52 = (bf16[2,128,2048]{2,1,0:T(8,128)(2,1)S(1)}, bf16[2,128,2048]{2,1,0:T(8,128)(2,1)}, u32[]{:S(2)}, u32[]{:S(2)}) collective-permute-start(bf16[2,128,2048]{2,1,0:T(8,128)(2,1)S(1)} %pad_maximum_fusion.17), channel_id=1, source_target_pairs={{0,2},{2,0},{4,6},{6,4},{1,3},{3,1},{5,7},{7,5},{8,10},{10,8},{12,... | collective-permute-start | bytes 3145736 | tf_op jit(solution)/shard_map/ppermute | solution.py:26
  529.2 30.4 %collective-permute-start.53 = (bf16[2,128,2048]{2,1,0:T(8,128)(2,1)}, bf16[2,128,2048]{2,1,0:T(8,128)(2,1)}, u32[]{:S(2)}, u32[]{:S(2)}) collective-permute-start(bf16[2,128,2048]{2,1,0:T(8,128)(2,1)} %pad_maximum_fusion.18), channel_id=1, source_target_pairs={{0,4},{2,6},{4,0},{6,2},{1,5},{3,7},{5,1},{7,3},{8,12},{10,14},{12... | collective-permute-start | bytes 3145736 | tf_op jit(solution)/shard_map/ppermute | solution.py:26
  603.7 23.6 %collective-permute-start.58 = (bf16[2048,960]{0,1:T(8,128)(2,1)}, bf16[2048,960]{0,1:T(8,128)(2,1)}, u32[]{:S(2)}, u32[]{:S(2)}) collective-permute-start(bf16[2048,960]{0,1:T(8,128)(2,1)} %pad_maximum_fusion.1), channel_id=1, source_target_pairs={{0,1},{1,0},{2,3},{3,2},{4,5},{5,4},{6,7},{7,6},{8,9},{9,8},{10,11... | collective-permute-start | bytes 11796488 | tf_op jit(solution)/shard_map/ppermute | solution.py:110
  625.2 45.7 %collective-permute-start.57 = (bf16[2,128,2048]{2,1,0:T(8,128)(2,1)}, bf16[2,128,2048]{2,1,0:T(8,128)(2,1)}, u32[]{:S(2)}, u32[]{:S(2)}) collective-permute-start(bf16[2,128,2048]{2,1,0:T(8,128)(2,1)} %get-tuple-element.236), channel_id=1, source_target_pairs={{0,1},{1,0},{2,3},{3,2},{4,5},{5,4},{6,7},{7,6},{8,9},{9,8},{10,11... | collective-permute-start | bytes 3145736 | tf_op jit(solution)/shard_map/ppermute | solution.py:110
  644.8 15.1 %collective-permute-start.59 = (bf16[1,128,2048]{2,1,0:T(8,128)(2,1)}, bf16[1,128,2048]{2,1,0:T(8,128)(2,1)}, u32[]{:S(2)}, u32[]{:S(2)}) collective-permute-start(bf16[1,128,2048]{2,1,0:T(8,128)(2,1)} %get-tuple-element.263), channel_id=1, source_target_pairs={{0,4},{2,6},{4,0},{6,2},{1,5},{3,7},{5,1},{7,3},{8,12},{10,14},{12... | collective-permute-start | bytes 1572872 | tf_op jit(solution)/shard_map/ppermute | solution.py:26
  646.3 15.0 %collective-permute-start.61 = (bf16[1,128,2048]{2,1,0:T(8,128)(2,1)}, bf16[1,128,2048]{2,1,0:T(8,128)(2,1)}, u32[]{:S(2)}, u32[]{:S(2)}) collective-permute-start(bf16[1,128,2048]{2,1,0:T(8,128)(2,1)} %get-tuple-element.265), channel_id=1, source_target_pairs={{0,2},{2,0},{4,6},{6,4},{1,3},{3,1},{5,7},{7,5},{8,10},{10,8},{12,... | collective-permute-start | bytes 1572872 | tf_op jit(solution)/shard_map/ppermute | solution.py:26
  651.7 17.6 %collective-permute-start.66 = (f32[2,2048]{1,0:T(2,128)S(1)}, f32[2,2048]{1,0:T(2,128)S(1)}, u32[]{:S(2)}, u32[]{:S(2)}) collective-permute-start(f32[2,2048]{1,0:T(2,128)S(1)} %fusion.143), channel_id=1, source_target_pairs={{0,2},{2,0},{4,6},{6,4},{1,3},{3,1},{5,7},{7,5},{8,10},{10,8},{12,... | collective-permute-start | bytes 49160 | tf_op jit(solution)/shard_map/ppermute | solution.py:156
  664.3 27.6 %collective-permute-start.60 = (bf16[2,128,2048]{2,1,0:T(8,128)(2,1)}, bf16[2,128,2048]{2,1,0:T(8,128)(2,1)}, u32[]{:S(2)}, u32[]{:S(2)}) collective-permute-start(bf16[2,128,2048]{2,1,0:T(8,128)(2,1)} %pad_maximum_fusion.19), channel_id=1, source_target_pairs={{0,2},{2,0},{4,6},{6,4},{1,3},{3,1},{5,7},{7,5},{8,10},{10,8},{12,... | collective-permute-start | bytes 3145736 | tf_op jit(solution)/shard_map/ppermute | solution.py:26
  666.8 25.1 %collective-permute-start.62 = (bf16[2,128,2048]{2,1,0:T(8,128)(2,1)}, bf16[2,128,2048]{2,1,0:T(8,128)(2,1)}, u32[]{:S(2)}, u32[]{:S(2)}) collective-permute-start(bf16[2,128,2048]{2,1,0:T(8,128)(2,1)} %pad_maximum_fusion.20), channel_id=1, source_target_pairs={{0,4},{2,6},{4,0},{6,2},{1,5},{3,7},{5,1},{7,3},{8,12},{10,14},{12... | collective-permute-start | bytes 3145736 | tf_op jit(solution)/shard_map/ppermute | solution.py:26
  669.3 22.5 %collective-permute-start.64 = (bf16[320,368]{1,0:T(8,128)(2,1)S(1)}, bf16[320,368]{1,0:T(8,128)(2,1)S(1)}, u32[]{:S(2)}, u32[]{:S(2)}) collective-permute-start(bf16[320,368]{1,0:T(8,128)(2,1)S(1)} %slice.688), channel_id=1, source_target_pairs={{0,1},{1,0},{2,3},{3,2},{4,5},{5,4},{6,7},{7,6},{8,9},{9,8},{10,11... | collective-permute-start | bytes 706568 | tf_op jit(solution)/shard_map/ppermute | solution.py:110
  669.4 22.4 %collective-permute-start.67 = (f32[2,2048]{1,0:T(2,128)S(1)}, f32[2,2048]{1,0:T(2,128)S(1)}, u32[]{:S(2)}, u32[]{:S(2)}) collective-permute-start(f32[2,2048]{1,0:T(2,128)S(1)} %fusion.182), channel_id=1, source_target_pairs={{0,4},{2,6},{4,0},{6,2},{1,5},{3,7},{5,1},{7,3},{8,12},{10,14},{12... | collective-permute-start | bytes 49160 | tf_op jit(solution)/shard_map/ppermute | solution.py:156
  694.6 13.0 %collective-permute-start.78 = (bf16[128,1536]{1,0:T(8,128)(2,1)S(1)}, bf16[128,1536]{1,0:T(8,128)(2,1)S(1)}, u32[]{:S(2)}, u32[]{:S(2)}) collective-permute-start(bf16[128,1536]{1,0:T(8,128)(2,1)S(1)} %get-tuple-element.328), channel_id=1, source_target_pairs={{0,6},{2,4},{4,2},{6,0},{1,7},{3,5},{5,3},{7,1},{8,14},{10,12},{12... | collective-permute-start | bytes 1179656 | tf_op jit(solution)/shard_map/ppermute | solution.py:26
  695.3 17.6 %collective-permute-start.79 = (bf16[128,1536]{1,0:T(8,128)(2,1)S(1)}, bf16[128,1536]{1,0:T(8,128)(2,1)S(1)}, u32[]{:S(2)}, u32[]{:S(2)}) collective-permute-start(bf16[128,1536]{1,0:T(8,128)(2,1)S(1)} %get-tuple-element.327), channel_id=1, source_target_pairs={{0,4},{2,6},{4,0},{6,2},{1,5},{3,7},{5,1},{7,3},{8,12},{10,14},{12... | collective-permute-start | bytes 1179656 | tf_op jit(solution)/shard_map/ppermute | solution.py:26
  696.7 16.2 %collective-permute-start.80 = (bf16[128,1536]{1,0:T(8,128)(2,1)S(1)}, bf16[128,1536]{1,0:T(8,128)(2,1)S(1)}, u32[]{:S(2)}, u32[]{:S(2)}) collective-permute-start(bf16[128,1536]{1,0:T(8,128)(2,1)S(1)} %get-tuple-element.326), channel_id=1, source_target_pairs={{0,2},{2,0},{4,6},{6,4},{1,3},{3,1},{5,7},{7,5},{8,10},{10,8},{12,... | collective-permute-start | bytes 1179656 | tf_op jit(solution)/shard_map/ppermute | solution.py:26
  701.9 13.9 %collective-permute-start.63 = (bf16[2,128,2048]{2,1,0:T(8,128)(2,1)S(1)}, bf16[2,128,2048]{2,1,0:T(8,128)(2,1)S(1)}, u32[]{:S(2)}, u32[]{:S(2)}) collective-permute-start(bf16[2,128,2048]{2,1,0:T(8,128)(2,1)S(1)} %get-tuple-element.234), channel_id=1, source_target_pairs={{0,1},{1,0},{2,3},{3,2},{4,5},{5,4},{6,7},{7,6},{8,9},{9,8},{10,11... | collective-permute-start | bytes 3145736 | tf_op jit(solution)/shard_map/ppermute | solution.py:110
  720.6 13.3 %collective-permute-start.73 = (f32[2,2048]{1,0:T(2,128)S(1)}, f32[2,2048]{1,0:T(2,128)S(1)}, u32[]{:S(2)}, u32[]{:S(2)}) collective-permute-start(f32[2,2048]{1,0:T(2,128)S(1)} %add.762), channel_id=1, source_target_pairs={{0,16},{8,24},{16,0},{24,8},{1,17},{9,25},{17,1},{25,9},{2,18},{10... | collective-permute-start | bytes 49160 | tf_op jit(solution)/shard_map/ppermute | solution.py:145
  722.3 14.4 %collective-permute-start.74 = (f32[2,2048]{1,0:T(2,128)S(1)}, f32[2,2048]{1,0:T(2,128)S(1)}, u32[]{:S(2)}, u32[]{:S(2)}) collective-permute-start(f32[2,2048]{1,0:T(2,128)S(1)} %add.762), channel_id=1, source_target_pairs={{0,24},{8,0},{16,8},{24,16},{1,25},{9,1},{17,9},{25,17},{2,26},{10... | collective-permute-start | bytes 49160 | tf_op jit(solution)/shard_map/ppermute | solution.py:145
  (150 other events, 1749.2 us)
Sparse Core Ops, SparseCore 0:
  46.0 73.5 all-gather.3
  131.9 165.6 all-gather.5
  404.7 57.4 reduce-scatter.3
  481.9 108.9 reduce-scatter.5
  647.9 71.3 reduce-scatter.7
